TPU v7x, 32 devices: a whole 2x2x4 slice. The times are simulated.
32 devices in a mesh: dp: 8 (over z, y), tensor: 4 (over x, core).
Axes of the slice: x: 2, y: 2, z: 4, core: 2. Of those that a mesh axis runs over, the one named last changes fastest.
Arguments:
- table_cells: bfloat16 [8, 32, 89, 512], P('dp'), may hold values from -6 to 6
- splits: int32 [8], P('dp'), may hold values from 2 to 30, as said below
- feat_qkv: bfloat16 [512, 3, 512], P(None, None, 'tensor'), may hold values from -0.25 to 0.25
- feat_out: bfloat16 [512, 512], P('tensor'), may hold values from -1 to 1
- feat_out_bias: bfloat16 [512], replicated, may hold values from -1.5 to 1.5
- row_qkv: bfloat16 [512, 3, 512], P(None, None, 'tensor'), may hold values from -0.25 to 0.25
- row_out: bfloat16 [512, 512], P('tensor'), may hold values from -1 to 1
- row_out_bias: bfloat16 [512], replicated, may hold values from -1.5 to 1.5
- up_weight: bfloat16 [512, 2048], P(None, 'tensor'), may hold values from -0.25 to 0.25
- up_bias: bfloat16 [2048], P('tensor'), may hold values from -2.5 to 2.5
- down_weight: bfloat16 [2048, 512], P('tensor'), may hold values from -0.125 to 0.125
- down_bias: bfloat16 [512], replicated, may hold values from -1.5 to 1.5
- norm_gains: bfloat16 [3, 512], replicated, may hold values from 0.5 to 1.5
- norm_biases: bfloat16 [3, 512], replicated, may hold values from -1.5 to 1.5
- cotangent: bfloat16 [8, 32, 89, 512], P('dp'), may hold values from -6 to 6
Outputs:
- output: bfloat16 [8, 32, 89, 512], P('dp')
- input_grad: bfloat16 [8, 32, 89, 512], P('dp')
- feat_qkv_grad: float32 [512, 3, 512], P(None, None, 'tensor')
- feat_out_grad: float32 [512, 512], P('tensor')
- feat_out_bias_grad: float32 [512], replicated
- row_qkv_grad: float32 [512, 3, 512], P(None, None, 'tensor')
- row_out_grad: float32 [512, 512], P('tensor')
- row_out_bias_grad: float32 [512], replicated
- up_weight_grad: float32 [512, 2048], P(None, 'tensor')
- up_bias_grad: float32 [2048], P('tensor')
- down_weight_grad: float32 [2048, 512], P('tensor')
- down_bias_grad: float32 [512], replicated
- norm_gains_grad: float32 [3, 512], replicated
- norm_biases_grad: float32 [3, 512], replicated
Inputs may be any that keep to these rules, and one draw needn't show every extreme that they name: `splits`: a table's context rows are rows 0 to split - 1; every draw holds a table with the fewest and a table with the most.
All inputs are finite; a program needn't handle non-finite values.
Results may differ from a plain program's by a relative error of at most 0.028.
Values may be sent and summed in bfloat16 or wider, within the bound.
No kernel may reach another device: no remote copies, remote signals or barrier semaphores. Data moves between devices by JAX's collectives and lax.ppermute only.
A program may use at most 192 MiB of HBM per device.

v0:
```python
from functools import partial

import jax
import jax.numpy as jnp
from jax import lax
from jax.sharding import PartitionSpec as P

HD = 128


EPSILON = 1e-05
NEGATIVE = -1e30
FEATURE_SPECS = ("brfhe,brghe->brhfg", "brhfg,brghe->brfhe", "brhfg,brfhe->brghe")
ROW_SPECS = ("brfhe,btfhe->bfhrt", "bfhrt,btfhe->brfhe", "bfhrt,brfhe->btfhe")


def standardize(values):
    centered = values - jnp.mean(values, axis=-1, keepdims=True)
    inverse = lax.rsqrt(jnp.mean(centered * centered, axis=-1, keepdims=True) + EPSILON)
    return (centered * inverse, inverse)


def norm_backward(upstream, normed, inverse, gain):
    scaled = upstream * gain
    return inverse * (
        scaled
        - jnp.mean(scaled, axis=-1, keepdims=True)
        - normed * jnp.mean(scaled * normed, axis=-1, keepdims=True)
    )


def branch_total(partial_out):
    return lax.psum(partial_out.astype(jnp.bfloat16), "tensor").astype(jnp.float32)


def row_share(values):
    share_rows = values.shape[0] // lax.axis_size("tensor")
    return lax.dynamic_slice_in_dim(values, lax.axis_index("tensor") * share_rows, share_rows, 0)


def reduce_back(normed_grad, normed, inverse, gain, upstream):
    share_grad = lax.psum_scatter(
        normed_grad.astype(jnp.bfloat16), "tensor", scatter_dimension=0, tiled=True
    ).astype(jnp.float32)
    share_normed = row_share(normed)
    share_stream = row_share(upstream) + norm_backward(
        share_grad, share_normed, row_share(inverse), gain
    )
    stream_grad = lax.all_gather(
        share_stream.astype(jnp.bfloat16), "tensor", axis=0, tiled=True
    ).astype(share_stream.dtype)
    return (stream_grad, jnp.sum(share_grad * share_normed, axis=0), jnp.sum(share_grad, axis=0))


def split_heads(normed_rows, qkv_weight, cell_shape):
    packed = jnp.einsum(
        "nd,dck->nck", normed_rows, qkv_weight, preferred_element_type=jnp.float32
    ).astype(jnp.bfloat16)
    packed = packed.reshape(cell_shape[0], cell_shape[1], cell_shape[2], 3, -1, HD)
    return (packed[:, :, :, 0], packed[:, :, :, 1], packed[:, :, :, 2])


def scores_of(queries, key_heads, einsum_specs, allowed):
    scores = jnp.einsum(
        einsum_specs[0], queries, key_heads, preferred_element_type=jnp.float32
    ) * HD ** (-0.5)
    if allowed is not None:
        scores = jnp.where(allowed, scores, NEGATIVE)
    return scores


def attend_forward(normed_rows, qkv_weight, cell_shape, einsum_specs, allowed):
    queries, key_heads, values = split_heads(normed_rows, qkv_weight, cell_shape)
    scores = scores_of(queries, key_heads, einsum_specs, allowed)
    logsum = jax.nn.logsumexp(scores, axis=-1, keepdims=True)
    weights = jnp.exp(scores - logsum).astype(jnp.bfloat16)
    mixed_heads = jnp.einsum(
        einsum_specs[1], weights, values, preferred_element_type=jnp.float32
    ).astype(jnp.bfloat16)
    return (mixed_heads.reshape(normed_rows.shape[0], -1), logsum)


def attend_backward(
    normed_rows, qkv_weight, out_weight, logsum, upstream, cell_shape, einsum_specs, allowed
):
    queries, key_heads, values = split_heads(normed_rows, qkv_weight, cell_shape)
    scores = scores_of(queries, key_heads, einsum_specs, allowed)
    probabilities = jnp.exp(scores - logsum)
    weights = probabilities.astype(jnp.bfloat16)
    mixed_heads = jnp.einsum(
        einsum_specs[1], weights, values, preferred_element_type=jnp.float32
    ).astype(jnp.bfloat16)
    cell_count = normed_rows.shape[0]
    upstream_low = upstream.astype(jnp.bfloat16)
    out_grad = jnp.einsum(
        "nk,nd->kd",
        mixed_heads.reshape(cell_count, -1),
        upstream_low,
        preferred_element_type=jnp.float32,
    )
    mixed_grad = (
        jnp.einsum("nd,kd->nk", upstream_low, out_weight, preferred_element_type=jnp.float32)
        .astype(jnp.bfloat16)
        .reshape(mixed_heads.shape)
    )
    prob_grad = jnp.einsum(einsum_specs[0], mixed_grad, values, preferred_element_type=jnp.float32)
    score_grad = probabilities * (
        prob_grad - jnp.sum(prob_grad * probabilities, axis=-1, keepdims=True)
    )
    score_grad = score_grad.astype(jnp.bfloat16)
    score_scale = HD ** (-0.5)
    query_grad = (
        jnp.einsum(einsum_specs[1], score_grad, key_heads, preferred_element_type=jnp.float32)
        * score_scale
    )
    key_grad = (
        jnp.einsum(einsum_specs[2], score_grad, queries, preferred_element_type=jnp.float32)
        * score_scale
    )
    value_grad = jnp.einsum(
        einsum_specs[2], weights, mixed_grad, preferred_element_type=jnp.float32
    )
    packed_grad = jnp.stack([query_grad, key_grad, value_grad], axis=3).astype(jnp.bfloat16)
    packed_grad = packed_grad.reshape(cell_count, 3, -1)
    weight_grad = jnp.einsum(
        "nd,nck->dck", normed_rows, packed_grad, preferred_element_type=jnp.float32
    )
    normed_grad = jnp.einsum(
        "nck,dck->nd", packed_grad, qkv_weight, preferred_element_type=jnp.float32
    )
    return (weight_grad, out_grad, normed_grad)


def shards(
    table_cells,
    splits,
    feat_qkv,
    feat_out,
    feat_out_bias,
    row_qkv,
    row_out,
    row_out_bias,
    up_weight,
    up_bias,
    down_weight,
    down_bias,
    norm_gains,
    norm_biases,
    cotangent,
):
    cell_shape = table_cells.shape
    row_count = cell_shape[1]
    cell_count = cell_shape[0] * cell_shape[1] * cell_shape[2]
    model_width = cell_shape[3]
    norm_gain = norm_gains.astype(jnp.float32)
    norm_shift = norm_biases.astype(jnp.float32)
    allowed = (jnp.arange(row_count)[None, :] < splits[:, None]).reshape(
        cell_shape[0], 1, 1, 1, row_count
    )
    stream_zero = table_cells.astype(jnp.float32).reshape(cell_count, model_width)
    normed_zero, inverse_zero = standardize(stream_zero)
    input_first = (normed_zero * norm_gain[0] + norm_shift[0]).astype(jnp.bfloat16)
    mixed_first, logsum_first = attend_forward(
        input_first, feat_qkv, cell_shape, FEATURE_SPECS, None
    )
    stream_one = stream_zero + branch_total(
        jnp.dot(mixed_first, feat_out, preferred_element_type=jnp.float32)
    )
    stream_one = stream_one + feat_out_bias.astype(jnp.float32)
    normed_one, inverse_one = standardize(stream_one)
    input_second = (normed_one * norm_gain[1] + norm_shift[1]).astype(jnp.bfloat16)
    mixed_second, logsum_second = attend_forward(
        input_second, row_qkv, cell_shape, ROW_SPECS, allowed
    )
    stream_two = stream_one + branch_total(
        jnp.dot(mixed_second, row_out, preferred_element_type=jnp.float32)
    )
    stream_two = stream_two + row_out_bias.astype(jnp.float32)
    normed_two, inverse_two = standardize(stream_two)
    input_third = (normed_two * norm_gain[2] + norm_shift[2]).astype(jnp.bfloat16)
    hidden_pre = jnp.dot(
        input_third, up_weight, preferred_element_type=jnp.float32
    ) + up_bias.astype(jnp.float32)
    hidden = jax.nn.gelu(hidden_pre, approximate=False).astype(jnp.bfloat16)
    stream_three = stream_two + branch_total(
        jnp.dot(hidden, down_weight, preferred_element_type=jnp.float32)
    )
    stream_three = stream_three + down_bias.astype(jnp.float32)
    output = stream_three.astype(jnp.bfloat16).reshape(cell_shape)
    grad_top = cotangent.astype(jnp.float32).reshape(cell_count, model_width)
    grad_low = grad_top.astype(jnp.bfloat16)
    pre_again = jnp.dot(
        input_third, up_weight, preferred_element_type=jnp.float32
    ) + up_bias.astype(jnp.float32)
    hidden_again, gelu_pull = jax.vjp(partial(jax.nn.gelu, approximate=False), pre_again)
    down_grad = jnp.einsum(
        "nf,nd->fd", hidden_again.astype(jnp.bfloat16), grad_low, preferred_element_type=jnp.float32
    )
    hidden_grad = jnp.einsum("nd,fd->nf", grad_low, down_weight, preferred_element_type=jnp.float32)
    pre_grad = gelu_pull(hidden_grad)[0].astype(jnp.bfloat16)
    up_bias_grad = jnp.sum(pre_grad.astype(jnp.float32), axis=0)
    up_grad = jnp.einsum("nd,nf->df", input_third, pre_grad, preferred_element_type=jnp.float32)
    third_grad = jnp.einsum("nf,df->nd", pre_grad, up_weight, preferred_element_type=jnp.float32)
    down_bias_grad = jnp.sum(row_share(grad_top), axis=0)
    grad_second, gain_three, shift_three = reduce_back(
        third_grad, normed_two, inverse_two, norm_gain[2], grad_top
    )
    row_bias_grad = jnp.sum(row_share(grad_second), axis=0)
    row_qkv_grad, row_out_grad, second_grad = attend_backward(
        input_second, row_qkv, row_out, logsum_second, grad_second, cell_shape, ROW_SPECS, allowed
    )
    grad_first, gain_two, shift_two = reduce_back(
        second_grad, normed_one, inverse_one, norm_gain[1], grad_second
    )
    feat_bias_grad = jnp.sum(row_share(grad_first), axis=0)
    feat_qkv_grad, feat_out_grad, first_grad = attend_backward(
        input_first, feat_qkv, feat_out, logsum_first, grad_first, cell_shape, FEATURE_SPECS, None
    )
    grad_input, gain_one, shift_one = reduce_back(
        first_grad, normed_zero, inverse_zero, norm_gain[0], grad_first
    )
    summed = lax.psum(
        (
            feat_qkv_grad,
            feat_out_grad,
            row_qkv_grad,
            row_out_grad,
            up_grad,
            up_bias_grad,
            down_grad,
        ),
        "dp",
    )
    shared = lax.psum(
        (
            feat_bias_grad,
            row_bias_grad,
            down_bias_grad,
            jnp.stack([gain_one, gain_two, gain_three]),
            jnp.stack([shift_one, shift_two, shift_three]),
        ),
        ("dp", "tensor"),
    )
    return (
        output,
        grad_input.astype(jnp.bfloat16).reshape(cell_shape),
        summed[0],
        summed[1],
        shared[0],
        summed[2],
        summed[3],
        shared[1],
        summed[4],
        summed[5],
        summed[6],
        shared[2],
        shared[3],
        shared[4],
    )


def solution(mesh):
    return jax.shard_map(
        shards,
        mesh=mesh,
        in_specs=(
            P("dp", None, None, None),
            P("dp"),
            P(None, None, "tensor"),
            P("tensor", None),
            P(),
            P(None, None, "tensor"),
            P("tensor", None),
            P(),
            P(None, "tensor"),
            P("tensor"),
            P("tensor", None),
            P(),
            P(),
            P(),
            P("dp", None, None, None),
        ),
        out_specs=(
            P("dp", None, None, None),
            P("dp", None, None, None),
            P(None, None, "tensor"),
            P("tensor", None),
            P(),
            P(None, None, "tensor"),
            P("tensor", None),
            P(),
            P(None, "tensor"),
            P("tensor"),
            P("tensor", None),
            P(),
            P(),
            P(),
        ),
        check_vma=False,
    )
```

profile of v0, /device:TPU:0, one launch (start us, length us, event | category | flops | bytes accessed | tf_op | source)
XLA Modules:
  0.0 739.8 jit_solution(89666200625754370)
XLA Ops:
  7.2 2.4 convert_reduce_fusion.1
  10.0 4.4 copy.89
  17.1 6.0 reshape.437
  23.2 3.5 subtract_multiply_fusion
  26.7 2.5 copy-done.9
  36.1 2.5 fusion.35
  40.0 2.5 convolution_convert_fusion.3
  44.0 66.1 %all-reduce.7.cloned.1.call-done = bf16[2848,512]{1,0:T(8,128)(2,1)} async-done(((bf16[2848,512]{1,0:T(8,128)(2,1)}), bf16[2848,512]{1,0:T(8,128)(2,1)}) %all-reduce.7.cloned.1.call-update) | async-done | bytes 2916368 | tf_op jit(solution)/shard_map/psum | solution.py:33
  110.1 4.5 fusion.61
  114.6 4.2 multiply_reduce_fusion.1
  120.7 2.5 copy-done.10
  123.2 3.0 convolution_convert_fusion.4
  126.3 4.1 reshape.443
  137.9 3.6 convolution_convert_fusion.2
  144.5 5.2 copy.102
  149.7 4.5 reshape.449
  154.2 52.3 %all-reduce.9.cloned.1.call-done = bf16[2848,512]{1,0:T(8,128)(2,1)} async-done(((bf16[2848,512]{1,0:T(8,128)(2,1)}), bf16[2848,512]{1,0:T(8,128)(2,1)}) %all-reduce.9.cloned.1.call-update) | async-done | bytes 2916368 | tf_op jit(solution)/shard_map/psum | solution.py:33
  206.5 5.8 fusion.63
  220.4 16.7 %convert_reduce_fusion = (f32[512]{0:T(512)}, bf16[2848,512]{1,0:T(8,128)(2,1)S(1)}, f32[2848,512]{1,0:T(8,128)}) fusion(f32[2848,512]{1,0:T(8,128)S(1)} %fusion.46, f32[512]{0:T(512)S(1)} %copy-done.59, bf16[2848,512]{1,0:T(8,128)(2,1)S(1)} %copy-done.16, bf16[512,512]{1,0:T(8,128)(2,1)S(1)} %copy-done), kind=kOutput, calls=%fused_computation.4 | convolution fusion | flops 1602534912 | bytes 18026496 | tf_op jit(solution)/shard_map/nd,fd->nf/dot_general | solution.py:199
  238.8 3.4 convolution_convert_fusion
  243.7 35.4 %reduce-scatter.4.cloned.1.call-done = bf16[712,512]{1,0:T(8,128)(2,1)} async-done(((bf16[2848,512]{1,0:T(8,128)(2,1)}), bf16[712,512]{1,0:T(8,128)(2,1)}) %reduce-scatter.4.cloned.1.call-update) | async-done | bytes 729104 | tf_op jit(solution)/shard_map/reduce_scatter | solution.py:42
  279.1 2.7 fusion.30
  281.7 3.7 convert_reduce_fusion.7
  285.7 27.2 %all-gather.4.cloned.1.call-done = bf16[2848,512]{1,0:T(8,128)(2,1)} async-done(((bf16[712,512]{1,0:T(8,128)(2,1)}), bf16[2848,512]{1,0:T(8,128)(2,1)}) %all-gather.4.cloned.1.call-update) | async-done | bytes 2916368 | tf_op jit(solution)/shard_map/all_gather | solution.py:49
  312.9 3.6 convolution_convert_fusion.7
  334.8 3.3 bitcast_convert_fusion.1
  339.0 35.9 %reduce-scatter.6.cloned.1.call-done = bf16[712,512]{1,0:T(8,128)(2,1)} async-done(((bf16[2848,512]{1,0:T(8,128)(2,1)}), bf16[712,512]{1,0:T(8,128)(2,1)}) %reduce-scatter.6.cloned.1.call-update) | async-done | bytes 729104 | tf_op jit(solution)/shard_map/reduce_scatter | solution.py:42
  377.0 3.2 convert_reduce_fusion.6
  380.4 27.1 %all-gather.6.cloned.1.call-done = bf16[2848,512]{1,0:T(8,128)(2,1)} async-done(((bf16[712,512]{1,0:T(8,128)(2,1)}), bf16[2848,512]{1,0:T(8,128)(2,1)}) %all-gather.6.cloned.1.call-update) | async-done | bytes 2916368 | tf_op jit(solution)/shard_map/all_gather | solution.py:49
  407.6 3.6 convolution_convert_fusion.6
  421.9 3.3 bitcast_convert_fusion
  425.9 5.9 multiply_convert_fusion
  433.4 3.3 convolution_convert_fusion.1
  437.0 25.0 %reduce-scatter.8.cloned.1.call-done = bf16[712,512]{1,0:T(8,128)(2,1)} async-done(((bf16[2848,512]{1,0:T(8,128)(2,1)}), bf16[712,512]{1,0:T(8,128)(2,1)}) %reduce-scatter.8.cloned.1.call-update) | async-done | bytes 729104 | tf_op jit(solution)/shard_map/reduce_scatter | solution.py:42
  464.1 2.9 convert_reduce_fusion.5
  467.4 5.6 fusion.71
  473.1 5.7 fusion.45
  480.6 2.7 fusion.55
  485.0 2.7 fusion.58
  488.4 21.9 %psum.115 = f32[512]{0:T(512)} all-reduce(f32[512]{0:T(512)S(1)} %copy-done.61), channel_id=1, replica_groups=mesh['dp'=8,'tensor'=4] {'dp'}, use_global_device_ids=true, to_apply=%region_34.35 | all-reduce | flops 512 | bytes 4096 | tf_op jit(solution)/shard_map/psum | solution.py:222
  510.3 19.5 %all-reduce.11.cloned.1.call-done = bf16[2848,512]{1,0:T(8,128)(2,1)} async-done(((bf16[2848,512]{1,0:T(8,128)(2,1)}), bf16[2848,512]{1,0:T(8,128)(2,1)}) %all-reduce.11.cloned.1.call-update) | async-done | bytes 2916368 | tf_op jit(solution)/shard_map/psum | solution.py:33
  529.8 4.5 add_convert_fusion.1
  534.3 2.5 reshape.448
  536.9 5.4 copy.110
  542.3 40.7 %all-reduce = (f32[512]{0:T(512)}, f32[512]{0:T(512)}, f32[512]{0:T(512)}, f32[3,512]{1,0:T(4,128)}, f32[3,512]{1,0:T(4,128)}) all-reduce(f32[512]{0:T(512)S(1)} %get-tuple-element.102, f32[512]{0:T(512)S(1)} %get-tuple-element.100, f32[512]{0:T(512)S(1)} %copy-done.56, ...), channel_id=1, replica_groups=mesh['dp'=8,'tensor'=4] {'dp','tensor'}, use_global_device_ids=true, to_apply=%region_27.28 | all-reduce | flops 4608 | bytes 36864 | tf_op jit(solution)/shard_map/psum | solution.py:234
  583.0 4.5 reshape.453
  587.5 5.1 copy.111
  592.6 131.3 %all-reduce.13.cloned.1.call-done = (f32[512,3,128]{2,0,1:T(8,128)}, f32[128,512]{1,0:T(8,128)}, f32[512,3,128]{2,0,1:T(8,128)}, f32[128,512]{1,0:T(8,128)}, f32[512,512]{1,0:T(8,128)}, /*index=5*/f32[512,512]{1,0:T(8,128)}) async-done(((f32[512,3,128]{2,0,1:T(8,128)}, f32[128,512]{1,0:T(8,128)}, f32[512,3,128]{2,0,1:T(8,128)}, f32[128,512]{1,0:T(8,128)}, f32[512,512]{1,0:T(8,128)}, ...) | async-done | bytes 4194320 | tf_op jit(solution)/shard_map/psum | solution.py:222
  (266 shorter events, 85.5 us)
Async XLA Ops:
  7.2 212.3 %copy-start = (bf16[512,512]{1,0:T(8,128)(2,1)S(1)}, bf16[512,512]{1,0:T(8,128)(2,1)}, u32[]{:S(2)}) copy-start(bf16[512,512]{1,0:T(8,128)(2,1)} %param.25) | copy-start | bytes 1572868
  7.2 102.9 %all-reduce.7.cloned.1.call-start = ((), (), s32[]{:S(2)}) async-start(), calls=%async_computation.3 | async-start | bytes 5832704 | tf_op jit(solution)/shard_map/psum | solution.py:33
  10.0 4.4 copy-start.54
  10.0 5.0 copy-start.55
  15.0 11.7 %copy-start.50 = (f32[1,512]{1,0:T(1,128)}, f32[1,512]{1,0:T(1,128)S(1)}, u32[]{:S(2)}) copy-start(f32[1,512]{1,0:T(1,128)S(1)} %get-tuple-element.109) | copy-start | bytes 6148
  17.0 6.2 copy-start.43
  23.1 6.1 copy-start.62
  23.1 6.1 copy-start.70
  35.2 4.8 copy-start.32
  42.5 164.0 %all-reduce.9.cloned.1.call-start = ((), (), s32[]{:S(2)}) async-start(), calls=%async_computation.4 | async-start | bytes 5832704 | tf_op jit(solution)/shard_map/psum | solution.py:33
  43.5 75.4 %copy-start.49 = (f32[512]{0:T(512)}, f32[512]{0:T(512)S(1)}, u32[]{:S(2)}) copy-start(f32[512]{0:T(512)S(1)} %convert_element_type.172) | copy-start | bytes 6148
  110.1 4.5 copy-start.3
  110.1 8.8 %slice-start = ((s8[5832704]{0:T(1024)(128)(4,1)}), s8[4194304]{0:T(1024)(128)(4,1)S(1)}, s32[]{:S(2)}) async-start(s8[5832704]{0:T(1024)(128)(4,1)} %bitcast.153), calls=%async_computation.13 | async-start | bytes 8388608
  114.6 4.3 slice-start.1
  118.9 4.3 copy-start.52
  118.9 4.3 copy-start.64
  118.9 4.3 copy-start.68
  141.6 137.5 %reduce-scatter.4.cloned.1.call-start = ((), (), s32[]{:S(2)}) async-start(), calls=%async_computation.6 | async-start | bytes 3645440 | tf_op jit(solution)/shard_map/reduce_scatter | solution.py:42
  216.5 3.9 copy-start.16
  220.4 16.7 %copy-start.4 = (f32[2848,512]{1,0:T(8,128)}, f32[2848,512]{1,0:T(8,128)S(1)}, u32[]{:S(2)}) copy-start(f32[2848,512]{1,0:T(8,128)S(1)} %fusion.46) | copy-start | bytes 17498116
  242.2 70.6 %all-gather.4.cloned.1.call-start = ((), (), s32[]{:S(2)}) async-start(), calls=%async_computation.7 | async-start | bytes 3645440 | tf_op jit(solution)/shard_map/all_gather | solution.py:49
  285.5 89.3 %reduce-scatter.6.cloned.1.call-start = ((), (), s32[]{:S(2)}) async-start(), calls=%async_computation.8 | async-start | bytes 3645440 | tf_op jit(solution)/shard_map/reduce_scatter | solution.py:42
  329.8 5.0 copy-start.69
  338.1 36.7 %copy-start.53 = (f32[1,512]{1,0:T(1,128)S(1)}, f32[1,512]{1,0:T(1,128)}, u32[]{:S(2)}) copy-start(f32[1,512]{1,0:T(1,128)} %get-tuple-element.108) | copy-start | bytes 6148
  338.1 69.4 %all-gather.6.cloned.1.call-start = ((), (), s32[]{:S(2)}) async-start(), calls=%async_computation.9 | async-start | bytes 3645440 | tf_op jit(solution)/shard_map/all_gather | solution.py:49
  339.0 68.6 %copy-start.33 = (bf16[128,512]{1,0:T(8,128)(2,1)S(1)}, bf16[128,512]{1,0:T(8,128)(2,1)}, u32[]{:S(2)}) copy-start(bf16[128,512]{1,0:T(8,128)(2,1)} %param.18) | copy-start | bytes 393220
  380.2 32.3 %copy-start.35 = (f32[32,89]{1,0:T(8,128)S(1)}, f32[32,89]{1,0:T(8,128)}, u32[]{:S(2)}) copy-start(f32[32,89]{1,0:T(8,128)} %copy-done.34) | copy-start | bytes 34180
  380.2 81.8 %reduce-scatter.8.cloned.1.call-start = ((), (), s32[]{:S(2)}) async-start(), calls=%async_computation.10 | async-start | bytes 3645440 | tf_op jit(solution)/shard_map/reduce_scatter | solution.py:42
  425.3 104.5 %all-reduce.11.cloned.1.call-start = ((), (), s32[]{:S(2)}) async-start(), calls=%async_computation.5 | async-start | bytes 5832704 | tf_op jit(solution)/shard_map/psum | solution.py:33
  436.7 25.3 %copy-start.51 = (f32[1,512]{1,0:T(1,128)S(1)}, f32[1,512]{1,0:T(1,128)}, u32[]{:S(2)}) copy-start(f32[1,512]{1,0:T(1,128)} %copy-done.50) | copy-start | bytes 6148
  436.7 27.4 %copy-start.7 = (bf16[2848,512]{1,0:T(8,128)(2,1)S(1)}, bf16[2848,512]{1,0:T(8,128)(2,1)}, u32[]{:S(2)}) copy-start(bf16[2848,512]{1,0:T(8,128)(2,1)} %all-gather.6.cloned.1.call-done) | copy-start | bytes 8749060
  436.7 146.3 %all-gather.8.cloned.1.call-start = ((), (), s32[]{:S(2)}) async-start(), calls=%async_computation.11 | async-start | bytes 3645440 | tf_op jit(solution)/shard_map/all_gather | solution.py:49
  467.1 6.0 copy-start.42
  467.1 6.0 copy-start.46
  467.1 256.8 %all-reduce.13.cloned.1.call-start = ((), (), s32[]{:S(2)}) async-start(), calls=%async_computation.12 | async-start | bytes 8388608 | tf_op jit(solution)/shard_map/psum | solution.py:222
  467.4 5.7 copy-start.23
  467.4 12.8 %slice-start.4 = ((s8[5832704]{0:T(1024)(128)(4,1)}), s8[4194304]{0:T(1024)(128)(4,1)S(1)}, s32[]{:S(2)}) async-start(s8[5832704]{0:T(1024)(128)(4,1)} %bitcast.162), calls=%async_computation.17 | async-start | bytes 8388608
  473.1 5.8 copy-start.6
  473.1 5.7 copy-start.13
  473.1 7.1 slice-start.5
  473.1 11.6 %slice-start.2 = ((s8[5832704]{0:T(1024)(128)(4,1)}), s8[1638400]{0:T(1024)(128)(4,1)S(1)}, s32[]{:S(2)}) async-start(s8[5832704]{0:T(1024)(128)(4,1)} %bitcast.160), calls=%async_computation.15 | async-start | bytes 3276800
  480.6 4.1 slice-start.3
  536.9 5.4 copy-start.58
  536.9 5.4 copy-start.57
  536.9 5.4 copy-start.56
  723.9 6.0 copy-start.36
  723.9 6.7 copy-start.30
  723.9 7.6 %copy-start.29 = (f32[512,512]{1,0:T(8,128)S(1)}, f32[512,512]{1,0:T(8,128)}, u32[]{:S(2)}) copy-start(f32[512,512]{1,0:T(8,128)} %get-tuple-element.133) | copy-start | bytes 3145732
  (41 other events, 81.8 us)
Sparse Core Ops, SparseCore 0:
  42.6 67.3 all-reduce.6
  141.7 64.8 all-reduce.8
  242.4 36.6 reduce-scatter.3
  285.6 27.2 all-gather.3
  338.3 36.5 reduce-scatter.5
  380.3 27.2 all-gather.5
  425.4 36.5 reduce-scatter.7
  465.0 64.7 all-reduce.10
  531.4 27.9 all-gather.7
  565.5 158.3 all-reduce.12
where the time goes:
time: 748 us; the launch traced here: 740 us
  waiting for transfers between devices  420 us (56%)
  local copies, waits for them, and re-layouts  97.9 us (13%)
  matrix products  83.2 us (11%)
  blocking collectives  62.6 us (8%)
  other arithmetic  58.4 us (8%)
  between operations  16.3 us (2%)
    psum x3, waiting for transfers between devices, branch_total(): lax.psum(partial_out.astype(jnp.bfloat16), 'tensor').astype(jnp.float32)  138 us
    psum x1, waiting for transfers between devices, shards(): lax.psum((feat_qkv_grad, feat_out_grad, row_qkv_grad, row_out_grad, up_gr...  131 us
    reduce_scatter x3, waiting for transfers between devices, reduce_back(): lax.psum_scatter(normed_grad.astype(jnp.bfloat16), 'tensor', scatter_dime...  96.2 us
    all_gather x3, waiting for transfers between devices, reduce_back(): lax.all_gather(share_stream.astype(jnp.bfloat16), 'tensor', axis=0, tiled...  54.3 us
    unnamed x171, local copies, waits for them, and re-layouts  46.8 us
    psum x1, blocking collectives, shards(): lax.psum((feat_bias_grad, row_bias_grad, down_bias_grad, jnp.stack([gain_...  40.7 us
    psum x1, blocking collectives, shards(): lax.psum((feat_qkv_grad, feat_out_grad, row_qkv_grad, row_out_grad, up_gr...  21.9 us
    dot_general x1, matrix products, shards(): jnp.einsum('nd,fd->nf', grad_low, down_weight, preferred_element_type=jnp...  16.7 us
  transfers between devices with their start and end apart: 10, of which 9 were waited for; matrix products, arithmetic and copies ran while one was open for 10% of the time, Pallas kernels for 0%

commit v1 on v0

v1 whole, which is shorter than its diff:
```python
from functools import partial

import jax
import jax.numpy as jnp
from jax import lax
from jax.experimental import pallas as pl
from jax.experimental.pallas import tpu as pltpu
from jax.sharding import PartitionSpec as P

HD = 128
EPSILON = 1e-05
NEGATIVE = -1e30
SCALE = HD**-0.5
BF = jnp.bfloat16
F32 = jnp.float32
SUB = 8
MIB = 1 << 20


def mm(a, b):
    return jnp.dot(a, b, preferred_element_type=F32)


def mm_nt(a, b):
    return lax.dot_general(a, b, (((1,), (1,)), ((), ())), preferred_element_type=F32)


def mm_tn(a, b):
    return lax.dot_general(a, b, (((0,), (0,)), ((), ())), preferred_element_type=F32)


def standardize(values):
    centered = values - jnp.mean(values, axis=-1, keepdims=True)
    inverse = lax.rsqrt(jnp.mean(centered * centered, axis=-1, keepdims=True) + EPSILON)
    return centered * inverse, inverse


def norm_backward(upstream, normed, inverse, gain):
    scaled = upstream * gain
    return inverse * (
        scaled
        - jnp.mean(scaled, axis=-1, keepdims=True)
        - normed * jnp.mean(scaled * normed, axis=-1, keepdims=True)
    )


def column_sum(values):
    return jnp.sum(values, axis=0, keepdims=True)


def softmax_rows(scores):
    top = jnp.max(scores, axis=-1, keepdims=True)
    grown = jnp.exp(scores - top)
    return grown * (1.0 / jnp.sum(grown, axis=-1, keepdims=True))


def gelu_parts(z):
    t = 1.0 / (1.0 + (0.3275911 * 0.7071067811865476) * jnp.abs(z))
    e = jnp.exp(-0.5 * z * z)
    poly = t * (
        0.127414796 + t * (-0.142248368 + t * (0.7107068705 + t * (-0.7265760135 + t * 0.5307027145)))
    )
    tail = poly * e
    cdf = jnp.where(z >= 0, 1.0 - tail, tail)
    return z * cdf, cdf + z * (e * 0.3989422804014327)


def feature_probabilities(q, k, feature_count):
    scores = mm_nt(q, k) * SCALE
    column = lax.broadcasted_iota(jnp.int32, scores.shape, 1)
    return softmax_rows(jnp.where(column < feature_count, scores, NEGATIVE))


def feature_forward_kernel(
    t_ref, cells_ref, gains_ref, shifts_ref, w_ref, o0, o1, o2, o3, cell_scr, mix_scr
):
    rows, feature_count, width = cells_ref.shape
    padded = cell_scr.shape[1]

    @pl.when(pl.program_id(0) == 0)
    def _():
        cell_scr[...] = jnp.zeros_like(cell_scr)

    cell_scr[:, 0:feature_count, :] = cells_ref[...].astype(F32)
    normed, _ = standardize(cell_scr[...].reshape(rows * padded, width))
    low = (normed * gains_ref[...].astype(F32)[0:1] + shifts_ref[...].astype(F32)[0:1]).astype(BF)
    qkv = mm(low, w_ref[...]).astype(BF)
    for r in range(rows):
        part = qkv[r * padded : (r + 1) * padded]
        p = feature_probabilities(part[:, :HD], part[:, HD : 2 * HD], feature_count)
        mixed = mm(p.astype(BF), part[:, 2 * HD :])
        mix_scr[r] = mixed.reshape(padded // SUB, SUB, HD)
    groups = o0.shape[0]
    for k, out in enumerate((o0, o1, o2, o3)):
        dest = lax.bitwise_xor(t_ref[0], k)
        piece = mix_scr[:, pl.ds(dest * groups, groups)]
        piece = jnp.transpose(piece, (1, 0, 2, 3))
        out[...] = piece.reshape(groups, rows * SUB, HD).astype(BF)


def feature_forward(t, cells, gains, shifts, weight, start, count, step):
    _, feature_count, width = cells.shape
    groups = -(-feature_count // (4 * SUB))
    padded = 4 * groups * SUB
    first = start // step
    out = jax.ShapeDtypeStruct((groups, count * SUB, HD), BF)
    whole = lambda i: (0, 0)
    return pl.pallas_call(
        feature_forward_kernel,
        grid=(count // step,),
        out_shape=[out] * 4,
        in_specs=[
            pl.BlockSpec(memory_space=pltpu.SMEM),
            pl.BlockSpec((step, feature_count, width), lambda i: (i + first, 0, 0)),
            pl.BlockSpec(gains.shape, whole),
            pl.BlockSpec(shifts.shape, whole),
            pl.BlockSpec(weight.shape, whole),
        ],
        out_specs=[pl.BlockSpec((groups, step * SUB, HD), lambda i: (0, i, 0))] * 4,
        scratch_shapes=[
            pltpu.VMEM((step, padded, width), F32),
            pltpu.VMEM((step, padded // SUB, SUB, HD), F32),
        ],
        compiler_params=pltpu.CompilerParams(vmem_limit_bytes=40 * MIB),
        cost_estimate=pl.CostEstimate(
            flops=2 * count * padded * (width * 3 * HD + 2 * padded * HD),
            bytes_accessed=4 * MIB,
            transcendentals=0,
        ),
        name="feature_forward",
    )(t, cells, gains, shifts, weight)


def columns_kernel(t_ref, cells_ref, grad_ref, cells_out, grad_out, scr):
    rows, feature_count, width = cells_ref.shape
    groups = cells_out.shape[0]

    @pl.when(pl.program_id(0) == 0)
    def _():
        scr[...] = jnp.zeros_like(scr)

    for source, out in ((cells_ref, cells_out), (grad_ref, grad_out)):
        scr[:, 0:feature_count, :] = source[...].astype(F32)
        for g in range(groups):
            at = pl.multiple_of((t_ref[0] * groups + g) * SUB, SUB)
            piece = scr[:, pl.ds(at, SUB), :]
            out[g] = piece.reshape(rows * SUB, width).astype(BF)


def feature_columns(t, cells, grads, step):
    row_count, feature_count, width = cells.shape
    groups = -(-feature_count // (4 * SUB))
    out = jax.ShapeDtypeStruct((groups, row_count * SUB, width), BF)
    block = pl.BlockSpec((step, feature_count, width), lambda i: (i, 0, 0))
    return pl.pallas_call(
        columns_kernel,
        grid=(row_count // step,),
        out_shape=[out] * 2,
        in_specs=[pl.BlockSpec(memory_space=pltpu.SMEM), block, block],
        out_specs=[pl.BlockSpec((groups, step * SUB, width), lambda i: (0, i, 0))] * 2,
        scratch_shapes=[pltpu.VMEM((step, 4 * groups * SUB, width), F32)],
        compiler_params=pltpu.CompilerParams(vmem_limit_bytes=24 * MIB),
        cost_estimate=pl.CostEstimate(flops=MIB, bytes_accessed=8 * MIB, transcendentals=0),
        name="feature_columns",
    )(t, cells, grads)


def row_forward_kernel(
    split_ref, m0, m1, m2, m3, cells_ref, wo_ref, wo_bias, gains_ref, shifts_ref, wq0, wq1, wq2, wq3,
    wr_ref, wr_bias, first_ref, n2_ref, qkv_ref, p_ref, o2_ref, second_ref, n3_ref, bias_scr,
):
    cells = cells_ref.shape[1]

    @pl.when(pl.program_id(0) == 0)
    def _():
        query = lax.broadcasted_iota(jnp.int32, (cells, cells), 0)
        key = lax.broadcasted_iota(jnp.int32, (cells, cells), 1)
        same = lax.bitwise_and(query, SUB - 1) == lax.bitwise_and(key, SUB - 1)
        live = jnp.logical_and(same, key < split_ref[0] * SUB)
        bias_scr[...] = jnp.where(live, 0.0, NEGATIVE)

    gains = gains_ref[...].astype(F32)
    shifts = shifts_ref[...].astype(F32)
    mixed = jnp.concatenate([m[0] for m in (m0, m1, m2, m3)], axis=-1)
    first = cells_ref[0].astype(F32) + mm(mixed, wo_ref[...]) + wo_bias[...].astype(F32)
    first_ref[0] = first
    normed, _ = standardize(first)
    low = (normed * gains[1:2] + shifts[1:2]).astype(BF)
    n2_ref[0] = low
    outs = []
    for h, wq in enumerate((wq0, wq1, wq2, wq3)):
        qkv = mm(low, wq[...]).astype(BF)
        qkv_ref[0, :, 3 * HD * h : 3 * HD * (h + 1)] = qkv
        scores = mm_nt(qkv[:, :HD], qkv[:, HD : 2 * HD]) * SCALE + bias_scr[...]
        p = softmax_rows(scores).astype(BF)
        p_ref[0, h] = p
        outs.append(mm(p, qkv[:, 2 * HD :]).astype(BF))
    mixed = jnp.concatenate(outs, axis=-1)
    o2_ref[0] = mixed
    second = first + mm(mixed, wr_ref[...]) + wr_bias[...].astype(F32)
    second_ref[0] = second
    normed, _ = standardize(second)
    n3_ref[0] = (normed * gains[2:3] + shifts[2:3]).astype(BF)


def row_forward(split, mixed, cells, wo, wo_bias, gains, shifts, wqs, wr, wr_bias):
    groups, n, width = cells.shape
    per_group = lambda i: (i, 0, 0)
    block = lambda w: pl.BlockSpec((1, n, w), per_group)
    full = lambda a: pl.BlockSpec(a.shape, lambda i: (0,) * a.ndim)
    shape = lambda w, dt: jax.ShapeDtypeStruct((groups, n, w), dt)
    wide = 12 * HD
    return pl.pallas_call(
        row_forward_kernel,
        grid=(groups,),
        out_shape=[
            shape(width, F32), shape(width, BF), shape(wide, BF),
            jax.ShapeDtypeStruct((groups, 4, n, n), BF), shape(4 * HD, BF), shape(width, F32), shape(width, BF),
        ],
        in_specs=[pl.BlockSpec(memory_space=pltpu.SMEM)]
        + [block(HD)] * 4
        + [block(width), full(wo), full(wo_bias), full(gains), full(shifts)]
        + [full(w) for w in wqs]
        + [full(wr), full(wr_bias)],
        out_specs=[
            block(width), block(width), block(wide),
            pl.BlockSpec((1, 4, n, n), lambda i: (i, 0, 0, 0)), block(4 * HD), block(width), block(width),
        ],
        scratch_shapes=[pltpu.VMEM((n, n), F32)],
        compiler_params=pltpu.CompilerParams(vmem_limit_bytes=48 * MIB),
        cost_estimate=pl.CostEstimate(
            flops=2 * groups * n * (width * wide + 2 * width * 4 * HD + 8 * n * HD),
            bytes_accessed=16 * MIB, transcendentals=0,
        ),
        name="row_forward",
    )(split, *mixed, cells, wo, wo_bias, gains, shifts, *wqs, wr, wr_bias)


def hidden_part(n3, n3_t, gl, gl_t, up, bias, down, i, last, up_acc, down_acc, bias_acc, grad_ref):
    z = mm(n3, up) + bias
    act, slope = gelu_parts(z)
    m = act.astype(BF)
    out = mm(m, down)
    dz = (mm_nt(gl, down) * slope).astype(BF)
    dn3 = mm_nt(dz, up)
    width = up.shape[1]

    up_grad = mm(n3_t, dz)
    down_grad = mm(gl_t, m)
    bias_grad = column_sum(dz.astype(F32))

    @pl.when(i == 0)
    def _():
        up_acc[...] = up_grad
        down_acc[...] = down_grad
        bias_acc[...] = bias_grad

    @pl.when(i > 0)
    def _():
        up_acc[...] += up_grad
        down_acc[...] += down_grad
        bias_acc[...] += bias_grad

    @pl.when(i == last)
    def _():
        grad_ref[:, :width] = up_acc[...].astype(BF)
        grad_ref[:, width:] = down_acc[...].astype(BF)

    return out, dn3


def hidden_first_kernel(
    n3_ref, gl_ref, up0, up1, bias0, bias1, down0, down1, out_ref, dn3_ref, grad0, grad1, bg0, bg1,
    ua0, ua1, da0, da1,
):
    i, last = pl.program_id(0), pl.num_programs(0) - 1
    n3, gl = n3_ref[0], gl_ref[0]
    n3_t, gl_t = n3.T, gl.T
    a, da = hidden_part(
        n3, n3_t, gl, gl_t, up0[...], bias0[...].astype(F32), down0[...], i, last, ua0, da0, bg0, grad0)
    b, db = hidden_part(
        n3, n3_t, gl, gl_t, up1[...], bias1[...].astype(F32), down1[...], i, last, ua1, da1, bg1, grad1)
    out_ref[0] = a + b
    dn3_ref[0] = da + db


def hidden_second_kernel(
    n3_ref, gl_ref, up0, up1, bias0, bias1, down0, down1, out_in, dn3_in, second_ref, down_bias, gains_ref,
    out_ref, g2_ref, gl2_ref, grad0, grad1, bg0, bg1, stats_ref, ua0, ua1, da0, da1,
):
    i, last = pl.program_id(0), pl.num_programs(0) - 1
    n3, gl = n3_ref[0], gl_ref[0]
    n3_t, gl_t = n3.T, gl.T
    a, da = hidden_part(
        n3, n3_t, gl, gl_t, up0[...], bias0[...].astype(F32), down0[...], i, last, ua0, da0, bg0, grad0)
    b, db = hidden_part(
        n3, n3_t, gl, gl_t, up1[...], bias1[...].astype(F32), down1[...], i, last, ua1, da1, bg1, grad1)
    second = second_ref[0]
    out_ref[0] = (second + out_in[0] + a + b + down_bias[...].astype(F32)).astype(BF)
    dn3 = dn3_in[0] + da + db
    normed, inverse = standardize(second)
    g3 = gl.astype(F32)
    g2 = g3 + norm_backward(dn3, normed, inverse, gains_ref[...].astype(F32)[2:3])
    g2_ref[0] = g2
    gl2_ref[0] = g2.astype(BF)
    stats = jnp.concatenate(
        [column_sum(g3), column_sum(g2), column_sum(dn3 * normed), column_sum(dn3),
         jnp.zeros((4, g3.shape[1]), F32)], axis=0)

    @pl.when(i == 0)
    def _():
        stats_ref[...] = stats

    @pl.when(i > 0)
    def _():
        stats_ref[...] += stats


def hidden_call(n3, gl, ups, biases, downs, extra=None):
    groups, n, width = n3.shape
    hidden = ups[0].shape[1]
    block = lambda w: pl.BlockSpec((1, n, w), lambda i: (i, 0, 0))
    full = lambda a: pl.BlockSpec(a.shape, lambda i: (0,) * len(a.shape))
    cells = lambda dt: jax.ShapeDtypeStruct((groups, n, width), dt)
    grad = jax.ShapeDtypeStruct((width, hidden + width), BF)
    bias_grad = jax.ShapeDtypeStruct((1, hidden), F32)
    args = [n3, gl, *ups, *biases, *downs]
    specs = [block(width), block(width)] + [full(a) for a in args[2:]]
    if extra is None:
        kernel = hidden_first_kernel
        outs = [cells(F32), cells(F32), grad, grad, bias_grad, bias_grad]
        out_specs = [block(width)] * 2 + [full(o) for o in outs[2:]]
    else:
        kernel = hidden_second_kernel
        args += extra
        specs += [block(width)] * 3 + [full(a) for a in extra[3:]]
        outs = [cells(BF), cells(F32), cells(BF), grad, grad, bias_grad, bias_grad,
                jax.ShapeDtypeStruct((8, width), F32)]
        out_specs = [block(width)] * 3 + [full(o) for o in outs[3:]]
    return pl.pallas_call(
        kernel,
        grid=(groups,),
        out_shape=outs,
        in_specs=specs,
        out_specs=out_specs,
        scratch_shapes=[pltpu.VMEM((width, hidden), F32)] * 2 + [pltpu.VMEM((width, width), F32)] * 2,
        compiler_params=pltpu.CompilerParams(vmem_limit_bytes=48 * MIB),
        cost_estimate=pl.CostEstimate(
            flops=2 * groups * n * width * hidden * 12, bytes_accessed=16 * MIB, transcendentals=0),
        name="hidden_first" if extra is None else "hidden_second",
    )(*args)


def attention_backward(q, k, v, p, do):
    dp = mm_nt(do, v)
    pf = p.astype(F32)
    ds = (pf * (dp - jnp.sum(dp * pf, axis=-1, keepdims=True))).astype(BF)
    dq = mm(ds, k) * SCALE
    dk = mm_tn(ds, q) * SCALE
    dv = mm_tn(p, do)
    return jnp.concatenate([dq, dk, dv], axis=-1).astype(BF)


def row_backward_kernel(
    t_ref, g2_ref, first_ref, qkv_ref, p_ref, gains_ref, wq0, wq1, wq2, wq3, wr_ref,
    dqkv_ref, gl1_ref, s0, s1, s2, s3, stats_ref, g1_scr,
):
    i = pl.program_id(0)
    g2 = g2_ref[0]
    do = mm_nt(g2.astype(BF), wr_ref[...]).astype(BF)
    dn2 = None
    for h, wq in enumerate((wq0, wq1, wq2, wq3)):
        at = 3 * HD * h
        grads = attention_backward(
            qkv_ref[0, :, at : at + HD], qkv_ref[0, :, at + HD : at + 2 * HD],
            qkv_ref[0, :, at + 2 * HD : at + 3 * HD], p_ref[0, h], do[:, HD * h : HD * (h + 1)])
        dqkv_ref[0, :, at : at + 3 * HD] = grads
        term = mm_nt(grads, wq[...])
        dn2 = term if dn2 is None else dn2 + term
    normed, inverse = standardize(first_ref[0])
    g1 = g2 + norm_backward(dn2, normed, inverse, gains_ref[...].astype(F32)[1:2])
    g1_scr[...] = g1
    gl1_ref[0] = g1.astype(BF)
    rows = s0.shape[1]
    for k, out in enumerate((s0, s1, s2, s3)):
        at = pl.multiple_of(lax.bitwise_xor(t_ref[0], k) * rows, rows)
        out[0] = g1_scr[pl.ds(at, rows), :].astype(BF)
    stats = jnp.concatenate(
        [column_sum(g1), column_sum(dn2 * normed), column_sum(dn2), jnp.zeros((5, g1.shape[1]), F32)], axis=0)

    @pl.when(i == 0)
    def _():
        stats_ref[...] = stats

    @pl.when(i > 0)
    def _():
        stats_ref[...] += stats


def row_backward(t, g2, first, qkv, p, gains, wqs, wr):
    groups, n, width = g2.shape
    block = lambda w, m=n: pl.BlockSpec((1, m, w), lambda i: (i, 0, 0))
    full = lambda a: pl.BlockSpec(a.shape, lambda i: (0,) * len(a.shape))
    wide = qkv.shape[2]
    send = jax.ShapeDtypeStruct((groups, n // 4, width), BF)
    return pl.pallas_call(
        row_backward_kernel,
        grid=(groups,),
        out_shape=[
            jax.ShapeDtypeStruct((groups, n, wide), BF), jax.ShapeDtypeStruct((groups, n, width), BF),
            send, send, send, send, jax.ShapeDtypeStruct((8, width), F32),
        ],
        in_specs=[pl.BlockSpec(memory_space=pltpu.SMEM), block(width), block(width), block(wide),
                  pl.BlockSpec((1, 4, n, n), lambda i: (i, 0, 0, 0)), full(gains)]
        + [full(w) for w in wqs] + [full(wr)],
        out_specs=[block(wide), block(width)] + [block(width, n // 4)] * 4
        + [pl.BlockSpec((8, width), lambda i: (0, 0))],
        scratch_shapes=[pltpu.VMEM((n, width), F32)],
        compiler_params=pltpu.CompilerParams(vmem_limit_bytes=48 * MIB),
        cost_estimate=pl.CostEstimate(
            flops=2 * groups * n * (width * wide + width * 4 * HD + 16 * n * HD),
            bytes_accessed=16 * MIB, transcendentals=0),
        name="row_backward",
    )(t, g2, first, qkv, p, gains, *wqs, wr)


def row_weights_kernel(n2_ref, dqkv_ref, gl2_ref, o2_ref, gl1_ref, m0, m1, m2, m3, keep_ref, send_ref):
    groups, n, width = n2_ref.shape
    cells = groups * n
    n2_t = n2_ref[...].reshape(cells, width).T
    gl2_t = gl2_ref[...].reshape(cells, width).T
    gl1_t = gl1_ref[...].reshape(cells, width).T
    for h, m in enumerate((m0, m1, m2, m3)):
        out = (keep_ref, send_ref)[h % 2]
        at = 3 * HD * h
        out[h // 2, :, 0 : 3 * HD] = mm(
            n2_t, dqkv_ref[:, :, at : at + 3 * HD].reshape(cells, 3 * HD)).astype(BF)
        out[h // 2, :, 3 * HD : 4 * HD] = mm(
            gl2_t, o2_ref[:, :, HD * h : HD * (h + 1)].reshape(cells, HD)).astype(BF)
        out[h // 2, :, 4 * HD : 5 * HD] = mm(gl1_t, m[...].reshape(cells, HD)).astype(BF)


def row_weights(n2, dqkv, gl2, o2, gl1, mixed):
    groups, n, width = n2.shape
    out = jax.ShapeDtypeStruct((2, width, 5 * HD), BF)
    vmem = pl.BlockSpec(memory_space=pltpu.VMEM)
    return pl.pallas_call(
        row_weights_kernel,
        out_shape=[out] * 2,
        in_specs=[vmem] * 9,
        out_specs=[vmem] * 2,
        compiler_params=pltpu.CompilerParams(vmem_limit_bytes=48 * MIB),
        cost_estimate=pl.CostEstimate(
            flops=2 * groups * n * width * 20 * HD, bytes_accessed=10 * MIB, transcendentals=0),
        name="row_weights",
    )(n2, dqkv, gl2, o2, gl1, *mixed)


def feature_again_kernel(
    t_ref, cells_ref, gains_ref, shifts_ref, wq0, wq1, wq2, wq3, n1_ref, qkv_ref, p_ref, cell_scr
):
    rows, feature_count, width = cells_ref.shape
    padded = cell_scr.shape[1]

    @pl.when(pl.program_id(0) == 0)
    def _():
        cell_scr[...] = jnp.zeros_like(cell_scr)

    cell_scr[:, 0:feature_count, :] = cells_ref[...].astype(F32)
    normed, _ = standardize(cell_scr[...].reshape(rows * padded, width))
    low = (normed * gains_ref[...].astype(F32)[0:1] + shifts_ref[...].astype(F32)[0:1]).astype(BF)
    n1_ref[...] = low
    for h, wq in enumerate((wq0, wq1, wq2, wq3)):
        qkv = mm(low, wq[...]).astype(BF)
        qkv_ref[:, 3 * HD * h : 3 * HD * (h + 1)] = qkv
        for r in range(rows):
            part = qkv[r * padded : (r + 1) * padded]
            p = feature_probabilities(part[:, :HD], part[:, HD : 2 * HD], feature_count)
            p_ref[r, h] = p.astype(BF)


def feature_again(t, cells, gains, shifts, wqs, own, step):
    _, feature_count, width = cells.shape
    groups = -(-feature_count // (4 * SUB))
    padded = 4 * groups * SUB
    steps = own // step
    grid_spec = pltpu.PrefetchScalarGridSpec(
        num_scalar_prefetch=1,
        grid=(steps,),
        in_specs=[
            pl.BlockSpec((step, feature_count, width), lambda i, t: (t[0] * steps + i, 0, 0)),
            pl.BlockSpec(gains.shape, lambda i, t: (0, 0)),
            pl.BlockSpec(shifts.shape, lambda i, t: (0, 0)),
        ]
        + [pl.BlockSpec(w.shape, lambda i, t: (0, 0)) for w in wqs],
        out_specs=[
            pl.BlockSpec((step * padded, width), lambda i, t: (i, 0)),
            pl.BlockSpec((step * padded, 12 * HD), lambda i, t: (i, 0)),
            pl.BlockSpec((step, 4, padded, padded), lambda i, t: (i, 0, 0, 0)),
        ],
        scratch_shapes=[pltpu.VMEM((step, padded, width), F32)],
    )
    return pl.pallas_call(
        feature_again_kernel,
        grid_spec=grid_spec,
        out_shape=[
            jax.ShapeDtypeStruct((own * padded, width), BF),
            jax.ShapeDtypeStruct((own * padded, 12 * HD), BF),
            jax.ShapeDtypeStruct((own, 4, padded, padded), BF),
        ],
        compiler_params=pltpu.CompilerParams(vmem_limit_bytes=40 * MIB),
        cost_estimate=pl.CostEstimate(
            flops=2 * own * padded * (width * 12 * HD + 4 * padded * HD), bytes_accessed=8 * MIB, transcendentals=0),
        name="feature_again",
    )(t, cells, gains, shifts, *wqs)


def feature_backward_kernel(t_ref, r0, r1, r2, r3, wo_ref, qkv_ref, p_ref, dqkv_ref, g1_ref):
    rows, padded, width = g1_ref.shape
    groups = r0.shape[0]
    for k, piece in enumerate((r0, r1, r2, r3)):
        for g in range(groups):
            at = pl.multiple_of((lax.bitwise_xor(t_ref[0], k) * groups + g) * SUB, SUB)
            g1_ref[:, pl.ds(at, SUB), :] = piece[g].astype(F32).reshape(rows, SUB, width)
    gl = g1_ref[...].reshape(rows * padded, width).astype(BF)
    do = mm_nt(gl, wo_ref[...]).astype(BF)
    for r in range(rows):
        span = slice(r * padded, (r + 1) * padded)
        for h in range(4):
            at = 3 * HD * h
            dqkv_ref[span, at : at + 3 * HD] = attention_backward(
                qkv_ref[span, at : at + HD], qkv_ref[span, at + HD : at + 2 * HD],
                qkv_ref[span, at + 2 * HD : at + 3 * HD], p_ref[r, h], do[span, HD * h : HD * (h + 1)])


def feature_backward(t, pieces, wo, qkv, p, step):
    own, _, padded, _ = p.shape
    groups, _, width = pieces[0].shape
    wide = qkv.shape[1]
    return pl.pallas_call(
        feature_backward_kernel,
        grid=(own // step,),
        out_shape=[
            jax.ShapeDtypeStruct((own * padded, wide), BF),
            jax.ShapeDtypeStruct((own, padded, width), F32),
        ],
        in_specs=[pl.BlockSpec(memory_space=pltpu.SMEM)]
        + [pl.BlockSpec((groups, step * SUB, width), lambda i: (0, i, 0))] * 4
        + [
            pl.BlockSpec(wo.shape, lambda i: (0, 0)),
            pl.BlockSpec((step * padded, wide), lambda i: (i, 0)),
            pl.BlockSpec((step, 4, padded, padded), lambda i: (i, 0, 0, 0)),
        ],
        out_specs=[
            pl.BlockSpec((step * padded, wide), lambda i: (i, 0)),
            pl.BlockSpec((step, padded, width), lambda i: (i, 0, 0)),
        ],
        compiler_params=pltpu.CompilerParams(vmem_limit_bytes=40 * MIB),
        cost_estimate=pl.CostEstimate(
            flops=2 * own * padded * (width * 4 * HD + 20 * padded * HD), bytes_accessed=9 * MIB, transcendentals=0),
        name="feature_backward",
    )(t, *pieces, wo, qkv, p)


def feature_weights_kernel(n1_ref, dqkv_ref, keep_ref, send_ref):
    n1_t = n1_ref[...].T
    for h in range(4):
        out = (keep_ref, send_ref)[h % 2]
        out[h // 2] = mm(n1_t, dqkv_ref[:, 3 * HD * h : 3 * HD * (h + 1)]).astype(BF)


def feature_weights(n1, dqkv):
    cells, width = n1.shape
    out = jax.ShapeDtypeStruct((2, width, 3 * HD), BF)
    vmem = pl.BlockSpec(memory_space=pltpu.VMEM)
    return pl.pallas_call(
        feature_weights_kernel,
        out_shape=[out] * 2,
        in_specs=[vmem] * 2,
        out_specs=[vmem] * 2,
        compiler_params=pltpu.CompilerParams(vmem_limit_bytes=40 * MIB),
        cost_estimate=pl.CostEstimate(
            flops=2 * cells * width * 12 * HD, bytes_accessed=5 * MIB, transcendentals=0),
        name="feature_weights",
    )(n1, dqkv)


def feature_input_kernel(t_ref, cells_ref, g1_ref, dqkv_ref, gains_ref, wq0, wq1, wq2, wq3, out_ref, stats_ref, scr):
    i = pl.program_id(0)
    rows, feature_count, width = cells_ref.shape
    padded = scr.shape[1]

    @pl.when(i == 0)
    def _():
        scr[...] = jnp.zeros_like(scr)

    scr[:, 0:feature_count, :] = cells_ref[...].astype(F32)
    normed, inverse = standardize(scr[...].reshape(rows * padded, width))
    dn1 = None
    for h, wq in enumerate((wq0, wq1, wq2, wq3)):
        term = mm_nt(dqkv_ref[:, 3 * HD * h : 3 * HD * (h + 1)], wq[...])
        dn1 = term if dn1 is None else dn1 + term
    g1 = g1_ref[...].reshape(rows * padded, width)
    g0 = g1 + norm_backward(dn1, normed, inverse, gains_ref[...].astype(F32)[0:1])
    g0 = g0.reshape(rows, padded, width)
    out_ref[...] = g0[:, 0:feature_count, :].astype(BF)
    stats = jnp.concatenate(
        [column_sum(dn1 * normed), column_sum(dn1), jnp.zeros((6, width), F32)], axis=0)

    @pl.when(i == 0)
    def _():
        stats_ref[...] = stats

    @pl.when(i > 0)
    def _():
        stats_ref[...] += stats


def feature_input(t, cells, g1, dqkv, gains, wqs, step):
    own, padded, width = g1.shape
    feature_count = cells.shape[1]
    steps = own // step
    grid_spec = pltpu.PrefetchScalarGridSpec(
        num_scalar_prefetch=1,
        grid=(steps,),
        in_specs=[
            pl.BlockSpec((step, feature_count, width), lambda i, t: (t[0] * steps + i, 0, 0)),
            pl.BlockSpec((step, padded, width), lambda i, t: (i, 0, 0)),
            pl.BlockSpec((step * padded, dqkv.shape[1]), lambda i, t: (i, 0)),
            pl.BlockSpec(gains.shape, lambda i, t: (0, 0)),
        ]
        + [pl.BlockSpec(w.shape, lambda i, t: (0, 0)) for w in wqs],
        out_specs=[
            pl.BlockSpec((step, feature_count, width), lambda i, t: (i, 0, 0)),
            pl.BlockSpec((8, width), lambda i, t: (0, 0)),
        ],
        scratch_shapes=[pltpu.VMEM((step, padded, width), F32)],
    )
    return pl.pallas_call(
        feature_input_kernel,
        grid_spec=grid_spec,
        out_shape=[
            jax.ShapeDtypeStruct((own, feature_count, width), BF),
            jax.ShapeDtypeStruct((8, width), F32),
        ],
        compiler_params=pltpu.CompilerParams(vmem_limit_bytes=40 * MIB),
        cost_estimate=pl.CostEstimate(
            flops=2 * own * padded * width * 12 * HD, bytes_accessed=8 * MIB, transcendentals=0),
        name="feature_input",
    )(t, cells, g1, dqkv, gains, *wqs)


def rows_kernel(t_ref, p0, p1, p2, p3, out_ref, scr):
    rows, feature_count, width = out_ref.shape
    groups = p0.shape[0]
    for k, piece in enumerate((p0, p1, p2, p3)):
        for g in range(groups):
            at = pl.multiple_of((lax.bitwise_xor(t_ref[0], k) * groups + g) * SUB, SUB)
            scr[:, pl.ds(at, SUB), :] = piece[g].astype(F32).reshape(rows, SUB, width)
    out_ref[...] = scr[:, 0:feature_count, :].astype(BF)


def from_columns(t, pieces, row_count, feature_count, step):
    groups, _, width = pieces[0].shape
    return pl.pallas_call(
        rows_kernel,
        grid=(row_count // step,),
        out_shape=jax.ShapeDtypeStruct((row_count, feature_count, width), BF),
        in_specs=[pl.BlockSpec(memory_space=pltpu.SMEM)]
        + [pl.BlockSpec((groups, step * SUB, width), lambda i: (0, i, 0))] * 4,
        out_specs=pl.BlockSpec((step, feature_count, width), lambda i: (i, 0, 0)),
        scratch_shapes=[pltpu.VMEM((step, 4 * groups * SUB, width), F32)],
        compiler_params=pltpu.CompilerParams(vmem_limit_bytes=24 * MIB),
        cost_estimate=pl.CostEstimate(flops=MIB, bytes_accessed=6 * MIB, transcendentals=0),
        name="from_columns",
    )(t, *pieces)


def swap(values, axis, mask):
    count = lax.axis_size(axis)
    return lax.ppermute(values, axis, [(i, i ^ mask) for i in range(count)])


def gather_groups(own):
    far = swap(own, "tensor", 2)
    return own, swap(own, "tensor", 1), far, swap(far, "tensor", 1)


def dp_radices(count):
    radices = [2]
    rest = count // 2
    while rest > 1:
        step = 4 if rest % 4 == 0 else 2
        radices.append(step)
        rest //= step
    return radices


def digit_of(shift, radix):
    return lax.rem(lax.div(lax.axis_index("dp"), shift), radix)


def scatter_digit(values, shift, radix):
    rows = values.shape[-2] // radix
    mine = digit_of(shift, radix)
    cut = lambda j: lax.dynamic_slice_in_dim(values, lax.bitwise_xor(mine, j) * rows, rows, values.ndim - 2)
    total = cut(0).astype(F32)
    arrived = [swap(cut(j), "dp", j * shift) for j in range(1, radix)]
    for piece in arrived:
        total = total + piece.astype(F32)
    return total.astype(BF)


def gather_digit(values, shift, radix):
    rows = values.shape[-2]
    mine = digit_of(shift, radix)
    out = jnp.zeros(values.shape[:-2] + (rows * radix, values.shape[-1]), values.dtype)
    pieces = [values] + [swap(values, "dp", j * shift) for j in range(1, radix)]
    for j, piece in enumerate(pieces):
        out = lax.dynamic_update_slice_in_dim(out, piece, lax.bitwise_xor(mine, j) * rows, out.ndim - 2)
    return out


def reduce_groups(keep, send, order):
    values = (keep.astype(F32) + swap(send, "tensor", 1).astype(F32)).astype(BF)
    radices = dp_radices(lax.axis_size("dp"))
    shifts = [1]
    for radix in radices[:-1]:
        shifts.append(shifts[-1] * radix)
    done = []
    for stage in order(len(radices)):
        if stage == "x":
            values = (values[0].astype(F32) + swap(values[1], "tensor", 2).astype(F32)).astype(BF)
        else:
            values = scatter_digit(values, shifts[stage], radices[stage])
            done.append(stage)
    for stage in reversed(done):
        values = gather_digit(values, shifts[stage], radices[stage])
    return values.astype(F32)


def y_first(digits):
    return [0, "x"] + list(range(1, digits))


def z_first(digits):
    return list(range(1, digits)) + ["x", 0]


def x_first(digits):
    return ["x"] + list(range(digits))


def sum_everywhere(values):
    for mask in (1, 2):
        values = values + swap(values, "tensor", mask)
    shift = 1
    while shift < lax.axis_size("dp"):
        values = values + swap(values, "dp", shift)
        shift *= 2
    return values


def shards(
    table_cells, splits, feat_qkv, feat_out, feat_out_bias, row_qkv, row_out, row_out_bias,
    up_weight, up_bias, down_weight, down_bias, norm_gains, norm_biases, cotangent,
):
    shape = table_cells.shape
    _, row_count, feature_count, width = shape
    own_rows = row_count // 4
    hidden = up_weight.shape[1]
    t = lax.axis_index("tensor").astype(jnp.int32).reshape(1)
    cells = table_cells.reshape(shape[1:])
    grads = cotangent.reshape(shape[1:])
    fob, rob, dnb = (b.reshape(1, width) for b in (feat_out_bias, row_out_bias, down_bias))
    fq = feat_qkv.reshape(width, 3 * HD)
    rq = row_qkv.reshape(width, 3 * HD)

    outs_own = jnp.concatenate(
        [feat_out, row_out, jnp.broadcast_to(up_bias.reshape(1, hidden), (16, hidden))], axis=0)
    outs = gather_groups(outs_own)
    rqs = gather_groups(rq)
    ups = gather_groups(up_weight)
    downs = gather_groups(down_weight)
    fqs = gather_groups(fq)
    fo = jnp.concatenate([w[:HD] for w in outs], axis=0)
    ro = jnp.concatenate([w[HD : 2 * HD] for w in outs], axis=0)
    ubs = [w[2 * HD : 2 * HD + 1] for w in outs]

    mixed = feature_forward(t, cells, norm_gains, norm_biases, fq, 0, row_count, 8)
    mixed = [mixed[0]] + [swap(mixed[k], "tensor", k) for k in (1, 2, 3)]
    cells_f, grads_f = feature_columns(t, cells, grads, 8)

    first, n2, row_packed, row_p, o2, second, n3 = row_forward(
        splits, mixed, cells_f, fo, fob, norm_gains, norm_biases, rqs, ro, rob)
    out_a, dn3_a, hg0, hg1, bg0, bg1 = hidden_call(n3, grads_f, ups[:2], ubs[:2], downs[:2])
    out_f, g2, gl2, hg2, hg3, bg2, bg3, stats_a = hidden_call(
        n3, grads_f, ups[2:], ubs[2:], downs[2:], [out_a, dn3_a, second, dnb, norm_gains])
    dqkv_r, gl1, s0, s1, s2, s3, stats_b = row_backward(t, g2, first, row_packed, row_p, norm_gains, rqs, ro)
    pieces = [s0] + [swap(s, "tensor", k) for k, s in ((1, s1), (2, s2), (3, s3))]

    n1, feat_packed, feat_p = feature_again(t, cells, norm_gains, norm_biases, fqs, own_rows, 4)
    row_keep, row_send = row_weights(n2, dqkv_r, gl2, o2, gl1, mixed)
    out_pieces = gather_groups(out_f)
    output = from_columns(t, out_pieces, row_count, feature_count, 8).reshape(shape)

    dqkv_f, g1 = feature_backward(t, pieces, fo, feat_packed, feat_p, 4)
    feat_keep, feat_send = feature_weights(n1, dqkv_f)
    g0, stats_c = feature_input(t, cells, g1, dqkv_f, norm_gains, fqs, 4)

    hidden_keep, hidden_send = jnp.stack([hg0, hg2]), jnp.stack([hg1, hg3])
    up_grad = reduce_groups(hidden_keep[:, :, :hidden], hidden_send[:, :, :hidden], y_first)
    down_grad = reduce_groups(hidden_keep[:, :, hidden:], hidden_send[:, :, hidden:], z_first)
    row_grad = reduce_groups(row_keep, row_send, y_first)
    feat_grad = reduce_groups(feat_keep, feat_send, x_first)

    far = bg0 + swap(bg1, "tensor", 1), bg2 + swap(bg3, "tensor", 1)
    up_bias_part = far[0] + swap(far[1], "tensor", 2)
    shift = 1
    while shift < lax.axis_size("dp"):
        up_bias_part = up_bias_part + swap(up_bias_part, "dp", shift)
        shift *= 2

    small = sum_everywhere(jnp.concatenate([stats_a[:4], stats_b[:3], stats_c[:2]], axis=0))

    g0s = gather_groups(g0)
    input_grad = jnp.zeros((row_count, feature_count, width), BF)
    for k, piece in enumerate(g0s):
        input_grad = lax.dynamic_update_slice_in_dim(
            input_grad, piece, lax.bitwise_xor(t[0], k) * own_rows, 0)

    return (
        output,
        input_grad.reshape(shape),
        feat_grad.reshape(width, 3, HD),
        row_grad[:, 4 * HD :].T,
        small[4],
        row_grad[:, : 3 * HD].reshape(width, 3, HD),
        row_grad[:, 3 * HD : 4 * HD].T,
        small[1],
        up_grad,
        up_bias_part.reshape(hidden),
        down_grad.T,
        small[0],
        jnp.stack([small[7], small[5], small[2]]),
        jnp.stack([small[8], small[6], small[3]]),
    )


def solution(mesh):
    return jax.shard_map(
        shards,
        mesh=mesh,
        in_specs=(
            P("dp", None, None, None), P("dp"), P(None, None, "tensor"), P("tensor", None), P(),
            P(None, None, "tensor"), P("tensor", None), P(), P(None, "tensor"), P("tensor"),
            P("tensor", None), P(), P(), P(), P("dp", None, None, None),
        ),
        out_specs=(
            P("dp", None, None, None), P("dp", None, None, None), P(None, None, "tensor"),
            P("tensor", None), P(), P(None, None, "tensor"), P("tensor", None), P(),
            P(None, "tensor"), P("tensor"), P("tensor", None), P(), P(), P(),
        ),
        check_vma=False,
    )
```

time: 748 us -> 353 us (0.47)
  waiting for transfers between devices: 420 us -> 79.9 us
  Pallas kernels: 0 us -> 92.6 us
  matrix products: 83.2 us -> 0 us
  starting transfers between devices: 1.67 us -> 82.2 us
  blocking collectives: 62.6 us -> 0 us
  other arithmetic: 58.4 us -> 13.5 us
  local copies, waits for them, and re-layouts: 97.9 us -> 78.6 us
  between operations: 16.3 us -> 2.63 us
    psum x4 -> x0, waiting for transfers between devices: 269 us -> none  [the longest x3 138 us: branch_total(): lax.psum(partial_out.astype(jnp.bfloat16), 'tensor').astype(jnp.float32)]
    reduce_scatter x3 -> x0, waiting for transfers between devices: 96.2 us -> none  [reduce_back(): lax.psum_scatter(normed_grad.astype(jnp.bfloat16), 'tensor', scatter_dime...]
    pallas_call x0 -> x12, Pallas kernels: none -> 92.6 us  [the longest x2 25.5 us: hidden_call(): pl.pallas_call(kernel, grid=(groups,), out_shape=outs, in_specs=specs, ou...]
    dot_general x30 -> x0, matrix products: 83.2 us -> none  [the longest x1 16.7 us: shards(): jnp.einsum('nd,fd->nf', grad_low, down_weight, preferred_element_type=jnp...]
    ppermute x0 -> x78, starting transfers between devices: none -> 82.2 us  [swap(): return lax.ppermute(values, axis, [(i, i ^ mask) for i in range(count)])]
    ppermute x0 -> x78, waiting for transfers between devices: none -> 79.9 us  [swap(): return lax.ppermute(values, axis, [(i, i ^ mask) for i in range(count)])]
    psum x2 -> x0, blocking collectives: 62.6 us -> none  [the longest x1 40.7 us: shards(): lax.psum((feat_bias_grad, row_bias_grad, down_bias_grad, jnp.stack([gain_...]
    all_gather x3 -> x0, waiting for transfers between devices: 54.3 us -> none  [reduce_back(): lax.all_gather(share_stream.astype(jnp.bfloat16), 'tensor', axis=0, tiled...]
  transfers between devices with their start and end apart: 10 -> 78, of which waited for: 9 -> 18; matrix products, arithmetic and copies ran while one was open for 10% -> 20% of each run, Pallas kernels for 0% -> 26%
where the time goes in v1:
time: 353 us; the launch traced here: 349 us
  Pallas kernels  92.6 us (26%)
  starting transfers between devices  82.2 us (23%)
  waiting for transfers between devices  79.9 us (23%)
  local copies, waits for them, and re-layouts  78.6 us (22%)
  other arithmetic  13.5 us (4%)
    ppermute x78, starting transfers between devices, swap(): return lax.ppermute(values, axis, [(i, i ^ mask) for i in range(count)])  82.2 us
    ppermute x78, waiting for transfers between devices, swap(): return lax.ppermute(values, axis, [(i, i ^ mask) for i in range(count)])  79.9 us
    unnamed x124, local copies, waits for them, and re-layouts  32.8 us
    pallas_call x2, Pallas kernels, hidden_call(): pl.pallas_call(kernel, grid=(groups,), out_shape=outs, in_specs=specs, ou...  25.5 us
    dynamic_update_slice x24, local copies, waits for them, and re-layouts, gather_digit(): lax.dynamic_update_slice_in_dim(out, piece, lax.bitwise_xor(mine, j) * ro...  18.8 us
    pallas_call x1, Pallas kernels, feature_forward(): pl.pallas_call(feature_forward_kernel, grid=(count // step,), out_shape=[...  14 us
    pallas_call x1, Pallas kernels, row_backward(): pl.pallas_call(row_backward_kernel, grid=(groups,), out_shape=[jax.ShapeD...  11.1 us
    pallas_call x1, Pallas kernels, feature_backward(): pl.pallas_call(feature_backward_kernel, grid=(own // step,), out_shape=[j...  10.8 us
  transfers between devices with their start and end apart: 78, of which 18 were waited for; matrix products, arithmetic and copies ran while one was open for 20% of the time, Pallas kernels for 26%

profile of v1, /device:TPU:0, one launch (start us, length us, event | category | flops | bytes accessed | tf_op | source)
XLA Modules:
  0.0 349.4 jit_solution(5526570989653269631)
XLA Ops:
  3.0 2.9 collective-permute-start.4
  7.4 3.5 copy.122
  10.9 14.0 %feature_forward.1 = (bf16[3,256,128]{2,1,0:T(8,128)(2,1)S(1)}, bf16[3,256,128]{2,1,0:T(8,128)(2,1)}, bf16[3,256,128]{2,1,0:T(8,128)(2,1)}, bf16[3,256,128]{2,1,0:T(8,128)(2,1)}) custom-call(s32[1]{0:T(128)} %bitcast.t_ref, bf16[32,89,512]{2,1,0:T(8,128)(2,1)S(1)} %bitcast.62, bf16[3,512]{1,0:T(4,128)(2,1)S(1)} %copy-done.16, bf16[3,512]{1,0:T(4,128)(2,1)S(1)} %copy-done.26, ...), custom_call_target="tpu_custom_call" | custom-call | flops 1358954496 | bytes 4194304 | tf_op jit(solution)/shard_map/feature_forward/pallas_call | solution.py:108
  25.6 1.9 collective-permute-start.2
  27.8 3.4 copy.121
  31.1 1.9 copy.88
  33.0 1.9 copy.91.wq0
  37.7 1.9 copy-done
  47.1 5.9 %collective-permute-done.7.wq2 = bf16[512,384]{1,0:T(8,128)(2,1)S(1)} collective-permute-done((bf16[512,384]{1,0:T(8,128)(2,1)S(1)}, bf16[512,384]{1,0:T(8,128)(2,1)S(1)}, u32[]{:S(2)}, u32[]{:S(2)}) %collective-permute-start.7) | collective-permute-done | bytes 393248 | tf_op jit(solution)/shard_map/ppermute | solution.py:681
  53.6 10.6 %collective-permute-done.9.up0 = bf16[512,512]{1,0:T(8,128)(2,1)S(1)} collective-permute-done((bf16[512,512]{1,0:T(8,128)(2,1)S(1)}, bf16[512,512]{1,0:T(8,128)(2,1)S(1)}, u32[]{:S(2)}, u32[]{:S(2)}) %collective-permute-start.9) | collective-permute-done | bytes 524320 | tf_op jit(solution)/shard_map/ppermute | solution.py:681
  64.4 11.0 %collective-permute-done.11.down0 = bf16[512,512]{1,0:T(8,128)(2,1)S(1)} collective-permute-done((bf16[512,512]{1,0:T(8,128)(2,1)S(1)}, bf16[512,512]{1,0:T(8,128)(2,1)S(1)}, u32[]{:S(2)}, u32[]{:S(2)}) %collective-permute-start.11) | collective-permute-done | bytes 524320 | tf_op jit(solution)/shard_map/ppermute | solution.py:681
  75.9 10.0 %row_forward.1 = (f32[3,256,512]{2,1,0:T(8,128)}, bf16[3,256,512]{2,1,0:T(8,128)(2,1)S(1)}, bf16[3,256,1536]{2,1,0:T(8,128)(2,1)}, bf16[3,4,256,256]{3,2,1,0:T(8...) custom-call(s32[1]{0:T(128)S(6)} %copy.151.split_ref, ...), custom_call_target="tpu_custom_call" | custom-call | flops 2415919104 | bytes 16777216 | tf_op jit(solution)/shard_map/row_forward/pallas_call | solution.py:213
  88.3 11.1 %hidden_first.1 = (f32[3,256,512]{2,1,0:T(8,128)}, f32[3,256,512]{2,1,0:T(8,128)}, bf16[512,1024]{1,0:T(8,128)(2,1)S(1)}, bf16[512,1024]{1,0:T(8,128)(2,1)S(1)},...) custom-call(bf16[3,256,512]{2,1,0:T(8,128)(2,1)S(1)} %get-tuple-element.64.n3_ref, ...), custom_call_target="tpu_custom_call" | custom-call | flops 4831838208 | bytes 16777216 | tf_op jit(solution)/shard_map/hidden_first/pallas_call | solution.py:340
  102.0 14.3 %hidden_second.1 = (bf16[3,256,512]{2,1,0:T(8,128)(2,1)S(1)}, f32[3,256,512]{2,1,0:T(8,128)}, bf16[3,256,512]{2,1,0:T(8,128)(2,1)S(1)}, bf16[512,1024]{1,0:T(8,1...) custom-call(bf16[3,256,512]{2,1,0:T(8,128)(2,1)S(1)} %get-tuple-elemen, ...), custom_call_target="tpu_custom_call" | custom-call | flops 4831838208 | bytes 16777216 | tf_op jit(solution)/shard_map/hidden_second/pallas_call | solution.py:340
  119.5 11.1 %row_backward.1 = (bf16[3,256,1536]{2,1,0:T(8,128)(2,1)}, bf16[3,256,512]{2,1,0:T(8,128)(2,1)S(1)}, bf16[3,64,512]{2,1,0:T(8,128)(2,1)S(1)}, bf16[3,64,512]{2,1,...) custom-call(s32[1]{0:T(128)} %bitcast.t_ref, ...), custom_call_target="tpu_custom_call" | custom-call | flops 2415919104 | bytes 16777216 | tf_op jit(solution)/shard_map/row_backward/pallas_call | solution.py:406
  135.3 5.3 %feature_again.1 = (bf16[768,512]{1,0:T(8,128)(2,1)S(1)}, bf16[768,1536]{1,0:T(8,128)(2,1)S(1)}, bf16[8,4,96,96]{3,2,1,0:T(8,128)(2,1)S(1)}) custom-call(s32[1]{0:T(128)} %bitcast.t_ref, bf16[32,89,512]{2,1,0:T(8,128)(2,1)S(1)} %bitcast.64, bf16[3,512]{1,0:T(4,128)(2,1)S(1)} %copy-done.16, bf16[3,512]{1,0:T(4,128)(2,1)S(1)} %copy-done.26, ...), custom_call_target="tpu_custom_call" | custom-call | flops 1283457024 | bytes 8388608 | tf_op jit(solution)/shard_map/feature_again/pallas_call | solution.py:503
  141.9 2.3 collective-permute-done.20.r3
  144.2 10.8 %feature_backward.1 = (bf16[768,1536]{1,0:T(8,128)(2,1)S(1)}, f32[8,96,512]{2,1,0:T(8,128)S(1)}) custom-call(s32[1]{0:T(128)} %bitcast.t_ref, bf16[3,64,512]{2,1,0:T(8,128)(2,1)S(1)} %copy-done.15, bf16[3,64,512]{2,1,0:T(8,128)(2,1)} %collective-permute-done.18.r1, bf16[3,64,512]{2,1,0:T(8,128)(2,1)} %collective-permute-done.19.r2, ...), custom_call_target="tpu_custom_call" | custom-call | flops 780140544 | bytes 9437184 | tf_op jit(solution)/shard_map/feature_backward/pallas_call | solution.py:540
  155.0 4.9 %feature_input.1 = (bf16[8,89,512]{2,1,0:T(8,128)(2,1)S(1)}, f32[8,512]{1,0:T(8,128)S(1)}) custom-call(s32[1]{0:T(128)} %bitcast.t_ref, bf16[32,89,512]{2,1,0:T(8,128)(2,1)S(1)} %bitcast.65, f32[8,96,512]{2,1,0:T(8,128)S(1)} %get-tuple-element.80.g1_ref, bf16[768,1536]{1,0:T(8,128)(2,1)S(1)} %get-tuple-element.81.dqkv_ref, bf16[3,512]{1,0:T(4,128)(2,1)S(1)} %copy-done.16, ...), custom_call_target="tpu_custom_call" | custom-call | flops 1207959552 | bytes 8388608 | tf_op jit(solution)/shard_map/feature_input/pallas_call | solution.py:639
  162.8 2.1 collective-permute-done.65
  171.3 2.7 collective-permute-start.67
  176.1 6.3 %row_weights.1 = (bf16[2,512,640]{2,1,0:T(8,128)(2,1)S(1)}, bf16[2,512,640]{2,1,0:T(8,128)(2,1)}) custom-call(bf16[3,256,512]{2,1,0:T(8,128)(2,1)S(1)} %copy-done.32, bf16[3,256,1536]{2,1,0:T(8,128)(2,1)} %get-tuple-element.87.dqkv_ref, bf16[3,256,512]{2,1,0:T(8,128)(2,1)S(1)} %copy-done.36, bf16[3,256,512]{2,1,0:T(8,128)(2,1)S(1)} %copy-done.34, ...), custom_call_target="tpu_custom_call" | custom-call | flops 2013265920 | bytes 10485760 | tf_op jit(solution)/shard_map/row_weights/pallas_call | solution.py:447
  184.1 2.0 reshape.106
  187.9 1.8 feature_weights.1
  189.7 2.6 collective-permute-done.51
  195.0 10.4 %collective-permute-done.25 = bf16[8,89,512]{2,0,1:T(8,128)(2,1)} collective-permute-done((bf16[8,89,512]{2,0,1:T(8,128)(2,1)S(1)}, bf16[8,89,512]{2,0,1:T(8,128)(2,1)}, u32[]{:S(2)}, u32[]{:S(2)}) %collective-permute-start.25) | collective-permute-done | bytes 729120 | tf_op jit(solution)/shard_map/ppermute | solution.py:681
  205.4 2.2 bitcast_dynamic-update-slice_fusion.1
  209.4 2.8 collective-permute-start.70
  214.7 8.6 %collective-permute-done.69 = bf16[2,128,512]{2,1,0:T(8,128)(2,1)S(1)} collective-permute-done((bf16[2,128,512]{2,1,0:T(8,128)(2,1)S(1)}, bf16[2,128,512]{2,1,0:T(8,128)(2,1)S(1)}, u32[]{:S(2)}, u32[]{:S(2)}) %collective-permute-start.69) | collective-permute-done | bytes 262176 | tf_op jit(solution)/shard_map/ppermute | solution.py:681
  224.9 6.3 %collective-permute-done.71 = bf16[2,128,512]{2,1,0:T(8,128)(2,1)S(1)} collective-permute-done((bf16[2,128,512]{2,1,0:T(8,128)(2,1)S(1)}, bf16[2,128,512]{2,1,0:T(8,128)(2,1)S(1)}, u32[]{:S(2)}, u32[]{:S(2)}) %collective-permute-start.71) | collective-permute-done | bytes 262176 | tf_op jit(solution)/shard_map/ppermute | solution.py:681
  236.5 3.5 %collective-permute-done.72 = bf16[128,512]{1,0:T(8,128)(2,1)S(1)} collective-permute-done((bf16[128,512]{1,0:T(8,128)(2,1)S(1)}, bf16[128,512]{1,0:T(8,128)(2,1)S(1)}, u32[]{:S(2)}, u32[]{:S(2)}) %collective-permute-start.72) | collective-permute-done | bytes 131104 | tf_op jit(solution)/shard_map/ppermute | solution.py:681
  242.4 3.7 %collective-permute-done.73 = bf16[64,512]{1,0:T(8,128)(2,1)S(1)} collective-permute-done((bf16[64,512]{1,0:T(8,128)(2,1)S(1)}, bf16[64,512]{1,0:T(8,128)(2,1)S(1)}, u32[]{:S(2)}, u32[]{:S(2)}) %collective-permute-start.73) | collective-permute-done | bytes 65568 | tf_op jit(solution)/shard_map/ppermute | solution.py:681
  257.3 5.1 %collective-permute-start.30 = (bf16[64,384]{1,0:T(8,128)(2,1)S(1)}, bf16[64,384]{1,0:T(8,128)(2,1)S(1)}, u32[]{:S(2)}, u32[]{:S(2)}) collective-permute-start(bf16[64,384]{1,0:T(8,128)(2,1)S(1)} %get-tuple-element.167), channel_id=1, source_target_pairs={{0,8},{4,12},{8,0},{12,4},{16,24},{20,28},{24,16},{28,20},{1,9},{5... | collective-permute-start | bytes 147464 | tf_op jit(solution)/shard_map/ppermute | solution.py:681
  263.4 1.9 dynamic_update_slice.111
  265.3 3.9 %collective-permute-start.31 = (bf16[64,384]{1,0:T(8,128)(2,1)S(1)}, bf16[64,384]{1,0:T(8,128)(2,1)S(1)}, u32[]{:S(2)}, u32[]{:S(2)}) collective-permute-start(bf16[64,384]{1,0:T(8,128)(2,1)S(1)} %get-tuple-element.169), channel_id=1, source_target_pairs={{0,16},{4,20},{8,24},{12,28},{16,0},{20,4},{24,8},{28,12},{1,17},{... | collective-permute-start | bytes 147464 | tf_op jit(solution)/shard_map/ppermute | solution.py:681
  274.6 3.2 copy.114
  280.9 2.4 collective-permute-start.34
  285.6 2.0 bitcast_dynamic-update-slice_fusion
  287.6 2.1 collective-permute-start.76
  296.6 2.4 collective-permute-done.54
  300.5 2.7 collective-permute-start.56
  307.8 2.3 collective-permute-done.57
  310.2 2.2 collective-permute-start.58
  316.1 2.1 collective-permute-start.41
  327.3 1.8 collective-permute-start.44
  333.5 2.5 dynamic_update_slice.99
  337.7 2.1 dynamic_update_slice.101
  342.3 4.6 %collective-permute-done.46 = bf16[256,640]{0,1:T(8,128)(2,1)S(1)} collective-permute-done((bf16[256,640]{0,1:T(8,128)(2,1)S(1)}, bf16[256,640]{0,1:T(8,128)(2,1)S(1)}, u32[]{:S(2)}, u32[]{:S(2)}) %collective-permute-start.46) | collective-permute-done | bytes 327712 | tf_op jit(solution)/shard_map/ppermute | solution.py:681
  (360 shorter events, 119.5 us)
Async XLA Ops:
  3.0 40.1 %collective-permute-start.4 = (bf16[272,512]{1,0:T(8,128)(2,1)}, bf16[272,512]{1,0:T(8,128)(2,1)}, u32[]{:S(2)}, u32[]{:S(2)}) collective-permute-start(bf16[272,512]{1,0:T(8,128)(2,1)} %pad_maximum_fusion.4), channel_id=1, source_target_pairs={{0,2},{1,3},{2,0},{3,1},{4,6},{5,7},{6,4},{7,5},{8,10},{9,11},{10,... | collective-permute-start | bytes 835592 | tf_op jit(solution)/shard_map/ppermute | solution.py:681
  25.6 15.3 %collective-permute-start = (bf16[3,256,128]{2,1,0:T(8,128)(2,1)}, bf16[3,256,128]{2,1,0:T(8,128)(2,1)}, u32[]{:S(2)}, u32[]{:S(2)}) collective-permute-start(bf16[3,256,128]{2,1,0:T(8,128)(2,1)} %get-tuple-element.60), channel_id=1, source_target_pairs={{0,1},{1,0},{2,3},{3,2},{4,5},{5,4},{6,7},{7,6},{8,9},{9,8},{10,11... | collective-permute-start | bytes 589832 | tf_op jit(solution)/shard_map/ppermute | solution.py:681
  25.6 15.5 %collective-permute-start.1 = (bf16[3,256,128]{2,1,0:T(8,128)(2,1)}, bf16[3,256,128]{2,1,0:T(8,128)(2,1)}, u32[]{:S(2)}, u32[]{:S(2)}) collective-permute-start(bf16[3,256,128]{2,1,0:T(8,128)(2,1)} %get-tuple-element.61), channel_id=1, source_target_pairs={{0,2},{1,3},{2,0},{3,1},{4,6},{5,7},{6,4},{7,5},{8,10},{9,11},{10,... | collective-permute-start | bytes 589832 | tf_op jit(solution)/shard_map/ppermute | solution.py:681
  25.6 15.7 %collective-permute-start.2 = (bf16[3,256,128]{2,1,0:T(8,128)(2,1)}, bf16[3,256,128]{2,1,0:T(8,128)(2,1)}, u32[]{:S(2)}, u32[]{:S(2)}) collective-permute-start(bf16[3,256,128]{2,1,0:T(8,128)(2,1)} %get-tuple-element.62), channel_id=1, source_target_pairs={{0,3},{1,2},{2,1},{3,0},{4,7},{5,6},{6,5},{7,4},{8,11},{9,10},{10,... | collective-permute-start | bytes 589832 | tf_op jit(solution)/shard_map/ppermute | solution.py:681
  27.5 16.8 %collective-permute-start.3 = (bf16[272,512]{1,0:T(8,128)(2,1)}, bf16[272,512]{1,0:T(8,128)(2,1)}, u32[]{:S(2)}, u32[]{:S(2)}) collective-permute-start(bf16[272,512]{1,0:T(8,128)(2,1)} %pad_maximum_fusion.4), channel_id=1, source_target_pairs={{0,1},{1,0},{2,3},{3,2},{4,5},{5,4},{6,7},{7,6},{8,9},{9,8},{10,11... | collective-permute-start | bytes 835592 | tf_op jit(solution)/shard_map/ppermute | solution.py:681
  40.9 12.0 %collective-permute-start.7 = (bf16[512,384]{1,0:T(8,128)(2,1)S(1)}, bf16[512,384]{1,0:T(8,128)(2,1)S(1)}, u32[]{:S(2)}, u32[]{:S(2)}) collective-permute-start(bf16[512,384]{1,0:T(8,128)(2,1)S(1)} %copy-done.7), channel_id=1, source_target_pairs={{0,2},{1,3},{2,0},{3,1},{4,6},{5,7},{6,4},{7,5},{8,10},{9,11},{10,... | collective-permute-start | bytes 1179656 | tf_op jit(solution)/shard_map/ppermute | solution.py:681
  41.1 11.8 %collective-permute-start.6 = (bf16[512,384]{1,0:T(8,128)(2,1)S(1)}, bf16[512,384]{1,0:T(8,128)(2,1)S(1)}, u32[]{:S(2)}, u32[]{:S(2)}) collective-permute-start(bf16[512,384]{1,0:T(8,128)(2,1)S(1)} %copy-done.7), channel_id=1, source_target_pairs={{0,1},{1,0},{2,3},{3,2},{4,5},{5,4},{6,7},{7,6},{8,9},{9,8},{10,11... | collective-permute-start | bytes 1179656 | tf_op jit(solution)/shard_map/ppermute | solution.py:681
  41.3 22.9 %collective-permute-start.9 = (bf16[512,512]{1,0:T(8,128)(2,1)S(1)}, bf16[512,512]{1,0:T(8,128)(2,1)S(1)}, u32[]{:S(2)}, u32[]{:S(2)}) collective-permute-start(bf16[512,512]{1,0:T(8,128)(2,1)S(1)} %copy-done.24), channel_id=1, source_target_pairs={{0,2},{1,3},{2,0},{3,1},{4,6},{5,7},{6,4},{7,5},{8,10},{9,11},{10,... | collective-permute-start | bytes 1572872 | tf_op jit(solution)/shard_map/ppermute | solution.py:681
  43.1 10.3 %collective-permute-start.5 = (bf16[272,512]{1,0:T(8,128)(2,1)}, bf16[272,512]{1,0:T(8,128)(2,1)S(1)}, u32[]{:S(2)}, u32[]{:S(2)}) collective-permute-start(bf16[272,512]{1,0:T(8,128)(2,1)} %collective-permute-done.4), channel_id=1, source_target_pairs={{0,1},{1,0},{2,3},{3,2},{4,5},{5,4},{6,7},{7,6},{8,9},{9,8},{10,11... | collective-permute-start | bytes 835592 | tf_op jit(solution)/shard_map/ppermute | solution.py:681
  44.3 31.1 %collective-permute-start.11 = (bf16[512,512]{1,0:T(8,128)(2,1)S(1)}, bf16[512,512]{1,0:T(8,128)(2,1)S(1)}, u32[]{:S(2)}, u32[]{:S(2)}) collective-permute-start(bf16[512,512]{1,0:T(8,128)(2,1)S(1)} %copy-done.25), channel_id=1, source_target_pairs={{0,2},{1,3},{2,0},{3,1},{4,6},{5,7},{6,4},{7,5},{8,10},{9,11},{10,... | collective-permute-start | bytes 1572872 | tf_op jit(solution)/shard_map/ppermute | solution.py:681
  53.0 34.9 %collective-permute-start.13 = (bf16[512,512]{1,0:T(8,128)(2,1)S(1)}, bf16[512,512]{1,0:T(8,128)(2,1)S(1)}, u32[]{:S(2)}, u32[]{:S(2)}) collective-permute-start(bf16[512,512]{1,0:T(8,128)(2,1)S(1)} %copy-done.24), channel_id=1, source_target_pairs={{0,1},{1,0},{2,3},{3,2},{4,5},{5,4},{6,7},{7,6},{8,9},{9,8},{10,11... | collective-permute-start | bytes 1572872 | tf_op jit(solution)/shard_map/ppermute | solution.py:681
  53.0 35.3 %collective-permute-start.14 = (bf16[512,512]{1,0:T(8,128)(2,1)S(1)}, bf16[512,512]{1,0:T(8,128)(2,1)S(1)}, u32[]{:S(2)}, u32[]{:S(2)}) collective-permute-start(bf16[512,512]{1,0:T(8,128)(2,1)S(1)} %copy-done.25), channel_id=1, source_target_pairs={{0,1},{1,0},{2,3},{3,2},{4,5},{5,4},{6,7},{7,6},{8,9},{9,8},{10,11... | collective-permute-start | bytes 1572872 | tf_op jit(solution)/shard_map/ppermute | solution.py:681
  53.5 22.0 %collective-permute-start.8 = (bf16[512,384]{1,0:T(8,128)(2,1)S(1)}, bf16[512,384]{1,0:T(8,128)(2,1)S(1)}, u32[]{:S(2)}, u32[]{:S(2)}) collective-permute-start(bf16[512,384]{1,0:T(8,128)(2,1)S(1)} %collective-permute-done.7.wq2), channel_id=1, source_target_pairs={{0,1},{1,0},{2,3},{3,2},{4,5},{5,4},{6,7},{7,6},{8,9},{9,8},{10,11... | collective-permute-start | bytes 1179656 | tf_op jit(solution)/shard_map/ppermute | solution.py:681
  64.2 23.6 %collective-permute-start.22 = (bf16[512,384]{1,0:T(8,128)(2,1)S(1)}, bf16[512,384]{1,0:T(8,128)(2,1)}, u32[]{:S(2)}, u32[]{:S(2)}) collective-permute-start(bf16[512,384]{1,0:T(8,128)(2,1)S(1)} %copy.86.w_ref.wq0), channel_id=1, source_target_pairs={{0,2},{1,3},{2,0},{3,1},{4,6},{5,7},{6,4},{7,5},{8,10},{9,11},{10,... | collective-permute-start | bytes 1179656 | tf_op jit(solution)/shard_map/ppermute | solution.py:681
  75.4 26.0 %collective-permute-start.10 = (bf16[512,512]{1,0:T(8,128)(2,1)S(1)}, bf16[512,512]{1,0:T(8,128)(2,1)S(1)}, u32[]{:S(2)}, u32[]{:S(2)}) collective-permute-start(bf16[512,512]{1,0:T(8,128)(2,1)S(1)} %collective-permute-done.9.up0), channel_id=1, source_target_pairs={{0,1},{1,0},{2,3},{3,2},{4,5},{5,4},{6,7},{7,6},{8,9},{9,8},{10,11... | collective-permute-start | bytes 1572872 | tf_op jit(solution)/shard_map/ppermute | solution.py:681
  75.4 26.0 %collective-permute-start.12 = (bf16[512,512]{1,0:T(8,128)(2,1)S(1)}, bf16[512,512]{1,0:T(8,128)(2,1)S(1)}, u32[]{:S(2)}, u32[]{:S(2)}) collective-permute-start(bf16[512,512]{1,0:T(8,128)(2,1)S(1)} %collective-permute-done.11.down0), channel_id=1, source_target_pairs={{0,1},{1,0},{2,3},{3,2},{4,5},{5,4},{6,7},{7,6},{8,9},{9,8},{10,11... | collective-permute-start | bytes 1572872 | tf_op jit(solution)/shard_map/ppermute | solution.py:681
  87.8 46.9 %collective-permute-start.21 = (bf16[512,384]{1,0:T(8,128)(2,1)S(1)}, bf16[512,384]{1,0:T(8,128)(2,1)}, u32[]{:S(2)}, u32[]{:S(2)}) collective-permute-start(bf16[512,384]{1,0:T(8,128)(2,1)S(1)} %copy.86.w_ref.wq0), channel_id=1, source_target_pairs={{0,1},{1,0},{2,3},{3,2},{4,5},{5,4},{6,7},{7,6},{8,9},{9,8},{10,11... | collective-permute-start | bytes 1179656 | tf_op jit(solution)/shard_map/ppermute | solution.py:681
  87.8 47.2 %collective-permute-start.23 = (bf16[512,384]{1,0:T(8,128)(2,1)}, bf16[512,384]{1,0:T(8,128)(2,1)}, u32[]{:S(2)}, u32[]{:S(2)}) collective-permute-start(bf16[512,384]{1,0:T(8,128)(2,1)} %collective-permute-done.22.wq2), channel_id=1, source_target_pairs={{0,1},{1,0},{2,3},{3,2},{4,5},{5,4},{6,7},{7,6},{8,9},{9,8},{10,11... | collective-permute-start | bytes 1179656 | tf_op jit(solution)/shard_map/ppermute | solution.py:681
  133.0 11.2 %collective-permute-start.20 = (bf16[3,64,512]{2,1,0:T(8,128)(2,1)}, bf16[3,64,512]{2,1,0:T(8,128)(2,1)}, u32[]{:S(2)}, u32[]{:S(2)}) collective-permute-start(bf16[3,64,512]{2,1,0:T(8,128)(2,1)} %get-tuple-element.77), channel_id=1, source_target_pairs={{0,3},{1,2},{2,1},{3,0},{4,7},{5,6},{6,5},{7,4},{8,11},{9,10},{10,... | collective-permute-start | bytes 589832 | tf_op jit(solution)/shard_map/ppermute | solution.py:681
  134.7 26.5 %collective-permute-start.62 = (f32[1,512]{1,0:T(1,128)}, f32[1,512]{1,0:T(1,128)S(1)}, u32[]{:S(2)}, u32[]{:S(2)}) collective-permute-start(f32[1,512]{1,0:T(1,128)} %copy-done.27), channel_id=1, source_target_pairs={{0,1},{1,0},{2,3},{3,2},{4,5},{5,4},{6,7},{7,6},{8,9},{9,8},{10,11... | collective-permute-start | bytes 6152 | tf_op jit(solution)/shard_map/ppermute | solution.py:681
  141.5 19.7 %collective-permute-start.64 = (f32[1,512]{1,0:T(1,128)S(1)}, f32[1,512]{1,0:T(1,128)S(1)}, u32[]{:S(2)}, u32[]{:S(2)}) collective-permute-start(f32[1,512]{1,0:T(1,128)S(1)} %add.223), channel_id=1, source_target_pairs={{0,2},{1,3},{2,0},{3,1},{4,6},{5,7},{6,4},{7,5},{8,10},{9,11},{10,... | collective-permute-start | bytes 6152 | tf_op jit(solution)/shard_map/ppermute | solution.py:681
  169.6 38.7 %collective-permute-start.52 = (bf16[2,512,512]{2,1,0:T(8,128)(2,1)S(1)}, bf16[2,512,512]{2,1,0:T(8,128)(2,1)S(1)}, u32[]{:S(2)}, u32[]{:S(2)}) collective-permute-start(bf16[2,512,512]{2,1,0:T(8,128)(2,1)S(1)} %get-tuple-element.149), channel_id=1, source_target_pairs={{0,1},{1,0},{2,3},{3,2},{4,5},{5,4},{6,7},{7,6},{8,9},{9,8},{10,11... | collective-permute-start | bytes 3145736 | tf_op jit(solution)/shard_map/ppermute | solution.py:681
  169.7 37.9 %collective-permute-start.16 = (bf16[3,256,512]{2,1,0:T(8,128)(2,1)S(1)}, bf16[3,256,512]{2,1,0:T(8,128)(2,1)S(1)}, u32[]{:S(2)}, u32[]{:S(2)}) collective-permute-start(bf16[3,256,512]{2,1,0:T(8,128)(2,1)S(1)} %copy-done.13), channel_id=1, source_target_pairs={{0,2},{1,3},{2,0},{3,1},{4,6},{5,7},{6,4},{7,5},{8,10},{9,11},{10,... | collective-permute-start | bytes 2359304 | tf_op jit(solution)/shard_map/ppermute | solution.py:681
  171.3 11.1 %collective-permute-start.67 = (f32[1,512]{1,0:T(1,128)S(1)}, f32[1,512]{1,0:T(1,128)S(1)}, u32[]{:S(2)}, u32[]{:S(2)}) collective-permute-start(f32[1,512]{1,0:T(1,128)S(1)} %add.226), channel_id=1, source_target_pairs={{0,16},{4,20},{8,24},{12,28},{16,0},{20,4},{24,8},{28,12},{1,17},{... | collective-permute-start | bytes 6152 | tf_op jit(solution)/shard_map/ppermute | solution.py:681
  174.4 19.2 %collective-permute-start.24 = (bf16[8,89,512]{2,0,1:T(8,128)(2,1)S(1)}, bf16[8,89,512]{2,0,1:T(8,128)(2,1)S(1)}, u32[]{:S(2)}, u32[]{:S(2)}) collective-permute-start(bf16[8,89,512]{2,0,1:T(8,128)(2,1)S(1)} %copy.98), channel_id=1, source_target_pairs={{0,1},{1,0},{2,3},{3,2},{4,5},{5,4},{6,7},{7,6},{8,9},{9,8},{10,11... | collective-permute-start | bytes 2187272 | tf_op jit(solution)/shard_map/ppermute | solution.py:681
  183.0 22.4 %collective-permute-start.25 = (bf16[8,89,512]{2,0,1:T(8,128)(2,1)S(1)}, bf16[8,89,512]{2,0,1:T(8,128)(2,1)}, u32[]{:S(2)}, u32[]{:S(2)}) collective-permute-start(bf16[8,89,512]{2,0,1:T(8,128)(2,1)S(1)} %copy.98), channel_id=1, source_target_pairs={{0,2},{1,3},{2,0},{3,1},{4,6},{5,7},{6,4},{7,5},{8,10},{9,11},{10,... | collective-permute-start | bytes 2187272 | tf_op jit(solution)/shard_map/ppermute | solution.py:681
  192.3 15.6 %collective-permute-start.27 = (bf16[2,512,384]{2,1,0:T(8,128)(2,1)S(1)}, bf16[2,512,384]{2,1,0:T(8,128)(2,1)S(1)}, u32[]{:S(2)}, u32[]{:S(2)}) collective-permute-start(bf16[2,512,384]{2,1,0:T(8,128)(2,1)S(1)} %get-tuple-element.85), channel_id=1, source_target_pairs={{0,1},{1,0},{2,3},{3,2},{4,5},{5,4},{6,7},{7,6},{8,9},{9,8},{10,11... | collective-permute-start | bytes 2359304 | tf_op jit(solution)/shard_map/ppermute | solution.py:681
  193.6 14.8 %collective-permute-start.68 = (bf16[2,512,512]{2,1,0:T(8,128)(2,1)S(1)}, bf16[2,512,512]{2,1,0:T(8,128)(2,1)S(1)}, u32[]{:S(2)}, u32[]{:S(2)}) collective-permute-start(bf16[2,512,512]{2,1,0:T(8,128)(2,1)S(1)} %get-tuple-element.148), channel_id=1, source_target_pairs={{0,1},{1,0},{2,3},{3,2},{4,5},{5,4},{6,7},{7,6},{8,9},{9,8},{10,11... | collective-permute-start | bytes 3145736 | tf_op jit(solution)/shard_map/ppermute | solution.py:681
  207.6 63.7 %collective-permute-start.15 = (bf16[3,256,512]{2,1,0:T(8,128)(2,1)S(1)}, bf16[3,256,512]{2,1,0:T(8,128)(2,1)S(1)}, u32[]{:S(2)}, u32[]{:S(2)}) collective-permute-start(bf16[3,256,512]{2,1,0:T(8,128)(2,1)S(1)} %copy-done.13), channel_id=1, source_target_pairs={{0,1},{1,0},{2,3},{3,2},{4,5},{5,4},{6,7},{7,6},{8,9},{9,8},{10,11... | collective-permute-start | bytes 2359304 | tf_op jit(solution)/shard_map/ppermute | solution.py:681
  208.0 63.5 %collective-permute-start.17 = (bf16[3,256,512]{2,1,0:T(8,128)(2,1)S(1)}, bf16[3,256,512]{2,1,0:T(8,128)(2,1)S(1)}, u32[]{:S(2)}, u32[]{:S(2)}) collective-permute-start(bf16[3,256,512]{2,1,0:T(8,128)(2,1)S(1)} %collective-permute-done.16.p2), channel_id=1, source_target_pairs={{0,1},{1,0},{2,3},{3,2},{4,5},{5,4},{6,7},{7,6},{8,9},{9,8},{10,11... | collective-permute-start | bytes 2359304 | tf_op jit(solution)/shard_map/ppermute | solution.py:681
  209.1 14.2 %collective-permute-start.69 = (bf16[2,128,512]{2,1,0:T(8,128)(2,1)S(1)}, bf16[2,128,512]{2,1,0:T(8,128)(2,1)S(1)}, u32[]{:S(2)}, u32[]{:S(2)}) collective-permute-start(bf16[2,128,512]{2,1,0:T(8,128)(2,1)S(1)} %get-tuple-element.152), channel_id=1, source_target_pairs={{0,8},{4,12},{8,0},{12,4},{16,24},{20,28},{24,16},{28,20},{1,9},{5... | collective-permute-start | bytes 786440 | tf_op jit(solution)/shard_map/ppermute | solution.py:681
  209.4 14.0 %collective-permute-start.70 = (bf16[2,128,512]{2,1,0:T(8,128)(2,1)S(1)}, bf16[2,128,512]{2,1,0:T(8,128)(2,1)S(1)}, u32[]{:S(2)}, u32[]{:S(2)}) collective-permute-start(bf16[2,128,512]{2,1,0:T(8,128)(2,1)S(1)} %get-tuple-element.154), channel_id=1, source_target_pairs={{0,16},{4,20},{8,24},{12,28},{16,0},{20,4},{24,8},{28,12},{1,17},{... | collective-permute-start | bytes 786440 | tf_op jit(solution)/shard_map/ppermute | solution.py:681
  213.0 18.1 %collective-permute-start.71 = (bf16[2,128,512]{2,1,0:T(8,128)(2,1)S(1)}, bf16[2,128,512]{2,1,0:T(8,128)(2,1)S(1)}, u32[]{:S(2)}, u32[]{:S(2)}) collective-permute-start(bf16[2,128,512]{2,1,0:T(8,128)(2,1)S(1)} %get-tuple-element.153), channel_id=1, source_target_pairs={{0,24},{4,28},{8,16},{12,20},{16,8},{20,12},{24,0},{28,4},{1,25},{... | collective-permute-start | bytes 786440 | tf_op jit(solution)/shard_map/ppermute | solution.py:681
  223.4 60.5 %collective-permute-start.26 = (bf16[8,89,512]{2,0,1:T(8,128)(2,1)}, bf16[8,89,512]{2,0,1:T(8,128)(2,1)}, u32[]{:S(2)}, u32[]{:S(2)}) collective-permute-start(bf16[8,89,512]{2,0,1:T(8,128)(2,1)} %collective-permute-done.25), channel_id=1, source_target_pairs={{0,1},{1,0},{2,3},{3,2},{4,5},{5,4},{6,7},{7,6},{8,9},{9,8},{10,11... | collective-permute-start | bytes 2187272 | tf_op jit(solution)/shard_map/ppermute | solution.py:681
  223.4 11.5 %collective-permute-start.28 = (bf16[512,384]{1,0:T(8,128)(2,1)S(1)}, bf16[512,384]{1,0:T(8,128)(2,1)S(1)}, u32[]{:S(2)}, u32[]{:S(2)}) collective-permute-start(bf16[512,384]{1,0:T(8,128)(2,1)S(1)} %slice_bitcast_fusion), channel_id=1, source_target_pairs={{0,2},{1,3},{2,0},{3,1},{4,6},{5,7},{6,4},{7,5},{8,10},{9,11},{10,... | collective-permute-start | bytes 1179656 | tf_op jit(solution)/shard_map/ppermute | solution.py:681
  231.1 34.1 %collective-permute-start.53 = (bf16[2,256,512]{2,1,0:T(8,128)(2,1)}, bf16[2,256,512]{2,1,0:T(8,128)(2,1)}, u32[]{:S(2)}, u32[]{:S(2)}) collective-permute-start(bf16[2,256,512]{2,1,0:T(8,128)(2,1)} %constant_dynamic-slice_fusion.7), channel_id=1, source_target_pairs={{0,4},{4,0},{8,12},{12,8},{16,20},{20,16},{24,28},{28,24},{1,5},{5... | collective-permute-start | bytes 1572872 | tf_op jit(solution)/shard_map/ppermute | solution.py:681
  257.3 20.6 %collective-permute-start.30 = (bf16[64,384]{1,0:T(8,128)(2,1)S(1)}, bf16[64,384]{1,0:T(8,128)(2,1)S(1)}, u32[]{:S(2)}, u32[]{:S(2)}) collective-permute-start(bf16[64,384]{1,0:T(8,128)(2,1)S(1)} %get-tuple-element.167), channel_id=1, source_target_pairs={{0,8},{4,12},{8,0},{12,4},{16,24},{20,28},{24,16},{28,20},{1,9},{5... | collective-permute-start | bytes 147464 | tf_op jit(solution)/shard_map/ppermute | solution.py:681
  265.3 13.2 %collective-permute-start.31 = (bf16[64,384]{1,0:T(8,128)(2,1)S(1)}, bf16[64,384]{1,0:T(8,128)(2,1)S(1)}, u32[]{:S(2)}, u32[]{:S(2)}) collective-permute-start(bf16[64,384]{1,0:T(8,128)(2,1)S(1)} %get-tuple-element.169), channel_id=1, source_target_pairs={{0,16},{4,20},{8,24},{12,28},{16,0},{20,4},{24,8},{28,12},{1,17},{... | collective-permute-start | bytes 147464 | tf_op jit(solution)/shard_map/ppermute | solution.py:681
  272.2 31.4 %collective-permute-start.38 = (bf16[2,256,640]{2,1,0:T(8,128)(2,1)}, bf16[2,256,640]{2,1,0:T(8,128)(2,1)}, u32[]{:S(2)}, u32[]{:S(2)}) collective-permute-start(bf16[2,256,640]{2,1,0:T(8,128)(2,1)} %constant_dynamic-slice_fusion.11), channel_id=1, source_target_pairs={{0,4},{4,0},{8,12},{12,8},{16,20},{20,16},{24,28},{28,24},{1,5},{5... | collective-permute-start | bytes 1966088 | tf_op jit(solution)/shard_map/ppermute | solution.py:681
  277.9 16.8 %collective-permute-start.75 = (bf16[128,512]{0,1:T(8,128)(2,1)S(1)}, bf16[128,512]{0,1:T(8,128)(2,1)}, u32[]{:S(2)}, u32[]{:S(2)}) collective-permute-start(bf16[128,512]{0,1:T(8,128)(2,1)S(1)} %copy-done.50), channel_id=1, source_target_pairs={{0,8},{4,12},{8,0},{12,4},{16,24},{20,28},{24,16},{28,20},{1,9},{5... | collective-permute-start | bytes 393224 | tf_op jit(solution)/shard_map/ppermute | solution.py:681
  280.9 9.6 %collective-permute-start.34 = (bf16[64,384]{1,0:T(8,128)(2,1)S(1)}, bf16[64,384]{1,0:T(8,128)(2,1)S(1)}, u32[]{:S(2)}, u32[]{:S(2)}) collective-permute-start(bf16[64,384]{1,0:T(8,128)(2,1)S(1)} %add_convert_fusion.11), channel_id=1, source_target_pairs={{0,16},{4,20},{8,24},{12,28},{16,0},{20,4},{24,8},{28,12},{1,17},{... | collective-permute-start | bytes 147464 | tf_op jit(solution)/shard_map/ppermute | solution.py:681
  290.6 15.8 %collective-permute-start.77 = (bf16[128,512]{0,1:T(8,128)(2,1)S(1)}, bf16[128,512]{0,1:T(8,128)(2,1)}, u32[]{:S(2)}, u32[]{:S(2)}) collective-permute-start(bf16[128,512]{0,1:T(8,128)(2,1)S(1)} %copy-done.50), channel_id=1, source_target_pairs={{0,24},{4,28},{8,16},{12,20},{16,8},{20,12},{24,0},{28,4},{1,25},{... | collective-permute-start | bytes 393224 | tf_op jit(solution)/shard_map/ppermute | solution.py:681
  304.9 10.1 %collective-permute-start.39 = (bf16[256,640]{1,0:T(8,128)(2,1)S(1)}, bf16[256,640]{1,0:T(8,128)(2,1)S(1)}, u32[]{:S(2)}, u32[]{:S(2)}) collective-permute-start(bf16[256,640]{1,0:T(8,128)(2,1)S(1)} %slice_bitcast_fusion.2), channel_id=1, source_target_pairs={{0,2},{1,3},{2,0},{3,1},{4,6},{5,7},{6,4},{7,5},{8,10},{9,11},{10,... | collective-permute-start | bytes 983048 | tf_op jit(solution)/shard_map/ppermute | solution.py:681
  312.4 10.0 %collective-permute-start.59 = (bf16[64,512]{1,0:T(8,128)(2,1)S(1)}, bf16[64,512]{1,0:T(8,128)(2,1)S(1)}, u32[]{:S(2)}, u32[]{:S(2)}) collective-permute-start(bf16[64,512]{1,0:T(8,128)(2,1)S(1)} %add_convert_fusion.10), channel_id=1, source_target_pairs={{0,16},{4,20},{8,24},{12,28},{16,0},{20,4},{24,8},{28,12},{1,17},{... | collective-permute-start | bytes 196616 | tf_op jit(solution)/shard_map/ppermute | solution.py:681
  313.6 10.5 %collective-permute-start.60 = (bf16[64,512]{1,0:T(8,128)(2,1)S(1)}, bf16[64,512]{1,0:T(8,128)(2,1)S(1)}, u32[]{:S(2)}, u32[]{:S(2)}) collective-permute-start(bf16[64,512]{1,0:T(8,128)(2,1)S(1)} %add_convert_fusion.10), channel_id=1, source_target_pairs={{0,24},{4,28},{8,16},{12,20},{16,8},{20,12},{24,0},{28,4},{1,25},{... | collective-permute-start | bytes 196616 | tf_op jit(solution)/shard_map/ppermute | solution.py:681
  315.1 10.9 %collective-permute-start.40 = (bf16[64,640]{1,0:T(8,128)(2,1)S(1)}, bf16[64,640]{1,0:T(8,128)(2,1)S(1)}, u32[]{:S(2)}, u32[]{:S(2)}) collective-permute-start(bf16[64,640]{1,0:T(8,128)(2,1)S(1)} %get-tuple-element.155), channel_id=1, source_target_pairs={{0,8},{4,12},{8,0},{12,4},{16,24},{20,28},{24,16},{28,20},{1,9},{5... | collective-permute-start | bytes 245768 | tf_op jit(solution)/shard_map/ppermute | solution.py:681
  316.1 10.0 %collective-permute-start.41 = (bf16[64,640]{1,0:T(8,128)(2,1)S(1)}, bf16[64,640]{1,0:T(8,128)(2,1)S(1)}, u32[]{:S(2)}, u32[]{:S(2)}) collective-permute-start(bf16[64,640]{1,0:T(8,128)(2,1)S(1)} %get-tuple-element.157), channel_id=1, source_target_pairs={{0,16},{4,20},{8,24},{12,28},{16,0},{20,4},{24,8},{28,12},{1,17},{... | collective-permute-start | bytes 245768 | tf_op jit(solution)/shard_map/ppermute | solution.py:681
  325.1 16.0 %collective-permute-start.61 = (bf16[256,512]{0,1:T(8,128)(2,1)S(1)}, bf16[256,512]{0,1:T(8,128)(2,1)S(1)}, u32[]{:S(2)}, u32[]{:S(2)}) collective-permute-start(bf16[256,512]{0,1:T(8,128)(2,1)S(1)} %dynamic_update_slice.107), channel_id=1, source_target_pairs={{0,4},{4,0},{8,12},{12,8},{16,20},{20,16},{24,28},{28,24},{1,5},{5... | collective-permute-start | bytes 786440 | tf_op jit(solution)/shard_map/ppermute | solution.py:681
  (88 other events, 686.5 us)

commit v2 on v0

v2 whole, which is shorter than its diff:
```python
from functools import partial

import jax
import jax.numpy as jnp
from jax import lax
from jax.experimental import pallas as pl
from jax.experimental.pallas import tpu as pltpu
from jax.sharding import PartitionSpec as P

HD = 128
EPSILON = 1e-05
NEGATIVE = -1e30
SCALE = HD**-0.5
BF = jnp.bfloat16
F32 = jnp.float32
MIB = 1 << 20
FB = 8
RB = 16


def mm(a, b):
    return jnp.dot(a, b, preferred_element_type=F32)


def mm_nt(a, b):
    return lax.dot_general(a, b, (((1,), (1,)), ((), ())), preferred_element_type=F32)


def mm_tn(a, b):
    return lax.dot_general(a, b, (((0,), (0,)), ((), ())), preferred_element_type=F32)


def standardize(values):
    centered = values - jnp.mean(values, axis=-1, keepdims=True)
    inverse = lax.rsqrt(jnp.mean(centered * centered, axis=-1, keepdims=True) + EPSILON)
    return centered * inverse, inverse


def norm_backward(upstream, normed, inverse, gain):
    scaled = upstream * gain
    return inverse * (
        scaled
        - jnp.mean(scaled, axis=-1, keepdims=True)
        - normed * jnp.mean(scaled * normed, axis=-1, keepdims=True)
    )


def column_sum(values):
    return jnp.sum(values, axis=0, keepdims=True)


def softmax_keys(scores):
    grown = jnp.exp(scores - jnp.max(scores, axis=0, keepdims=True))
    return grown * (1.0 / jnp.sum(grown, axis=0, keepdims=True))


def gelu_parts(z):
    t = 1.0 / (1.0 + (0.3275911 * 0.7071067811865476) * jnp.abs(z))
    e = jnp.exp(-0.5 * z * z)
    poly = t * (
        0.127414796 + t * (-0.142248368 + t * (0.7107068705 + t * (-0.7265760135 + t * 0.5307027145)))
    )
    tail = poly * e
    cdf = jnp.where(z >= 0, 1.0 - tail, tail)
    return z * cdf, cdf + z * (e * 0.3989422804014327)


def feature_probabilities(q, k, feature_count):
    scores = mm_nt(k, q) * SCALE
    key = lax.broadcasted_iota(jnp.int32, scores.shape, 0)
    return softmax_keys(jnp.where(key < feature_count, scores, NEGATIVE)).astype(BF)


def three(w):
    return jnp.concatenate([w[0], w[1], w[2]], axis=-1)


def stacked(w):
    n = w.shape[0] // 3
    return jnp.concatenate([w[c * n : (c + 1) * n] for c in range(3)], axis=-1)


def wide(pieces):
    n = pieces[0].shape[0] // 4
    return jnp.concatenate(
        [jnp.concatenate([p[j * n : (j + 1) * n] for j in range(4)], axis=-1) for p in pieces], axis=0)


def live_columns(block, first, feature_count):
    values = block.astype(F32)
    index = first + lax.broadcasted_iota(jnp.int32, values.shape, 0)
    return jnp.where(index < feature_count, values, 0.0)


ANY = pl.BlockSpec(memory_space=pl.ANY)
VMEM = pl.BlockSpec(memory_space=pltpu.VMEM)


def full(a):
    zeros = (0,) * len(a.shape)
    return pl.BlockSpec(a.shape, lambda *_: zeros)


def shaped(shape, dtype=BF):
    return jax.ShapeDtypeStruct(shape, dtype)


def call(kernel, name, grid, t, ins, outs, scratch=(), vmem=32):
    spec = pltpu.PrefetchScalarGridSpec(
        num_scalar_prefetch=2,
        grid=grid,
        in_specs=[s for _, s in ins],
        out_specs=[s for _, s in outs],
        scratch_shapes=list(scratch),
    )
    return pl.pallas_call(
        kernel,
        grid_spec=spec,
        out_shape=[a for a, _ in outs],
        compiler_params=pltpu.CompilerParams(vmem_limit_bytes=vmem * MIB),
        cost_estimate=pl.CostEstimate(flops=1, bytes_accessed=1, transcendentals=0),
        name=name,
    )(*t, *[a for a, _ in ins])


def pack_kernel(t_ref, d_ref, rq_ref, fo_ref, ro_ref, ub_ref, out_ref):
    width = rq_ref.shape[1]
    for c in range(3):
        out_ref[c * width : (c + 1) * width] = rq_ref[c]
    at = 3 * width
    for source in (fo_ref, ro_ref):
        for j in range(4):
            out_ref[at : at + HD] = source[:, j * HD : (j + 1) * HD]
            at += HD
    bias = jnp.concatenate([ub_ref[...].astype(F32)[:, j * HD : (j + 1) * HD] for j in range(4)], axis=0)
    out_ref[at : at + 16] = jnp.concatenate([bias, jnp.zeros((12, HD), F32)], axis=0).astype(BF)


def pack(t, rq, fo, ro, ub):
    out = shaped((3 * rq.shape[1] + 8 * HD + 16, HD))
    return call(pack_kernel, "pack", (), t, [(a, VMEM) for a in (rq, fo, ro, ub)], [(out, VMEM)], vmem=8)[0]


def pack_part(pack, what):
    rows = pack.shape[0] - 8 * HD - 16
    size, at = {"qkv": (rows, 0), "feat_out": (4 * HD, rows), "row_out": (4 * HD, rows + 4 * HD),
                "bias": (16, rows + 8 * HD)}[what]
    return pl.BlockSpec((size, HD), lambda *_: (at // size, 0))


def pack_parts(packs, what):
    return [(p, pack_part(p, what)) for p in packs]


def feature_forward_kernel(
    t_ref, d_ref, cells_ref, gains_ref, shifts_ref, w_ref, o0, o1, o2, o3, qkv_scr, mix_scr
):
    feature_count, rows, width = cells_ref.shape
    padded = qkv_scr.shape[1] // rows

    @pl.when(pl.program_id(0) == 0)
    def _():
        qkv_scr[...] = jnp.zeros_like(qkv_scr)

    cells = cells_ref[...].astype(F32).reshape(feature_count * rows, width)
    normed, _ = standardize(cells)
    low = (normed * gains_ref[...].astype(F32)[0:1] + shifts_ref[...].astype(F32)[0:1]).astype(BF)
    qkv = mm(low, three(w_ref))
    for c in range(3):
        qkv_scr[c, 0 : feature_count * rows, :] = qkv[:, c * HD : (c + 1) * HD]
    for r in range(rows):
        every = pl.ds(r, padded, stride=rows)
        q, k, v = (qkv_scr[c, every, :].astype(BF) for c in range(3))
        mix_scr[every, :] = mm_tn(feature_probabilities(q, k, feature_count), v)
    count = o0.shape[1]
    for k, out in enumerate((o0, o1, o2, o3)):
        at = pl.multiple_of(lax.bitwise_xor(t_ref[0], k) * count, count)
        out[0] = mix_scr[pl.ds(at, count), :].astype(BF)


def feature_forward(t, cells, gains, shifts, weight, columns):
    feature_count, row_count, width = cells.shape
    padded = 4 * columns
    steps = row_count // RB
    out = (shaped((steps, columns * RB, HD)), pl.BlockSpec((1, columns * RB, HD), lambda i, t, d: (i, 0, 0)))
    return call(
        feature_forward_kernel, "feature_forward", (steps,), t,
        [(cells, pl.BlockSpec((feature_count, RB, width), lambda i, t, d: (0, i, 0)))]
        + [(a, full(a)) for a in (gains, shifts, weight)],
        [out] * 4,
        [pltpu.VMEM((3, padded * RB, HD), F32), pltpu.VMEM((padded * RB, HD), F32)], vmem=28,
    )


def column_block(array, columns):
    _, rows, width = array.shape
    return pl.BlockSpec((columns, rows, width), lambda i, t, d: (t[0], 0, 0))


def in_order(m, columns):
    steps = m.shape[0]
    halves = [m[i].reshape(columns, RB, HD) for i in range(steps)]
    return jnp.concatenate(halves, axis=1).reshape(columns * RB * steps, HD)


def row_forward_kernel(
    t_ref, d_ref, split_ref, m0, m1, m2, m3, cells_ref, f0, f1, f2, f3, r0, r1, r2, r3, w0, w1, w2, w3,
    wo_bias, wr_bias, gains_ref, shifts_ref,
    first_ref, n2_ref, qkv_ref, p_ref, o2_ref, second_ref, n3_ref, *, feature_count,
):
    columns, rows, width = cells_ref.shape
    cells = columns * rows
    side = p_ref.shape[2]
    key = lax.broadcasted_iota(jnp.int32, (side, side), 0)
    query = lax.broadcasted_iota(jnp.int32, (side, side), 1)
    same = lax.div(query, rows) == lax.div(key, rows)
    bias = jnp.where(jnp.logical_and(same, lax.rem(key, rows) < split_ref[0]), 0.0, NEGATIVE)

    gains = gains_ref[...].astype(F32)
    shifts = shifts_ref[...].astype(F32)
    stream = live_columns(cells_ref[...], t_ref[0] * columns, feature_count).reshape(cells, width)
    mixed = jnp.concatenate([in_order(m, columns) for m in (m0, m1, m2, m3)], axis=-1)
    first = stream + mm(mixed, wide((f0, f1, f2, f3))) + wo_bias[...].astype(F32)
    first_ref[...] = first
    normed, _ = standardize(first)
    low = (normed * gains[1:2] + shifts[1:2]).astype(BF)
    n2_ref[...] = low
    for h, w in enumerate((w0, w1, w2, w3)):
        base = 3 * HD * h
        qkv_ref[:, base : base + 3 * HD] = mm(low, stacked(w)).astype(BF)
        for b in range(0, cells, side):
            span = slice(b, b + side)
            q, k, v = (qkv_ref[span, base + c * HD : base + (c + 1) * HD] for c in range(3))
            p = softmax_keys(mm_nt(k, q) * SCALE + bias).astype(BF)
            p_ref[h, b // side] = p
            o2_ref[span, h * HD : (h + 1) * HD] = mm_tn(p, v).astype(BF)
    second = first + mm(o2_ref[...], wide((r0, r1, r2, r3))) + wr_bias[...].astype(F32)
    second_ref[...] = second
    normed, _ = standardize(second)
    n3_ref[...] = (normed * gains[2:3] + shifts[2:3]).astype(BF)


def whole(shape, dtype=BF):
    return shaped(shape, dtype), full(shaped(shape, dtype))


def row_forward(t, split, mixed, cells, packs, wo_bias, wr_bias, gains, shifts, columns):
    feature_count, rows, width = cells.shape
    n = columns * rows
    side = 4 * rows
    ins = [(split, pl.BlockSpec(memory_space=pltpu.SMEM))] + [(m, full(m)) for m in mixed]
    ins += [(cells, column_block(cells, columns))]
    ins += pack_parts(packs, "feat_out") + pack_parts(packs, "row_out") + pack_parts(packs, "qkv")
    ins += [(a, full(a)) for a in (wo_bias, wr_bias, gains, shifts)]
    return call(
        partial(row_forward_kernel, feature_count=feature_count), "row_forward", (1,), t, ins,
        [whole((n, width), F32), whole((n, width)), whole((n, 12 * HD)), whole((4, n // side, side, side)),
         whole((n, 4 * HD)), whole((n, width), F32), whole((n, width))],
    )


def hidden_pair(t_ref, n3_ref, grad_ref, ups, packs, downs, grads, bias_grads, feature_count):
    columns, rows, width = grad_ref.shape
    g3 = live_columns(grad_ref[...], t_ref[0] * columns, feature_count).reshape(columns * rows, width)
    n3, gl = n3_ref[...], g3.astype(BF)
    n3_t, gl_t = n3.T, gl.T
    ms, dzs = [], []
    for up, pack, down, grad_ref, bias_grad in zip(ups, packs, downs, grads, bias_grads):
        bias = jnp.concatenate([pack[...].astype(F32)[j : j + 1] for j in range(4)], axis=-1)
        act, slope = gelu_parts(mm(n3, up[...]) + bias)
        m = act.astype(BF)
        dz = (mm_nt(gl, down[...]) * slope).astype(BF)
        grad_ref[:width] = mm(n3_t, dz).astype(BF)
        grad_ref[width:] = mm(gl_t, m).astype(BF)
        bias_grad[...] = column_sum(dz.astype(F32))
        ms.append(m)
        dzs.append(dz)
    out = mm(jnp.concatenate(ms, axis=-1), jnp.concatenate([d[...] for d in downs], axis=0))
    dn3 = mm_nt(jnp.concatenate(dzs, axis=-1), jnp.concatenate([u[...] for u in ups], axis=-1))
    return g3, out, dn3


def hidden_first_kernel(
    t_ref, d_ref, n3_ref, grad_ref, up0, up1, b0, b1, down0, down1, out_ref, dn3_ref, wg0, wg1, bg0, bg1,
    *, feature_count,
):
    _, out, dn3 = hidden_pair(
        t_ref, n3_ref, grad_ref, (up0, up1), (b0, b1), (down0, down1), (wg0, wg1), (bg0, bg1), feature_count)
    out_ref[...] = out
    dn3_ref[...] = dn3


def hidden_second_kernel(
    t_ref, d_ref, n3_ref, grad_ref, up0, up1, b0, b1, down0, down1, out_in, dn3_in, second_ref, down_bias, gains_ref,
    out_ref, g2_ref, gl2_ref, stats_ref, wg0, wg1, bg0, bg1, *, feature_count,
):
    g3, out, dn3 = hidden_pair(
        t_ref, n3_ref, grad_ref, (up0, up1), (b0, b1), (down0, down1), (wg0, wg1), (bg0, bg1), feature_count)
    second = second_ref[...]
    out_ref[...] = (second + out_in[...] + out + down_bias[...].astype(F32)).astype(BF)
    dn3 = dn3_in[...] + dn3
    normed, inverse = standardize(second)
    g2 = g3 + norm_backward(dn3, normed, inverse, gains_ref[...].astype(F32)[2:3])
    g2_ref[...] = g2
    gl2_ref[...] = g2.astype(BF)
    stats_ref[...] = rows_of([g3, g2, dn3 * normed, dn3])


def rows_of(arrays):
    return jnp.concatenate(
        [column_sum(a) for a in arrays] + [jnp.zeros((8 - len(arrays), arrays[0].shape[1]), F32)], axis=0)


def hidden_call(t, n3, grads, ups, packs, downs, columns, extra=None):
    n, width = n3.shape
    hidden = ups[0].shape[1]
    tail = [whole((2 * width, hidden))] * 2 + [whole((1, hidden), F32)] * 2
    ins = [(n3, full(n3)), (grads, column_block(grads, columns))]
    ins += [(a, full(a)) for a in ups] + pack_parts(packs, "bias") + [(a, full(a)) for a in downs]
    if extra is None:
        kernel, name = hidden_first_kernel, "hidden_first"
        results = [whole((n, width), F32)] * 2 + tail
    else:
        kernel, name = hidden_second_kernel, "hidden_second"
        ins += [(a, full(a)) for a in extra]
        results = [whole((n, width)), whole((n, width), F32), whole((n, width)), whole((8, width), F32)] + tail
    return call(partial(kernel, feature_count=grads.shape[0]), name, (1,), t, ins, results)


def attention_backward(q, k, v, p, do):
    dp = mm_nt(v, do)
    pf = p.astype(F32)
    ds = (pf * (dp - jnp.sum(dp * pf, axis=0, keepdims=True))).astype(BF)
    return mm_tn(ds, k) * SCALE, mm(ds, q) * SCALE, mm(p, do)


def row_backward_kernel(
    t_ref, d_ref, g2_ref, first_ref, qkv_ref, p_ref, gains_ref, w0, w1, w2, w3, r0, r1, r2, r3,
    dqkv_ref, gl1_ref, s0, s1, s2, s3, stats_ref, g1_scr,
):
    g2 = g2_ref[...]
    cells, width = g2.shape
    side = p_ref.shape[2]
    do = mm_nt(g2.astype(BF), wide((r0, r1, r2, r3))).astype(BF)
    for h in range(4):
        at = 3 * HD * h
        for b in range(0, cells, side):
            span = slice(b, b + side)
            q, k, v = (qkv_ref[span, at + c * HD : at + (c + 1) * HD] for c in range(3))
            parts = attention_backward(q, k, v, p_ref[h, b // side], do[span, HD * h : HD * (h + 1)])
            for c, part in enumerate(parts):
                dqkv_ref[span, at + c * HD : at + (c + 1) * HD] = part.astype(BF)
    dn2 = mm_nt(dqkv_ref[...], jnp.concatenate([stacked(w) for w in (w0, w1, w2, w3)], axis=-1))
    normed, inverse = standardize(first_ref[...])
    g1 = g2 + norm_backward(dn2, normed, inverse, gains_ref[...].astype(F32)[1:2])
    columns, rows, _ = g1_scr.shape
    g1_scr[...] = g1.reshape(columns, rows, width)
    gl1_ref[...] = g1.astype(BF)
    share = rows // 4
    for k, out in enumerate((s0, s1, s2, s3)):
        at = pl.multiple_of(lax.bitwise_xor(t_ref[0], k) * share, share)
        out[...] = g1_scr[:, pl.ds(at, share), :].reshape(columns * share, width).astype(BF)
    stats_ref[...] = rows_of([g1, dn2 * normed, dn2])


def row_backward(t, g2, first, qkv, p, gains, packs, rows):
    n, width = g2.shape
    ins = [(a, full(a)) for a in (g2, first, qkv, p, gains)]
    ins += pack_parts(packs, "qkv") + pack_parts(packs, "row_out")
    return call(
        row_backward_kernel, "row_backward", (1,), t, ins,
        [whole(qkv.shape), whole((n, width))] + [whole((n // 4, width))] * 4 + [whole((8, width), F32)],
        [pltpu.VMEM((n // rows, rows, width), F32)],
    )


def row_weights_kernel(t_ref, d_ref, n2_ref, dqkv_ref, gl2_ref, o2_ref, gl1_ref, m0, m1, m2, m3, keep_ref, send_ref):
    width = n2_ref.shape[1]
    columns = m0.shape[1] // RB
    grad = mm(n2_ref[...].T, dqkv_ref[...])
    out_grad = mm(gl2_ref[...].T, o2_ref[...])
    feat_grad = mm(gl1_ref[...].T, jnp.concatenate([in_order(m, columns) for m in (m0, m1, m2, m3)], axis=-1))
    for h in range(4):
        out = (keep_ref, send_ref)[h % 2]
        for c in range(3):
            out[h // 2, c * width : (c + 1) * width, :] = grad[:, (3 * h + c) * HD : (3 * h + c + 1) * HD].astype(BF)
        out[h // 2, 3 * width : 4 * width, :] = out_grad[:, HD * h : HD * (h + 1)].astype(BF)
        out[h // 2, 4 * width : 5 * width, :] = feat_grad[:, HD * h : HD * (h + 1)].astype(BF)


def row_weights(t, n2, dqkv, gl2, o2, gl1, mixed):
    width = n2.shape[1]
    return call(
        row_weights_kernel, "row_weights", (1,), t,
        [(a, full(a)) for a in (n2, dqkv, gl2, o2, gl1, *mixed)], [whole((2, 5 * width, HD))] * 2, vmem=24,
    )


def own_rows(t_ref, cells_ref, cell_scr, share):
    feature_count, block_rows, width = cells_ref.shape
    cell_scr[0:feature_count] = cells_ref[...].astype(F32)
    cell_scr[feature_count:] = jnp.zeros_like(cell_scr[feature_count:])
    at = pl.multiple_of(lax.rem(t_ref[0], block_rows // share) * share, share)
    return cell_scr[:, pl.ds(at, share), :].reshape(cell_scr.shape[0] * share, width)


def row_block(cells, share):
    feature_count, _, width = cells.shape
    per = RB // share
    return pl.BlockSpec((feature_count, RB, width), lambda i, t, d: (0, lax.div(t[0], per), 0))


def feature_again_kernel(
    t_ref, d_ref, cells_ref, gains_ref, shifts_ref, w0, w1, w2, w3, n1_ref, qkv_ref, p_ref, cell_scr, qkv_scr
):
    feature_count = cells_ref.shape[0]
    share, padded, _ = qkv_ref.shape
    normed, _ = standardize(own_rows(t_ref, cells_ref, cell_scr, share))
    low = (normed * gains_ref[...].astype(F32)[0:1] + shifts_ref[...].astype(F32)[0:1]).astype(BF)
    n1_ref[...] = low
    for h, w in enumerate((w0, w1, w2, w3)):
        packed = mm(low, three(w))
        for c in range(3):
            qkv_scr[c] = packed[:, c * HD : (c + 1) * HD]
        for r in range(share):
            q, k, v = (qkv_scr[c, pl.ds(r, padded, stride=share), :].astype(BF) for c in range(3))
            for c, part in enumerate((q, k, v)):
                qkv_ref[r, :, (3 * h + c) * HD : (3 * h + c + 1) * HD] = part
            p_ref[r, h] = feature_probabilities(q, k, feature_count)


def feature_again(t, cells, gains, shifts, weights, columns, share):
    width = cells.shape[2]
    padded = 4 * columns
    return call(
        feature_again_kernel, "feature_again", (1,), t,
        [(cells, row_block(cells, share))] + [(a, full(a)) for a in (gains, shifts, *weights)],
        [whole((padded * share, width)), whole((share, padded, 12 * HD)), whole((share, 4, padded, padded))],
        [pltpu.VMEM((padded, RB, width), F32), pltpu.VMEM((3, padded * share, HD), F32)], vmem=28,
    )


def feature_backward_kernel(
    t_ref, d_ref, r0, r1, r2, r3, f0, f1, f2, f3, qkv_ref, p_ref, n1_ref,
    g1_ref, dqkv_ref, keep_ref, send_ref, low_scr, do_scr, dqkv_scr,
):
    width = g1_ref.shape[1]
    share, padded, _ = qkv_ref.shape
    for k, piece in enumerate((r0, r1, r2, r3)):
        count = piece.shape[0]
        at = pl.multiple_of(lax.bitwise_xor(t_ref[0], k) * count, count)
        low_scr[pl.ds(at, count), :] = piece[...]
        g1_ref[pl.ds(at, count), :] = piece[...].astype(F32)
    do = mm_nt(low_scr[...], wide((f0, f1, f2, f3)))
    for h in range(4):
        do_scr[h] = do[:, h * HD : (h + 1) * HD]
    n1_t = n1_ref[...].T
    for h in range(4):
        for r in range(share):
            every = pl.ds(r, padded, stride=share)
            q, k, v = (qkv_ref[r, :, (3 * h + c) * HD : (3 * h + c + 1) * HD] for c in range(3))
            parts = attention_backward(q, k, v, p_ref[r, h], do_scr[h, every, :].astype(BF))
            for c, part in enumerate(parts):
                dqkv_scr[3 * h + c, every, :] = part
        out = (keep_ref, send_ref)[h % 2]
        for c in range(3):
            dqkv_ref[:, (3 * h + c) * HD : (3 * h + c + 1) * HD] = dqkv_scr[3 * h + c].astype(BF)
        grad = mm(n1_t, dqkv_ref[:, 3 * HD * h : 3 * HD * (h + 1)]).astype(BF)
        for c in range(3):
            out[h // 2, c * width : (c + 1) * width, :] = grad[:, c * HD : (c + 1) * HD]


def feature_backward(t, pieces, packs, qkv, p, n1):
    share, _, padded, _ = p.shape
    width = pieces[0].shape[1]
    cells = share * padded
    return call(
        feature_backward_kernel, "feature_backward", (1,), t,
        [(a, full(a)) for a in pieces] + pack_parts(packs, "feat_out") + [(a, full(a)) for a in (qkv, p, n1)],
        [whole((cells, width), F32), whole((cells, 12 * HD))] + [whole((2, 3 * width, HD))] * 2,
        [pltpu.VMEM((cells, width), BF), pltpu.VMEM((4, cells, HD), F32), pltpu.VMEM((12, cells, HD), F32)],
    )


def feature_input_kernel(
    t_ref, d_ref, cells_ref, g1_ref, dqkv_ref, gains_ref, w0, w1, w2, w3, stats_a, stats_b, b0, b1, b2, b3,
    out_ref, stats_ref, cell_scr,
):
    cells, width = g1_ref.shape
    share = cells // cell_scr.shape[0]
    normed, inverse = standardize(own_rows(t_ref, cells_ref, cell_scr, share))
    dn1 = mm_nt(dqkv_ref[...], jnp.concatenate([three(w) for w in (w0, w1, w2, w3)], axis=-1))
    g0 = g1_ref[...] + norm_backward(dn1, normed, inverse, gains_ref[...].astype(F32)[0:1])
    out_ref[...] = g0[: out_ref.shape[0]].astype(BF)
    stats_ref[0:8] = stats_a[...]
    stats_ref[8:16] = stats_b[...]
    stats_ref[4:5] = column_sum(dn1 * normed)
    stats_ref[5:6] = column_sum(dn1)
    stats_ref[16:24] = jnp.zeros((8, width), F32)
    for k, row in enumerate((b0, b1, b2, b3)):
        stats_ref[pl.ds(16 + lax.bitwise_xor(t_ref[0], k), 1), :] = row[...]


def feature_input(t, cells, g1, dqkv, gains, weights, sums, share):
    count, width = g1.shape
    kept = (cells.shape[0] + 1) // 2 * 2 * share
    return call(
        feature_input_kernel, "feature_input", (1,), t,
        [(cells, row_block(cells, share))] + [(a, full(a)) for a in (g1, dqkv, gains, *weights, *sums)],
        [whole((kept, width)), whole((24, width), F32)],
        [pltpu.VMEM((count // share, RB, width), F32)], vmem=28,
    )


def columns_home_kernel(t_ref, d_ref, p0, p1, p2, p3, out_ref):
    for k, piece in enumerate((p0, p1, p2, p3)):

        @pl.when(pl.program_id(0) == lax.bitwise_xor(t_ref[0], k))
        def _():
            out_ref[...] = piece[...]


def columns_home(t, pieces, feature_count):
    columns, rows, width = pieces[0].shape
    return call(
        columns_home_kernel, "columns_home", (4,), t, [(p, full(p)) for p in pieces],
        [(shaped((feature_count, rows, width)), pl.BlockSpec((columns, rows, width), lambda i, t, d: (i, 0, 0)))], vmem=16,
    )[0]


def rows_home_kernel(t_ref, d_ref, p0, p1, p2, p3, out_ref, scr):
    columns, rows, width = scr.shape
    share = rows // 4
    for k, piece in enumerate((p0, p1, p2, p3)):
        at = pl.multiple_of(lax.bitwise_xor(t_ref[0], k) * share, share)
        scr[:, pl.ds(at, share), :] = piece[...].astype(F32).reshape(columns, share, width)
    out_ref[...] = scr[...].astype(BF)


def rows_home(t, pieces, feature_count, rows):
    count, width = pieces[0].shape
    share = rows // 4
    columns = count // share // 5
    return call(
        rows_home_kernel, "rows_home", (5,), t,
        [(p, pl.BlockSpec((columns * share, width), lambda i, t, d: (i, 0))) for p in pieces],
        [(shaped((feature_count, rows, width)), pl.BlockSpec((columns, rows, width), lambda i, t, d: (i, 0, 0)))],
        [pltpu.VMEM((columns, rows, width), F32)], vmem=12,
    )[0]


def swap(values, axis, mask):
    count = lax.axis_size(axis)
    return lax.ppermute(values, axis, [(i, i ^ mask) for i in range(count)])


def gather_groups(own):
    far = swap(own, "tensor", 2)
    return own, swap(own, "tensor", 1), far, swap(far, "tensor", 1)


def held(values, *others):
    if isinstance(values, tuple):
        return lax.optimization_barrier((values[0], *others))[0], *values[1:]
    return lax.optimization_barrier((values, *others))[0]


def dp_masks():
    masks, mask = [], 1
    while mask < lax.axis_size("dp"):
        masks.append(mask)
        mask *= 2
    return masks


def digit(d_ref, mask):
    return lax.rem(lax.div(d_ref[0], mask), 2)


def merge_kernel(t_ref, d_ref, *refs, jobs):
    at = 0
    ins = []
    for job in jobs:
        ins.append((refs[at : at + len(job["own"])], refs[at + len(job["own"]) : at + 2 * len(job["own"])]))
        at += 2 * len(job["own"])
    for job, (own, other) in zip(jobs, ins):
        outs = refs[at : at + job["outs"]]
        at += job["outs"]
        kind, mask = job["next"]
        if job["join"] is None:
            start, rows = job["rows"]

            def total(j, first, count):
                part = (Ellipsis, pl.ds(start + first, count), slice(None))
                return own[j][part].astype(F32) + other[j][part].astype(F32)

            if kind == "half":
                half = rows // 2
                for out, side in zip(outs, (digit(d_ref, mask), 1 - digit(d_ref, mask))):
                    first = pl.multiple_of(side * half, half)
                    for j in range(len(own)):
                        sums = total(j, first, half).astype(out.dtype)
                        if len(own) > 1:
                            out[j] = sums
                        else:
                            out[...] = sums
            elif kind == "group":
                sums = total(0, 0, rows)
                outs[0][...] = sums[0].astype(outs[0].dtype)
                outs[1][...] = sums[1].astype(outs[1].dtype)
            else:
                outs[0][...] = total(0, 0, rows).astype(outs[0].dtype)
        else:
            rows = own[0].shape[-2]
            side = digit(d_ref, job["join"])
            for source, place in ((own[0], side), (other[0], 1 - side)):
                first = pl.multiple_of(place * rows, rows)
                outs[0][..., pl.ds(first, rows), :] = source[...].astype(outs[0].dtype)


class Chain:
    def __init__(self, own, other, order, rows=None, low=BF):
        self.own, self.other, self.low = tuple(own), tuple(other), low
        dp = [m for m in order if m != "x"]
        halved = dp[:-1] if low == BF else []
        self.plan = []
        for m in order:
            if m == "x":
                self.plan.append(("group" if low == BF else "whole", "x", None))
            else:
                self.plan.append(("half" if m in halved else "whole", m, None))
        for m in reversed(halved):
            self.plan.append(("whole", m, m))
        self.join = None
        self.rows = rows
        self.result = None

    def job(self):
        n, w = self.own[0].shape[-2:]
        start, rows = self.rows or (0, n)
        lead = self.own[0].shape[:-2]
        if len(self.own) > 1:
            lead = (len(self.own),)
        kind, mask, _ = self.plan[0] if self.plan else ("final", None, None)
        if self.join is not None:
            shape = lead + (2 * n, w)
        elif kind == "half":
            shape = lead + (rows // 2, w)
        elif kind == "group":
            shape = (rows, w)
        else:
            shape = lead + (rows, w)
        out = shaped(shape, F32 if kind == "final" else self.low)
        count = 2 if kind in ("half", "group") else 1
        spec = {"own": self.own, "other": self.other, "next": (kind, mask), "join": self.join,
                "rows": (start, rows), "outs": count}
        return spec, [out] * count

    def take(self, outs):
        if not self.plan:
            self.result = outs[0]
            return
        kind, mask, join = self.plan.pop(0)
        sent = outs[-1]
        self.own = (outs[0],)
        self.other = (swap(sent, "tensor", 2) if mask == "x" else swap(sent, "dp", mask),)
        self.sent = sent
        self.join, self.rows = join, None


def merge(t, chains):
    jobs, outs, ins = [], [], []
    for chain in chains:
        spec, shapes = chain.job()
        ins += [*spec["own"], *spec["other"]]
        jobs.append({k: (v if k != "own" else [0] * len(v)) for k, v in spec.items() if k != "other"})
        outs.append(shapes)
    flat = [o for shapes in outs for o in shapes]
    results = call(partial(merge_kernel, jobs=jobs), "merge", (), t, [(a, VMEM) for a in ins], [(o, VMEM) for o in flat], vmem=20)
    at = 0
    for chain, shapes in zip(chains, outs):
        chain.take(results[at : at + len(shapes)])
        at += len(shapes)
    return results


def shards(
    table_cells, splits, feat_qkv, feat_out, feat_out_bias, row_qkv, row_out, row_out_bias,
    up_weight, up_bias, down_weight, down_bias, norm_gains, norm_biases, cotangent,
):
    shape = table_cells.shape
    _, row_count, feature_count, width = shape
    share = row_count // 4
    columns = -(-feature_count // (4 * FB)) * FB
    t = tuple(lax.axis_index(a).astype(jnp.int32).reshape(1) for a in ("tensor", "dp"))
    masks = dp_masks()
    cells = jnp.transpose(table_cells[0], (1, 0, 2))
    grads = jnp.transpose(cotangent[0], (1, 0, 2))
    fob, rob, dnb, upb = (b.reshape(1, width) for b in (feat_out_bias, row_out_bias, down_bias, up_bias))
    fq = jnp.transpose(feat_qkv, (1, 0, 2))
    rq = jnp.transpose(row_qkv, (1, 0, 2))

    packs = gather_groups(pack(t, rq, feat_out, row_out, upb))
    mixed = feature_forward(t, cells, norm_gains, norm_biases, fq, columns)
    mixed = [mixed[0]] + [swap(mixed[k], "tensor", k) for k in (1, 2, 3)]
    ups = gather_groups(held(up_weight, mixed[2], mixed[3]))
    downs = gather_groups(held(down_weight, mixed[2], mixed[3]))
    fqs = gather_groups(held(fq, downs[2]))

    first, n2, row_packed, row_p, o2, second, n3 = row_forward(
        t, splits, mixed, cells, packs, fob, rob, norm_gains, norm_biases, columns)
    out_a, dn3_a, hg0, hg1, bg0, bg1 = hidden_call(t, n3, grads, ups[:2], packs[:2], downs[:2], columns)
    out_f, g2, gl2, stats_a, hg2, hg3, bg2, bg3 = hidden_call(
        t, n3, grads, ups[2:], packs[2:], downs[2:], columns, [out_a, dn3_a, second, dnb, norm_gains])

    r1, r3 = swap(hg1, "tensor", 1), swap(hg3, "tensor", 1)
    up_chain = Chain((hg0, hg2), (r1, r3), [masks[0], "x"] + masks[1:], rows=(0, width))
    down_chain = Chain((hg0, hg2), (r1, r3), masks[1:] + ["x", masks[0]], rows=(width, width))
    sent = merge(t, [up_chain, down_chain])

    dqkv_r, gl1, s0, s1, s2, s3, stats_b = row_backward(
        held(t, *sent), g2, first, row_packed, row_p, norm_gains, packs, row_count)
    pieces = [s0] + [swap(s, "tensor", k) for k, s in ((1, s1), (2, s2), (3, s3))]

    row_keep, row_send = row_weights(t, n2, dqkv_r, gl2, o2, gl1, mixed)
    row_chain = Chain((row_keep,), (swap(row_send, "tensor", 1),), [masks[0], "x"] + masks[1:])
    sent = merge(held(t, row_send), [up_chain, down_chain])
    sent = merge(held(t, *sent), [row_chain])
    n1, feat_packed, feat_p = feature_again(
        held(t, *sent), cells, norm_gains, norm_biases, fqs, columns, share)
    out_pieces = gather_groups(held(out_f.reshape(columns, row_count, width), pieces[2], pieces[3]))

    g1, dqkv_f, feat_keep, feat_send = feature_backward(t, pieces, packs, feat_packed, feat_p, n1)
    sent = merge(held(t, dqkv_f), [up_chain, down_chain])
    feat_chain = Chain((feat_keep,), (swap(feat_send, "tensor", 1),), ["x"] + masks)
    g0, sums = feature_input(
        held(t, *sent), cells, g1, dqkv_f, norm_gains, fqs, (stats_a, stats_b, bg0, bg1, bg2, bg3), share)
    small_chain = Chain((sums,), (swap(sums, "tensor", 1),), ["x"] + masks, low=F32)

    chains = [feat_chain, small_chain, row_chain, up_chain, down_chain]
    sent = merge(held(t, sums), chains)
    g0s = gather_groups(held(g0, feat_chain.other[0]))
    output = columns_home(held(t, *sent), out_pieces, feature_count)
    sent = merge(held(t, output), [feat_chain, small_chain, up_chain, down_chain])
    while True:
        chains = [c for c in chains if c.result is None]
        if not chains:
            break
        sent = merge(held(t, *sent), chains)
    input_grad = rows_home(t, g0s, feature_count, row_count)

    up_grad, down_grad = up_chain.result, down_chain.result.T
    row_grad, feat_grad, small = row_chain.result, feat_chain.result, small_chain.result

    def qkv_shape(grad):
        return jnp.transpose(grad.reshape(3, width, HD), (1, 0, 2))

    home = lambda a: jnp.transpose(a, (1, 0, 2)).reshape(shape)
    return (
        home(output),
        home(input_grad),
        qkv_shape(feat_grad),
        row_grad[4 * width :].T,
        small[8],
        qkv_shape(row_grad[: 3 * width]),
        row_grad[3 * width : 4 * width].T,
        small[1],
        up_grad,
        lax.dynamic_index_in_dim(small, 16 + t[0][0], 0, keepdims=False),
        down_grad,
        small[0],
        jnp.stack([small[4], small[9], small[2]]),
        jnp.stack([small[5], small[10], small[3]]),
    )


def solution(mesh):
    return jax.shard_map(
        shards,
        mesh=mesh,
        in_specs=(
            P("dp", None, None, None), P("dp"), P(None, None, "tensor"), P("tensor", None), P(),
            P(None, None, "tensor"), P("tensor", None), P(), P(None, "tensor"), P("tensor"),
            P("tensor", None), P(), P(), P(), P("dp", None, None, None),
        ),
        out_specs=(
            P("dp", None, None, None), P("dp", None, None, None), P(None, None, "tensor"),
            P("tensor", None), P(), P(None, None, "tensor"), P("tensor", None), P(),
            P(None, "tensor"), P("tensor"), P("tensor", None), P(), P(), P(),
        ),
        check_vma=False,
    )
```

time: 748 us -> 273 us (0.36)
  waiting for transfers between devices: 420 us -> 123 us
  local copies, waits for them, and re-layouts: 97.9 us -> 13.8 us
  matrix products: 83.2 us -> 0 us
  Pallas kernels: 0 us -> 76.1 us
  blocking collectives: 62.6 us -> 0 us
  other arithmetic: 58.4 us -> 0.61 us
  starting transfers between devices: 1.67 us -> 53.6 us
  between operations: 16.3 us -> 2.11 us
    psum x4 -> x0, waiting for transfers between devices: 269 us -> none  [the longest x3 138 us: branch_total(): lax.psum(partial_out.astype(jnp.bfloat16), 'tensor').astype(jnp.float32)]
    ppermute x0 -> x57, waiting for transfers between devices: none -> 123 us  [swap(): return lax.ppermute(values, axis, [(i, i ^ mask) for i in range(count)])]
    reduce_scatter x3 -> x0, waiting for transfers between devices: 96.2 us -> none  [reduce_back(): lax.psum_scatter(normed_grad.astype(jnp.bfloat16), 'tensor', scatter_dime...]
    dot_general x30 -> x0, matrix products: 83.2 us -> none  [the longest x1 16.7 us: shards(): jnp.einsum('nd,fd->nf', grad_low, down_weight, preferred_element_type=jnp...]
    pallas_call x0 -> x23, Pallas kernels: none -> 76.1 us  [call(): pl.pallas_call(kernel, grid_spec=spec, out_shape=[a for a, _ in outs], co...]
    psum x2 -> x0, blocking collectives: 62.6 us -> none  [the longest x1 40.7 us: shards(): lax.psum((feat_bias_grad, row_bias_grad, down_bias_grad, jnp.stack([gain_...]
    all_gather x3 -> x0, waiting for transfers between devices: 54.3 us -> none  [reduce_back(): lax.all_gather(share_stream.astype(jnp.bfloat16), 'tensor', axis=0, tiled...]
    ppermute x0 -> x57, starting transfers between devices: none -> 53.6 us  [swap(): return lax.ppermute(values, axis, [(i, i ^ mask) for i in range(count)])]
  transfers between devices with their start and end apart: 10 -> 57, of which waited for: 9 -> 23; matrix products, arithmetic and copies ran while one was open for 10% -> 2% of each run, Pallas kernels for 0% -> 19%
where the time goes in v2:
time: 273 us; the launch traced here: 269 us
  waiting for transfers between devices  123 us (45%)
  Pallas kernels  76.1 us (28%)
  starting transfers between devices  53.6 us (20%)
  local copies, waits for them, and re-layouts  13.8 us (5%)
    ppermute x57, waiting for transfers between devices, swap(): return lax.ppermute(values, axis, [(i, i ^ mask) for i in range(count)])  123 us
    pallas_call x23, Pallas kernels, call(): pl.pallas_call(kernel, grid_spec=spec, out_shape=[a for a, _ in outs], co...  76.1 us
    ppermute x57, starting transfers between devices, swap(): return lax.ppermute(values, axis, [(i, i ^ mask) for i in range(count)])  53.6 us
    unnamed x39, local copies, waits for them, and re-layouts  10.5 us
  transfers between devices with their start and end apart: 57, of which 23 were waited for; matrix products, arithmetic and copies ran while one was open for 2% of the time, Pallas kernels for 19%

profile of v2, /device:TPU:0, one launch (start us, length us, event | category | flops | bytes accessed | tf_op | source)
XLA Modules:
  0.0 269.4 jit_solution(14568575234690223268)
XLA Ops:
  4.3 3.0 %collective-permute-start.4 = (bf16[2576,128]{1,0:T(8,128)(2,1)S(1)}, bf16[2576,128]{1,0:T(8,128)(2,1)S(1)}, u32[]{:S(2)}, u32[]{:S(2)}) collective-permute-start(bf16[2576,128]{1,0:T(8,128)(2,1)S(1)} %pack.1.f0.r0.w0.b0), channel_id=1, source_target_pairs={{0,2},{1,3},{2,0},{3,1},{4,6},{5,7},{6,4},{7,5},{8,10},{9,11},{10,... | collective-permute-start | bytes 1978376 | tf_op jit(solution)/shard_map/ppermute | solution.py:554
  7.3 1.8 copy-done
  10.5 11.9 %feature_forward.1 = (bf16[2,384,128]{2,1,0:T(8,128)(2,1)S(1)}, bf16[2,384,128]{2,1,0:T(8,128)(2,1)S(1)}, bf16[2,384,128]{2,1,0:T(8,128)(2,1)S(1)}, bf16[2,384,128]{2,1,0:T(8,128)(2,1)S(1)}) custom-call(s32[1]{0:T(128)} %bitcast.t_ref, s32[1]{0:T(128)} %bitcast.1.d_ref, bf16[89,32,512]{2,1,0:T(8,128)(2,1)S(1)} %bitcast.32, bf16[3,512]{1,0:T(4,128)(2,1)S(1)} %copy-done.9, ...), custom_call_target="tpu_custom_call" | custom-call | flops 1 | bytes 1 | tf_op jit(solution)/shard_map/feature_forward/pallas_call | solution.py:116
  24.6 5.7 %collective-permute-done.1.m2 = bf16[2,384,128]{2,1,0:T(8,128)(2,1)S(1)} collective-permute-done((bf16[2,384,128]{2,1,0:T(8,128)(2,1)S(1)}, bf16[2,384,128]{2,1,0:T(8,128)(2,1)S(1)}, u32[]{:S(2)}, u32[]{:S(2)}) %collective-permute-start.1) | collective-permute-done | bytes 196640 | tf_op jit(solution)/shard_map/ppermute | solution.py:554
  30.3 1.3 collective-permute-done.2.m3
  35.9 10.3 %collective-permute-done.10.down0 = bf16[512,512]{1,0:T(8,128)(2,1)S(1)} collective-permute-done((bf16[512,512]{1,0:T(8,128)(2,1)}, bf16[512,512]{1,0:T(8,128)(2,1)S(1)}, u32[]{:S(2)}, u32[]{:S(2)}) %collective-permute-start.10) | collective-permute-done | bytes 524320 | tf_op jit(solution)/shard_map/ppermute | solution.py:554
  47.0 10.5 %collective-permute-done.8.up0 = bf16[512,512]{1,0:T(8,128)(2,1)S(1)} collective-permute-done((bf16[512,512]{1,0:T(8,128)(2,1)S(1)}, bf16[512,512]{1,0:T(8,128)(2,1)S(1)}, u32[]{:S(2)}, u32[]{:S(2)}) %collective-permute-start.8) | collective-permute-done | bytes 524320 | tf_op jit(solution)/shard_map/ppermute | solution.py:554
  58.4 9.1 %row_forward.1 = (f32[768,512]{1,0:T(8,128)S(1)}, bf16[768,512]{1,0:T(8,128)(2,1)S(1)}, bf16[768,1536]{1,0:T(8,128)(2,1)S(1)}, bf16[4,6,128,128]{3,2,1,0:T(8,128...) custom-call(s32[1]{0:T(128)} %bitcast.t_ref, s32[1]{0:T(128)} %bitcast.1.d_ref, ...), custom_call_target="tpu_custom_call" | custom-call | flops 1 | bytes 1 | tf_op jit(solution)/shard_map/row_forward/pallas_call | solution.py:116
  68.4 7.1 %hidden_first.1 = (f32[768,512]{1,0:T(8,128)S(1)}, f32[768,512]{1,0:T(8,128)S(1)}, bf16[1024,512]{1,0:T(8,128)(2,1)S(1)}, bf16[1024,512]{1,0:T(8,128)(2,1)S(1)},...) custom-call(s32[1]{0:T(128)} %bitcast.t_ref, s32[1]{0:T(128)} %bitcast.1.d_ref, ...), custom_call_target="tpu_custom_call" | custom-call | flops 1 | bytes 1 | tf_op jit(solution)/shard_map/hidden_first/pallas_call | solution.py:116
  75.6 8.0 %hidden_second.1 = (bf16[768,512]{1,0:T(8,128)(2,1)S(1)}, f32[768,512]{1,0:T(8,128)S(1)}, bf16[768,512]{1,0:T(8,128)(2,1)S(1)}, f32[8,512]{1,0:T(8,128)S(1)}, bf...) custom-call(s32[1]{0:T(128)} %bitcast.t_ref, ...), custom_call_target="tpu_custom_call" | custom-call | flops 1 | bytes 1 | tf_op jit(solution)/shard_map/hidden_second/pallas_call | solution.py:116
  84.1 2.1 collective-permute-done.13.refs_3_.refs_7_
  86.3 1.5 collective-permute-done.12.refs_2_.refs_6_
  88.2 8.9 %row_backward.1 = (bf16[768,1536]{1,0:T(8,128)(2,1)S(1)}, bf16[768,512]{1,0:T(8,128)(2,1)S(1)}, bf16[192,512]{1,0:T(8,128)(2,1)S(1)}, bf16[192,512]{1,0:T(8,128)...) custom-call(s32[1]{0:T(128)} %bitcast.t_ref, s32[1]{0:T(128)} %bitcast.1.d_ref, ...), custom_call_target="tpu_custom_call" | custom-call | flops 1 | bytes 1 | tf_op jit(solution)/shard_map/row_backward/pallas_call | solution.py:116
  97.2 2.3 row_weights.1
  100.8 1.8 collective-permute-start.17
  102.6 1.6 collective-permute-start.18
  105.0 6.8 %collective-permute-done.21.w2 = bf16[3,512,128]{2,1,0:T(8,128)(2,1)S(1)} collective-permute-done((bf16[3,512,128]{2,1,0:T(8,128)(2,1)S(1)}, bf16[3,512,128]{2,1,0:T(8,128)(2,1)S(1)}, u32[]{:S(2)}, u32[]{:S(2)}) %collective-permute-start.21) | collective-permute-done | bytes 393248 | tf_op jit(solution)/shard_map/ppermute | solution.py:554
  111.8 3.8 %collective-permute-done.15.r2 = bf16[192,512]{1,0:T(8,128)(2,1)S(1)} collective-permute-done((bf16[192,512]{1,0:T(8,128)(2,1)S(1)}, bf16[192,512]{1,0:T(8,128)(2,1)S(1)}, u32[]{:S(2)}, u32[]{:S(2)}) %collective-permute-start.15) | collective-permute-done | bytes 196640 | tf_op jit(solution)/shard_map/ppermute | solution.py:554
  115.6 3.5 %collective-permute-done.16.r3 = bf16[192,512]{1,0:T(8,128)(2,1)S(1)} collective-permute-done((bf16[192,512]{1,0:T(8,128)(2,1)S(1)}, bf16[192,512]{1,0:T(8,128)(2,1)S(1)}, u32[]{:S(2)}, u32[]{:S(2)}) %collective-permute-start.16) | collective-permute-done | bytes 196640 | tf_op jit(solution)/shard_map/ppermute | solution.py:554
  120.9 4.1 %feature_again.1 = (bf16[768,512]{1,0:T(8,128)(2,1)S(1)}, bf16[8,96,1536]{2,1,0:T(8,128)(2,1)S(1)}, bf16[8,4,96,96]{3,2,1,0:T(8,128)(2,1)S(1)}) custom-call(s32[1]{0:T(128)} %bitcast.t_ref, s32[1]{0:T(128)} %bitcast.1.d_ref, bf16[89,32,512]{2,1,0:T(8,128)(2,1)S(1)} %bitcast.34, bf16[3,512]{1,0:T(4,128)(2,1)S(1)} %copy-done.10, ...), custom_call_target="tpu_custom_call" | custom-call | flops 1 | bytes 1 | tf_op jit(solution)/shard_map/feature_again/pallas_call | solution.py:116
  125.0 10.9 %feature_backward.1 = (f32[768,512]{1,0:T(8,128)S(1)}, bf16[768,1536]{1,0:T(8,128)(2,1)S(1)}, bf16[2,1536,128]{2,1,0:T(8,128)(2,1)S(1)}, bf16[2,1536,128]{2,1,0:T(8,128)(2,1)S(1)}) custom-call(s32[1]{0:T(128)} %bitcast.t_ref, s32[1]{0:T(128)} %bitcast.1.d_ref, bf16[192,512]{1,0:T(8,128)(2,1)S(1)} %get-tuple-element.144.r0, ...), custom_call_target="tpu_custom_call" | custom-call | flops 1 | bytes 1 | tf_op jit(solution)/shard_map/feature_backward/pallas_call | solution.py:116
  136.4 1.8 collective-permute-start.27
  139.0 2.6 collective-permute-start.24
  141.6 4.6 %collective-permute-done.23.refs_1_ = bf16[256,512]{1,0:T(8,128)(2,1)S(1)} collective-permute-done((bf16[256,512]{1,0:T(8,128)(2,1)S(1)}, bf16[256,512]{1,0:T(8,128)(2,1)S(1)}, u32[]{:S(2)}, u32[]{:S(2)}) %collective-permute-start.23) | collective-permute-done | bytes 262176 | tf_op jit(solution)/shard_map/ppermute | solution.py:554
  146.2 7.1 %collective-permute-done.24.refs_3_ = bf16[2,128,512]{2,1,0:T(8,128)(2,1)S(1)} collective-permute-done((bf16[2,128,512]{2,1,0:T(8,128)(2,1)S(1)}, bf16[2,128,512]{2,1,0:T(8,128)(2,1)S(1)}, u32[]{:S(2)}, u32[]{:S(2)}) %collective-permute-start.24) | collective-permute-done | bytes 262176 | tf_op jit(solution)/shard_map/ppermute | solution.py:554
  153.4 2.4 feature_input.1
  157.8 4.9 %collective-permute-done.28.refs_7_ = bf16[128,512]{1,0:T(8,128)(2,1)S(1)} collective-permute-done((bf16[128,512]{1,0:T(8,128)(2,1)S(1)}, bf16[128,512]{1,0:T(8,128)(2,1)S(1)}, u32[]{:S(2)}, u32[]{:S(2)}) %collective-permute-start.28) | collective-permute-done | bytes 131104 | tf_op jit(solution)/shard_map/ppermute | solution.py:554
  163.8 3.8 %collective-permute-done.29.refs_9_ = bf16[128,512]{1,0:T(8,128)(2,1)S(1)} collective-permute-done((bf16[128,512]{1,0:T(8,128)(2,1)S(1)}, bf16[128,512]{1,0:T(8,128)(2,1)S(1)}, u32[]{:S(2)}, u32[]{:S(2)}) %collective-permute-start.29) | collective-permute-done | bytes 131104 | tf_op jit(solution)/shard_map/ppermute | solution.py:554
  168.0 1.2 collective-permute-start.33
  170.1 2.4 collective-permute-start.38
  172.5 7.6 %collective-permute-done.33.refs_1_ = bf16[1536,128]{1,0:T(8,128)(2,1)S(1)} collective-permute-done((bf16[1536,128]{1,0:T(8,128)(2,1)S(1)}, bf16[1536,128]{1,0:T(8,128)(2,1)S(1)}, u32[]{:S(2)}, u32[]{:S(2)}) %collective-permute-start.33) | collective-permute-done | bytes 393248 | tf_op jit(solution)/shard_map/ppermute | solution.py:554
  182.7 2.1 columns_home.1
  184.8 16.4 %collective-permute-done.37.refs_3_ = f32[24,512]{1,0:T(8,128)S(1)} collective-permute-done((f32[24,512]{1,0:T(8,128)S(1)}, f32[24,512]{1,0:T(8,128)S(1)}, u32[]{:S(2)}, u32[]{:S(2)}) %collective-permute-start.37) | collective-permute-done | bytes 49184 | tf_op jit(solution)/shard_map/ppermute | solution.py:554
  202.6 3.4 %collective-permute-start.44 = (bf16[128,512]{1,0:T(8,128)(2,1)S(1)}, bf16[128,512]{1,0:T(8,128)(2,1)S(1)}, u32[]{:S(2)}, u32[]{:S(2)}) collective-permute-start(bf16[128,512]{1,0:T(8,128)(2,1)S(1)} %get-tuple-element.203.refs_8_), channel_id=1, source_target_pairs={{0,16},{4,20},{8,24},{12,28},{16,0},{20,4},{24,8},{28,12},{1,17},{... | collective-permute-start | bytes 393224 | tf_op jit(solution)/shard_map/ppermute | solution.py:554
  206.0 1.5 collective-permute-start.41
  207.5 3.0 %collective-permute-done.41.refs_3_ = f32[24,512]{1,0:T(8,128)S(1)} collective-permute-done((f32[24,512]{1,0:T(8,128)S(1)}, f32[24,512]{1,0:T(8,128)S(1)}, u32[]{:S(2)}, u32[]{:S(2)}) %collective-permute-start.41) | collective-permute-done | bytes 49184 | tf_op jit(solution)/shard_map/ppermute | solution.py:554
  210.7 1.6 collective-permute-start.48
  215.3 6.7 %collective-permute-done.46.refs_3_ = f32[24,512]{1,0:T(8,128)S(1)} collective-permute-done((f32[24,512]{1,0:T(8,128)S(1)}, f32[24,512]{1,0:T(8,128)S(1)}, u32[]{:S(2)}, u32[]{:S(2)}) %collective-permute-start.46) | collective-permute-done | bytes 49184 | tf_op jit(solution)/shard_map/ppermute | solution.py:554
  223.0 4.1 %collective-permute-done.45.refs_1_ = bf16[384,128]{1,0:T(8,128)(2,1)S(1)} collective-permute-done((bf16[384,128]{1,0:T(8,128)(2,1)S(1)}, bf16[384,128]{1,0:T(8,128)(2,1)S(1)}, u32[]{:S(2)}, u32[]{:S(2)}) %collective-permute-start.45) | collective-permute-done | bytes 98336 | tf_op jit(solution)/shard_map/ppermute | solution.py:554
  228.2 2.5 collective-permute-start.52
  231.1 2.5 collective-permute-start.51
  233.6 5.7 %collective-permute-done.51.refs_3_ = f32[24,512]{1,0:T(8,128)S(1)} collective-permute-done((f32[24,512]{1,0:T(8,128)S(1)}, f32[24,512]{1,0:T(8,128)S(1)}, u32[]{:S(2)}, u32[]{:S(2)}) %collective-permute-start.51) | collective-permute-done | bytes 49184 | tf_op jit(solution)/shard_map/ppermute | solution.py:554
  241.2 1.4 collective-permute-start.53
  242.6 1.3 copy.31
  243.9 3.7 %collective-permute-done.53.refs_1_ = bf16[384,128]{1,0:T(8,128)(2,1)} collective-permute-done((bf16[384,128]{1,0:T(8,128)(2,1)S(1)}, bf16[384,128]{1,0:T(8,128)(2,1)}, u32[]{:S(2)}, u32[]{:S(2)}) %collective-permute-start.53) | collective-permute-done | bytes 98336 | tf_op jit(solution)/shard_map/ppermute | solution.py:554
  250.7 1.5 fusion
  252.8 8.2 %collective-permute-done.55.refs_1_ = bf16[768,128]{1,0:T(8,128)(2,1)S(1)} collective-permute-done((bf16[768,128]{1,0:T(8,128)(2,1)S(1)}, bf16[768,128]{1,0:T(8,128)(2,1)S(1)}, u32[]{:S(2)}, u32[]{:S(2)}) %collective-permute-start.55) | collective-permute-done | bytes 196640 | tf_op jit(solution)/shard_map/ppermute | solution.py:554
  264.6 4.3 %rows_home.1 = bf16[89,32,512]{2,1,0:T(8,128)(2,1)} custom-call(s32[1]{0:T(128)} %bitcast.t_ref, s32[1]{0:T(128)} %bitcast.1.d_ref, bf16[720,512]{1,0:T(8,128)(2,1)S(1)} %get-tuple-element.197.p0, bf16[720,512]{1,0:T(8,128)(2,1)S(1)} %collective-permute-done.34.p1, bf16[720,512]{1,0:T(8,128)(2,1)S(1)} %collective-permute-done.35.p2, ...), custom_call_target="tpu_custom_call" | custom-call | flops 1 | bytes 1 | tf_op jit(solution)/shard_map/rows_home/pallas_call | solution.py:116
  (136 shorter events, 43.1 us)
Async XLA Ops:
  4.3 30.1 %collective-permute-start.4 = (bf16[2576,128]{1,0:T(8,128)(2,1)S(1)}, bf16[2576,128]{1,0:T(8,128)(2,1)S(1)}, u32[]{:S(2)}, u32[]{:S(2)}) collective-permute-start(bf16[2576,128]{1,0:T(8,128)(2,1)S(1)} %pack.1.f0.r0.w0.b0), channel_id=1, source_target_pairs={{0,2},{1,3},{2,0},{3,1},{4,6},{5,7},{6,4},{7,5},{8,10},{9,11},{10,... | collective-permute-start | bytes 1978376 | tf_op jit(solution)/shard_map/ppermute | solution.py:554
  22.4 7.9 %collective-permute-start.1 = (bf16[2,384,128]{2,1,0:T(8,128)(2,1)S(1)}, bf16[2,384,128]{2,1,0:T(8,128)(2,1)S(1)}, u32[]{:S(2)}, u32[]{:S(2)}) collective-permute-start(bf16[2,384,128]{2,1,0:T(8,128)(2,1)S(1)} %get-tuple-element.123), channel_id=1, source_target_pairs={{0,2},{1,3},{2,0},{3,1},{4,6},{5,7},{6,4},{7,5},{8,10},{9,11},{10,... | collective-permute-start | bytes 589832 | tf_op jit(solution)/shard_map/ppermute | solution.py:554
  22.5 9.1 %collective-permute-start.2 = (bf16[2,384,128]{2,1,0:T(8,128)(2,1)S(1)}, bf16[2,384,128]{2,1,0:T(8,128)(2,1)S(1)}, u32[]{:S(2)}, u32[]{:S(2)}) collective-permute-start(bf16[2,384,128]{2,1,0:T(8,128)(2,1)S(1)} %get-tuple-element.124), channel_id=1, source_target_pairs={{0,3},{1,2},{2,1},{3,0},{4,7},{5,6},{6,5},{7,4},{8,11},{9,10},{10,... | collective-permute-start | bytes 589832 | tf_op jit(solution)/shard_map/ppermute | solution.py:554
  23.4 12.4 %collective-permute-start.3 = (bf16[2576,128]{1,0:T(8,128)(2,1)S(1)}, bf16[2576,128]{1,0:T(8,128)(2,1)S(1)}, u32[]{:S(2)}, u32[]{:S(2)}) collective-permute-start(bf16[2576,128]{1,0:T(8,128)(2,1)S(1)} %pack.1.f0.r0.w0.b0), channel_id=1, source_target_pairs={{0,1},{1,0},{2,3},{3,2},{4,5},{5,4},{6,7},{7,6},{8,9},{9,8},{10,11... | collective-permute-start | bytes 1978376 | tf_op jit(solution)/shard_map/ppermute | solution.py:554
  31.6 14.7 %collective-permute-start.10 = (bf16[512,512]{1,0:T(8,128)(2,1)}, bf16[512,512]{1,0:T(8,128)(2,1)S(1)}, u32[]{:S(2)}, u32[]{:S(2)}) collective-permute-start(bf16[512,512]{1,0:T(8,128)(2,1)} %down0), channel_id=1, source_target_pairs={{0,2},{1,3},{2,0},{3,1},{4,6},{5,7},{6,4},{7,5},{8,10},{9,11},{10,... | collective-permute-start | bytes 1572872 | tf_op jit(solution)/shard_map/ppermute | solution.py:554
  32.6 24.9 %collective-permute-start.8 = (bf16[512,512]{1,0:T(8,128)(2,1)S(1)}, bf16[512,512]{1,0:T(8,128)(2,1)S(1)}, u32[]{:S(2)}, u32[]{:S(2)}) collective-permute-start(bf16[512,512]{1,0:T(8,128)(2,1)S(1)} %copy-done.6), channel_id=1, source_target_pairs={{0,2},{1,3},{2,0},{3,1},{4,6},{5,7},{6,4},{7,5},{8,10},{9,11},{10,... | collective-permute-start | bytes 1572872 | tf_op jit(solution)/shard_map/ppermute | solution.py:554
  34.4 24.0 %collective-permute-start.5 = (bf16[2576,128]{1,0:T(8,128)(2,1)S(1)}, bf16[2576,128]{1,0:T(8,128)(2,1)S(1)}, u32[]{:S(2)}, u32[]{:S(2)}) collective-permute-start(bf16[2576,128]{1,0:T(8,128)(2,1)S(1)} %collective-permute-done.4.f2.r2.w2.b0), channel_id=1, source_target_pairs={{0,1},{1,0},{2,3},{3,2},{4,5},{5,4},{6,7},{7,6},{8,9},{9,8},{10,11... | collective-permute-start | bytes 1978376 | tf_op jit(solution)/shard_map/ppermute | solution.py:554
  35.4 32.9 %collective-permute-start.6 = (bf16[512,512]{1,0:T(8,128)(2,1)S(1)}, bf16[512,512]{1,0:T(8,128)(2,1)S(1)}, u32[]{:S(2)}, u32[]{:S(2)}) collective-permute-start(bf16[512,512]{1,0:T(8,128)(2,1)S(1)} %copy-done.6), channel_id=1, source_target_pairs={{0,1},{1,0},{2,3},{3,2},{4,5},{5,4},{6,7},{7,6},{8,9},{9,8},{10,11... | collective-permute-start | bytes 1572872 | tf_op jit(solution)/shard_map/ppermute | solution.py:554
  35.8 32.6 %collective-permute-start.7 = (bf16[512,512]{1,0:T(8,128)(2,1)}, bf16[512,512]{1,0:T(8,128)(2,1)S(1)}, u32[]{:S(2)}, u32[]{:S(2)}) collective-permute-start(bf16[512,512]{1,0:T(8,128)(2,1)} %down0), channel_id=1, source_target_pairs={{0,1},{1,0},{2,3},{3,2},{4,5},{5,4},{6,7},{7,6},{8,9},{9,8},{10,11... | collective-permute-start | bytes 1572872 | tf_op jit(solution)/shard_map/ppermute | solution.py:554
  46.3 29.3 %collective-permute-start.11 = (bf16[512,512]{1,0:T(8,128)(2,1)S(1)}, bf16[512,512]{1,0:T(8,128)(2,1)S(1)}, u32[]{:S(2)}, u32[]{:S(2)}) collective-permute-start(bf16[512,512]{1,0:T(8,128)(2,1)S(1)} %collective-permute-done.10.down0), channel_id=1, source_target_pairs={{0,1},{1,0},{2,3},{3,2},{4,5},{5,4},{6,7},{7,6},{8,9},{9,8},{10,11... | collective-permute-start | bytes 1572872 | tf_op jit(solution)/shard_map/ppermute | solution.py:554
  57.5 18.1 %collective-permute-start.9 = (bf16[512,512]{1,0:T(8,128)(2,1)S(1)}, bf16[512,512]{1,0:T(8,128)(2,1)S(1)}, u32[]{:S(2)}, u32[]{:S(2)}) collective-permute-start(bf16[512,512]{1,0:T(8,128)(2,1)S(1)} %collective-permute-done.8.up0), channel_id=1, source_target_pairs={{0,1},{1,0},{2,3},{3,2},{4,5},{5,4},{6,7},{7,6},{8,9},{9,8},{10,11... | collective-permute-start | bytes 1572872 | tf_op jit(solution)/shard_map/ppermute | solution.py:554
  99.4 21.1 %collective-permute-start.19 = (bf16[2,2560,128]{2,1,0:T(8,128)(2,1)S(1)}, bf16[2,2560,128]{2,1,0:T(8,128)(2,1)S(1)}, u32[]{:S(2)}, u32[]{:S(2)}) collective-permute-start(bf16[2,2560,128]{2,1,0:T(8,128)(2,1)S(1)} %get-tuple-element.153), channel_id=1, source_target_pairs={{0,1},{1,0},{2,3},{3,2},{4,5},{5,4},{6,7},{7,6},{8,9},{9,8},{10,11... | collective-permute-start | bytes 3932168 | tf_op jit(solution)/shard_map/ppermute | solution.py:554
  99.9 12.0 %collective-permute-start.21 = (bf16[3,512,128]{2,1,0:T(8,128)(2,1)S(1)}, bf16[3,512,128]{2,1,0:T(8,128)(2,1)S(1)}, u32[]{:S(2)}, u32[]{:S(2)}) collective-permute-start(bf16[3,512,128]{2,1,0:T(8,128)(2,1)S(1)} %bitcast.39), channel_id=1, source_target_pairs={{0,2},{1,3},{2,0},{3,1},{4,6},{5,7},{6,4},{7,5},{8,10},{9,11},{10,... | collective-permute-start | bytes 1179656 | tf_op jit(solution)/shard_map/ppermute | solution.py:554
  100.8 18.5 %collective-permute-start.17 = (bf16[2,256,512]{2,1,0:T(8,128)(2,1)S(1)}, bf16[2,256,512]{2,1,0:T(8,128)(2,1)S(1)}, u32[]{:S(2)}, u32[]{:S(2)}) collective-permute-start(bf16[2,256,512]{2,1,0:T(8,128)(2,1)S(1)} %get-tuple-element.136), channel_id=1, source_target_pairs={{0,4},{4,0},{8,12},{12,8},{16,20},{20,16},{24,28},{28,24},{1,5},{5... | collective-permute-start | bytes 1572872 | tf_op jit(solution)/shard_map/ppermute | solution.py:554
  102.6 17.7 %collective-permute-start.18 = (bf16[2,256,512]{2,1,0:T(8,128)(2,1)S(1)}, bf16[2,256,512]{2,1,0:T(8,128)(2,1)S(1)}, u32[]{:S(2)}, u32[]{:S(2)}) collective-permute-start(bf16[2,256,512]{2,1,0:T(8,128)(2,1)S(1)} %get-tuple-element.138), channel_id=1, source_target_pairs={{0,8},{4,12},{8,0},{12,4},{16,24},{20,28},{24,16},{28,20},{1,9},{5... | collective-permute-start | bytes 1572872 | tf_op jit(solution)/shard_map/ppermute | solution.py:554
  104.2 11.5 %collective-permute-start.15 = (bf16[192,512]{1,0:T(8,128)(2,1)S(1)}, bf16[192,512]{1,0:T(8,128)(2,1)S(1)}, u32[]{:S(2)}, u32[]{:S(2)}) collective-permute-start(bf16[192,512]{1,0:T(8,128)(2,1)S(1)} %get-tuple-element.146), channel_id=1, source_target_pairs={{0,2},{1,3},{2,0},{3,1},{4,6},{5,7},{6,4},{7,5},{8,10},{9,11},{10,... | collective-permute-start | bytes 589832 | tf_op jit(solution)/shard_map/ppermute | solution.py:554
  111.8 7.3 %collective-permute-start.16 = (bf16[192,512]{1,0:T(8,128)(2,1)S(1)}, bf16[192,512]{1,0:T(8,128)(2,1)S(1)}, u32[]{:S(2)}, u32[]{:S(2)}) collective-permute-start(bf16[192,512]{1,0:T(8,128)(2,1)S(1)} %get-tuple-element.147), channel_id=1, source_target_pairs={{0,3},{1,2},{2,1},{3,0},{4,7},{5,6},{6,5},{7,4},{8,11},{9,10},{10,... | collective-permute-start | bytes 589832 | tf_op jit(solution)/shard_map/ppermute | solution.py:554
  115.6 5.3 %collective-permute-start.20 = (bf16[3,512,128]{2,1,0:T(8,128)(2,1)S(1)}, bf16[3,512,128]{2,1,0:T(8,128)(2,1)S(1)}, u32[]{:S(2)}, u32[]{:S(2)}) collective-permute-start(bf16[3,512,128]{2,1,0:T(8,128)(2,1)S(1)} %bitcast.40), channel_id=1, source_target_pairs={{0,1},{1,0},{2,3},{3,2},{4,5},{5,4},{6,7},{7,6},{8,9},{9,8},{10,11... | collective-permute-start | bytes 1179656 | tf_op jit(solution)/shard_map/ppermute | solution.py:554
  119.3 36.6 %collective-permute-start.31 = (bf16[24,32,512]{2,1,0:T(8,128)(2,1)S(1)}, bf16[24,32,512]{2,1,0:T(8,128)(2,1)S(1)}, u32[]{:S(2)}, u32[]{:S(2)}) collective-permute-start(bf16[24,32,512]{2,1,0:T(8,128)(2,1)S(1)} %bitcast.44), channel_id=1, source_target_pairs={{0,2},{1,3},{2,0},{3,1},{4,6},{5,7},{6,4},{7,5},{8,10},{9,11},{10,... | collective-permute-start | bytes 2359304 | tf_op jit(solution)/shard_map/ppermute | solution.py:554
  135.9 31.7 %collective-permute-start.25 = (bf16[2,1536,128]{2,1,0:T(8,128)(2,1)S(1)}, bf16[2,1536,128]{2,1,0:T(8,128)(2,1)S(1)}, u32[]{:S(2)}, u32[]{:S(2)}) collective-permute-start(bf16[2,1536,128]{2,1,0:T(8,128)(2,1)S(1)} %get-tuple-element.185), channel_id=1, source_target_pairs={{0,1},{1,0},{2,3},{3,2},{4,5},{5,4},{6,7},{7,6},{8,9},{9,8},{10,11... | collective-permute-start | bytes 2359304 | tf_op jit(solution)/shard_map/ppermute | solution.py:554
  136.4 31.2 %collective-permute-start.27 = (bf16[2,1280,128]{2,1,0:T(8,128)(2,1)S(1)}, bf16[2,1280,128]{2,1,0:T(8,128)(2,1)S(1)}, u32[]{:S(2)}, u32[]{:S(2)}) collective-permute-start(bf16[2,1280,128]{2,1,0:T(8,128)(2,1)S(1)} %get-tuple-element.162), channel_id=1, source_target_pairs={{0,4},{4,0},{8,12},{12,8},{16,20},{20,16},{24,28},{28,24},{1,5},{5... | collective-permute-start | bytes 1966088 | tf_op jit(solution)/shard_map/ppermute | solution.py:554
  138.2 8.0 %collective-permute-start.23 = (bf16[256,512]{1,0:T(8,128)(2,1)S(1)}, bf16[256,512]{1,0:T(8,128)(2,1)S(1)}, u32[]{:S(2)}, u32[]{:S(2)}) collective-permute-start(bf16[256,512]{1,0:T(8,128)(2,1)S(1)} %get-tuple-element.156), channel_id=1, source_target_pairs={{0,2},{1,3},{2,0},{3,1},{4,6},{5,7},{6,4},{7,5},{8,10},{9,11},{10,... | collective-permute-start | bytes 786440 | tf_op jit(solution)/shard_map/ppermute | solution.py:554
  139.0 14.3 %collective-permute-start.24 = (bf16[2,128,512]{2,1,0:T(8,128)(2,1)S(1)}, bf16[2,128,512]{2,1,0:T(8,128)(2,1)S(1)}, u32[]{:S(2)}, u32[]{:S(2)}) collective-permute-start(bf16[2,128,512]{2,1,0:T(8,128)(2,1)S(1)} %get-tuple-element.158), channel_id=1, source_target_pairs={{0,16},{4,20},{8,24},{12,28},{16,0},{20,4},{24,8},{28,12},{1,17},{... | collective-permute-start | bytes 786440 | tf_op jit(solution)/shard_map/ppermute | solution.py:554
  146.2 34.5 %collective-permute-start.30 = (bf16[24,32,512]{2,1,0:T(8,128)(2,1)S(1)}, bf16[24,32,512]{2,1,0:T(8,128)(2,1)S(1)}, u32[]{:S(2)}, u32[]{:S(2)}) collective-permute-start(bf16[24,32,512]{2,1,0:T(8,128)(2,1)S(1)} %bitcast.45), channel_id=1, source_target_pairs={{0,1},{1,0},{2,3},{3,2},{4,5},{5,4},{6,7},{7,6},{8,9},{9,8},{10,11... | collective-permute-start | bytes 2359304 | tf_op jit(solution)/shard_map/ppermute | solution.py:554
  155.9 25.9 %collective-permute-start.32 = (bf16[24,32,512]{2,1,0:T(8,128)(2,1)S(1)}, bf16[24,32,512]{2,1,0:T(8,128)(2,1)S(1)}, u32[]{:S(2)}, u32[]{:S(2)}) collective-permute-start(bf16[24,32,512]{2,1,0:T(8,128)(2,1)S(1)} %collective-permute-done.31.p2), channel_id=1, source_target_pairs={{0,1},{1,0},{2,3},{3,2},{4,5},{5,4},{6,7},{7,6},{8,9},{9,8},{10,11... | collective-permute-start | bytes 2359304 | tf_op jit(solution)/shard_map/ppermute | solution.py:554
  157.1 5.6 %collective-permute-start.28 = (bf16[128,512]{1,0:T(8,128)(2,1)S(1)}, bf16[128,512]{1,0:T(8,128)(2,1)S(1)}, u32[]{:S(2)}, u32[]{:S(2)}) collective-permute-start(bf16[128,512]{1,0:T(8,128)(2,1)S(1)} %get-tuple-element.171), channel_id=1, source_target_pairs={{0,8},{4,12},{8,0},{12,4},{16,24},{20,28},{24,16},{28,20},{1,9},{5... | collective-permute-start | bytes 393224 | tf_op jit(solution)/shard_map/ppermute | solution.py:554
  168.0 12.1 %collective-permute-start.33 = (bf16[1536,128]{1,0:T(8,128)(2,1)S(1)}, bf16[1536,128]{1,0:T(8,128)(2,1)S(1)}, u32[]{:S(2)}, u32[]{:S(2)}) collective-permute-start(bf16[1536,128]{1,0:T(8,128)(2,1)S(1)} %get-tuple-element.187), channel_id=1, source_target_pairs={{0,2},{1,3},{2,0},{3,1},{4,6},{5,7},{6,4},{7,5},{8,10},{9,11},{10,... | collective-permute-start | bytes 1179656 | tf_op jit(solution)/shard_map/ppermute | solution.py:554
  169.3 36.7 %collective-permute-start.42 = (bf16[1280,128]{1,0:T(8,128)(2,1)S(1)}, bf16[1280,128]{1,0:T(8,128)(2,1)S(1)}, u32[]{:S(2)}, u32[]{:S(2)}) collective-permute-start(bf16[1280,128]{1,0:T(8,128)(2,1)S(1)} %get-tuple-element.190), channel_id=1, source_target_pairs={{0,2},{1,3},{2,0},{3,1},{4,6},{5,7},{6,4},{7,5},{8,10},{9,11},{10,... | collective-permute-start | bytes 983048 | tf_op jit(solution)/shard_map/ppermute | solution.py:554
  170.1 31.1 %collective-permute-start.38 = (bf16[128,512]{1,0:T(8,128)(2,1)S(1)}, bf16[128,512]{1,0:T(8,128)(2,1)S(1)}, u32[]{:S(2)}, u32[]{:S(2)}) collective-permute-start(bf16[128,512]{1,0:T(8,128)(2,1)S(1)} %get-tuple-element.191.refs_4_), channel_id=1, source_target_pairs={{0,16},{4,20},{8,24},{12,28},{16,0},{20,4},{24,8},{28,12},{1,17},{... | collective-permute-start | bytes 393224 | tf_op jit(solution)/shard_map/ppermute | solution.py:554
  180.1 21.0 %collective-permute-start.39 = (bf16[128,512]{1,0:T(8,128)(2,1)S(1)}, bf16[128,512]{1,0:T(8,128)(2,1)S(1)}, u32[]{:S(2)}, u32[]{:S(2)}) collective-permute-start(bf16[128,512]{1,0:T(8,128)(2,1)S(1)} %get-tuple-element.192.refs_6_), channel_id=1, source_target_pairs={{0,4},{4,0},{8,12},{12,8},{16,20},{20,16},{24,28},{28,24},{1,5},{5... | collective-permute-start | bytes 393224 | tf_op jit(solution)/shard_map/ppermute | solution.py:554
  180.6 60.0 %collective-permute-start.35 = (bf16[720,512]{1,0:T(8,128)(2,1)S(1)}, bf16[720,512]{1,0:T(8,128)(2,1)S(1)}, u32[]{:S(2)}, u32[]{:S(2)}) collective-permute-start(bf16[720,512]{1,0:T(8,128)(2,1)S(1)} %get-tuple-element.197.p0), channel_id=1, source_target_pairs={{0,2},{1,3},{2,0},{3,1},{4,6},{5,7},{6,4},{7,5},{8,10},{9,11},{10,... | collective-permute-start | bytes 2211848 | tf_op jit(solution)/shard_map/ppermute | solution.py:554
  181.8 19.4 %collective-permute-start.37 = (f32[24,512]{1,0:T(8,128)S(1)}, f32[24,512]{1,0:T(8,128)S(1)}, u32[]{:S(2)}, u32[]{:S(2)}) collective-permute-start(f32[24,512]{1,0:T(8,128)S(1)} %get-tuple-element.188.refs_2_), channel_id=1, source_target_pairs={{0,2},{1,3},{2,0},{3,1},{4,6},{5,7},{6,4},{7,5},{8,10},{9,11},{10,... | collective-permute-start | bytes 147464 | tf_op jit(solution)/shard_map/ppermute | solution.py:554
  201.3 9.2 %collective-permute-start.40 = (bf16[768,128]{1,0:T(8,128)(2,1)S(1)}, bf16[768,128]{1,0:T(8,128)(2,1)S(1)}, u32[]{:S(2)}, u32[]{:S(2)}) collective-permute-start(bf16[768,128]{1,0:T(8,128)(2,1)S(1)} %get-tuple-element.200), channel_id=1, source_target_pairs={{0,4},{4,0},{8,12},{12,8},{16,20},{20,16},{24,28},{28,24},{1,5},{5... | collective-permute-start | bytes 589832 | tf_op jit(solution)/shard_map/ppermute | solution.py:554
  201.9 8.6 %collective-permute-start.43 = (bf16[128,512]{1,0:T(8,128)(2,1)S(1)}, bf16[128,512]{1,0:T(8,128)(2,1)S(1)}, u32[]{:S(2)}, u32[]{:S(2)}) collective-permute-start(bf16[128,512]{1,0:T(8,128)(2,1)S(1)} %get-tuple-element.202.refs_6_), channel_id=1, source_target_pairs={{0,8},{4,12},{8,0},{12,4},{16,24},{20,28},{24,16},{28,20},{1,9},{5... | collective-permute-start | bytes 393224 | tf_op jit(solution)/shard_map/ppermute | solution.py:554
  202.6 7.9 %collective-permute-start.44 = (bf16[128,512]{1,0:T(8,128)(2,1)S(1)}, bf16[128,512]{1,0:T(8,128)(2,1)S(1)}, u32[]{:S(2)}, u32[]{:S(2)}) collective-permute-start(bf16[128,512]{1,0:T(8,128)(2,1)S(1)} %get-tuple-element.203.refs_8_), channel_id=1, source_target_pairs={{0,16},{4,20},{8,24},{12,28},{16,0},{20,4},{24,8},{28,12},{1,17},{... | collective-permute-start | bytes 393224 | tf_op jit(solution)/shard_map/ppermute | solution.py:554
  210.7 16.4 %collective-permute-start.48 = (bf16[256,512]{1,0:T(8,128)(2,1)S(1)}, bf16[256,512]{1,0:T(8,128)(2,1)S(1)}, u32[]{:S(2)}, u32[]{:S(2)}) collective-permute-start(bf16[256,512]{1,0:T(8,128)(2,1)S(1)} %get-tuple-element.210.refs_6_), channel_id=1, source_target_pairs={{0,4},{4,0},{8,12},{12,8},{16,20},{20,16},{24,28},{28,24},{1,5},{5... | collective-permute-start | bytes 786440 | tf_op jit(solution)/shard_map/ppermute | solution.py:554
  212.3 14.8 %collective-permute-start.49 = (bf16[256,512]{1,0:T(8,128)(2,1)S(1)}, bf16[256,512]{1,0:T(8,128)(2,1)S(1)}, u32[]{:S(2)}, u32[]{:S(2)}) collective-permute-start(bf16[256,512]{1,0:T(8,128)(2,1)S(1)} %get-tuple-element.211.refs_8_), channel_id=1, source_target_pairs={{0,8},{4,12},{8,0},{12,4},{16,24},{20,28},{24,16},{28,20},{1,9},{5... | collective-permute-start | bytes 786440 | tf_op jit(solution)/shard_map/ppermute | solution.py:554
  213.3 13.8 %collective-permute-start.47 = (bf16[640,128]{1,0:T(8,128)(2,1)S(1)}, bf16[640,128]{1,0:T(8,128)(2,1)S(1)}, u32[]{:S(2)}, u32[]{:S(2)}) collective-permute-start(bf16[640,128]{1,0:T(8,128)(2,1)S(1)} %get-tuple-element.209), channel_id=1, source_target_pairs={{0,8},{4,12},{8,0},{12,4},{16,24},{20,28},{24,16},{28,20},{1,9},{5... | collective-permute-start | bytes 491528 | tf_op jit(solution)/shard_map/ppermute | solution.py:554
  214.3 7.7 %collective-permute-start.46 = (f32[24,512]{1,0:T(8,128)S(1)}, f32[24,512]{1,0:T(8,128)S(1)}, u32[]{:S(2)}, u32[]{:S(2)}) collective-permute-start(f32[24,512]{1,0:T(8,128)S(1)} %get-tuple-element.207.refs_2_), channel_id=1, source_target_pairs={{0,8},{4,12},{8,0},{12,4},{16,24},{20,28},{24,16},{28,20},{1,9},{5... | collective-permute-start | bytes 147464 | tf_op jit(solution)/shard_map/ppermute | solution.py:554
  228.2 11.1 %collective-permute-start.52 = (bf16[640,128]{1,0:T(8,128)(2,1)S(1)}, bf16[640,128]{1,0:T(8,128)(2,1)S(1)}, u32[]{:S(2)}, u32[]{:S(2)}) collective-permute-start(bf16[640,128]{1,0:T(8,128)(2,1)S(1)} %get-tuple-element.215.refs_4_), channel_id=1, source_target_pairs={{0,16},{4,20},{8,24},{12,28},{16,0},{20,4},{24,8},{28,12},{1,17},{... | collective-permute-start | bytes 491528 | tf_op jit(solution)/shard_map/ppermute | solution.py:554
  230.7 8.6 %collective-permute-start.50 = (bf16[384,128]{1,0:T(8,128)(2,1)S(1)}, bf16[384,128]{1,0:T(8,128)(2,1)S(1)}, u32[]{:S(2)}, u32[]{:S(2)}) collective-permute-start(bf16[384,128]{1,0:T(8,128)(2,1)S(1)} %get-tuple-element.213.refs_0_), channel_id=1, source_target_pairs={{0,16},{4,20},{8,24},{12,28},{16,0},{20,4},{24,8},{28,12},{1,17},{... | collective-permute-start | bytes 294920 | tf_op jit(solution)/shard_map/ppermute | solution.py:554
  231.1 8.2 %collective-permute-start.51 = (f32[24,512]{1,0:T(8,128)S(1)}, f32[24,512]{1,0:T(8,128)S(1)}, u32[]{:S(2)}, u32[]{:S(2)}) collective-permute-start(f32[24,512]{1,0:T(8,128)S(1)} %get-tuple-element.214.refs_2_), channel_id=1, source_target_pairs={{0,16},{4,20},{8,24},{12,28},{16,0},{20,4},{24,8},{28,12},{1,17},{... | collective-permute-start | bytes 147464 | tf_op jit(solution)/shard_map/ppermute | solution.py:554
  240.0 7.5 %collective-permute-start.54 = (bf16[640,128]{1,0:T(8,128)(2,1)S(1)}, bf16[640,128]{1,0:T(8,128)(2,1)}, u32[]{:S(2)}, u32[]{:S(2)}) collective-permute-start(bf16[640,128]{1,0:T(8,128)(2,1)S(1)} %get-tuple-element.221.refs_2_), channel_id=1, source_target_pairs={{0,8},{4,12},{8,0},{12,4},{16,24},{20,28},{24,16},{28,20},{1,9},{5... | collective-permute-start | bytes 491528 | tf_op jit(solution)/shard_map/ppermute | solution.py:554
  240.6 24.0 %collective-permute-start.34 = (bf16[720,512]{1,0:T(8,128)(2,1)S(1)}, bf16[720,512]{1,0:T(8,128)(2,1)S(1)}, u32[]{:S(2)}, u32[]{:S(2)}) collective-permute-start(bf16[720,512]{1,0:T(8,128)(2,1)S(1)} %get-tuple-element.197.p0), channel_id=1, source_target_pairs={{0,1},{1,0},{2,3},{3,2},{4,5},{5,4},{6,7},{7,6},{8,9},{9,8},{10,11... | collective-permute-start | bytes 2211848 | tf_op jit(solution)/shard_map/ppermute | solution.py:554
  240.6 24.0 %collective-permute-start.36 = (bf16[720,512]{1,0:T(8,128)(2,1)S(1)}, bf16[720,512]{1,0:T(8,128)(2,1)}, u32[]{:S(2)}, u32[]{:S(2)}) collective-permute-start(bf16[720,512]{1,0:T(8,128)(2,1)S(1)} %collective-permute-done.35.p2), channel_id=1, source_target_pairs={{0,1},{1,0},{2,3},{3,2},{4,5},{5,4},{6,7},{7,6},{8,9},{9,8},{10,11... | collective-permute-start | bytes 2211848 | tf_op jit(solution)/shard_map/ppermute | solution.py:554
  241.2 6.4 %collective-permute-start.53 = (bf16[384,128]{1,0:T(8,128)(2,1)S(1)}, bf16[384,128]{1,0:T(8,128)(2,1)}, u32[]{:S(2)}, u32[]{:S(2)}) collective-permute-start(bf16[384,128]{1,0:T(8,128)(2,1)S(1)} %get-tuple-element.219.refs_0_), channel_id=1, source_target_pairs={{0,8},{4,12},{8,0},{12,4},{16,24},{20,28},{24,16},{28,20},{1,9},{5... | collective-permute-start | bytes 294920 | tf_op jit(solution)/shard_map/ppermute | solution.py:554
  248.6 12.4 %collective-permute-start.56 = (bf16[1280,128]{1,0:T(8,128)(2,1)S(1)}, bf16[1280,128]{1,0:T(8,128)(2,1)S(1)}, u32[]{:S(2)}, u32[]{:S(2)}) collective-permute-start(bf16[1280,128]{1,0:T(8,128)(2,1)S(1)} %get-tuple-element.224.refs_2_), channel_id=1, source_target_pairs={{0,4},{4,0},{8,12},{12,8},{16,20},{20,16},{24,28},{28,24},{1,5},{5... | collective-permute-start | bytes 983048 | tf_op jit(solution)/shard_map/ppermute | solution.py:554
  249.5 11.5 %collective-permute-start.55 = (bf16[768,128]{1,0:T(8,128)(2,1)S(1)}, bf16[768,128]{1,0:T(8,128)(2,1)S(1)}, u32[]{:S(2)}, u32[]{:S(2)}) collective-permute-start(bf16[768,128]{1,0:T(8,128)(2,1)S(1)} %get-tuple-element.223.refs_0_), channel_id=1, source_target_pairs={{0,4},{4,0},{8,12},{12,8},{16,20},{20,16},{24,28},{28,24},{1,5},{5... | collective-permute-start | bytes 589832 | tf_op jit(solution)/shard_map/ppermute | solution.py:554
  (27 other events, 340.1 us)

commit v3 on v2

--- a/solution.py
+++ b/solution.py
@@ -105,7 +105,7 @@
     return jax.ShapeDtypeStruct(shape, dtype)
 
 
-def call(kernel, name, grid, t, ins, outs, scratch=(), vmem=32):
+def call(kernel, name, grid, t, ins, outs, scratch=(), vmem=32, us=1):
     spec = pltpu.PrefetchScalarGridSpec(
         num_scalar_prefetch=2,
         grid=grid,
@@ -138,7 +138,7 @@
 
 def pack(t, rq, fo, ro, ub):
     out = shaped((3 * rq.shape[1] + 8 * HD + 16, HD))
-    return call(pack_kernel, "pack", (), t, [(a, VMEM) for a in (rq, fo, ro, ub)], [(out, VMEM)], vmem=8)[0]
+    return call(pack_kernel, "pack", (), t, [(a, VMEM) for a in (rq, fo, ro, ub)], [(out, VMEM)], vmem=60)[0]
 
 
 def pack_part(pack, what):
@@ -188,7 +188,7 @@
         [(cells, pl.BlockSpec((feature_count, RB, width), lambda i, t, d: (0, i, 0)))]
         + [(a, full(a)) for a in (gains, shifts, weight)],
         [out] * 4,
-        [pltpu.VMEM((3, padded * RB, HD), F32), pltpu.VMEM((padded * RB, HD), F32)], vmem=28,
+        [pltpu.VMEM((3, padded * RB, HD), F32), pltpu.VMEM((padded * RB, HD), F32)], vmem=28, us=11
     )
 
 
@@ -255,7 +255,7 @@
     return call(
         partial(row_forward_kernel, feature_count=feature_count), "row_forward", (1,), t, ins,
         [whole((n, width), F32), whole((n, width)), whole((n, 12 * HD)), whole((4, n // side, side, side)),
-         whole((n, 4 * HD)), whole((n, width), F32), whole((n, width))],
+         whole((n, 4 * HD)), whole((n, width), F32), whole((n, width))], us=9
     )
 
 
@@ -324,7 +324,7 @@
         kernel, name = hidden_second_kernel, "hidden_second"
         ins += [(a, full(a)) for a in extra]
         results = [whole((n, width)), whole((n, width), F32), whole((n, width)), whole((8, width), F32)] + tail
-    return call(partial(kernel, feature_count=grads.shape[0]), name, (1,), t, ins, results)
+    return call(partial(kernel, feature_count=grads.shape[0]), name, (1,), t, ins, results, us=7)
 
 
 def attention_backward(q, k, v, p, do):
@@ -370,29 +370,38 @@
     return call(
         row_backward_kernel, "row_backward", (1,), t, ins,
         [whole(qkv.shape), whole((n, width))] + [whole((n // 4, width))] * 4 + [whole((8, width), F32)],
-        [pltpu.VMEM((n // rows, rows, width), F32)],
+        [pltpu.VMEM((n // rows, rows, width), F32)], us=9
     )
 
 
 def row_weights_kernel(t_ref, d_ref, n2_ref, dqkv_ref, gl2_ref, o2_ref, gl1_ref, m0, m1, m2, m3, keep_ref, send_ref):
     width = n2_ref.shape[1]
     columns = m0.shape[1] // RB
-    grad = mm(n2_ref[...].T, dqkv_ref[...])
-    out_grad = mm(gl2_ref[...].T, o2_ref[...])
-    feat_grad = mm(gl1_ref[...].T, jnp.concatenate([in_order(m, columns) for m in (m0, m1, m2, m3)], axis=-1))
+    grad = mm(n2_ref[...].T, dqkv_ref[...]).astype(BF)
+    out_grad = mm(gl2_ref[...].T, o2_ref[...]).astype(BF)
+    feat_grad = mm(gl1_ref[...].T, jnp.concatenate([in_order(m, columns) for m in (m0, m1, m2, m3)], axis=-1)).astype(BF)
     for h in range(4):
-        out = (keep_ref, send_ref)[h % 2]
-        for c in range(3):
-            out[h // 2, c * width : (c + 1) * width, :] = grad[:, (3 * h + c) * HD : (3 * h + c + 1) * HD].astype(BF)
-        out[h // 2, 3 * width : 4 * width, :] = out_grad[:, HD * h : HD * (h + 1)].astype(BF)
-        out[h // 2, 4 * width : 5 * width, :] = feat_grad[:, HD * h : HD * (h + 1)].astype(BF)
+        out = (keep_ref, send_ref)[h % 2].at[h // 2]
+        blocks = [grad[:, (3 * h + c) * HD : (3 * h + c + 1) * HD] for c in range(3)]
+        blocks += [out_grad[:, HD * h : HD * (h + 1)], feat_grad[:, HD * h : HD * (h + 1)]]
+        for at, first, count, lane in row_places(width):
+            out[at : at + count, lane * HD : (lane + 1) * HD] = blocks[first // width][first % width : first % width + count]
+
+
+def row_places(width):
+    tall = 5 * width // 4
+    first = 0
+    while first < 5 * width:
+        count = min(width - first % width, tall - first % tall)
+        yield first % tall, first, count, first // tall
+        first += count
 
 
 def row_weights(t, n2, dqkv, gl2, o2, gl1, mixed):
     width = n2.shape[1]
     return call(
         row_weights_kernel, "row_weights", (1,), t,
-        [(a, full(a)) for a in (n2, dqkv, gl2, o2, gl1, *mixed)], [whole((2, 5 * width, HD))] * 2, vmem=24,
+        [(a, full(a)) for a in (n2, dqkv, gl2, o2, gl1, *mixed)], [whole((2, 5 * width // 4, 4 * HD))] * 2, vmem=24,
     )
 
 
@@ -436,7 +445,7 @@
         feature_again_kernel, "feature_again", (1,), t,
         [(cells, row_block(cells, share))] + [(a, full(a)) for a in (gains, shifts, *weights)],
         [whole((padded * share, width)), whole((share, padded, 12 * HD)), whole((share, 4, padded, padded))],
-        [pltpu.VMEM((padded, RB, width), F32), pltpu.VMEM((3, padded * share, HD), F32)], vmem=28,
+        [pltpu.VMEM((padded, RB, width), F32), pltpu.VMEM((3, padded * share, HD), F32)], vmem=28, us=4
     )
 
 
@@ -478,13 +487,13 @@
         feature_backward_kernel, "feature_backward", (1,), t,
         [(a, full(a)) for a in pieces] + pack_parts(packs, "feat_out") + [(a, full(a)) for a in (qkv, p, n1)],
         [whole((cells, width), F32), whole((cells, 12 * HD))] + [whole((2, 3 * width, HD))] * 2,
-        [pltpu.VMEM((cells, width), BF), pltpu.VMEM((4, cells, HD), F32), pltpu.VMEM((12, cells, HD), F32)],
+        [pltpu.VMEM((cells, width), BF), pltpu.VMEM((4, cells, HD), F32), pltpu.VMEM((12, cells, HD), F32)], us=11
     )
 
 
 def feature_input_kernel(
     t_ref, d_ref, cells_ref, g1_ref, dqkv_ref, gains_ref, w0, w1, w2, w3, stats_a, stats_b, b0, b1, b2, b3,
-    out_ref, stats_ref, cell_scr,
+    out_ref, stats_ref, cell_scr, sums_scr,
 ):
     cells, width = g1_ref.shape
     share = cells // cell_scr.shape[0]
@@ -492,13 +501,15 @@
     dn1 = mm_nt(dqkv_ref[...], jnp.concatenate([three(w) for w in (w0, w1, w2, w3)], axis=-1))
     g0 = g1_ref[...] + norm_backward(dn1, normed, inverse, gains_ref[...].astype(F32)[0:1])
     out_ref[...] = g0[: out_ref.shape[0]].astype(BF)
-    stats_ref[0:8] = stats_a[...]
-    stats_ref[8:16] = stats_b[...]
-    stats_ref[4:5] = column_sum(dn1 * normed)
-    stats_ref[5:6] = column_sum(dn1)
-    stats_ref[16:24] = jnp.zeros((8, width), F32)
+    sums_scr[0:8] = stats_a[...]
+    sums_scr[8:16] = stats_b[...]
+    sums_scr[4:5] = column_sum(dn1 * normed)
+    sums_scr[5:6] = column_sum(dn1)
+    sums_scr[16:32] = jnp.zeros((16, width), F32)
     for k, row in enumerate((b0, b1, b2, b3)):
-        stats_ref[pl.ds(16 + lax.bitwise_xor(t_ref[0], k), 1), :] = row[...]
+        sums_scr[pl.ds(16 + lax.bitwise_xor(t_ref[0], k), 1), :] = row[...]
+    for j in range(4):
+        stats_ref[32 * j : 32 * (j + 1)] = sums_scr[:, j * HD : (j + 1) * HD]
 
 
 def feature_input(t, cells, g1, dqkv, gains, weights, sums, share):
@@ -507,8 +518,8 @@
     return call(
         feature_input_kernel, "feature_input", (1,), t,
         [(cells, row_block(cells, share))] + [(a, full(a)) for a in (g1, dqkv, gains, *weights, *sums)],
-        [whole((kept, width)), whole((24, width), F32)],
-        [pltpu.VMEM((count // share, RB, width), F32)], vmem=28,
+        [whole((kept, width)), whole((128, HD), F32)],
+        [pltpu.VMEM((count // share, RB, width), F32), pltpu.VMEM((32, width), F32)], vmem=28, us=2
     )
 
 
@@ -581,107 +592,168 @@
     at = 0
     ins = []
     for job in jobs:
-        ins.append((refs[at : at + len(job["own"])], refs[at + len(job["own"]) : at + 2 * len(job["own"])]))
-        at += 2 * len(job["own"])
+        count = len(job["parts"]) if job["parts"] else 1
+        ins.append((refs[at : at + count], refs[at + count : at + 2 * count]))
+        at += 2 * count
     for job, (own, other) in zip(jobs, ins):
         outs = refs[at : at + job["outs"]]
         at += job["outs"]
         kind, mask = job["next"]
-        if job["join"] is None:
-            start, rows = job["rows"]
-
-            def total(j, first, count):
-                part = (Ellipsis, pl.ds(start + first, count), slice(None))
-                return own[j][part].astype(F32) + other[j][part].astype(F32)
-
-            if kind == "half":
-                half = rows // 2
-                for out, side in zip(outs, (digit(d_ref, mask), 1 - digit(d_ref, mask))):
-                    first = pl.multiple_of(side * half, half)
-                    for j in range(len(own)):
-                        sums = total(j, first, half).astype(out.dtype)
-                        if len(own) > 1:
-                            out[j] = sums
-                        else:
-                            out[...] = sums
-            elif kind == "group":
-                sums = total(0, 0, rows)
-                outs[0][...] = sums[0].astype(outs[0].dtype)
-                outs[1][...] = sums[1].astype(outs[1].dtype)
-            else:
-                outs[0][...] = total(0, 0, rows).astype(outs[0].dtype)
-        else:
-            rows = own[0].shape[-2]
+        if job["join"] is not None:
+            rows = own[0].shape[0]
             side = digit(d_ref, job["join"])
             for source, place in ((own[0], side), (other[0], 1 - side)):
-                first = pl.multiple_of(place * rows, rows)
-                outs[0][..., pl.ds(first, rows), :] = source[...].astype(outs[0].dtype)
+                outs[0][pl.ds(pl.multiple_of(place * rows, rows), rows), :] = source[...].astype(outs[0].dtype)
+            continue
+        if job["parts"]:
+            def total(group, to):
+                base = 0
+                for mine, got, (groups, start, rows) in zip(own, other, job["parts"]):
+                    if group in groups:
+                        a, b = (r.at[group] if len(r.shape) == 3 else r for r in (mine, got))
+                        to[base : base + rows] = (
+                            a[start : start + rows].astype(F32) + b[start : start + rows].astype(F32))
+                        base += rows
+
+            scr = refs[-1]
+            for group in range(2):
+                total(group, scr)
+                place_sum(d_ref, scr, outs, kind, mask, group)
+        elif kind == "half":
+            rows = own[0].shape[-2] // 2
+            for out, side in zip(outs, (digit(d_ref, mask), 1 - digit(d_ref, mask))):
+                span = (Ellipsis, pl.ds(pl.multiple_of(side * rows, rows), rows), slice(None))
+                out[...] = (own[0][span].astype(F32) + other[0][span].astype(F32)).astype(out.dtype)
+        else:
+            sums = (own[0][...].astype(F32) + other[0][...].astype(F32)).astype(outs[0].dtype)
+            if kind == "group":
+                outs[0][...] = sums[0]
+                outs[1][...] = sums[1]
+            else:
+                outs[0][...] = sums
+
+
+def place_sum(d_ref, scr, outs, kind, mask, group):
+    if kind == "half":
+        rows = outs[0].shape[1]
+        for out, side in zip(outs, (digit(d_ref, mask), 1 - digit(d_ref, mask))):
+            out[group] = scr[pl.ds(pl.multiple_of(side * rows, rows), rows), :].astype(BF)
+    else:
+        outs[group][...] = scr[0 : outs[group].shape[0], :].astype(BF)
 
 
 class Chain:
-    def __init__(self, own, other, order, rows=None, low=BF):
-        self.own, self.other, self.low = tuple(own), tuple(other), low
+    def __init__(self, own, other, parts, order):
+        self.own, self.other, self.parts = tuple(own), tuple(other), parts
         dp = [m for m in order if m != "x"]
-        halved = dp[:-1] if low == BF else []
+        halved = dp[:2]
         self.plan = []
         for m in order:
-            if m == "x":
-                self.plan.append(("group" if low == BF else "whole", "x", None))
-            else:
-                self.plan.append(("half" if m in halved else "whole", m, None))
-        for m in reversed(halved):
-            self.plan.append(("whole", m, m))
+            self.plan.append(("group" if m == "x" else "half" if m in halved else "whole", m, None))
+        self.plan += [("whole", m, m) for m in reversed(halved)]
         self.join = None
-        self.rows = rows
-        self.result = None
+        self.ready = False
 
     def job(self):
-        n, w = self.own[0].shape[-2:]
-        start, rows = self.rows or (0, n)
-        lead = self.own[0].shape[:-2]
-        if len(self.own) > 1:
-            lead = (len(self.own),)
-        kind, mask, _ = self.plan[0] if self.plan else ("final", None, None)
+        kind, mask, _ = self.plan[0]
+        if self.parts:
+            lead = (2,)
+            rows = sum(count for groups, _, count in self.parts if 0 in groups)
+            w = self.own[0].shape[-1]
+        else:
+            lead = self.own[0].shape[:-2]
+            rows, w = self.own[0].shape[-2:]
         if self.join is not None:
-            shape = lead + (2 * n, w)
+            shape = (2 * rows, w)
         elif kind == "half":
             shape = lead + (rows // 2, w)
         elif kind == "group":
             shape = (rows, w)
         else:
             shape = lead + (rows, w)
-        out = shaped(shape, F32 if kind == "final" else self.low)
         count = 2 if kind in ("half", "group") else 1
-        spec = {"own": self.own, "other": self.other, "next": (kind, mask), "join": self.join,
-                "rows": (start, rows), "outs": count}
-        return spec, [out] * count
+        spec = {"parts": self.parts, "next": (kind, mask), "join": self.join, "outs": count}
+        scratch = [pltpu.VMEM((rows, w), F32)] if self.parts else []
+        return spec, [shaped(shape)] * count, scratch
 
     def take(self, outs):
-        if not self.plan:
-            self.result = outs[0]
-            return
         kind, mask, join = self.plan.pop(0)
-        sent = outs[-1]
         self.own = (outs[0],)
-        self.other = (swap(sent, "tensor", 2) if mask == "x" else swap(sent, "dp", mask),)
-        self.sent = sent
-        self.join, self.rows = join, None
+        self.other = (swap(outs[-1], "tensor", 2) if mask == "x" else swap(outs[-1], "dp", mask),)
+        self.join, self.parts = join, None
+        self.ready = not self.plan
 
 
 def merge(t, chains):
-    jobs, outs, ins = [], [], []
+    jobs, outs, ins, scratch = [], [], [], []
     for chain in chains:
-        spec, shapes = chain.job()
-        ins += [*spec["own"], *spec["other"]]
-        jobs.append({k: (v if k != "own" else [0] * len(v)) for k, v in spec.items() if k != "other"})
+        spec, shapes, scr = chain.job()
+        ins += [*chain.own, *chain.other]
+        jobs.append(spec)
         outs.append(shapes)
+        scratch = scratch or scr
     flat = [o for shapes in outs for o in shapes]
-    results = call(partial(merge_kernel, jobs=jobs), "merge", (), t, [(a, VMEM) for a in ins], [(o, VMEM) for o in flat], vmem=20)
+    results = call(
+        partial(merge_kernel, jobs=jobs), "merge", (), t, [(a, VMEM) for a in ins], [(o, VMEM) for o in flat],
+        scratch, vmem=16)
     at = 0
     for chain, shapes in zip(chains, outs):
         chain.take(results[at : at + len(shapes)])
         at += len(shapes)
     return results
+
+
+def joined(d_ref, own, other, mask, scr):
+    rows = own.shape[0]
+    side = digit(d_ref, mask)
+    for source, place in ((own, side), (other, 1 - side)):
+        scr[pl.ds(pl.multiple_of(place * rows, rows), rows), :] = source[...].astype(F32)
+
+
+def finish_kernel(t_ref, d_ref, a0, a1, b0, b1, up_ref, down_ref, qkv_ref, row_out_ref, feat_out_ref, scr_a, scr_b, tall, *, masks):
+    joined(d_ref, a0, a1, masks[0], scr_a)
+    joined(d_ref, b0, b1, masks[1], scr_b)
+    width = up_ref.shape[0]
+    half = scr_a.shape[0] - width
+    up_ref[...] = scr_a[0:width]
+    down_ref[...] = scr_b[0:width].T
+    for at, first, count, lane in row_places(width):
+        for scr, low, high in ((scr_a, 0, half), (scr_b, half, 2 * half)):
+            begin, end = max(at, low), min(at + count, high)
+            if begin < end:
+                to = first + begin - at
+                tall[to : to + end - begin, :] = scr[width + begin - low : width + end - low, lane * HD : (lane + 1) * HD]
+    qkv_ref[...] = tall[0 : 3 * width]
+    row_out_ref[...] = tall[3 * width : 4 * width].T
+    feat_out_ref[...] = tall[4 * width : 5 * width].T
+
+
+def finish(t, a, b, width):
+    rows, w = a.own[0].shape
+    scr = pltpu.VMEM((2 * rows, w), F32)
+    outs = [shaped(s, F32) for s in ((width, w), (w, width), (3 * width, HD), (HD, width), (HD, width))]
+    return call(
+        partial(finish_kernel, masks=(a.join, b.join)), "finish", (), t,
+        [(x, VMEM) for x in (*a.own, *a.other, *b.own, *b.other)], [(o, VMEM) for o in outs],
+        [scr, scr, pltpu.VMEM((5 * width, HD), F32)], vmem=24)
+
+
+def finish_feature_kernel(t_ref, d_ref, own, other, qkv_ref, sums_ref, scr, *, mask):
+    joined(d_ref, own, other, mask, scr)
+    rows = qkv_ref.shape[0]
+    qkv_ref[...] = scr[0:rows]
+    tall = sums_ref.shape[0]
+    for j in range(4):
+        sums_ref[:, j * HD : (j + 1) * HD] = scr[rows + j * tall : rows + (j + 1) * tall]
+
+
+def finish_feature(t, chain, width, sums):
+    rows, w = chain.own[0].shape
+    return call(
+        partial(finish_feature_kernel, mask=chain.join), "finish_feature", (), t,
+        [(x, VMEM) for x in (*chain.own, *chain.other)],
+        [(shaped((3 * width, w), F32), VMEM), (shaped((sums, 4 * HD), F32), VMEM)],
+        [pltpu.VMEM((2 * rows, w), F32)], vmem=16)
 
 
 def shards(
@@ -700,57 +772,71 @@
     fq = jnp.transpose(feat_qkv, (1, 0, 2))
     rq = jnp.transpose(row_qkv, (1, 0, 2))
 
-    packs = gather_groups(pack(t, rq, feat_out, row_out, upb))
+    own = pack(t, rq, feat_out, row_out, upb)
+    own_far = swap(own, "tensor", 2)
     mixed = feature_forward(t, cells, norm_gains, norm_biases, fq, columns)
+    packs = own, swap(own, "tensor", 1), own_far, swap(held(own_far, mixed[0]), "tensor", 1)
     mixed = [mixed[0]] + [swap(mixed[k], "tensor", k) for k in (1, 2, 3)]
-    ups = gather_groups(held(up_weight, mixed[2], mixed[3]))
-    downs = gather_groups(held(down_weight, mixed[2], mixed[3]))
-    fqs = gather_groups(held(fq, downs[2]))
+    up_far, down_far = (swap(held(w, mixed[2], mixed[3]), "tensor", 2) for w in (up_weight, down_weight))
 
     first, n2, row_packed, row_p, o2, second, n3 = row_forward(
         t, splits, mixed, cells, packs, fob, rob, norm_gains, norm_biases, columns)
-    out_a, dn3_a, hg0, hg1, bg0, bg1 = hidden_call(t, n3, grads, ups[:2], packs[:2], downs[:2], columns)
+    ups, downs = [up_weight, swap(up_weight, "tensor", 1)], [down_weight, swap(down_weight, "tensor", 1)]
+    out_a, dn3_a, hg0, hg1, bg0, bg1 = hidden_call(t, n3, grads, ups, packs[:2], downs, columns)
+    ups, downs = ([far, swap(held(far, hg0), "tensor", 1)] for far in (up_far, down_far))
+    fq_far = swap(held(fq, hg0), "tensor", 2)
     out_f, g2, gl2, stats_a, hg2, hg3, bg2, bg3 = hidden_call(
-        t, n3, grads, ups[2:], packs[2:], downs[2:], columns, [out_a, dn3_a, second, dnb, norm_gains])
-
+        t, n3, grads, ups, packs[2:], downs, columns, [out_a, dn3_a, second, dnb, norm_gains])
+    dqkv_r, gl1, s0, s1, s2, s3, stats_b = row_backward(
+        held(t, hg2), g2, first, row_packed, row_p, norm_gains, packs, row_count)
+    pieces = [s0] + [swap(s, "tensor", k) for k, s in ((1, s1), (2, s2), (3, s3))]
+
+    fqs = fq, swap(held(fq, s0), "tensor", 1), fq_far, swap(held(fq_far, s0), "tensor", 1)
     r1, r3 = swap(hg1, "tensor", 1), swap(hg3, "tensor", 1)
-    up_chain = Chain((hg0, hg2), (r1, r3), [masks[0], "x"] + masks[1:], rows=(0, width))
-    down_chain = Chain((hg0, hg2), (r1, r3), masks[1:] + ["x", masks[0]], rows=(width, width))
-    sent = merge(t, [up_chain, down_chain])
-
-    dqkv_r, gl1, s0, s1, s2, s3, stats_b = row_backward(
-        held(t, *sent), g2, first, row_packed, row_p, norm_gains, packs, row_count)
-    pieces = [s0] + [swap(s, "tensor", k) for k, s in ((1, s1), (2, s2), (3, s3))]
-
     row_keep, row_send = row_weights(t, n2, dqkv_r, gl2, o2, gl1, mixed)
-    row_chain = Chain((row_keep,), (swap(row_send, "tensor", 1),), [masks[0], "x"] + masks[1:])
-    sent = merge(held(t, row_send), [up_chain, down_chain])
-    sent = merge(held(t, *sent), [row_chain])
+    row_got = swap(row_send, "tensor", 1)
     n1, feat_packed, feat_p = feature_again(
-        held(t, *sent), cells, norm_gains, norm_biases, fqs, columns, share)
+        held(t, row_send), cells, norm_gains, norm_biases, fqs, columns, share)
+    near, far = masks[:2], masks[2:]
+    half = row_keep.shape[1] // 2
+
+    def parts(first, at):
+        return [((0,), first, width), ((1,), first, width), ((0, 1), at, half)]
+
+    partials = (hg0, hg2, row_keep), (r1, r3, row_got)
+    chain_a = Chain(*partials, parts(0, 0), [near[0], near[1], "x"] + far)
+    chain_b = Chain(*partials, parts(width, half), [near[1], near[0], "x"] + far)
+    sent = merge(held(t, feat_p), [chain_a, chain_b])
     out_pieces = gather_groups(held(out_f.reshape(columns, row_count, width), pieces[2], pieces[3]))
 
-    g1, dqkv_f, feat_keep, feat_send = feature_backward(t, pieces, packs, feat_packed, feat_p, n1)
-    sent = merge(held(t, dqkv_f), [up_chain, down_chain])
-    feat_chain = Chain((feat_keep,), (swap(feat_send, "tensor", 1),), ["x"] + masks)
-    g0, sums = feature_input(
-        held(t, *sent), cells, g1, dqkv_f, norm_gains, fqs, (stats_a, stats_b, bg0, bg1, bg2, bg3), share)
-    small_chain = Chain((sums,), (swap(sums, "tensor", 1),), ["x"] + masks, low=F32)
-
-    chains = [feat_chain, small_chain, row_chain, up_chain, down_chain]
-    sent = merge(held(t, sums), chains)
-    g0s = gather_groups(held(g0, feat_chain.other[0]))
-    output = columns_home(held(t, *sent), out_pieces, feature_count)
-    sent = merge(held(t, output), [feat_chain, small_chain, up_chain, down_chain])
+    g1, dqkv_f, feat_keep, feat_send = feature_backward(held(t, *sent), pieces, packs, feat_packed, feat_p, n1)
+    g0, sums = feature_input(t, cells, g1, dqkv_f, norm_gains, fqs, (stats_a, stats_b, bg0, bg1, bg2, bg3), share)
+    chain_f = Chain(
+        (feat_keep, sums), (swap(feat_send, "tensor", 1), swap(sums, "tensor", 1)),
+        [((0, 1), 0, 3 * width), ((0, 1), 0, sums.shape[0])], ["x"] + masks)
+
+    sent = merge(held(t, sums), [chain_f])
+    g0s = gather_groups(held(g0, *sent))
+    step = 0
+    grads_ab = None
     while True:
-        chains = [c for c in chains if c.result is None]
-        if not chains:
+        if not chain_a.ready:
+            sent = merge(held(t, *sent), [chain_a, chain_b])
+        elif grads_ab is None:
+            grads_ab = sent = finish(held(t, *sent), chain_a, chain_b, width)
+        if step == 1:
+            output = columns_home(held(t, *sent), out_pieces, feature_count)
+            sent = (*sent, output)
+        if step == 4:
+            input_grad = rows_home(held(t, *sent), g0s, feature_count, row_count)
+            sent = (*sent, input_grad)
+        if not chain_f.ready:
+            sent = merge(held(t, *sent), [chain_f])
+        elif grads_ab is not None:
             break
-        sent = merge(held(t, *sent), chains)
-    input_grad = rows_home(t, g0s, feature_count, row_count)
-
-    up_grad, down_grad = up_chain.result, down_chain.result.T
-    row_grad, feat_grad, small = row_chain.result, feat_chain.result, small_chain.result
+        step += 1
+    feat_grad, small = finish_feature(held(t, *sent), chain_f, width, sums.shape[0] // 4)
+    up_grad, down_grad, row_grad, row_out_grad, feat_out_grad = grads_ab
 
     def qkv_shape(grad):
         return jnp.transpose(grad.reshape(3, width, HD), (1, 0, 2))
@@ -760,10 +846,10 @@
         home(output),
         home(input_grad),
         qkv_shape(feat_grad),
-        row_grad[4 * width :].T,
+        feat_out_grad,
         small[8],
-        qkv_shape(row_grad[: 3 * width]),
-        row_grad[3 * width : 4 * width].T,
+        qkv_shape(row_grad),
+        row_out_grad,
         small[1],
         up_grad,
         lax.dynamic_index_in_dim(small, 16 + t[0][0], 0, keepdims=False),

time: 273 us -> 228 us (0.84)
  waiting for transfers between devices: 123 us -> 97.8 us
  starting transfers between devices: 53.6 us -> 36.9 us
  local copies, waits for them, and re-layouts: 13.8 us -> 8.13 us
  Pallas kernels: 76.1 us -> 79 us
    ppermute x57 -> x47, waiting for transfers between devices: 123 us -> 97.8 us  [swap(): return lax.ppermute(values, axis, [(i, i ^ mask) for i in range(count)])]
    ppermute x57 -> x47, starting transfers between devices: 53.6 us -> 36.9 us  [swap(): return lax.ppermute(values, axis, [(i, i ^ mask) for i in range(count)])]
    unnamed x39 -> x38, local copies, waits for them, and re-layouts: 10.5 us -> 6.21 us
    pallas_call x23 -> x26, Pallas kernels: 76.1 us -> 79 us  [call(): pl.pallas_call(kernel, grid_spec=spec, out_shape=[a for a, _ in outs], co...]
  transfers between devices with their start and end apart: 57 -> 47, of which waited for: 23 -> 23; matrix products, arithmetic and copies ran while one was open for 2% -> 0% of each run, Pallas kernels for 19% -> 21%
where the time goes in v3:
time: 228 us; the launch traced here: 225 us
  waiting for transfers between devices  97.8 us (43%)
  Pallas kernels  79 us (35%)
  starting transfers between devices  36.9 us (16%)
  local copies, waits for them, and re-layouts  8.13 us (4%)
    ppermute x47, waiting for transfers between devices, swap(): return lax.ppermute(values, axis, [(i, i ^ mask) for i in range(count)])  97.8 us
    pallas_call x26, Pallas kernels, call(): pl.pallas_call(kernel, grid_spec=spec, out_shape=[a for a, _ in outs], co...  79 us
    ppermute x47, starting transfers between devices, swap(): return lax.ppermute(values, axis, [(i, i ^ mask) for i in range(count)])  36.9 us
    unnamed x38, local copies, waits for them, and re-layouts  6.21 us
  transfers between devices with their start and end apart: 47, of which 23 were waited for; matrix products, arithmetic and copies ran while one was open for 0% of the time, Pallas kernels for 21%

profile of v3, /device:TPU:0, one launch (start us, length us, event | category | flops | bytes accessed | tf_op | source)
XLA Modules:
  0.0 224.6 jit_solution(2220742363851082557)
XLA Ops:
  0.7 1.3 reshape.63.ub_ref
  2.0 2.0 pack.1.f0.r0.w0.b0
  4.0 2.9 %collective-permute-start.4 = (bf16[2576,128]{1,0:T(8,128)(2,1)}, bf16[2576,128]{1,0:T(8,128)(2,1)S(1)}, u32[]{:S(2)}, u32[]{:S(2)}) collective-permute-start(bf16[2576,128]{1,0:T(8,128)(2,1)} %pack.1.f0.r0.w0.b0), channel_id=1, source_target_pairs={{0,2},{1,3},{2,0},{3,1},{4,6},{5,7},{6,4},{7,5},{8,10},{9,11},{10,... | collective-permute-start | bytes 1978376 | tf_op jit(solution)/shard_map/ppermute | solution.py:565
  6.9 1.8 copy-done
  10.1 11.9 %feature_forward.1 = (bf16[2,384,128]{2,1,0:T(8,128)(2,1)S(1)}, bf16[2,384,128]{2,1,0:T(8,128)(2,1)S(1)}, bf16[2,384,128]{2,1,0:T(8,128)(2,1)S(1)}, bf16[2,384,128]{2,1,0:T(8,128)(2,1)S(1)}) custom-call(s32[1]{0:T(128)} %bitcast.t_ref, s32[1]{0:T(128)} %bitcast.1.d_ref, bf16[89,32,512]{2,1,0:T(8,128)(2,1)S(1)} %bitcast.27, bf16[3,512]{1,0:T(4,128)(2,1)S(1)} %copy-done.8, ...), custom_call_target="tpu_custom_call" | custom-call | flops 1 | bytes 1 | tf_op jit(solution)/shard_map/feature_forward/pallas_call | solution.py:116
  22.1 1.9 collective-permute-start.2
  24.5 5.3 %collective-permute-done.1.m2 = bf16[2,384,128]{2,1,0:T(8,128)(2,1)S(1)} collective-permute-done((bf16[2,384,128]{2,1,0:T(8,128)(2,1)S(1)}, bf16[2,384,128]{2,1,0:T(8,128)(2,1)S(1)}, u32[]{:S(2)}, u32[]{:S(2)}) %collective-permute-start.1) | collective-permute-done | bytes 196640 | tf_op jit(solution)/shard_map/ppermute | solution.py:565
  29.8 3.5 %collective-permute-done.2.m3 = bf16[2,384,128]{2,1,0:T(8,128)(2,1)S(1)} collective-permute-done((bf16[2,384,128]{2,1,0:T(8,128)(2,1)S(1)}, bf16[2,384,128]{2,1,0:T(8,128)(2,1)S(1)}, u32[]{:S(2)}, u32[]{:S(2)}) %collective-permute-start.2) | collective-permute-done | bytes 196640 | tf_op jit(solution)/shard_map/ppermute | solution.py:565
  33.9 1.6 collective-permute-start.6
  37.3 9.1 %row_forward.1 = (f32[768,512]{1,0:T(8,128)S(1)}, bf16[768,512]{1,0:T(8,128)(2,1)S(1)}, bf16[768,1536]{1,0:T(8,128)(2,1)S(1)}, bf16[4,6,128,128]{3,2,1,0:T(8,128...) custom-call(s32[1]{0:T(128)} %bitcast.t_ref, s32[1]{0:T(128)} %bitcast.1.d_ref, ...), custom_call_target="tpu_custom_call" | custom-call | flops 1 | bytes 1 | tf_op jit(solution)/shard_map/row_forward/pallas_call | solution.py:116
  46.5 8.6 %hidden_first.1 = (f32[768,512]{1,0:T(8,128)S(1)}, f32[768,512]{1,0:T(8,128)S(1)}, bf16[1024,512]{1,0:T(8,128)(2,1)S(1)}, bf16[1024,512]{1,0:T(8,128)(2,1)S(1)},...) custom-call(s32[1]{0:T(128)} %bitcast.t_ref, s32[1]{0:T(128)} %bitcast.1.d_ref, ...), custom_call_target="tpu_custom_call" | custom-call | flops 1 | bytes 1 | tf_op jit(solution)/shard_map/hidden_first/pallas_call | solution.py:116
  56.1 3.0 %collective-permute-done.6.up0 = bf16[512,512]{1,0:T(8,128)(2,1)S(1)} collective-permute-done((bf16[512,512]{1,0:T(8,128)(2,1)}, bf16[512,512]{1,0:T(8,128)(2,1)S(1)}, u32[]{:S(2)}, u32[]{:S(2)}) %collective-permute-start.6) | collective-permute-done | bytes 524320 | tf_op jit(solution)/shard_map/ppermute | solution.py:565
  59.1 1.9 collective-permute-done.9.up1
  61.0 7.8 %hidden_second.1 = (bf16[768,512]{1,0:T(8,128)(2,1)S(1)}, f32[768,512]{1,0:T(8,128)S(1)}, bf16[768,512]{1,0:T(8,128)(2,1)S(1)}, f32[8,512]{1,0:T(8,128)S(1)}, bf...) custom-call(s32[1]{0:T(128)} %bitcast.t_ref, ...), custom_call_target="tpu_custom_call" | custom-call | flops 1 | bytes 1 | tf_op jit(solution)/shard_map/hidden_second/pallas_call | solution.py:116
  68.9 8.8 %row_backward.1 = (bf16[768,1536]{1,0:T(8,128)(2,1)S(1)}, bf16[768,512]{1,0:T(8,128)(2,1)S(1)}, bf16[192,512]{1,0:T(8,128)(2,1)S(1)}, bf16[192,512]{1,0:T(8,128)...) custom-call(s32[1]{0:T(128)} %bitcast.t_ref, s32[1]{0:T(128)} %bitcast.1.d_ref, ...), custom_call_target="tpu_custom_call" | custom-call | flops 1 | bytes 1 | tf_op jit(solution)/shard_map/row_backward/pallas_call | solution.py:116
  77.7 2.2 row_weights.1
  81.1 10.9 %collective-permute-done.13.w2 = bf16[3,512,128]{2,1,0:T(8,128)(2,1)S(1)} collective-permute-done((bf16[3,512,128]{2,1,0:T(8,128)(2,1)S(1)}, bf16[3,512,128]{2,1,0:T(8,128)(2,1)S(1)}, u32[]{:S(2)}, u32[]{:S(2)}) %collective-permute-start.13) | collective-permute-done | bytes 393248 | tf_op jit(solution)/shard_map/ppermute | solution.py:565
  95.8 4.1 %feature_again.1 = (bf16[768,512]{1,0:T(8,128)(2,1)S(1)}, bf16[8,96,1536]{2,1,0:T(8,128)(2,1)S(1)}, bf16[8,4,96,96]{3,2,1,0:T(8,128)(2,1)S(1)}) custom-call(s32[1]{0:T(128)} %bitcast.t_ref, s32[1]{0:T(128)} %bitcast.1.d_ref, bf16[89,32,512]{2,1,0:T(8,128)(2,1)S(1)} %bitcast.29, bf16[3,512]{1,0:T(4,128)(2,1)S(1)} %copy-done.9, bf16[3,512]{1,0:T(4,128)(2,1)S(1)} %copy-done.11, ...), custom_call_target="tpu_custom_call" | custom-call | flops 1 | bytes 1 | tf_op jit(solution)/shard_map/feature_again/pallas_call | solution.py:116
  99.9 1.7 merge.12
  102.5 2.2 collective-permute-done.20.r3
  104.7 10.9 %feature_backward.1 = (f32[768,512]{1,0:T(8,128)S(1)}, bf16[768,1536]{1,0:T(8,128)(2,1)S(1)}, bf16[2,1536,128]{2,1,0:T(8,128)(2,1)S(1)}, bf16[2,1536,128]{2,1,0:T(8,128)(2,1)S(1)}) custom-call(s32[1]{0:T(128)} %bitcast.t_ref, s32[1]{0:T(128)} %bitcast.1.d_ref, bf16[192,512]{1,0:T(8,128)(2,1)S(1)} %get-tuple-element.144.r0, ...), custom_call_target="tpu_custom_call" | custom-call | flops 1 | bytes 1 | tf_op jit(solution)/shard_map/feature_backward/pallas_call | solution.py:116
  116.3 1.5 collective-permute-start.23
  118.4 1.6 collective-permute-start.24
  119.9 2.4 %feature_input.1 = (bf16[720,512]{1,0:T(8,128)(2,1)S(1)}, f32[128,128]{1,0:T(8,128)S(1)}) custom-call(s32[1]{0:T(128)} %bitcast.t_ref, s32[1]{0:T(128)} %bitcast.1.d_ref, bf16[89,32,512]{2,1,0:T(8,128)(2,1)S(1)} %bitcast.30, f32[768,512]{1,0:T(8,128)S(1)} %get-tuple-element.163.g1_ref, bf16[768,1536]{1,0:T(8,128)(2,1)S(1)} %get-tuple-element.164.dqkv_ref, ...), custom_call_target="tpu_custom_call" | custom-call | flops 1 | bytes 1 | tf_op jit(solution)/shard_map/feature_input/pallas_call | solution.py:116
  123.8 1.5 collective-permute-start.25
  125.3 12.9 %collective-permute-done.29.p2 = bf16[24,32,512]{2,1,0:T(8,128)(2,1)S(1)} collective-permute-done((bf16[24,32,512]{2,1,0:T(8,128)(2,1)S(1)}, bf16[24,32,512]{2,1,0:T(8,128)(2,1)S(1)}, u32[]{:S(2)}, u32[]{:S(2)}) %collective-permute-start.29) | collective-permute-done | bytes 786464 | tf_op jit(solution)/shard_map/ppermute | solution.py:565
  139.2 1.6 collective-permute-start.26
  140.8 6.5 %collective-permute-done.25.refs_1_ = bf16[1664,128]{1,0:T(8,128)(2,1)S(1)} collective-permute-done((bf16[1664,128]{1,0:T(8,128)(2,1)S(1)}, bf16[1664,128]{1,0:T(8,128)(2,1)S(1)}, u32[]{:S(2)}, u32[]{:S(2)}) %collective-permute-start.25) | collective-permute-done | bytes 426016 | tf_op jit(solution)/shard_map/ppermute | solution.py:565
  148.0 3.2 %collective-permute-done.26.refs_1_ = bf16[2,208,512]{2,1,0:T(8,128)(2,1)S(1)} collective-permute-done((bf16[2,208,512]{2,1,0:T(8,128)(2,1)S(1)}, bf16[2,208,512]{2,1,0:T(8,128)(2,1)S(1)}, u32[]{:S(2)}, u32[]{:S(2)}) %collective-permute-start.26) | collective-permute-done | bytes 426016 | tf_op jit(solution)/shard_map/ppermute | solution.py:565
  151.6 7.5 %collective-permute-done.27.refs_3_ = bf16[2,208,512]{2,1,0:T(8,128)(2,1)S(1)} collective-permute-done((bf16[2,208,512]{2,1,0:T(8,128)(2,1)S(1)}, bf16[2,208,512]{2,1,0:T(8,128)(2,1)S(1)}, u32[]{:S(2)}, u32[]{:S(2)}) %collective-permute-start.27) | collective-permute-done | bytes 426016 | tf_op jit(solution)/shard_map/ppermute | solution.py:565
  159.9 1.4 collective-permute-start.33
  161.4 1.8 collective-permute-done.41.p2
  163.1 2.1 columns_home.1
  165.3 2.4 %collective-permute-done.32.refs_1_ = bf16[208,512]{1,0:T(8,128)(2,1)S(1)} collective-permute-done((bf16[208,512]{1,0:T(8,128)(2,1)S(1)}, bf16[208,512]{1,0:T(8,128)(2,1)S(1)}, u32[]{:S(2)}, u32[]{:S(2)}) %collective-permute-start.32) | collective-permute-done | bytes 213024 | tf_op jit(solution)/shard_map/ppermute | solution.py:565
  167.7 3.4 %collective-permute-done.33.refs_3_ = bf16[208,512]{1,0:T(8,128)(2,1)S(1)} collective-permute-done((bf16[208,512]{1,0:T(8,128)(2,1)S(1)}, bf16[208,512]{1,0:T(8,128)(2,1)S(1)}, u32[]{:S(2)}, u32[]{:S(2)}) %collective-permute-start.33) | collective-permute-done | bytes 213024 | tf_op jit(solution)/shard_map/ppermute | solution.py:565
  171.2 2.7 %collective-permute-start.35 = (bf16[208,512]{1,0:T(8,128)(2,1)S(1)}, bf16[208,512]{1,0:T(8,128)(2,1)S(1)}, u32[]{:S(2)}, u32[]{:S(2)}) collective-permute-start(bf16[208,512]{1,0:T(8,128)(2,1)S(1)} %get-tuple-element.197.refs_0_), channel_id=1, source_target_pairs={{0,16},{4,20},{8,24},{12,28},{16,0},{20,4},{24,8},{28,12},{1,17},{... | collective-permute-start | bytes 638984 | tf_op jit(solution)/shard_map/ppermute | solution.py:565
  174.2 1.6 collective-permute-start.34
  175.7 8.6 %collective-permute-done.34.refs_1_ = bf16[416,128]{1,0:T(8,128)(2,1)S(1)} collective-permute-done((bf16[416,128]{1,0:T(8,128)(2,1)S(1)}, bf16[416,128]{1,0:T(8,128)(2,1)S(1)}, u32[]{:S(2)}, u32[]{:S(2)}) %collective-permute-start.34) | collective-permute-done | bytes 106528 | tf_op jit(solution)/shard_map/ppermute | solution.py:565
  184.4 4.2 %collective-permute-done.35.refs_1_ = bf16[208,512]{1,0:T(8,128)(2,1)S(1)} collective-permute-done((bf16[208,512]{1,0:T(8,128)(2,1)S(1)}, bf16[208,512]{1,0:T(8,128)(2,1)S(1)}, u32[]{:S(2)}, u32[]{:S(2)}) %collective-permute-start.35) | collective-permute-done | bytes 213024 | tf_op jit(solution)/shard_map/ppermute | solution.py:565
  188.5 3.4 %collective-permute-done.36.refs_3_ = bf16[208,512]{1,0:T(8,128)(2,1)S(1)} collective-permute-done((bf16[208,512]{1,0:T(8,128)(2,1)S(1)}, bf16[208,512]{1,0:T(8,128)(2,1)S(1)}, u32[]{:S(2)}, u32[]{:S(2)}) %collective-permute-start.36) | collective-permute-done | bytes 213024 | tf_op jit(solution)/shard_map/ppermute | solution.py:565
  193.3 3.4 %collective-permute-start.37 = (bf16[416,128]{1,0:T(8,128)(2,1)S(1)}, bf16[416,128]{1,0:T(8,128)(2,1)S(1)}, u32[]{:S(2)}, u32[]{:S(2)}) collective-permute-start(bf16[416,128]{1,0:T(8,128)(2,1)S(1)} %merge.19.refs_0_), channel_id=1, source_target_pairs={{0,16},{4,20},{8,24},{12,28},{16,0},{20,4},{24,8},{28,12},{1,17},{... | collective-permute-start | bytes 319496 | tf_op jit(solution)/shard_map/ppermute | solution.py:565
  196.7 3.1 %collective-permute-done.37.refs_1_ = bf16[416,128]{1,0:T(8,128)(2,1)S(1)} collective-permute-done((bf16[416,128]{1,0:T(8,128)(2,1)S(1)}, bf16[416,128]{1,0:T(8,128)(2,1)S(1)}, u32[]{:S(2)}, u32[]{:S(2)}) %collective-permute-start.37) | collective-permute-done | bytes 106528 | tf_op jit(solution)/shard_map/ppermute | solution.py:565
  201.2 3.4 %collective-permute-start.45 = (bf16[416,512]{1,0:T(8,128)(2,1)S(1)}, bf16[416,512]{1,0:T(8,128)(2,1)S(1)}, u32[]{:S(2)}, u32[]{:S(2)}) collective-permute-start(bf16[416,512]{1,0:T(8,128)(2,1)S(1)} %get-tuple-element.206.b0), channel_id=1, source_target_pairs={{0,8},{4,12},{8,0},{12,4},{16,24},{20,28},{24,16},{28,20},{1,9},{5... | collective-permute-start | bytes 1277960 | tf_op jit(solution)/shard_map/ppermute | solution.py:565
  204.6 2.9 %rows_home.1 = bf16[89,32,512]{2,1,0:T(8,128)(2,1)} custom-call(s32[1]{0:T(128)} %bitcast.t_ref, s32[1]{0:T(128)} %bitcast.1.d_ref, bf16[720,512]{1,0:T(8,128)(2,1)S(1)} %get-tuple-element.209.p0, bf16[720,512]{1,0:T(8,128)(2,1)S(1)} %collective-permute-done.40.p1, bf16[720,512]{1,0:T(8,128)(2,1)S(1)} %collective-permute-done.41.p2, ...), custom_call_target="tpu_custom_call" | custom-call | flops 1 | bytes 1 | tf_op jit(solution)/shard_map/rows_home/pallas_call | solution.py:116
  207.5 8.6 %collective-permute-done.43.refs_1_ = bf16[416,128]{1,0:T(8,128)(2,1)S(1)} collective-permute-done((bf16[416,128]{1,0:T(8,128)(2,1)S(1)}, bf16[416,128]{1,0:T(8,128)(2,1)S(1)}, u32[]{:S(2)}, u32[]{:S(2)}) %collective-permute-start.43) | collective-permute-done | bytes 106528 | tf_op jit(solution)/shard_map/ppermute | solution.py:565
  216.1 1.6 collective-permute-start.46
  217.7 2.3 %finish.1 = (f32[512,512]{1,0:T(8,128)}, f32[512,512]{1,0:T(8,128)}, f32[1536,128]{1,0:T(8,128)}, f32[128,512]{1,0:T(8,128)}, f32[128,512]{1,0:T(8,128)}) custom-call(s32[1]{0:T(128)} %bitcast.t_ref, s32[1]{0:T(128)} %bitcast.1.d_ref, bf16[416,512]{1,0:T(8,128)(2,1)S(1)} %get-tuple-element.205.a0, bf16[416,512]{1,0:T(8,128)(2,1)S(1)} %collective-permute-done.44.a1, ...), custom_call_target="tpu_custom_call" | custom-call | flops 1 | bytes 1 | tf_op jit(solution)/shard_map/finish/pallas_call | solution.py:116
  220.0 2.0 collective-permute-done.46.other
  (116 shorter events, 21.8 us)
Async XLA Ops:
  4.0 20.3 %collective-permute-start.4 = (bf16[2576,128]{1,0:T(8,128)(2,1)}, bf16[2576,128]{1,0:T(8,128)(2,1)S(1)}, u32[]{:S(2)}, u32[]{:S(2)}) collective-permute-start(bf16[2576,128]{1,0:T(8,128)(2,1)} %pack.1.f0.r0.w0.b0), channel_id=1, source_target_pairs={{0,2},{1,3},{2,0},{3,1},{4,6},{5,7},{6,4},{7,5},{8,10},{9,11},{10,... | collective-permute-start | bytes 1978376 | tf_op jit(solution)/shard_map/ppermute | solution.py:565
  6.9 27.0 %collective-permute-start.3 = (bf16[2576,128]{1,0:T(8,128)(2,1)}, bf16[2576,128]{1,0:T(8,128)(2,1)S(1)}, u32[]{:S(2)}, u32[]{:S(2)}) collective-permute-start(bf16[2576,128]{1,0:T(8,128)(2,1)} %pack.1.f0.r0.w0.b0), channel_id=1, source_target_pairs={{0,1},{1,0},{2,3},{3,2},{4,5},{5,4},{6,7},{7,6},{8,9},{9,8},{10,11... | collective-permute-start | bytes 1978376 | tf_op jit(solution)/shard_map/ppermute | solution.py:565
  10.1 26.1 %copy-start.11 = (bf16[3,512]{1,0:T(4,128)(2,1)S(1)}, bf16[3,512]{1,0:T(4,128)(2,1)}, u32[]{:S(2)}) copy-start(bf16[3,512]{1,0:T(4,128)(2,1)} %shifts_ref.5) | copy-start | bytes 9220
  22.1 7.8 %collective-permute-start.1 = (bf16[2,384,128]{2,1,0:T(8,128)(2,1)S(1)}, bf16[2,384,128]{2,1,0:T(8,128)(2,1)S(1)}, u32[]{:S(2)}, u32[]{:S(2)}) collective-permute-start(bf16[2,384,128]{2,1,0:T(8,128)(2,1)S(1)} %get-tuple-element.119), channel_id=1, source_target_pairs={{0,2},{1,3},{2,0},{3,1},{4,6},{5,7},{6,4},{7,5},{8,10},{9,11},{10,... | collective-permute-start | bytes 589832 | tf_op jit(solution)/shard_map/ppermute | solution.py:565
  22.1 11.1 %collective-permute-start.2 = (bf16[2,384,128]{2,1,0:T(8,128)(2,1)S(1)}, bf16[2,384,128]{2,1,0:T(8,128)(2,1)S(1)}, u32[]{:S(2)}, u32[]{:S(2)}) collective-permute-start(bf16[2,384,128]{2,1,0:T(8,128)(2,1)S(1)} %get-tuple-element.120), channel_id=1, source_target_pairs={{0,3},{1,2},{2,1},{3,0},{4,7},{5,6},{6,5},{7,4},{8,11},{9,10},{10,... | collective-permute-start | bytes 589832 | tf_op jit(solution)/shard_map/ppermute | solution.py:565
  24.0 9.5 %collective-permute-start = (bf16[2,384,128]{2,1,0:T(8,128)(2,1)S(1)}, bf16[2,384,128]{2,1,0:T(8,128)(2,1)S(1)}, u32[]{:S(2)}, u32[]{:S(2)}) collective-permute-start(bf16[2,384,128]{2,1,0:T(8,128)(2,1)S(1)} %get-tuple-element.118), channel_id=1, source_target_pairs={{0,1},{1,0},{2,3},{3,2},{4,5},{5,4},{6,7},{7,6},{8,9},{9,8},{10,11... | collective-permute-start | bytes 589832 | tf_op jit(solution)/shard_map/ppermute | solution.py:565
  24.3 11.9 %collective-permute-start.5 = (bf16[2576,128]{1,0:T(8,128)(2,1)S(1)}, bf16[2576,128]{1,0:T(8,128)(2,1)S(1)}, u32[]{:S(2)}, u32[]{:S(2)}) collective-permute-start(bf16[2576,128]{1,0:T(8,128)(2,1)S(1)} %collective-permute-done.4.f2.r2.w2.b0), channel_id=1, source_target_pairs={{0,1},{1,0},{2,3},{3,2},{4,5},{5,4},{6,7},{7,6},{8,9},{9,8},{10,11... | collective-permute-start | bytes 1978376 | tf_op jit(solution)/shard_map/ppermute | solution.py:565
  29.8 16.6 %collective-permute-start.7 = (bf16[512,512]{1,0:T(8,128)(2,1)}, bf16[512,512]{1,0:T(8,128)(2,1)S(1)}, u32[]{:S(2)}, u32[]{:S(2)}) collective-permute-start(bf16[512,512]{1,0:T(8,128)(2,1)} %up0.1), channel_id=1, source_target_pairs={{0,1},{1,0},{2,3},{3,2},{4,5},{5,4},{6,7},{7,6},{8,9},{9,8},{10,11... | collective-permute-start | bytes 1572872 | tf_op jit(solution)/shard_map/ppermute | solution.py:565
  33.3 13.2 %collective-permute-start.8 = (bf16[512,512]{1,0:T(8,128)(2,1)}, bf16[512,512]{1,0:T(8,128)(2,1)S(1)}, u32[]{:S(2)}, u32[]{:S(2)}) collective-permute-start(bf16[512,512]{1,0:T(8,128)(2,1)} %down0.1), channel_id=1, source_target_pairs={{0,1},{1,0},{2,3},{3,2},{4,5},{5,4},{6,7},{7,6},{8,9},{9,8},{10,11... | collective-permute-start | bytes 1572872 | tf_op jit(solution)/shard_map/ppermute | solution.py:565
  33.5 22.6 %collective-permute-start.10 = (bf16[512,512]{1,0:T(8,128)(2,1)}, bf16[512,512]{1,0:T(8,128)(2,1)S(1)}, u32[]{:S(2)}, u32[]{:S(2)}) collective-permute-start(bf16[512,512]{1,0:T(8,128)(2,1)} %down0.1), channel_id=1, source_target_pairs={{0,2},{1,3},{2,0},{3,1},{4,6},{5,7},{6,4},{7,5},{8,10},{9,11},{10,... | collective-permute-start | bytes 1572872 | tf_op jit(solution)/shard_map/ppermute | solution.py:565
  33.9 25.2 %collective-permute-start.6 = (bf16[512,512]{1,0:T(8,128)(2,1)}, bf16[512,512]{1,0:T(8,128)(2,1)S(1)}, u32[]{:S(2)}, u32[]{:S(2)}) collective-permute-start(bf16[512,512]{1,0:T(8,128)(2,1)} %up0.1), channel_id=1, source_target_pairs={{0,2},{1,3},{2,0},{3,1},{4,6},{5,7},{6,4},{7,5},{8,10},{9,11},{10,... | collective-permute-start | bytes 1572872 | tf_op jit(solution)/shard_map/ppermute | solution.py:565
  56.1 3.0 %collective-permute-start.11 = (bf16[512,512]{1,0:T(8,128)(2,1)S(1)}, bf16[512,512]{1,0:T(8,128)(2,1)S(1)}, u32[]{:S(2)}, u32[]{:S(2)}) collective-permute-start(bf16[512,512]{1,0:T(8,128)(2,1)S(1)} %collective-permute-done.10.down0), channel_id=1, source_target_pairs={{0,1},{1,0},{2,3},{3,2},{4,5},{5,4},{6,7},{7,6},{8,9},{9,8},{10,11... | collective-permute-start | bytes 1572872 | tf_op jit(solution)/shard_map/ppermute | solution.py:565
  59.1 1.9 collective-permute-start.9
  80.0 20.0 %collective-permute-start.17 = (bf16[2,640,512]{2,1,0:T(8,128)(2,1)S(1)}, bf16[2,640,512]{2,1,0:T(8,128)(2,1)S(1)}, u32[]{:S(2)}, u32[]{:S(2)}) collective-permute-start(bf16[2,640,512]{2,1,0:T(8,128)(2,1)S(1)} %get-tuple-element.142), channel_id=1, source_target_pairs={{0,1},{1,0},{2,3},{3,2},{4,5},{5,4},{6,7},{7,6},{8,9},{9,8},{10,11... | collective-permute-start | bytes 3932168 | tf_op jit(solution)/shard_map/ppermute | solution.py:565
  80.2 14.7 %collective-permute-start.15 = (bf16[1024,512]{1,0:T(8,128)(2,1)S(1)}, bf16[1024,512]{1,0:T(8,128)(2,1)S(1)}, u32[]{:S(2)}, u32[]{:S(2)}) collective-permute-start(bf16[1024,512]{1,0:T(8,128)(2,1)S(1)} %copy-done.13), channel_id=1, source_target_pairs={{0,1},{1,0},{2,3},{3,2},{4,5},{5,4},{6,7},{7,6},{8,9},{9,8},{10,11... | collective-permute-start | bytes 3145736 | tf_op jit(solution)/shard_map/ppermute | solution.py:565
  80.5 19.4 %collective-permute-start.16 = (bf16[1024,512]{1,0:T(8,128)(2,1)}, bf16[1024,512]{1,0:T(8,128)(2,1)S(1)}, u32[]{:S(2)}, u32[]{:S(2)}) collective-permute-start(bf16[1024,512]{1,0:T(8,128)(2,1)} %get-tuple-element.152), channel_id=1, source_target_pairs={{0,1},{1,0},{2,3},{3,2},{4,5},{5,4},{6,7},{7,6},{8,9},{9,8},{10,11... | collective-permute-start | bytes 3145736 | tf_op jit(solution)/shard_map/ppermute | solution.py:565
  80.7 11.4 %collective-permute-start.13 = (bf16[3,512,128]{2,1,0:T(8,128)(2,1)S(1)}, bf16[3,512,128]{2,1,0:T(8,128)(2,1)S(1)}, u32[]{:S(2)}, u32[]{:S(2)}) collective-permute-start(bf16[3,512,128]{2,1,0:T(8,128)(2,1)S(1)} %bitcast.34), channel_id=1, source_target_pairs={{0,2},{1,3},{2,0},{3,1},{4,6},{5,7},{6,4},{7,5},{8,10},{9,11},{10,... | collective-permute-start | bytes 1179656 | tf_op jit(solution)/shard_map/ppermute | solution.py:565
  92.1 1.7 collective-permute-start.14
  92.1 2.3 %collective-permute-start.12 = (bf16[3,512,128]{2,1,0:T(8,128)(2,1)S(1)}, bf16[3,512,128]{2,1,0:T(8,128)(2,1)S(1)}, u32[]{:S(2)}, u32[]{:S(2)}) collective-permute-start(bf16[3,512,128]{2,1,0:T(8,128)(2,1)S(1)} %bitcast.35), channel_id=1, source_target_pairs={{0,1},{1,0},{2,3},{3,2},{4,5},{5,4},{6,7},{7,6},{8,9},{9,8},{10,11... | collective-permute-start | bytes 1179656 | tf_op jit(solution)/shard_map/ppermute | solution.py:565
  93.8 8.7 %collective-permute-start.18 = (bf16[192,512]{1,0:T(8,128)(2,1)S(1)}, bf16[192,512]{1,0:T(8,128)(2,1)S(1)}, u32[]{:S(2)}, u32[]{:S(2)}) collective-permute-start(bf16[192,512]{1,0:T(8,128)(2,1)S(1)} %get-tuple-element.158), channel_id=1, source_target_pairs={{0,1},{1,0},{2,3},{3,2},{4,5},{5,4},{6,7},{7,6},{8,9},{9,8},{10,11... | collective-permute-start | bytes 589832 | tf_op jit(solution)/shard_map/ppermute | solution.py:565
  94.4 8.2 %collective-permute-start.19 = (bf16[192,512]{1,0:T(8,128)(2,1)S(1)}, bf16[192,512]{1,0:T(8,128)(2,1)S(1)}, u32[]{:S(2)}, u32[]{:S(2)}) collective-permute-start(bf16[192,512]{1,0:T(8,128)(2,1)S(1)} %get-tuple-element.159), channel_id=1, source_target_pairs={{0,2},{1,3},{2,0},{3,1},{4,6},{5,7},{6,4},{7,5},{8,10},{9,11},{10,... | collective-permute-start | bytes 589832 | tf_op jit(solution)/shard_map/ppermute | solution.py:565
  94.8 9.9 %collective-permute-start.20 = (bf16[192,512]{1,0:T(8,128)(2,1)S(1)}, bf16[192,512]{1,0:T(8,128)(2,1)S(1)}, u32[]{:S(2)}, u32[]{:S(2)}) collective-permute-start(bf16[192,512]{1,0:T(8,128)(2,1)S(1)} %get-tuple-element.160), channel_id=1, source_target_pairs={{0,3},{1,2},{2,1},{3,0},{4,7},{5,6},{6,5},{7,4},{8,11},{9,10},{10,... | collective-permute-start | bytes 589832 | tf_op jit(solution)/shard_map/ppermute | solution.py:565
  115.6 8.0 %collective-permute-start.21 = (bf16[2,1536,128]{2,1,0:T(8,128)(2,1)S(1)}, bf16[2,1536,128]{2,1,0:T(8,128)(2,1)S(1)}, u32[]{:S(2)}, u32[]{:S(2)}) collective-permute-start(bf16[2,1536,128]{2,1,0:T(8,128)(2,1)S(1)} %get-tuple-element.174), channel_id=1, source_target_pairs={{0,1},{1,0},{2,3},{3,2},{4,5},{5,4},{6,7},{7,6},{8,9},{9,8},{10,11... | collective-permute-start | bytes 2359304 | tf_op jit(solution)/shard_map/ppermute | solution.py:565
  116.3 21.9 %collective-permute-start.23 = (bf16[2,416,512]{2,1,0:T(8,128)(2,1)}, bf16[2,416,512]{2,1,0:T(8,128)(2,1)S(1)}, u32[]{:S(2)}, u32[]{:S(2)}) collective-permute-start(bf16[2,416,512]{2,1,0:T(8,128)(2,1)} %get-tuple-element.154), channel_id=1, source_target_pairs={{0,4},{4,0},{8,12},{12,8},{16,20},{20,16},{24,28},{28,24},{1,5},{5... | collective-permute-start | bytes 2555912 | tf_op jit(solution)/shard_map/ppermute | solution.py:565
  117.8 20.4 %collective-permute-start.29 = (bf16[24,32,512]{2,1,0:T(8,128)(2,1)S(1)}, bf16[24,32,512]{2,1,0:T(8,128)(2,1)S(1)}, u32[]{:S(2)}, u32[]{:S(2)}) collective-permute-start(bf16[24,32,512]{2,1,0:T(8,128)(2,1)S(1)} %bitcast.38), channel_id=1, source_target_pairs={{0,2},{1,3},{2,0},{3,1},{4,6},{5,7},{6,4},{7,5},{8,10},{9,11},{10,... | collective-permute-start | bytes 2359304 | tf_op jit(solution)/shard_map/ppermute | solution.py:565
  118.4 20.4 %collective-permute-start.24 = (bf16[2,416,512]{2,1,0:T(8,128)(2,1)S(1)}, bf16[2,416,512]{2,1,0:T(8,128)(2,1)S(1)}, u32[]{:S(2)}, u32[]{:S(2)}) collective-permute-start(bf16[2,416,512]{2,1,0:T(8,128)(2,1)S(1)} %copy-done.15), channel_id=1, source_target_pairs={{0,8},{4,12},{8,0},{12,4},{16,24},{20,28},{24,16},{28,20},{1,9},{5... | collective-permute-start | bytes 2555912 | tf_op jit(solution)/shard_map/ppermute | solution.py:565
  122.3 1.3 collective-permute-start.22
  123.8 23.5 %collective-permute-start.25 = (bf16[1664,128]{1,0:T(8,128)(2,1)S(1)}, bf16[1664,128]{1,0:T(8,128)(2,1)S(1)}, u32[]{:S(2)}, u32[]{:S(2)}) collective-permute-start(bf16[1664,128]{1,0:T(8,128)(2,1)S(1)} %get-tuple-element.176), channel_id=1, source_target_pairs={{0,2},{1,3},{2,0},{3,1},{4,6},{5,7},{6,4},{7,5},{8,10},{9,11},{10,... | collective-permute-start | bytes 1277960 | tf_op jit(solution)/shard_map/ppermute | solution.py:565
  125.3 34.6 %collective-permute-start.28 = (bf16[24,32,512]{2,1,0:T(8,128)(2,1)S(1)}, bf16[24,32,512]{2,1,0:T(8,128)(2,1)S(1)}, u32[]{:S(2)}, u32[]{:S(2)}) collective-permute-start(bf16[24,32,512]{2,1,0:T(8,128)(2,1)S(1)} %bitcast.39), channel_id=1, source_target_pairs={{0,1},{1,0},{2,3},{3,2},{4,5},{5,4},{6,7},{7,6},{8,9},{9,8},{10,11... | collective-permute-start | bytes 2359304 | tf_op jit(solution)/shard_map/ppermute | solution.py:565
  138.2 23.2 %collective-permute-start.30 = (bf16[24,32,512]{2,1,0:T(8,128)(2,1)S(1)}, bf16[24,32,512]{2,1,0:T(8,128)(2,1)S(1)}, u32[]{:S(2)}, u32[]{:S(2)}) collective-permute-start(bf16[24,32,512]{2,1,0:T(8,128)(2,1)S(1)} %collective-permute-done.29.p2), channel_id=1, source_target_pairs={{0,1},{1,0},{2,3},{3,2},{4,5},{5,4},{6,7},{7,6},{8,9},{9,8},{10,11... | collective-permute-start | bytes 2359304 | tf_op jit(solution)/shard_map/ppermute | solution.py:565
  138.2 24.9 %collective-permute-start.41 = (bf16[720,512]{1,0:T(8,128)(2,1)S(1)}, bf16[720,512]{1,0:T(8,128)(2,1)S(1)}, u32[]{:S(2)}, u32[]{:S(2)}) collective-permute-start(bf16[720,512]{1,0:T(8,128)(2,1)S(1)} %get-tuple-element.209.p0), channel_id=1, source_target_pairs={{0,2},{1,3},{2,0},{3,1},{4,6},{5,7},{6,4},{7,5},{8,10},{9,11},{10,... | collective-permute-start | bytes 2211848 | tf_op jit(solution)/shard_map/ppermute | solution.py:565
  139.2 12.0 %collective-permute-start.26 = (bf16[2,208,512]{2,1,0:T(8,128)(2,1)S(1)}, bf16[2,208,512]{2,1,0:T(8,128)(2,1)S(1)}, u32[]{:S(2)}, u32[]{:S(2)}) collective-permute-start(bf16[2,208,512]{2,1,0:T(8,128)(2,1)S(1)} %get-tuple-element.179), channel_id=1, source_target_pairs={{0,8},{4,12},{8,0},{12,4},{16,24},{20,28},{24,16},{28,20},{1,9},{5... | collective-permute-start | bytes 1277960 | tf_op jit(solution)/shard_map/ppermute | solution.py:565
  147.3 11.7 %collective-permute-start.27 = (bf16[2,208,512]{2,1,0:T(8,128)(2,1)S(1)}, bf16[2,208,512]{2,1,0:T(8,128)(2,1)S(1)}, u32[]{:S(2)}, u32[]{:S(2)}) collective-permute-start(bf16[2,208,512]{2,1,0:T(8,128)(2,1)S(1)} %get-tuple-element.181), channel_id=1, source_target_pairs={{0,4},{4,0},{8,12},{12,8},{16,20},{20,16},{24,28},{28,24},{1,5},{5... | collective-permute-start | bytes 1277960 | tf_op jit(solution)/shard_map/ppermute | solution.py:565
  151.2 14.0 %collective-permute-start.31 = (bf16[832,128]{1,0:T(8,128)(2,1)S(1)}, bf16[832,128]{1,0:T(8,128)(2,1)S(1)}, u32[]{:S(2)}, u32[]{:S(2)}) collective-permute-start(bf16[832,128]{1,0:T(8,128)(2,1)S(1)} %get-tuple-element.184), channel_id=1, source_target_pairs={{0,4},{4,0},{8,12},{12,8},{16,20},{20,16},{24,28},{28,24},{1,5},{5... | collective-permute-start | bytes 638984 | tf_op jit(solution)/shard_map/ppermute | solution.py:565
  159.3 8.4 %collective-permute-start.32 = (bf16[208,512]{1,0:T(8,128)(2,1)S(1)}, bf16[208,512]{1,0:T(8,128)(2,1)S(1)}, u32[]{:S(2)}, u32[]{:S(2)}) collective-permute-start(bf16[208,512]{1,0:T(8,128)(2,1)S(1)} %get-tuple-element.187), channel_id=1, source_target_pairs={{0,2},{1,3},{2,0},{3,1},{4,6},{5,7},{6,4},{7,5},{8,10},{9,11},{10,... | collective-permute-start | bytes 638984 | tf_op jit(solution)/shard_map/ppermute | solution.py:565
  159.9 11.2 %collective-permute-start.33 = (bf16[208,512]{1,0:T(8,128)(2,1)S(1)}, bf16[208,512]{1,0:T(8,128)(2,1)S(1)}, u32[]{:S(2)}, u32[]{:S(2)}) collective-permute-start(bf16[208,512]{1,0:T(8,128)(2,1)S(1)} %get-tuple-element.189), channel_id=1, source_target_pairs={{0,2},{1,3},{2,0},{3,1},{4,6},{5,7},{6,4},{7,5},{8,10},{9,11},{10,... | collective-permute-start | bytes 638984 | tf_op jit(solution)/shard_map/ppermute | solution.py:565
  161.4 43.2 %collective-permute-start.40 = (bf16[720,512]{1,0:T(8,128)(2,1)S(1)}, bf16[720,512]{1,0:T(8,128)(2,1)S(1)}, u32[]{:S(2)}, u32[]{:S(2)}) collective-permute-start(bf16[720,512]{1,0:T(8,128)(2,1)S(1)} %get-tuple-element.209.p0), channel_id=1, source_target_pairs={{0,1},{1,0},{2,3},{3,2},{4,5},{5,4},{6,7},{7,6},{8,9},{9,8},{10,11... | collective-permute-start | bytes 2211848 | tf_op jit(solution)/shard_map/ppermute | solution.py:565
  163.1 41.5 %collective-permute-start.42 = (bf16[720,512]{1,0:T(8,128)(2,1)S(1)}, bf16[720,512]{1,0:T(8,128)(2,1)S(1)}, u32[]{:S(2)}, u32[]{:S(2)}) collective-permute-start(bf16[720,512]{1,0:T(8,128)(2,1)S(1)} %collective-permute-done.41.p2), channel_id=1, source_target_pairs={{0,1},{1,0},{2,3},{3,2},{4,5},{5,4},{6,7},{7,6},{8,9},{9,8},{10,11... | collective-permute-start | bytes 2211848 | tf_op jit(solution)/shard_map/ppermute | solution.py:565
  171.2 17.3 %collective-permute-start.35 = (bf16[208,512]{1,0:T(8,128)(2,1)S(1)}, bf16[208,512]{1,0:T(8,128)(2,1)S(1)}, u32[]{:S(2)}, u32[]{:S(2)}) collective-permute-start(bf16[208,512]{1,0:T(8,128)(2,1)S(1)} %get-tuple-element.197.refs_0_), channel_id=1, source_target_pairs={{0,16},{4,20},{8,24},{12,28},{16,0},{20,4},{24,8},{28,12},{1,17},{... | collective-permute-start | bytes 638984 | tf_op jit(solution)/shard_map/ppermute | solution.py:565
  173.8 18.1 %collective-permute-start.36 = (bf16[208,512]{1,0:T(8,128)(2,1)S(1)}, bf16[208,512]{1,0:T(8,128)(2,1)S(1)}, u32[]{:S(2)}, u32[]{:S(2)}) collective-permute-start(bf16[208,512]{1,0:T(8,128)(2,1)S(1)} %get-tuple-element.198.refs_2_), channel_id=1, source_target_pairs={{0,16},{4,20},{8,24},{12,28},{16,0},{20,4},{24,8},{28,12},{1,17},{... | collective-permute-start | bytes 638984 | tf_op jit(solution)/shard_map/ppermute | solution.py:565
  174.2 10.2 %collective-permute-start.34 = (bf16[416,128]{1,0:T(8,128)(2,1)S(1)}, bf16[416,128]{1,0:T(8,128)(2,1)S(1)}, u32[]{:S(2)}, u32[]{:S(2)}) collective-permute-start(bf16[416,128]{1,0:T(8,128)(2,1)S(1)} %get-tuple-element.195), channel_id=1, source_target_pairs={{0,8},{4,12},{8,0},{12,4},{16,24},{20,28},{24,16},{28,20},{1,9},{5... | collective-permute-start | bytes 319496 | tf_op jit(solution)/shard_map/ppermute | solution.py:565
  192.0 8.5 %collective-permute-start.38 = (bf16[208,512]{1,0:T(8,128)(2,1)S(1)}, bf16[208,512]{1,0:T(8,128)(2,1)S(1)}, u32[]{:S(2)}, u32[]{:S(2)}) collective-permute-start(bf16[208,512]{1,0:T(8,128)(2,1)S(1)} %get-tuple-element.201.refs_0_), channel_id=1, source_target_pairs={{0,8},{4,12},{8,0},{12,4},{16,24},{20,28},{24,16},{28,20},{1,9},{5... | collective-permute-start | bytes 638984 | tf_op jit(solution)/shard_map/ppermute | solution.py:565
  192.8 7.7 %collective-permute-start.39 = (bf16[208,512]{1,0:T(8,128)(2,1)S(1)}, bf16[208,512]{1,0:T(8,128)(2,1)S(1)}, u32[]{:S(2)}, u32[]{:S(2)}) collective-permute-start(bf16[208,512]{1,0:T(8,128)(2,1)S(1)} %get-tuple-element.202.refs_2_), channel_id=1, source_target_pairs={{0,4},{4,0},{8,12},{12,8},{16,20},{20,16},{24,28},{28,24},{1,5},{5... | collective-permute-start | bytes 638984 | tf_op jit(solution)/shard_map/ppermute | solution.py:565
  193.3 6.5 %collective-permute-start.37 = (bf16[416,128]{1,0:T(8,128)(2,1)S(1)}, bf16[416,128]{1,0:T(8,128)(2,1)S(1)}, u32[]{:S(2)}, u32[]{:S(2)}) collective-permute-start(bf16[416,128]{1,0:T(8,128)(2,1)S(1)} %merge.19.refs_0_), channel_id=1, source_target_pairs={{0,16},{4,20},{8,24},{12,28},{16,0},{20,4},{24,8},{28,12},{1,17},{... | collective-permute-start | bytes 319496 | tf_op jit(solution)/shard_map/ppermute | solution.py:565
  200.6 17.1 %collective-permute-start.44 = (bf16[416,512]{1,0:T(8,128)(2,1)S(1)}, bf16[416,512]{1,0:T(8,128)(2,1)S(1)}, u32[]{:S(2)}, u32[]{:S(2)}) collective-permute-start(bf16[416,512]{1,0:T(8,128)(2,1)S(1)} %get-tuple-element.205.a0), channel_id=1, source_target_pairs={{0,4},{4,0},{8,12},{12,8},{16,20},{20,16},{24,28},{28,24},{1,5},{5... | collective-permute-start | bytes 1277960 | tf_op jit(solution)/shard_map/ppermute | solution.py:565
  201.2 16.5 %collective-permute-start.45 = (bf16[416,512]{1,0:T(8,128)(2,1)S(1)}, bf16[416,512]{1,0:T(8,128)(2,1)S(1)}, u32[]{:S(2)}, u32[]{:S(2)}) collective-permute-start(bf16[416,512]{1,0:T(8,128)(2,1)S(1)} %get-tuple-element.206.b0), channel_id=1, source_target_pairs={{0,8},{4,12},{8,0},{12,4},{16,24},{20,28},{24,16},{28,20},{1,9},{5... | collective-permute-start | bytes 1277960 | tf_op jit(solution)/shard_map/ppermute | solution.py:565
  204.6 11.5 %collective-permute-start.43 = (bf16[416,128]{1,0:T(8,128)(2,1)S(1)}, bf16[416,128]{1,0:T(8,128)(2,1)S(1)}, u32[]{:S(2)}, u32[]{:S(2)}) collective-permute-start(bf16[416,128]{1,0:T(8,128)(2,1)S(1)} %merge.21.refs_0_), channel_id=1, source_target_pairs={{0,8},{4,12},{8,0},{12,4},{16,24},{20,28},{24,16},{28,20},{1,9},{5... | collective-permute-start | bytes 319496 | tf_op jit(solution)/shard_map/ppermute | solution.py:565
  216.1 5.9 %collective-permute-start.46 = (bf16[832,128]{1,0:T(8,128)(2,1)S(1)}, bf16[832,128]{1,0:T(8,128)(2,1)S(1)}, u32[]{:S(2)}, u32[]{:S(2)}) collective-permute-start(bf16[832,128]{1,0:T(8,128)(2,1)S(1)} %merge.23.own), channel_id=1, source_target_pairs={{0,4},{4,0},{8,12},{12,8},{16,20},{20,16},{24,28},{28,24},{1,5},{5... | collective-permute-start | bytes 638984 | tf_op jit(solution)/shard_map/ppermute | solution.py:565
  (18 other events, 179.9 us)

commit v4 on v3

v4 whole, which is shorter than its diff:
```python
from functools import partial

import jax
import jax.numpy as jnp
from jax import lax
from jax.experimental import pallas as pl
from jax.experimental.pallas import tpu as pltpu
from jax.sharding import PartitionSpec as P

HD = 128
EPSILON = 1e-05
NEGATIVE = -1e30
SCALE = HD**-0.5
BF = jnp.bfloat16
F32 = jnp.float32
MIB = 1 << 20
KNOBS = {'cost': 0, 'window': 'AM2', 'tail': 'OFpFOFOcFOgFOrF', 'out_tie': 'w', 'hs_tie': 's0', 'g_tie': 'O3', 'rb_need': 1}
FB = 8
RB = 16


def mm(a, b):
    return jnp.dot(a, b, preferred_element_type=F32)


def mm_nt(a, b):
    return lax.dot_general(a, b, (((1,), (1,)), ((), ())), preferred_element_type=F32)


def mm_tn(a, b):
    return lax.dot_general(a, b, (((0,), (0,)), ((), ())), preferred_element_type=F32)


def standardize(values):
    centered = values - jnp.mean(values, axis=-1, keepdims=True)
    inverse = lax.rsqrt(jnp.mean(centered * centered, axis=-1, keepdims=True) + EPSILON)
    return centered * inverse, inverse


def norm_backward(upstream, normed, inverse, gain):
    scaled = upstream * gain
    return inverse * (
        scaled
        - jnp.mean(scaled, axis=-1, keepdims=True)
        - normed * jnp.mean(scaled * normed, axis=-1, keepdims=True)
    )


def column_sum(values):
    return jnp.sum(values, axis=0, keepdims=True)


def softmax_keys(scores):
    grown = jnp.exp(scores - jnp.max(scores, axis=0, keepdims=True))
    return grown * (1.0 / jnp.sum(grown, axis=0, keepdims=True))


def gelu_parts(z):
    t = 1.0 / (1.0 + (0.3275911 * 0.7071067811865476) * jnp.abs(z))
    e = jnp.exp(-0.5 * z * z)
    poly = t * (
        0.127414796 + t * (-0.142248368 + t * (0.7107068705 + t * (-0.7265760135 + t * 0.5307027145)))
    )
    tail = poly * e
    cdf = jnp.where(z >= 0, 1.0 - tail, tail)
    return z * cdf, cdf + z * (e * 0.3989422804014327)


def feature_probabilities(q, k, feature_count):
    scores = mm_nt(k, q) * SCALE
    key = lax.broadcasted_iota(jnp.int32, scores.shape, 0)
    return softmax_keys(jnp.where(key < feature_count, scores, NEGATIVE)).astype(BF)


def three(w):
    return jnp.concatenate([w[0], w[1], w[2]], axis=-1)


def stacked(w):
    n = w.shape[0] // 3
    return jnp.concatenate([w[c * n : (c + 1) * n] for c in range(3)], axis=-1)


def unpacked(w):
    tall = jnp.concatenate([w[:, j * HD : (j + 1) * HD] for j in range(4)], axis=0)
    return stacked(tall)


def four_weights(fq, fq_far, near):
    tall = 3 * fq.shape[1] // 4
    packed = [(near, pl.BlockSpec((tall, 4 * HD), partial(lambda j, *_: (j, 0), j))) for j in range(2)]
    return [(fq, full(fq)), packed[0], (fq_far, full(fq_far)), packed[1]]


def wide(pieces):
    n = pieces[0].shape[0] // 4
    return jnp.concatenate(
        [jnp.concatenate([p[j * n : (j + 1) * n] for j in range(4)], axis=-1) for p in pieces], axis=0)


def live_columns(block, first, feature_count):
    values = block.astype(F32)
    index = first + lax.broadcasted_iota(jnp.int32, values.shape, 0)
    return jnp.where(index < feature_count, values, 0.0)


ANY = pl.BlockSpec(memory_space=pl.ANY)
VMEM = pl.BlockSpec(memory_space=pltpu.VMEM)


def full(a):
    zeros = (0,) * len(a.shape)
    return pl.BlockSpec(a.shape, lambda *_: zeros)


def shaped(shape, dtype=BF):
    return jax.ShapeDtypeStruct(shape, dtype)


def call(kernel, name, grid, t, ins, outs, scratch=(), vmem=32, us=1):
    t, after = t[:2], [a for a in t[2:]]
    count = 2 + len(ins)

    def body(*refs):
        kernel(*refs[:count], *refs[count + len(after) :])

    spec = pltpu.PrefetchScalarGridSpec(
        num_scalar_prefetch=2,
        grid=grid,
        in_specs=[s for _, s in ins] + [ANY] * len(after),
        out_specs=[s for _, s in outs],
        scratch_shapes=list(scratch),
    )
    return pl.pallas_call(
        body,
        grid_spec=spec,
        out_shape=[a for a, _ in outs],
        compiler_params=pltpu.CompilerParams(vmem_limit_bytes=vmem * MIB),
        cost_estimate=pl.CostEstimate(flops=us * KNOBS["cost"] * 1_000_000 + 1, bytes_accessed=1, transcendentals=0),
        name=name,
    )(*t, *[a for a, _ in ins], *after)


def pack_kernel(t_ref, d_ref, rq_ref, fo_ref, ro_ref, ub_ref, out_ref):
    width = rq_ref.shape[1]
    for c in range(3):
        out_ref[c * width : (c + 1) * width] = rq_ref[c]
    at = 3 * width
    for source in (fo_ref, ro_ref):
        for j in range(4):
            out_ref[at : at + HD] = source[:, j * HD : (j + 1) * HD]
            at += HD
    bias = [ub_ref[j * HD : (j + 1) * HD].astype(F32).reshape(1, HD) for j in range(4)]
    out_ref[at : at + 16] = jnp.concatenate(bias + [jnp.zeros((12, HD), F32)], axis=0).astype(BF)


def pack(t, rq, fo, ro, ub):
    out = shaped((3 * rq.shape[1] + 8 * HD + 16, HD))
    return call(pack_kernel, "pack", (), t, [(a, VMEM) for a in (rq, fo, ro, ub)], [(out, VMEM)], vmem=60)[0]


def pack_part(pack, what):
    rows = pack.shape[0] - 8 * HD - 16
    size, at = {"qkv": (rows, 0), "feat_out": (4 * HD, rows), "row_out": (4 * HD, rows + 4 * HD),
                "bias": (16, rows + 8 * HD)}[what]
    return pl.BlockSpec((size, HD), lambda *_: (at // size, 0))


def pack_parts(packs, what):
    return [(p, pack_part(p, what)) for p in packs]


def feature_forward_kernel(
    t_ref, d_ref, cells_ref, gains_ref, shifts_ref, w_ref, up_ref, down_ref, o0, o1, o2, o3, both_ref, qkv_scr, mix_scr
):
    feature_count, rows, width = cells_ref.shape
    padded = qkv_scr.shape[1] // rows

    @pl.when(pl.program_id(0) == 0)
    def _():
        qkv_scr[...] = jnp.zeros_like(qkv_scr)
        both_ref[: up_ref.shape[0]] = up_ref[...]
        both_ref[up_ref.shape[0] :] = down_ref[...]

    cells = cells_ref[...].astype(F32).reshape(feature_count * rows, width)
    normed, _ = standardize(cells)
    low = (normed * gains_ref[...].astype(F32)[0:1] + shifts_ref[...].astype(F32)[0:1]).astype(BF)
    qkv = mm(low, three(w_ref))
    for c in range(3):
        qkv_scr[c, 0 : feature_count * rows, :] = qkv[:, c * HD : (c + 1) * HD]
    for r in range(rows):
        every = pl.ds(r, padded, stride=rows)
        q, k, v = (qkv_scr[c, every, :].astype(BF) for c in range(3))
        mix_scr[every, :] = mm_tn(feature_probabilities(q, k, feature_count), v)
    count = o0.shape[1]
    for k, out in enumerate((o0, o1, o2, o3)):
        at = pl.multiple_of(lax.bitwise_xor(t_ref[0], k) * count, count)
        out[0] = mix_scr[pl.ds(at, count), :].astype(BF)


def feature_forward(t, cells, gains, shifts, weight, up, down, columns):
    feature_count, row_count, width = cells.shape
    padded = 4 * columns
    steps = row_count // RB
    out = (shaped((steps, columns * RB, HD)), pl.BlockSpec((1, columns * RB, HD), lambda i, t, d: (i, 0, 0)))
    return call(
        feature_forward_kernel, "feature_forward", (steps,), t,
        [(cells, pl.BlockSpec((feature_count, RB, width), lambda i, t, d: (0, i, 0)))]
        + [(a, full(a)) for a in (gains, shifts, weight, up, down)],
        [out] * 4 + [whole((up.shape[0] + down.shape[0], up.shape[1]))],
        [pltpu.VMEM((3, padded * RB, HD), F32), pltpu.VMEM((padded * RB, HD), F32)], vmem=60, us=11
    )


def column_block(array, columns):
    _, rows, width = array.shape
    return pl.BlockSpec((columns, rows, width), lambda i, t, d: (t[0], 0, 0))


def in_order(m, columns):
    steps = m.shape[0]
    halves = [m[i].reshape(columns, RB, HD) for i in range(steps)]
    return jnp.concatenate(halves, axis=1).reshape(columns * RB * steps, HD)


def row_forward_kernel(
    t_ref, d_ref, split_ref, m0, m1, m2, m3, cells_ref, f0, f1, f2, f3, r0, r1, r2, r3, w0, w1, w2, w3,
    wo_bias, wr_bias, gains_ref, shifts_ref,
    first_ref, n2_ref, qkv_ref, p_ref, o2_ref, second_ref, n3_ref, *, feature_count,
):
    columns, rows, width = cells_ref.shape
    cells = columns * rows
    side = p_ref.shape[2]
    key = lax.broadcasted_iota(jnp.int32, (side, side), 0)
    query = lax.broadcasted_iota(jnp.int32, (side, side), 1)
    same = lax.div(query, rows) == lax.div(key, rows)
    bias = jnp.where(jnp.logical_and(same, lax.rem(key, rows) < split_ref[0]), 0.0, NEGATIVE)

    gains = gains_ref[...].astype(F32)
    shifts = shifts_ref[...].astype(F32)
    stream = live_columns(cells_ref[...], t_ref[0] * columns, feature_count).reshape(cells, width)
    mixed = jnp.concatenate([in_order(m, columns) for m in (m0, m1, m2, m3)], axis=-1)
    first = stream + mm(mixed, wide((f0, f1, f2, f3))) + wo_bias[...].astype(F32)
    first_ref[...] = first
    normed, _ = standardize(first)
    low = (normed * gains[1:2] + shifts[1:2]).astype(BF)
    n2_ref[...] = low
    for h, w in enumerate((w0, w1, w2, w3)):
        base = 3 * HD * h
        qkv_ref[:, base : base + 3 * HD] = mm(low, stacked(w)).astype(BF)
        for b in range(0, cells, side):
            span = slice(b, b + side)
            q, k, v = (qkv_ref[span, base + c * HD : base + (c + 1) * HD] for c in range(3))
            p = softmax_keys(mm_nt(k, q) * SCALE + bias).astype(BF)
            p_ref[h, b // side] = p
            o2_ref[span, h * HD : (h + 1) * HD] = mm_tn(p, v).astype(BF)
    second = first + mm(o2_ref[...], wide((r0, r1, r2, r3))) + wr_bias[...].astype(F32)
    second_ref[...] = second
    normed, _ = standardize(second)
    n3_ref[...] = (normed * gains[2:3] + shifts[2:3]).astype(BF)


def whole(shape, dtype=BF):
    return shaped(shape, dtype), full(shaped(shape, dtype))


def row_forward(t, split, mixed, cells, packs, wo_bias, wr_bias, gains, shifts, columns):
    feature_count, rows, width = cells.shape
    n = columns * rows
    side = 4 * rows
    ins = [(split, pl.BlockSpec(memory_space=pltpu.SMEM))] + [(m, full(m)) for m in mixed]
    ins += [(cells, column_block(cells, columns))]
    ins += pack_parts(packs, "feat_out") + pack_parts(packs, "row_out") + pack_parts(packs, "qkv")
    ins += [(a, full(a)) for a in (wo_bias, wr_bias, gains, shifts)]
    return call(
        partial(row_forward_kernel, feature_count=feature_count), "row_forward", (1,), t, ins,
        [whole((n, width), F32), whole((n, width)), whole((n, 12 * HD)), whole((4, n // side, side, side)),
         whole((n, 4 * HD)), whole((n, width), F32), whole((n, width))], us=9
    )


def hidden_pair(t_ref, n3_ref, grad_ref, ups, packs, downs, grads, bias_grads, feature_count):
    columns, rows, width = grad_ref.shape
    g3 = live_columns(grad_ref[...], t_ref[0] * columns, feature_count).reshape(columns * rows, width)
    n3, gl = n3_ref[...], g3.astype(BF)
    n3_t, gl_t = n3.T, gl.T
    ms, dzs = [], []
    for up, pack, down, grad_ref, bias_grad in zip(ups, packs, downs, grads, bias_grads):
        bias = jnp.concatenate([pack[...].astype(F32)[j : j + 1] for j in range(4)], axis=-1)
        act, slope = gelu_parts(mm(n3, up[...]) + bias)
        m = act.astype(BF)
        dz = (mm_nt(gl, down[...]) * slope).astype(BF)
        grad_ref[:width] = mm(n3_t, dz).astype(BF)
        grad_ref[width:] = mm(gl_t, m).astype(BF)
        bias_grad[...] = column_sum(dz.astype(F32))
        ms.append(m)
        dzs.append(dz)
    out = mm(jnp.concatenate(ms, axis=-1), jnp.concatenate([d[...] for d in downs], axis=0))
    dn3 = mm_nt(jnp.concatenate(dzs, axis=-1), jnp.concatenate([u[...] for u in ups], axis=-1))
    return g3, out, dn3


def hidden_first_kernel(
    t_ref, d_ref, n3_ref, grad_ref, up0, up1, b0, b1, down0, down1, out_ref, dn3_ref, wg0, wg1, bg0, bg1,
    *, feature_count,
):
    _, out, dn3 = hidden_pair(
        t_ref, n3_ref, grad_ref, (up0, up1), (b0, b1), (down0, down1), (wg0, wg1), (bg0, bg1), feature_count)
    out_ref[...] = out
    dn3_ref[...] = dn3


def hidden_second_kernel(
    t_ref, d_ref, n3_ref, grad_ref, up0, up1, b0, b1, down0, down1, out_in, dn3_in, second_ref, down_bias, gains_ref,
    earlier_ref, out_ref, g2_ref, stats_ref, wg0, sent_ref, bg0, bg1, *, feature_count,
):
    tall = earlier_ref.shape[0]
    sent_ref[:tall] = earlier_ref[...]
    g3, out, dn3 = hidden_pair(
        t_ref, n3_ref, grad_ref, (up0, up1), (b0, b1), (down0, down1), (wg0, sent_ref.at[pl.ds(tall, tall)]), (bg0, bg1),
        feature_count)
    second = second_ref[...]
    out_ref[...] = (second + out_in[...] + out + down_bias[...].astype(F32)).astype(BF)
    dn3 = dn3_in[...] + dn3
    normed, inverse = standardize(second)
    g2 = g3 + norm_backward(dn3, normed, inverse, gains_ref[...].astype(F32)[2:3])
    g2_ref[...] = g2
    stats_ref[...] = rows_of([g3, g2, dn3 * normed, dn3])


def rows_of(arrays):
    return jnp.concatenate(
        [column_sum(a) for a in arrays] + [jnp.zeros((8 - len(arrays), arrays[0].shape[1]), F32)], axis=0)


def hidden_call(t, n3, grads, both, packs, columns, extra=None):
    n, width = n3.shape
    hidden = both[0].shape[1]
    ins = [(n3, full(n3)), (grads, column_block(grads, columns))]
    ins += [(a, pl.BlockSpec((width, hidden), lambda *_: (0, 0))) for a in both] + pack_parts(packs, "bias")
    ins += [(a, pl.BlockSpec((hidden, width), lambda *_: (1, 0))) for a in both]
    bias_grads = [whole((1, hidden), F32)] * 2
    if extra is None:
        kernel, name = hidden_first_kernel, "hidden_first"
        results = [whole((n, width), F32)] * 2 + [whole((2 * width, hidden))] * 2 + bias_grads
    else:
        kernel, name = hidden_second_kernel, "hidden_second"
        ins += [(a, full(a)) for a in extra]
        results = [whole((n, width)), whole((n, width), F32), whole((8, width), F32)]
        results += [whole((2 * width, hidden)), whole((4 * width, hidden))] + bias_grads
    return call(partial(kernel, feature_count=grads.shape[0]), name, (1,), t, ins, results, us=7)


def attention_backward(q, k, v, p, do):
    dp = mm_nt(v, do)
    pf = p.astype(F32)
    ds = (pf * (dp - jnp.sum(dp * pf, axis=0, keepdims=True))).astype(BF)
    return mm_tn(ds, k) * SCALE, mm(ds, q) * SCALE, mm(p, do)


def row_backward_kernel(
    t_ref, d_ref, g2_ref, first_ref, qkv_ref, p_ref, gains_ref, n2_ref, o2_ref, m0, m1, m2, m3, fq0, fq2,
    w0, w1, w2, w3, r0, r1, r2, r3, s0, near_ref, s2, s3, stats_ref, keep_ref, send_ref, g1_scr, dqkv_ref,
):
    width = fq0.shape[1]
    for j, weights in enumerate((fq0, fq2)):
        tall = 3 * width // 4
        for lane in range(4):
            for at, first, count in stretches(lane * tall, tall, width):
                near_ref[j * tall + at : j * tall + at + count, lane * HD : (lane + 1) * HD] = (
                    weights[first // width, first % width : first % width + count, :])
    g2 = g2_ref[...]
    cells, width = g2.shape
    side = p_ref.shape[2]
    gl2 = g2.astype(BF)
    do = mm_nt(gl2, wide((r0, r1, r2, r3))).astype(BF)
    for h in range(4):
        at = 3 * HD * h
        for b in range(0, cells, side):
            span = slice(b, b + side)
            q, k, v = (qkv_ref[span, at + c * HD : at + (c + 1) * HD] for c in range(3))
            parts = attention_backward(q, k, v, p_ref[h, b // side], do[span, HD * h : HD * (h + 1)])
            for c, part in enumerate(parts):
                dqkv_ref[span, at + c * HD : at + (c + 1) * HD] = part.astype(BF)
    dn2 = mm_nt(dqkv_ref[...], jnp.concatenate([stacked(w) for w in (w0, w1, w2, w3)], axis=-1))
    normed, inverse = standardize(first_ref[...])
    g1 = g2 + norm_backward(dn2, normed, inverse, gains_ref[...].astype(F32)[1:2])
    columns, rows, _ = g1_scr.shape
    g1_scr[...] = g1.reshape(columns, rows, width)
    share = rows // 4
    for k, out in enumerate((s0, near_ref.at[pl.ds(6 * width // 4, columns * share)], s2, s3)):
        at = pl.multiple_of(lax.bitwise_xor(t_ref[0], k) * share, share)
        out[...] = g1_scr[:, pl.ds(at, share), :].reshape(columns * share, width).astype(BF)
    stats_ref[...] = rows_of([g1, dn2 * normed, dn2])
    mixed = [in_order(m, columns) for m in (m0, m1, m2, m3)]
    row_grads(n2_ref[...], dqkv_ref[...], gl2, o2_ref[...], g1.astype(BF), mixed, keep_ref, send_ref)


def stretches(first, count, size):
    at = 0
    while at < count:
        rows = min(count - at, size - (first + at) % size)
        yield at, first + at, rows
        at += rows


def row_grads(n2, dqkv, gl2, o2, gl1, mixed, keep_ref, send_ref):
    width = n2.shape[1]
    grad = mm(n2.T, dqkv).astype(BF)
    out_grad = mm(gl2.T, o2).astype(BF)
    feat_grad = mm(gl1.T, jnp.concatenate(mixed, axis=-1)).astype(BF)
    for h in range(4):
        out = (keep_ref, send_ref)[h % 2].at[h // 2]
        blocks = [grad[:, (3 * h + c) * HD : (3 * h + c + 1) * HD] for c in range(3)]
        blocks += [out_grad[:, HD * h : HD * (h + 1)], feat_grad[:, HD * h : HD * (h + 1)]]
        for at, first, count, lane in row_places(width):
            out[at : at + count, lane * HD : (lane + 1) * HD] = blocks[first // width][first % width : first % width + count]


def row_backward(t, g2, first, qkv, p, gains, n2, o2, mixed, fq, fq_far, packs, rows):
    n, width = g2.shape
    ins = [(a, full(a)) for a in (g2, first, qkv, p, gains, n2, o2, *mixed, fq, fq_far)]
    ins += pack_parts(packs, "qkv") + pack_parts(packs, "row_out")
    piece = whole((n // 4, width))
    return call(
        row_backward_kernel, "row_backward", (1,), t, ins,
        [piece, whole((6 * width // 4 + n // 4, width)), piece, piece, whole((8, width), F32)]
        + [whole((2, 5 * width // 4, 4 * HD))] * 2,
        [pltpu.VMEM((n // rows, rows, width), F32), pltpu.VMEM(qkv.shape, BF)], us=11,
    )


def row_places(width):
    tall = 5 * width // 4
    first = 0
    while first < 5 * width:
        count = min(width - first % width, tall - first % tall)
        yield first % tall, first, count, first // tall
        first += count


def own_rows(t_ref, cells_ref, cell_scr, share):
    feature_count, block_rows, width = cells_ref.shape
    cell_scr[0:feature_count] = cells_ref[...].astype(F32)
    cell_scr[feature_count:] = jnp.zeros_like(cell_scr[feature_count:])
    at = pl.multiple_of(lax.rem(t_ref[0], block_rows // share) * share, share)
    return cell_scr[:, pl.ds(at, share), :].reshape(cell_scr.shape[0] * share, width)


def row_block(cells, share):
    feature_count, _, width = cells.shape
    per = RB // share
    return pl.BlockSpec((feature_count, RB, width), lambda i, t, d: (0, lax.div(t[0], per), 0))


def feature_again_kernel(
    t_ref, d_ref, cells_ref, gains_ref, shifts_ref, w0, w1, w2, w3, n1_ref, qkv_ref, p_ref, cell_scr, qkv_scr
):
    feature_count = cells_ref.shape[0]
    share, padded, _ = qkv_ref.shape
    normed, _ = standardize(own_rows(t_ref, cells_ref, cell_scr, share))
    low = (normed * gains_ref[...].astype(F32)[0:1] + shifts_ref[...].astype(F32)[0:1]).astype(BF)
    n1_ref[...] = low
    for h, w in enumerate((three(w0), unpacked(w1), three(w2), unpacked(w3))):
        packed = mm(low, w)
        for c in range(3):
            qkv_scr[c] = packed[:, c * HD : (c + 1) * HD]
        for r in range(share):
            q, k, v = (qkv_scr[c, pl.ds(r, padded, stride=share), :].astype(BF) for c in range(3))
            for c, part in enumerate((q, k, v)):
                qkv_ref[r, :, (3 * h + c) * HD : (3 * h + c + 1) * HD] = part
            p_ref[r, h] = feature_probabilities(q, k, feature_count)


def feature_again(t, cells, gains, shifts, fq, fq_far, near, columns, share):
    width = cells.shape[2]
    padded = 4 * columns
    return call(
        feature_again_kernel, "feature_again", (1,), t,
        [(cells, row_block(cells, share))] + [(a, full(a)) for a in (gains, shifts)] + four_weights(fq, fq_far, near),
        [whole((padded * share, width)), whole((share, padded, 12 * HD)), whole((share, 4, padded, padded))],
        [pltpu.VMEM((padded, RB, width), F32), pltpu.VMEM((3, padded * share, HD), F32)], vmem=28, us=4
    )


def feature_backward_kernel(
    t_ref, d_ref, r0, r1, r2, r3, f0, f1, f2, f3, qkv_ref, p_ref, n1_ref,
    g1_ref, dqkv_ref, keep0, keep1, send0, send1, low_scr, do_scr, dqkv_scr,
):
    width = g1_ref.shape[1]
    share, padded, _ = qkv_ref.shape
    for k, piece in enumerate((r0, r1, r2, r3)):
        count = piece.shape[0]
        at = pl.multiple_of(lax.bitwise_xor(t_ref[0], k) * count, count)
        low_scr[pl.ds(at, count), :] = piece[...]
        g1_ref[pl.ds(at, count), :] = piece[...].astype(F32)
    do = mm_nt(low_scr[...], wide((f0, f1, f2, f3)))
    for h in range(4):
        do_scr[h] = do[:, h * HD : (h + 1) * HD]
    n1_t = n1_ref[...].T
    for h in range(4):
        for r in range(share):
            every = pl.ds(r, padded, stride=share)
            q, k, v = (qkv_ref[r, :, (3 * h + c) * HD : (3 * h + c + 1) * HD] for c in range(3))
            parts = attention_backward(q, k, v, p_ref[r, h], do_scr[h, every, :].astype(BF))
            for c, part in enumerate(parts):
                dqkv_scr[3 * h + c, every, :] = part
        out = ((keep0, keep1), (send0, send1))[h % 2]
        for c in range(3):
            dqkv_ref[:, (3 * h + c) * HD : (3 * h + c + 1) * HD] = dqkv_scr[3 * h + c].astype(BF)
        grad = mm(n1_t, dqkv_ref[:, 3 * HD * h : 3 * HD * (h + 1)]).astype(BF)
        for c in range(3):
            out[h // 2][c * width : (c + 1) * width, :] = grad[:, c * HD : (c + 1) * HD]


def feature_backward(t, pieces, packs, qkv, p, n1):
    share, _, padded, _ = p.shape
    width = pieces[0].shape[1]
    cells = share * padded
    return call(
        feature_backward_kernel, "feature_backward", (1,), t,
        [(a, pl.BlockSpec(pieces[0].shape, partial(lambda j, *_: (j, 0), 0 if k != 1 else a.shape[0] // pieces[0].shape[0] - 1)))
         for k, a in enumerate(pieces)] + pack_parts(packs, "feat_out") + [(a, full(a)) for a in (qkv, p, n1)],
        [whole((cells, width), F32), whole((cells, 12 * HD))] + [whole((3 * width, HD))] * 4,
        [pltpu.VMEM((cells, width), BF), pltpu.VMEM((4, cells, HD), F32), pltpu.VMEM((12, cells, HD), F32)], us=11
    )


def feature_input_kernel(
    t_ref, d_ref, cells_ref, g1_ref, dqkv_ref, gains_ref, w0, w1, w2, w3, stats_a, stats_b, b0, b1, b2, b3,
    out_ref, stats_ref, cell_scr, sums_scr,
):
    cells, width = g1_ref.shape
    share = cells // cell_scr.shape[0]
    normed, inverse = standardize(own_rows(t_ref, cells_ref, cell_scr, share))
    dn1 = mm_nt(dqkv_ref[...], jnp.concatenate([three(w0), unpacked(w1), three(w2), unpacked(w3)], axis=-1))
    g0 = g1_ref[...] + norm_backward(dn1, normed, inverse, gains_ref[...].astype(F32)[0:1])
    out_ref[...] = g0[: out_ref.shape[0]].astype(BF)
    sums_scr[0:8] = stats_a[...]
    sums_scr[8:16] = stats_b[...]
    sums_scr[4:5] = column_sum(dn1 * normed)
    sums_scr[5:6] = column_sum(dn1)
    sums_scr[16:32] = jnp.zeros((16, width), F32)
    for k, row in enumerate((b0, b1, b2, b3)):
        sums_scr[pl.ds(16 + lax.bitwise_xor(t_ref[0], k), 1), :] = row[...]
    for j in range(4):
        stats_ref[32 * j : 32 * (j + 1)] = sums_scr[:, j * HD : (j + 1) * HD]


def feature_input(t, cells, g1, dqkv, gains, fq, fq_far, near, sums, share):
    count, width = g1.shape
    kept = (cells.shape[0] + 1) // 2 * 2 * share
    ins = [(cells, row_block(cells, share))] + [(a, full(a)) for a in (g1, dqkv, gains)]
    ins += four_weights(fq, fq_far, near) + [(a, full(a)) for a in sums]
    return call(
        feature_input_kernel, "feature_input", (1,), t, ins, [whole((kept, width)), whole((128, HD), F32)],
        [pltpu.VMEM((count // share, RB, width), F32), pltpu.VMEM((32, width), F32)], vmem=28, us=2,
    )


def pair_kernel(t_ref, d_ref, own, far, out_ref):
    out_ref[: own.shape[0]] = own[...]
    out_ref[own.shape[0] :] = far[...]


def pair(t, own, far):
    return call(pair_kernel, "pair", (), t, [(own, VMEM), (far, VMEM)], [(shaped((2 * own.shape[0], own.shape[1])), VMEM)], vmem=12)[0]


def columns_home_kernel(t_ref, d_ref, p0, p1, p2, p3, out_ref):
    for k, piece in enumerate((p0, p1, p2, p3)):

        @pl.when(pl.program_id(0) == lax.bitwise_xor(t_ref[0], k))
        def _():
            out_ref[...] = piece[...].reshape(out_ref.shape)


def columns_home(t, own, far, near, feature_count, rows):
    count, width = own.shape
    columns = count // rows
    block = lambda i: pl.BlockSpec((count, width), lambda *_: (i, 0))
    return call(
        columns_home_kernel, "columns_home", (4,), t,
        [(own, block(0)), (near, block(0)), (far, block(0)), (near, block(1))],
        [(shaped((feature_count, rows, width)), pl.BlockSpec((columns, rows, width), lambda i, t, d: (i, 0, 0)))], vmem=16,
    )[0]


def rows_home_kernel(t_ref, d_ref, p0, p1, p2, p3, out_ref, scr):
    columns, rows, width = scr.shape
    share = rows // 4
    for k, piece in enumerate((p0, p1, p2, p3)):
        at = pl.multiple_of(lax.bitwise_xor(t_ref[0], k) * share, share)
        scr[:, pl.ds(at, share), :] = piece[...].astype(F32).reshape(columns, share, width)
    out_ref[...] = scr[...].astype(BF)


def rows_home(t, own, far, near, feature_count, rows):
    count, width = own.shape
    share = rows // 4
    steps = 5
    columns = count // share // steps
    block = lambda first: pl.BlockSpec((columns * share, width), lambda i, t, d: (first + i, 0))
    return call(
        rows_home_kernel, "rows_home", (steps,), t,
        [(own, block(0)), (near, block(0)), (far, block(0)), (near, block(steps))],
        [(shaped((feature_count, rows, width)), pl.BlockSpec((columns, rows, width), lambda i, t, d: (i, 0, 0)))],
        [pltpu.VMEM((columns, rows, width), F32)], vmem=16,
    )[0]


def swap(values, axis, mask):
    count = lax.axis_size(axis)
    return lax.ppermute(values, axis, [(i, i ^ mask) for i in range(count)])


def gather_groups(own):
    far = swap(own, "tensor", 2)
    return own, swap(own, "tensor", 1), far, swap(far, "tensor", 1)


class Box:
    def __init__(self, value):
        self.value = value


def tied(values, *boxes):
    many = isinstance(values, tuple)
    values = values if many else (values,)
    out = lax.optimization_barrier((*values, *[b.value for b in boxes]))
    for box, value in zip(boxes, out[len(values) :]):
        box.value = value
    return out[: len(values)] if many else out[0]


def dp_masks():
    masks, mask = [], 1
    while mask < lax.axis_size("dp"):
        masks.append(mask)
        mask *= 2
    return masks


def digit(d_ref, mask):
    return lax.rem(lax.div(d_ref[0], mask), 2)


def halves(d_ref, mask, rows):
    side = digit(d_ref, mask)
    return [pl.multiple_of(s * rows, rows) for s in (side, 1 - side)]


def added(a, b):
    return a.astype(F32) + b.astype(F32)


def merge(name, kernel, t, ins, outs, scratch=(), vmem=16):
    return call(kernel, name, (), t, [(a, VMEM) for a in ins], [(shaped(o), VMEM) for o in outs], scratch, vmem=vmem)


def first_halves(t, hg0, hg2, row_keep, got, row_got, masks):
    hidden = hg0.shape[0] // 2
    half = row_keep.shape[1] // 2
    rows, width = hidden + half, hg0.shape[1]

    def kernel(t_ref, d_ref, g0, g2, keep, r, row_r, ak, as_, bk, bs, scr):
        for group, mine in enumerate((g0, g2)):
            for which, (kept, sent, mask) in enumerate(((ak, as_, masks[0]), (bk, bs, masks[1]))):
                at = which * hidden
                scr[:hidden] = added(mine[at : at + hidden], r[2 * hidden * group + at : 2 * hidden * group + at + hidden])
                at = which * half
                scr[hidden:] = added(keep[group, at : at + half], row_r[group, at : at + half])
                for out, first in zip((kept, sent), halves(d_ref, mask, rows // 2)):
                    out[group] = scr[pl.ds(first, rows // 2), :].astype(BF)

    return merge("ab_first", kernel, t, (hg0, hg2, row_keep, got, row_got), [(2, rows // 2, width)] * 4,
                 [pltpu.VMEM((rows, width), F32)], vmem=20)


def second_halves(t, a, ar, b, br, masks):
    _, rows, width = a.shape

    def kernel(t_ref, d_ref, a, ar, b, br, ak, as_, bk, bs):
        for x, y, kept, sent, mask in ((a, ar, ak, as_, masks[1]), (b, br, bk, bs, masks[0])):
            for out, first in zip((kept, sent), halves(d_ref, mask, rows // 2)):
                span = (slice(None), pl.ds(first, rows // 2), slice(None))
                out[...] = added(x[span], y[span]).astype(BF)

    return merge("ab_second", kernel, t, (a, ar, b, br), [(2, rows // 2, width)] * 4)


def groups_apart(t, a, ar, b, br):
    _, rows, width = a.shape

    def kernel(t_ref, d_ref, a, ar, b, br, kept, sent):
        for group, out in enumerate((kept, sent)):
            out[:rows] = added(a[group], ar[group]).astype(BF)
            out[rows:] = added(b[group], br[group]).astype(BF)

    return merge("ab_groups", kernel, t, (a, ar, b, br), [(2 * rows, width)] * 2)


def sums(t, k, r):
    def kernel(t_ref, d_ref, k, r, out):
        out[...] = added(k[...], r[...]).astype(BF)

    return merge("sums", kernel, t, (k, r), [k.shape])


def sums_apart(t, k, r):
    rows, width = k.shape[0] // 2, k.shape[1]

    def kernel(t_ref, d_ref, k, r, a, b):
        a[...] = added(k[:rows], r[:rows]).astype(BF)
        b[...] = added(k[rows:], r[rows:]).astype(BF)

    return merge("ab_apart", kernel, t, (k, r), [(rows, width)] * 2)


def joins(t, pairs, masks):
    def kernel(t_ref, d_ref, *refs):
        for j, mask in enumerate(masks):
            own, other, out = refs[2 * j], refs[2 * j + 1], refs[2 * len(masks) + j]
            for source, first in zip((own, other), halves(d_ref, mask, own.shape[0])):
                out[pl.ds(first, own.shape[0]), :] = source[...]

    return merge("joins", kernel, t, [a for p in pairs for a in p], [(2 * p[0].shape[0], p[0].shape[1]) for p in pairs])


def feature_groups(t, own, got, mine, theirs):
    rows, width = own[0].shape
    more = mine.shape[0]

    def kernel(t_ref, d_ref, a0, a2, b0, b2, sa, sb, kept, sent):
        small = added(sa[...], sb[...]).astype(BF)
        for out, a, b in ((kept, a0, b0), (sent, a2, b2)):
            out[:rows] = added(a[...], b[...]).astype(BF)
            out[rows:] = small

    return merge("f_groups", kernel, t, (*own, *got, mine, theirs), [(rows + more, width)] * 2)


def half_sums(t, k, r, mask):
    rows, width = k.shape[0] // 2, k.shape[1]

    def kernel(t_ref, d_ref, k, r, kept, sent):
        for out, first in zip((kept, sent), halves(d_ref, mask, rows)):
            span = (pl.ds(first, rows), slice(None))
            out[...] = added(k[span], r[span]).astype(BF)

    return merge("f_half", kernel, t, (k, r), [(rows, width)] * 2)


def joined(d_ref, own, other, mask, scr):
    rows = own.shape[0]
    side = digit(d_ref, mask)
    for source, place in ((own, side), (other, 1 - side)):
        scr[pl.ds(pl.multiple_of(place * rows, rows), rows), :] = source[...].astype(F32)


def finish_kernel(t_ref, d_ref, a0, a1, b0, b1, up_ref, down_ref, qkv_ref, row_out_ref, feat_out_ref, scr_a, scr_b, tall, *, masks):
    joined(d_ref, a0, a1, masks[0], scr_a)
    joined(d_ref, b0, b1, masks[1], scr_b)
    width = up_ref.shape[0]
    half = scr_a.shape[0] - width
    up_ref[...] = scr_a[0:width]
    down_ref[...] = scr_b[0:width].T
    for at, first, count, lane in row_places(width):
        for scr, low, high in ((scr_a, 0, half), (scr_b, half, 2 * half)):
            begin, end = max(at, low), min(at + count, high)
            if begin < end:
                to = first + begin - at
                tall[to : to + end - begin, :] = scr[width + begin - low : width + end - low, lane * HD : (lane + 1) * HD]
    qkv_ref[...] = tall[0 : 3 * width]
    row_out_ref[...] = tall[3 * width : 4 * width].T
    feat_out_ref[...] = tall[4 * width : 5 * width].T


def finish(t, a, b, masks, width):
    rows, w = a[0].shape
    scr = pltpu.VMEM((2 * rows, w), F32)
    outs = [shaped(s, F32) for s in ((width, w), (w, width), (3 * width, HD), (HD, width), (HD, width))]
    return call(
        partial(finish_kernel, masks=masks), "finish", (), t,
        [(x, VMEM) for x in (*a, *b)], [(o, VMEM) for o in outs],
        [scr, scr, pltpu.VMEM((5 * width, HD), F32)], vmem=24)


def finish_feature_kernel(t_ref, d_ref, own, other, qkv_ref, sums_ref, scr, *, mask):
    joined(d_ref, own, other, mask, scr)
    rows = qkv_ref.shape[0]
    qkv_ref[...] = scr[0:rows]
    tall = sums_ref.shape[0]
    for j in range(4):
        sums_ref[:, j * HD : (j + 1) * HD] = scr[rows + j * tall : rows + (j + 1) * tall]


def finish_feature(t, own, other, mask, width, small):
    rows, w = own.shape
    return call(
        partial(finish_feature_kernel, mask=mask), "finish_feature", (), t, [(own, VMEM), (other, VMEM)],
        [(shaped((3 * width, w), F32), VMEM), (shaped((small, 4 * HD), F32), VMEM)],
        [pltpu.VMEM((2 * rows, w), F32)], vmem=16)


def shards(
    table_cells, splits, feat_qkv, feat_out, feat_out_bias, row_qkv, row_out, row_out_bias,
    up_weight, up_bias, down_weight, down_bias, norm_gains, norm_biases, cotangent,
):
    shape = table_cells.shape
    _, row_count, feature_count, width = shape
    share = row_count // 4
    columns = -(-feature_count // (4 * FB)) * FB
    t = tuple(lax.axis_index(a).astype(jnp.int32).reshape(1) for a in ("tensor", "dp"))
    masks = dp_masks()
    cells = jnp.transpose(table_cells[0], (1, 0, 2))
    grads = jnp.transpose(cotangent[0], (1, 0, 2))
    fob, rob, dnb = (b.reshape(1, width) for b in (feat_out_bias, row_out_bias, down_bias))
    fq = jnp.transpose(feat_qkv, (1, 0, 2))
    rq = jnp.transpose(row_qkv, (1, 0, 2))

    near, far = masks[:2], masks[2:]
    over = lambda v, mask: swap(v, "tensor", 2) if mask == "x" else swap(v, "dp", mask)
    core = lambda v: swap(v, "tensor", 1)

    own = pack(t, rq, feat_out, row_out, up_bias)
    own_far = swap(own, "tensor", 2)
    *mixed, both = feature_forward(t, cells, norm_gains, norm_biases, fq, up_weight, down_weight, columns)
    kept = Box(mixed[0])
    own_far = tied(own_far, kept)
    packs = own, core(own), own_far, core(own_far)
    mixed = [kept.value] + [swap(mixed[k], "tensor", k) for k in (1, 2, 3)]
    a2, a3 = Box(mixed[2]), Box(mixed[3])
    both_far = swap(tied(both, a2, a3), "tensor", 2)
    mixed[2:] = a2.value, a3.value

    first, n2, row_packed, row_p, o2, second, n3 = row_forward(
        t, splits, mixed, cells, packs, fob, rob, norm_gains, norm_biases, columns)
    out_a, dn3_a, hg0, hg1, bg0, bg1 = hidden_call(t, n3, grads, (both, core(both)), packs[:2], columns)
    kept, fq_kept = Box(out_a), Box(hg0)
    both_far = tied(both_far, kept)
    fq_far = swap(tied(fq, fq_kept), "tensor", 2)
    hg0 = fq_kept.value
    out_f, g2, stats_a, hg2, hidden_send, bg2, bg3 = hidden_call(
        t, n3, grads, (both_far, core(both_far)), packs[2:], columns,
        [kept.value, dn3_a, second, dnb, norm_gains, hg1])
    s0, near_send, s2, s3, stats_b, row_keep, row_send = row_backward(
        (*t, out_f), g2, first, row_packed, row_p, norm_gains, n2, o2, mixed, fq, fq_far, packs, row_count)
    pieces = [s0, core(near_send), swap(s2, "tensor", 2), swap(s3, "tensor", 3)]
    near_got = pieces[1]
    K = KNOBS
    boxes = {"s0": Box(s0), "rs": Box(row_send)}
    hidden_got = core(tied(hidden_send, boxes[K["hs_tie"]]) if K["hs_tie"] else hidden_send)
    pieces[0] = boxes["s0"].value
    row_got = core(boxes["rs"].value)

    last = [s0]
    boxes.update(out=Box(out_f), w=Box(pieces[3]), w2=Box(pieces[2]))
    out_far = None
    if K["out_tie"] == "s0":
        out_far = swap(tied(out_f, boxes["s0"]), "tensor", 2)
        pieces[0] = boxes["s0"].value
    if K["out_tie"] == "hs":
        out_far = swap(out_f, "tensor", 2)
    for what in K["window"]:
        if what == "A":
            n1, feat_packed, feat_p = feature_again(
                (*t, *last), cells, norm_gains, norm_biases, fq, fq_far, near_got, columns, share)
            last = [feat_p]
        elif what == "M":
            ak, a_sent, bk, b_sent = first_halves((*t, *last), hg0, hg2, row_keep, hidden_got, row_got, near)
            last = [ak]
            ar, br = over(a_sent, near[0]), over(b_sent, near[1])
        else:
            last = [*last, pieces[2], pieces[3]]
    if K["out_tie"] == "w":
        out_far = swap(tied(out_f, boxes["w"], boxes["w2"]), "tensor", 2)
        pieces[2:] = boxes["w2"].value, boxes["w"].value

    g1, dqkv_f, f0, f2, f1, f3 = feature_backward((*t, *last), pieces, packs, feat_packed, feat_p, n1)
    g0, small = feature_input(
        t, cells, g1, dqkv_f, norm_gains, fq, fq_far, near_got, (stats_a, stats_b, bg0, bg1, bg2, bg3), share)
    f_got = core(f1), core(f3)
    small_got = core(small)
    last = [small]

    state = {"O": 0, "F": 0}
    grads_other = feat_grad = None

    def step_other(last):
        nonlocal ak, ar, bk, br, ab, abr, grads_other
        here = state["O"]
        tt = (*t, *last)
        if here == 0:
            ak, a_sent, bk, b_sent = out = second_halves(tt, ak, ar, bk, br, near)
            ar, br = over(a_sent, near[1]), over(b_sent, near[0])
        elif here == 1:
            ab, sent = out = groups_apart(tt, ak, ar, bk, br)
            abr = over(sent, "x")
        elif here < 2 + len(far):
            ab, = out = sums(tt, ab, abr)
            abr = over(ab, far[here - 2])
        elif here == 2 + len(far):
            ak, bk = out = sums_apart(tt, ab, abr)
            ar, br = over(ak, near[1]), over(bk, near[0])
        elif here == 3 + len(far):
            ak, bk = out = joins(tt, ((ak, ar), (bk, br)), (near[1], near[0]))
            ar, br = over(ak, near[0]), over(bk, near[1])
        else:
            grads_other = out = finish(tt, (ak, ar), (bk, br), near, width)
        state["O"] += 1
        return out[:1]

    def step_feature(last):
        nonlocal fk, fr, feat_grad, small_sums
        here = state["F"]
        tt = (*t, *last)
        if here == 0:
            fk, sent = out = feature_groups(tt, (f0, f2), f_got, small, small_got)
            fr = over(sent, "x")
        elif here < 3:
            fk, sent = out = half_sums(tt, fk, fr, near[here - 1])
            fr = over(sent, near[here - 1])
        elif here < 3 + len(far):
            fk, = out = sums(tt, fk, fr)
            fr = over(fk, far[here - 3])
        elif here == 3 + len(far):
            fk, = out = sums(tt, fk, fr)
            fr = over(fk, near[1])
        elif here == 4 + len(far):
            fk, = out = joins(tt, ((fk, fr),), (near[1],))
            fr = over(fk, near[0])
        else:
            feat_grad, small_sums = out = finish_feature(tt, fk, fr, near[0], width, small.shape[0] // 4)
        state["F"] += 1
        return out[:1]

    ab = abr = fk = fr = small_sums = g0_far = None
    steps = list(K["tail"])
    while steps or grads_other is None or feat_grad is None:
        what = steps.pop(0) if steps else ("O" if grads_other is None else "F")
        if what == "O" and grads_other is None:
            last = step_other(last)
        elif what == "F" and feat_grad is None:
            last = step_feature(last)
        elif what == "p":
            out_pair = pair((*t, *last), out_f, out_far)
            out_near = core(out_pair)
            last = [out_pair]
        elif what == "c":
            output = columns_home((*t, *last), out_f, out_far, out_near, feature_count, row_count)
            last = [output]
        elif what == "g":
            g0_pair = pair((*t, *last), g0, g0_far)
            g0_near = core(g0_pair)
            last = [g0_pair]
        elif what == "r":
            input_grad = rows_home((*t, *last), g0, g0_far, g0_near, feature_count, row_count)
            last = [input_grad]
        key = what + str(state.get(what, ""))
        if g0_far is None and key == K["g_tie"]:
            box = Box(last[0])
            g0_far = swap(tied(g0, box), "tensor", 2)
            last = [box.value]
    small = small_sums

    def qkv_shape(grad):
        return jnp.transpose(grad.reshape(3, width, HD), (1, 0, 2))

    home = lambda a: jnp.transpose(a, (1, 0, 2)).reshape(shape)
    return (
        home(output),
        home(input_grad),
        qkv_shape(feat_grad),
        grads_other[4],
        small[8],
        qkv_shape(grads_other[2]),
        grads_other[3],
        small[1],
        grads_other[0],
        lax.dynamic_index_in_dim(small, 16 + t[0][0], 0, keepdims=False),
        grads_other[1],
        small[0],
        jnp.stack([small[4], small[9], small[2]]),
        jnp.stack([small[5], small[10], small[3]]),
    )


def solution(mesh):
    return jax.shard_map(
        shards,
        mesh=mesh,
        in_specs=(
            P("dp", None, None, None), P("dp"), P(None, None, "tensor"), P("tensor", None), P(),
            P(None, None, "tensor"), P("tensor", None), P(), P(None, "tensor"), P("tensor"),
            P("tensor", None), P(), P(), P(), P("dp", None, None, None),
        ),
        out_specs=(
            P("dp", None, None, None), P("dp", None, None, None), P(None, None, "tensor"),
            P("tensor", None), P(), P(None, None, "tensor"), P("tensor", None), P(),
            P(None, "tensor"), P("tensor"), P("tensor", None), P(), P(), P(),
        ),
        check_vma=False,
    )
```

time: 228 us -> 208 us (0.912)
  waiting for transfers between devices: 97.8 us -> 63.6 us
  Pallas kernels: 79 us -> 87.3 us
  local copies, waits for them, and re-layouts: 8.13 us -> 14.3 us
    ppermute x47 -> x38, waiting for transfers between devices: 97.8 us -> 63.6 us  [swap(): return lax.ppermute(values, axis, [(i, i ^ mask) for i in range(count)])]
    pallas_call x26 -> x27, Pallas kernels: 79 us -> 87.3 us  [call(): pl.pallas_call(body, grid_spec=spec, out_shape=[a for a, _ in outs], comp...]
    unnamed x38 -> x54, local copies, waits for them, and re-layouts: 6.21 us -> 13.7 us
    ppermute x47 -> x38, starting transfers between devices: 36.9 us -> 36.7 us  [swap(): return lax.ppermute(values, axis, [(i, i ^ mask) for i in range(count)])]
  transfers between devices with their start and end apart: 47 -> 38, of which waited for: 23 -> 17; matrix products, arithmetic and copies ran while one was open for 0% -> 0% of each run, Pallas kernels for 21% -> 35%
where the time goes in v4:
time: 208 us; the launch traced here: 205 us
  Pallas kernels  87.3 us (42%)
  waiting for transfers between devices  63.6 us (31%)
  starting transfers between devices  36.7 us (18%)
  local copies, waits for them, and re-layouts  14.3 us (7%)
  between operations  2.12 us (1%)
    pallas_call x27, Pallas kernels, call(): pl.pallas_call(body, grid_spec=spec, out_shape=[a for a, _ in outs], comp...  87.3 us
    ppermute x38, waiting for transfers between devices, swap(): return lax.ppermute(values, axis, [(i, i ^ mask) for i in range(count)])  63.6 us
    ppermute x38, starting transfers between devices, swap(): return lax.ppermute(values, axis, [(i, i ^ mask) for i in range(count)])  36.7 us
    unnamed x54, local copies, waits for them, and re-layouts  13.7 us
  transfers between devices with their start and end apart: 38, of which 17 were waited for; matrix products, arithmetic and copies ran while one was open for 0% of the time, Pallas kernels for 35%

profile of v4, /device:TPU:0, one launch (start us, length us, event | category | flops | bytes accessed | tf_op | source)
XLA Modules:
  0.0 204.7 jit_solution(7660013798914886776)
XLA Ops:
  0.7 2.0 pack.1.refs_8_.refs_12_.refs_16_.refs_6_.refs_15_.refs_19_
  2.7 2.9 %collective-permute-start = (bf16[2576,128]{1,0:T(8,128)(2,1)}, bf16[2576,128]{1,0:T(8,128)(2,1)}, u32[]{:S(2)}, u32[]{:S(2)}) collective-permute-start(bf16[2576,128]{1,0:T(8,128)(2,1)} %pack.1.refs_8_.refs_12_.refs_16_.refs_6_.refs_15_.refs_19_), channel_id=1, source_target_pairs={{0,2},{1,3},{2,0},{3,1},{4,6},{5,7},{6,4},{7,5},{8,10},{9,11},{10,... | collective-permute-start | bytes 1978376 | tf_op jit(solution)/shard_map/ppermute | solution.py:614
  5.6 14.4 %feature_forward.1 = (bf16[2,384,128]{2,1,0:T(8,128)(2,1)}, bf16[2,384,128]{2,1,0:T(8,128)(2,1)}, bf16[2,384,128]{2,1,0:T(8,128)(2,1)}, bf16[2,384,128]{2,1,0:T(8,128)(2,1)}, bf16[1024,512]{1,0:T(8,128)(2,1)}) custom-call(s32[1]{0:T(128)} %bitcast.refs_0_, s32[1]{0:T(128)} %bitcast.1.refs_1_, bf16[89,32,512]{2,1,0:T(8,128)(2,1)} %bitcast.26, ...), custom_call_target="tpu_custom_call" | custom-call | flops 1 | bytes 1 | tf_op jit(solution)/shard_map/feature_forward/pallas_call | solution.py:134
  21.0 1.2 collective-permute-start.7
  22.2 5.9 %collective-permute-done.2.refs_5_.refs_11_ = bf16[2,384,128]{2,1,0:T(8,128)(2,1)S(1)} collective-permute-done((bf16[2,384,128]{2,1,0:T(8,128)(2,1)}, bf16[2,384,128]{2,1,0:T(8,128)(2,1)S(1)}, u32[]{:S(2)}, u32[]{:S(2)}) %collective-permute-start.2) | collective-permute-done | bytes 196640 | tf_op jit(solution)/shard_map/ppermute | solution.py:614
  28.1 1.3 collective-permute-done.3.refs_6_.refs_12_
  31.9 2.1 %collective-permute-done.1.refs_4_.refs_10_ = bf16[2,384,128]{2,1,0:T(8,128)(2,1)S(1)} collective-permute-done((bf16[2,384,128]{2,1,0:T(8,128)(2,1)}, bf16[2,384,128]{2,1,0:T(8,128)(2,1)S(1)}, u32[]{:S(2)}, u32[]{:S(2)}) %collective-permute-start.1) | collective-permute-done | bytes 196640 | tf_op jit(solution)/shard_map/ppermute | solution.py:614
  35.0 10.4 %row_forward.1 = (f32[768,512]{1,0:T(8,128)S(1)}, bf16[768,512]{1,0:T(8,128)(2,1)S(1)}, bf16[768,1536]{1,0:T(8,128)(2,1)S(1)}, bf16[4,6,128,128]{3,2,1,0:T(8,128...) custom-call(s32[1]{0:T(128)} %bitcast.refs_0_, s32[1]{0:T(128)} %bitcast.1.refs_1_, ...), custom_call_target="tpu_custom_call" | custom-call | flops 1 | bytes 1 | tf_op jit(solution)/shard_map/row_forward/pallas_call | solution.py:134
  48.3 7.2 %hidden_first.1 = (f32[768,512]{1,0:T(8,128)S(1)}, f32[768,512]{1,0:T(8,128)S(1)}, bf16[1024,512]{1,0:T(8,128)(2,1)S(1)}, bf16[1024,512]{1,0:T(8,128)(2,1)S(1)},...) custom-call(s32[1]{0:T(128)} %bitcast.refs_0_, s32[1]{0:T(128)} %bitcast.1.refs_1_, ...), custom_call_target="tpu_custom_call" | custom-call | flops 1 | bytes 1 | tf_op jit(solution)/shard_map/hidden_first/pallas_call | solution.py:134
  56.9 1.7 collective-permute-start.9
  59.3 1.4 copy-done.8
  60.8 1.4 copy-done.10
  62.2 10.0 %hidden_second.1 = (bf16[768,512]{1,0:T(8,128)(2,1)S(1)}, f32[768,512]{1,0:T(8,128)S(1)}, f32[8,512]{1,0:T(8,128)S(1)}, bf16[1024,512]{1,0:T(8,128)(2,1)S(1)}, b...) custom-call(s32[1]{0:T(128)} %bitcast.refs_0_, s32[1]{0:T(128)} %bitcast.1.refs_1_, ...), custom_call_target="tpu_custom_call" | custom-call | flops 1 | bytes 1 | tf_op jit(solution)/shard_map/hidden_second/pallas_call | solution.py:134
  73.2 12.0 %row_backward.1 = (bf16[192,512]{1,0:T(8,128)(2,1)S(1)}, bf16[960,512]{1,0:T(8,128)(2,1)S(1)}, bf16[192,512]{1,0:T(8,128)(2,1)S(1)}, bf16[192,512]{1,0:T(8,128)(...) custom-call(s32[1]{0:T(128)} %bitcast.refs_0_, ...), custom_call_target="tpu_custom_call" | custom-call | flops 1 | bytes 1 | tf_op jit(solution)/shard_map/row_backward/pallas_call | solution.py:134
  85.9 1.5 collective-permute-start.10
  87.9 4.8 %collective-permute-done.13.refs_6_.refs_8_.refs_3_.refs_7_.refs_9_ = bf16[960,512]{1,0:T(8,128)(2,1)S(1)} collective-permute-done((bf16[960,512]{1,0:T(8,128)(2,1)S(1)}, bf16[960,512]{1,0:T(8,128)(2,1)S(1)}, u32[]{:S(2)}, u32[]{:S(2)}) %collective-permute-start.13) | collective-permute-done | bytes 983072 | tf_op jit(solution)/shard_map/ppermute | solution.py:614
  92.6 4.0 %feature_again.1 = (bf16[768,512]{1,0:T(8,128)(2,1)S(1)}, bf16[8,96,1536]{2,1,0:T(8,128)(2,1)S(1)}, bf16[8,4,96,96]{3,2,1,0:T(8,128)(2,1)S(1)}) custom-call(s32[1]{0:T(128)} %bitcast.refs_0_, s32[1]{0:T(128)} %bitcast.1.refs_1_, bf16[89,32,512]{2,1,0:T(8,128)(2,1)S(1)} %bitcast.28, bf16[3,512]{1,0:T(4,128)(2,1)S(1)} %copy-done.22, ...), custom_call_target="tpu_custom_call" | custom-call | flops 1 | bytes 1 | tf_op jit(solution)/shard_map/feature_again/pallas_call | solution.py:134
  96.7 1.4 ab_first.1
  98.1 1.7 collective-permute-start.19
  99.8 1.6 collective-permute-start.20
  101.4 1.5 collective-permute-start.12
  102.9 11.9 %feature_backward.1 = (f32[768,512]{1,0:T(8,128)S(1)}, bf16[768,1536]{1,0:T(8,128)(2,1)S(1)}, bf16[1536,128]{1,0:T(8,128)(2,1)S(1)}, bf16[1536,128]{1,0:T(8,128)...) custom-call(s32[1]{0:T(128)} %bitcast.refs_0_, s32[1]{0:T(128)} %bitcast.1.refs_1_, ...), custom_call_target="tpu_custom_call" | custom-call | flops 1 | bytes 1 | tf_op jit(solution)/shard_map/feature_backward/pallas_call | solution.py:134
  115.3 2.4 %feature_input.1 = (bf16[720,512]{1,0:T(8,128)(2,1)S(1)}, f32[128,128]{1,0:T(8,128)S(1)}) custom-call(s32[1]{0:T(128)} %bitcast.refs_0_, s32[1]{0:T(128)} %bitcast.1.refs_1_, bf16[89,32,512]{2,1,0:T(8,128)(2,1)S(1)} %bitcast.29, f32[768,512]{1,0:T(8,128)S(1)} %get-tuple-element.148.refs_3_, bf16[768,1536]{1,0:T(8,128)(2,1)S(1)} %get-tuple-element.149.refs_4_, ...), custom_call_target="tpu_custom_call" | custom-call | flops 1 | bytes 1 | tf_op jit(solution)/shard_map/feature_input/pallas_call | solution.py:134
  117.7 1.6 collective-permute-done.19.refs_3_
  119.3 1.5 collective-permute-done.20.refs_5_
  121.4 1.6 collective-permute-start.24
  122.9 1.6 collective-permute-start.22
  125.8 6.9 %collective-permute-done.24.refs_3_ = bf16[1664,128]{1,0:T(8,128)(2,1)S(1)} collective-permute-done((bf16[1664,128]{1,0:T(8,128)(2,1)S(1)}, bf16[1664,128]{1,0:T(8,128)(2,1)S(1)}, u32[]{:S(2)}, u32[]{:S(2)}) %collective-permute-start.24) | collective-permute-done | bytes 426016 | tf_op jit(solution)/shard_map/ppermute | solution.py:614
  132.8 1.3 collective-permute-done.22.refs_3_
  134.1 1.3 collective-permute-done.23.refs_5_
  136.2 1.5 collective-permute-start.26
  137.7 4.3 %collective-permute-done.26.refs_3_ = bf16[832,128]{1,0:T(8,128)(2,1)S(1)} collective-permute-done((bf16[832,128]{1,0:T(8,128)(2,1)S(1)}, bf16[832,128]{1,0:T(8,128)(2,1)S(1)}, u32[]{:S(2)}, u32[]{:S(2)}) %collective-permute-start.26) | collective-permute-done | bytes 213024 | tf_op jit(solution)/shard_map/ppermute | solution.py:614
  142.1 3.5 %collective-permute-done.25.refs_3_ = bf16[416,512]{1,0:T(8,128)(2,1)S(1)} collective-permute-done((bf16[416,512]{1,0:T(8,128)(2,1)S(1)}, bf16[416,512]{1,0:T(8,128)(2,1)S(1)}, u32[]{:S(2)}, u32[]{:S(2)}) %collective-permute-start.25) | collective-permute-done | bytes 426016 | tf_op jit(solution)/shard_map/ppermute | solution.py:614
  146.3 2.6 %collective-permute-start.28 = (bf16[416,512]{1,0:T(8,128)(2,1)S(1)}, bf16[416,512]{1,0:T(8,128)(2,1)S(1)}, u32[]{:S(2)}, u32[]{:S(2)}) collective-permute-start(bf16[416,512]{1,0:T(8,128)(2,1)S(1)} %sums.3.refs_6_.refs_2_), channel_id=1, source_target_pairs={{0,16},{4,20},{8,24},{12,28},{16,0},{20,4},{24,8},{28,12},{1,17},{... | collective-permute-start | bytes 1277960 | tf_op jit(solution)/shard_map/ppermute | solution.py:614
  149.7 2.1 %columns_home.1.refs_4_ = bf16[89,32,512]{2,1,0:T(8,128)(2,1)} custom-call(s32[1]{0:T(128)} %bitcast.refs_0_, s32[1]{0:T(128)} %bitcast.1.refs_1_, bf16[768,512]{1,0:T(8,128)(2,1)S(1)} %get-tuple-element.128.refs_23_.refs_2_, bf16[1536,512]{1,0:T(8,128)(2,1)S(1)} %collective-permute-done.21.refs_3_.refs_5_, ...), custom_call_target="tpu_custom_call" | custom-call | flops 1 | bytes 1 | tf_op jit(solution)/shard_map/columns_home/pallas_call | solution.py:134
  151.8 5.8 %collective-permute-done.29.refs_3_ = bf16[416,128]{1,0:T(8,128)(2,1)S(1)} collective-permute-done((bf16[416,128]{1,0:T(8,128)(2,1)S(1)}, bf16[416,128]{1,0:T(8,128)(2,1)S(1)}, u32[]{:S(2)}, u32[]{:S(2)}) %collective-permute-start.29) | collective-permute-done | bytes 106528 | tf_op jit(solution)/shard_map/ppermute | solution.py:614
  157.5 1.8 copy-done.4
  159.4 5.7 %collective-permute-done.28.refs_3_ = bf16[416,512]{1,0:T(8,128)(2,1)S(1)} collective-permute-done((bf16[416,512]{1,0:T(8,128)(2,1)S(1)}, bf16[416,512]{1,0:T(8,128)(2,1)S(1)}, u32[]{:S(2)}, u32[]{:S(2)}) %collective-permute-start.28) | collective-permute-done | bytes 426016 | tf_op jit(solution)/shard_map/ppermute | solution.py:614
  165.8 2.5 %collective-permute-start.32 = (bf16[208,512]{1,0:T(8,128)(2,1)S(1)}, bf16[208,512]{1,0:T(8,128)(2,1)S(1)}, u32[]{:S(2)}, u32[]{:S(2)}) collective-permute-start(bf16[208,512]{1,0:T(8,128)(2,1)S(1)} %get-tuple-element.176.refs_4_), channel_id=1, source_target_pairs={{0,4},{4,0},{8,12},{12,8},{16,20},{20,16},{24,28},{28,24},{1,5},{5... | collective-permute-start | bytes 638984 | tf_op jit(solution)/shard_map/ppermute | solution.py:614
  168.2 3.4 %collective-permute-start.33 = (bf16[416,128]{1,0:T(8,128)(2,1)S(1)}, bf16[416,128]{1,0:T(8,128)(2,1)S(1)}, u32[]{:S(2)}, u32[]{:S(2)}) collective-permute-start(bf16[416,128]{1,0:T(8,128)(2,1)S(1)} %sums.4.refs_4_.refs_2_), channel_id=1, source_target_pairs={{0,16},{4,20},{8,24},{12,28},{16,0},{20,4},{24,8},{28,12},{1,17},{... | collective-permute-start | bytes 319496 | tf_op jit(solution)/shard_map/ppermute | solution.py:614
  171.6 5.3 %collective-permute-done.33.refs_3_ = bf16[416,128]{1,0:T(8,128)(2,1)S(1)} collective-permute-done((bf16[416,128]{1,0:T(8,128)(2,1)S(1)}, bf16[416,128]{1,0:T(8,128)(2,1)S(1)}, u32[]{:S(2)}, u32[]{:S(2)}) %collective-permute-start.33) | collective-permute-done | bytes 106528 | tf_op jit(solution)/shard_map/ppermute | solution.py:614
  178.6 2.0 collective-permute-start.37
  180.7 2.8 %rows_home.1.refs_4_ = bf16[89,32,512]{2,1,0:T(8,128)(2,1)} custom-call(s32[1]{0:T(128)} %bitcast.refs_0_, s32[1]{0:T(128)} %bitcast.1.refs_1_, bf16[720,512]{1,0:T(8,128)(2,1)S(1)} %get-tuple-element.173.refs_2_, bf16[1440,512]{1,0:T(8,128)(2,1)S(1)} %collective-permute-done.30.refs_3_.refs_5_, ...), custom_call_target="tpu_custom_call" | custom-call | flops 1 | bytes 1 | tf_op jit(solution)/shard_map/rows_home/pallas_call | solution.py:134
  183.5 9.1 %collective-permute-done.34.refs_3_ = bf16[416,128]{1,0:T(8,128)(2,1)S(1)} collective-permute-done((bf16[416,128]{1,0:T(8,128)(2,1)S(1)}, bf16[416,128]{1,0:T(8,128)(2,1)S(1)}, u32[]{:S(2)}, u32[]{:S(2)}) %collective-permute-start.34) | collective-permute-done | bytes 106528 | tf_op jit(solution)/shard_map/ppermute | solution.py:614
  192.7 1.8 copy-done.2
  194.9 3.6 %finish.1 = (f32[512,512]{1,0:T(8,128)}, f32[512,512]{1,0:T(8,128)}, f32[1536,128]{1,0:T(8,128)}, f32[128,512]{1,0:T(8,128)}, f32[128,512]{1,0:T(8,128)}) custom-call(s32[1]{0:T(128)} %bitcast.refs_0_, s32[1]{0:T(128)} %bitcast.1.refs_1_, bf16[416,512]{1,0:T(8,128)(2,1)S(1)} %get-tuple-element.177.refs_6_.refs_2_, ...), custom_call_target="tpu_custom_call" | custom-call | flops 1 | bytes 1 | tf_op jit(solution)/shard_map/finish/pallas_call | solution.py:134
  198.4 2.4 %collective-permute-done.35.refs_3_ = bf16[832,128]{1,0:T(8,128)(2,1)S(1)} collective-permute-done((bf16[832,128]{1,0:T(8,128)(2,1)S(1)}, bf16[832,128]{1,0:T(8,128)(2,1)S(1)}, u32[]{:S(2)}, u32[]{:S(2)}) %collective-permute-start.35) | collective-permute-done | bytes 213024 | tf_op jit(solution)/shard_map/ppermute | solution.py:614
  200.8 1.2 copy-done.11
  (114 shorter events, 20.8 us)
Async XLA Ops:
  2.7 28.1 %collective-permute-start = (bf16[2576,128]{1,0:T(8,128)(2,1)}, bf16[2576,128]{1,0:T(8,128)(2,1)}, u32[]{:S(2)}, u32[]{:S(2)}) collective-permute-start(bf16[2576,128]{1,0:T(8,128)(2,1)} %pack.1.refs_8_.refs_12_.refs_16_.refs_6_.refs_15_.refs_19_), channel_id=1, source_target_pairs={{0,2},{1,3},{2,0},{3,1},{4,6},{5,7},{6,4},{7,5},{8,10},{9,11},{10,... | collective-permute-start | bytes 1978376 | tf_op jit(solution)/shard_map/ppermute | solution.py:614
  5.6 24.9 %copy-start.1 = (bf16[2576,128]{1,0:T(8,128)(2,1)S(1)}, bf16[2576,128]{1,0:T(8,128)(2,1)}, u32[]{:S(2)}) copy-start(bf16[2576,128]{1,0:T(8,128)(2,1)} %pack.1.refs_8_.refs_12_.refs_16_.refs_6_.refs_15_.refs_19_) | copy-start | bytes 1978372
  5.6 25.6 %copy-start.24 = (bf16[512]{0:T(512)(128)(2,1)S(1)}, bf16[512]{0:T(512)(128)(2,1)}, u32[]{:S(2)}) copy-start(bf16[512]{0:T(512)(128)(2,1)} %param.19) | copy-start | bytes 3076
  5.6 25.7 %copy-start.25 = (bf16[512]{0:T(512)(128)(2,1)S(1)}, bf16[512]{0:T(512)(128)(2,1)}, u32[]{:S(2)}) copy-start(bf16[512]{0:T(512)(128)(2,1)} %param.22) | copy-start | bytes 3076
  5.6 28.5 %copy-start = (bf16[1,32,89,512]{3,1,2,0:T(8,128)(2,1)S(1)}, bf16[1,32,89,512]{3,1,2,0:T(8,128)(2,1)}, u32[]{:S(2)}) copy-start(bf16[1,32,89,512]{3,1,2,0:T(8,128)(2,1)} %param.15) | copy-start | bytes 8749060
  5.6 28.5 %copy-start.22 = (bf16[3,512]{1,0:T(4,128)(2,1)S(1)}, bf16[3,512]{1,0:T(4,128)(2,1)}, u32[]{:S(2)}) copy-start(bf16[3,512]{1,0:T(4,128)(2,1)} %refs_5_.3) | copy-start | bytes 9220
  5.6 28.5 %copy-start.23 = (bf16[3,512]{1,0:T(4,128)(2,1)S(1)}, bf16[3,512]{1,0:T(4,128)(2,1)}, u32[]{:S(2)}) copy-start(bf16[3,512]{1,0:T(4,128)(2,1)} %refs_4_.5) | copy-start | bytes 9220
  20.0 8.1 %collective-permute-start.2 = (bf16[2,384,128]{2,1,0:T(8,128)(2,1)}, bf16[2,384,128]{2,1,0:T(8,128)(2,1)S(1)}, u32[]{:S(2)}, u32[]{:S(2)}) collective-permute-start(bf16[2,384,128]{2,1,0:T(8,128)(2,1)} %get-tuple-element.104), channel_id=1, source_target_pairs={{0,2},{1,3},{2,0},{3,1},{4,6},{5,7},{6,4},{7,5},{8,10},{9,11},{10,... | collective-permute-start | bytes 589832 | tf_op jit(solution)/shard_map/ppermute | solution.py:614
  20.1 9.3 %collective-permute-start.3 = (bf16[2,384,128]{2,1,0:T(8,128)(2,1)}, bf16[2,384,128]{2,1,0:T(8,128)(2,1)S(1)}, u32[]{:S(2)}, u32[]{:S(2)}) collective-permute-start(bf16[2,384,128]{2,1,0:T(8,128)(2,1)} %get-tuple-element.105), channel_id=1, source_target_pairs={{0,3},{1,2},{2,1},{3,0},{4,7},{5,6},{6,5},{7,4},{8,11},{9,10},{10,... | collective-permute-start | bytes 589832 | tf_op jit(solution)/shard_map/ppermute | solution.py:614
  21.0 27.3 %collective-permute-start.7 = (bf16[1024,512]{1,0:T(8,128)(2,1)}, bf16[1024,512]{1,0:T(8,128)(2,1)S(1)}, u32[]{:S(2)}, u32[]{:S(2)}) collective-permute-start(bf16[1024,512]{1,0:T(8,128)(2,1)} %get-tuple-element.110.refs_4_.refs_8_), channel_id=1, source_target_pairs={{0,1},{1,0},{2,3},{3,2},{4,5},{5,4},{6,7},{7,6},{8,9},{9,8},{10,11... | collective-permute-start | bytes 3145736 | tf_op jit(solution)/shard_map/ppermute | solution.py:614
  29.4 27.3 %collective-permute-start.6 = (bf16[1024,512]{1,0:T(8,128)(2,1)}, bf16[1024,512]{1,0:T(8,128)(2,1)S(1)}, u32[]{:S(2)}, u32[]{:S(2)}) collective-permute-start(bf16[1024,512]{1,0:T(8,128)(2,1)} %get-tuple-element.110.refs_4_.refs_8_), channel_id=1, source_target_pairs={{0,2},{1,3},{2,0},{3,1},{4,6},{5,7},{6,4},{7,5},{8,10},{9,11},{10,... | collective-permute-start | bytes 3145736 | tf_op jit(solution)/shard_map/ppermute | solution.py:614
  30.5 3.5 %collective-permute-start.4 = (bf16[2576,128]{1,0:T(8,128)(2,1)S(1)}, bf16[2576,128]{1,0:T(8,128)(2,1)S(1)}, u32[]{:S(2)}, u32[]{:S(2)}) collective-permute-start(bf16[2576,128]{1,0:T(8,128)(2,1)S(1)} %copy-done.1), channel_id=1, source_target_pairs={{0,1},{1,0},{2,3},{3,2},{4,5},{5,4},{6,7},{7,6},{8,9},{9,8},{10,11... | collective-permute-start | bytes 1978376 | tf_op jit(solution)/shard_map/ppermute | solution.py:614
  30.7 3.3 %collective-permute-start.5 = (bf16[2576,128]{1,0:T(8,128)(2,1)}, bf16[2576,128]{1,0:T(8,128)(2,1)S(1)}, u32[]{:S(2)}, u32[]{:S(2)}) collective-permute-start(bf16[2576,128]{1,0:T(8,128)(2,1)} %collective-permute-done.refs_10_.refs_14_.refs_18_.refs_6_.refs_17_.refs_21_.refs_8_), channel_id=1, source_target_pairs={{0,1},{1,0},{2,3},{3,2},{4,5},{5,4},{6,7},{7,6},{8,9},{9,8},{10,11... | collective-permute-start | bytes 1978376 | tf_op jit(solution)/shard_map/ppermute | solution.py:614
  31.1 3.0 %collective-permute-start.1 = (bf16[2,384,128]{2,1,0:T(8,128)(2,1)}, bf16[2,384,128]{2,1,0:T(8,128)(2,1)S(1)}, u32[]{:S(2)}, u32[]{:S(2)}) collective-permute-start(bf16[2,384,128]{2,1,0:T(8,128)(2,1)} %get-tuple-element.102), channel_id=1, source_target_pairs={{0,1},{1,0},{2,3},{3,2},{4,5},{5,4},{6,7},{7,6},{8,9},{9,8},{10,11... | collective-permute-start | bytes 589832 | tf_op jit(solution)/shard_map/ppermute | solution.py:614
  31.9 16.4 %copy-start.6 = (bf16[1024,512]{1,0:T(8,128)(2,1)S(1)}, bf16[1024,512]{1,0:T(8,128)(2,1)}, u32[]{:S(2)}) copy-start(bf16[1024,512]{1,0:T(8,128)(2,1)} %get-tuple-element.110.refs_4_.refs_8_) | copy-start | bytes 3145732
  35.0 13.3 %copy-start.3 = (bf16[1,32,89,512]{3,1,2,0:T(8,128)(2,1)S(1)}, bf16[1,32,89,512]{3,1,2,0:T(8,128)(2,1)}, u32[]{:S(2)}) copy-start(bf16[1,32,89,512]{3,1,2,0:T(8,128)(2,1)} %param.29) | copy-start | bytes 8749060
  56.7 2.7 %collective-permute-start.8 = (bf16[1024,512]{1,0:T(8,128)(2,1)S(1)}, bf16[1024,512]{1,0:T(8,128)(2,1)S(1)}, u32[]{:S(2)}, u32[]{:S(2)}) collective-permute-start(bf16[1024,512]{1,0:T(8,128)(2,1)S(1)} %collective-permute-done.6.refs_4_.refs_8_), channel_id=1, source_target_pairs={{0,1},{1,0},{2,3},{3,2},{4,5},{5,4},{6,7},{7,6},{8,9},{9,8},{10,11... | collective-permute-start | bytes 3145736 | tf_op jit(solution)/shard_map/ppermute | solution.py:614
  56.9 16.2 %collective-permute-start.9 = (bf16[3,512,128]{2,1,0:T(8,128)(2,1)S(1)}, bf16[3,512,128]{2,1,0:T(8,128)(2,1)S(1)}, u32[]{:S(2)}, u32[]{:S(2)}) collective-permute-start(bf16[3,512,128]{2,1,0:T(8,128)(2,1)S(1)} %bitcast.35), channel_id=1, source_target_pairs={{0,2},{1,3},{2,0},{3,1},{4,6},{5,7},{6,4},{7,5},{8,10},{9,11},{10,... | collective-permute-start | bytes 1179656 | tf_op jit(solution)/shard_map/ppermute | solution.py:614
  62.2 11.0 %copy-start.19 = (bf16[768,512]{1,0:T(8,128)(2,1)S(1)}, bf16[768,512]{1,0:T(8,128)(2,1)}, u32[]{:S(2)}) copy-start(bf16[768,512]{1,0:T(8,128)(2,1)} %copy-done.18) | copy-start | bytes 2359300
  62.2 11.0 %copy-start.21 = (bf16[2,384,128]{2,1,0:T(8,128)(2,1)S(1)}, bf16[2,384,128]{2,1,0:T(8,128)(2,1)}, u32[]{:S(2)}) copy-start(bf16[2,384,128]{2,1,0:T(8,128)(2,1)} %get-tuple-element.101.refs_3_.refs_9_) | copy-start | bytes 589828
  85.1 11.6 %collective-permute-start.14 = (bf16[2048,512]{1,0:T(8,128)(2,1)}, bf16[2048,512]{1,0:T(8,128)(2,1)S(1)}, u32[]{:S(2)}, u32[]{:S(2)}) collective-permute-start(bf16[2048,512]{1,0:T(8,128)(2,1)} %get-tuple-element.141), channel_id=1, source_target_pairs={{0,1},{1,0},{2,3},{3,2},{4,5},{5,4},{6,7},{7,6},{8,9},{9,8},{10,11... | collective-permute-start | bytes 6291464 | tf_op jit(solution)/shard_map/ppermute | solution.py:614
  85.4 11.3 %collective-permute-start.15 = (bf16[2,640,512]{2,1,0:T(8,128)(2,1)S(1)}, bf16[2,640,512]{2,1,0:T(8,128)(2,1)S(1)}, u32[]{:S(2)}, u32[]{:S(2)}) collective-permute-start(bf16[2,640,512]{2,1,0:T(8,128)(2,1)S(1)} %get-tuple-element.142), channel_id=1, source_target_pairs={{0,1},{1,0},{2,3},{3,2},{4,5},{5,4},{6,7},{7,6},{8,9},{9,8},{10,11... | collective-permute-start | bytes 3932168 | tf_op jit(solution)/shard_map/ppermute | solution.py:614
  85.7 6.9 %collective-permute-start.13 = (bf16[960,512]{1,0:T(8,128)(2,1)S(1)}, bf16[960,512]{1,0:T(8,128)(2,1)S(1)}, u32[]{:S(2)}, u32[]{:S(2)}) collective-permute-start(bf16[960,512]{1,0:T(8,128)(2,1)S(1)} %get-tuple-element.132), channel_id=1, source_target_pairs={{0,1},{1,0},{2,3},{3,2},{4,5},{5,4},{6,7},{7,6},{8,9},{9,8},{10,11... | collective-permute-start | bytes 2949128 | tf_op jit(solution)/shard_map/ppermute | solution.py:614
  85.9 15.5 %collective-permute-start.10 = (bf16[192,512]{1,0:T(8,128)(2,1)S(1)}, bf16[192,512]{1,0:T(8,128)(2,1)S(1)}, u32[]{:S(2)}, u32[]{:S(2)}) collective-permute-start(bf16[192,512]{1,0:T(8,128)(2,1)S(1)} %get-tuple-element.126), channel_id=1, source_target_pairs={{0,3},{1,2},{2,1},{3,0},{4,7},{5,6},{6,5},{7,4},{8,11},{9,10},{10,... | collective-permute-start | bytes 589832 | tf_op jit(solution)/shard_map/ppermute | solution.py:614
  87.4 14.0 %collective-permute-start.11 = (bf16[192,512]{1,0:T(8,128)(2,1)S(1)}, bf16[192,512]{1,0:T(8,128)(2,1)S(1)}, u32[]{:S(2)}, u32[]{:S(2)}) collective-permute-start(bf16[192,512]{1,0:T(8,128)(2,1)S(1)} %get-tuple-element.127), channel_id=1, source_target_pairs={{0,2},{1,3},{2,0},{3,1},{4,6},{5,7},{6,4},{7,5},{8,10},{9,11},{10,... | collective-permute-start | bytes 589832 | tf_op jit(solution)/shard_map/ppermute | solution.py:614
  98.1 21.1 %collective-permute-start.19 = (bf16[2,416,512]{2,1,0:T(8,128)(2,1)S(1)}, bf16[2,416,512]{2,1,0:T(8,128)(2,1)S(1)}, u32[]{:S(2)}, u32[]{:S(2)}) collective-permute-start(bf16[2,416,512]{2,1,0:T(8,128)(2,1)S(1)} %get-tuple-element.157), channel_id=1, source_target_pairs={{0,4},{4,0},{8,12},{12,8},{16,20},{20,16},{24,28},{28,24},{1,5},{5... | collective-permute-start | bytes 2555912 | tf_op jit(solution)/shard_map/ppermute | solution.py:614
  99.8 20.9 %collective-permute-start.20 = (bf16[2,416,512]{2,1,0:T(8,128)(2,1)S(1)}, bf16[2,416,512]{2,1,0:T(8,128)(2,1)S(1)}, u32[]{:S(2)}, u32[]{:S(2)}) collective-permute-start(bf16[2,416,512]{2,1,0:T(8,128)(2,1)S(1)} %get-tuple-element.159), channel_id=1, source_target_pairs={{0,8},{4,12},{8,0},{12,4},{16,24},{20,28},{24,16},{28,20},{1,9},{5... | collective-permute-start | bytes 2555912 | tf_op jit(solution)/shard_map/ppermute | solution.py:614
  101.4 24.2 %collective-permute-start.12 = (bf16[768,512]{1,0:T(8,128)(2,1)S(1)}, bf16[768,512]{1,0:T(8,128)(2,1)S(1)}, u32[]{:S(2)}, u32[]{:S(2)}) collective-permute-start(bf16[768,512]{1,0:T(8,128)(2,1)S(1)} %get-tuple-element.128.refs_23_.refs_2_), channel_id=1, source_target_pairs={{0,2},{1,3},{2,0},{3,1},{4,6},{5,7},{6,4},{7,5},{8,10},{9,11},{10,... | collective-permute-start | bytes 2359304 | tf_op jit(solution)/shard_map/ppermute | solution.py:614
  114.8 6.4 %collective-permute-start.16 = (bf16[1536,128]{1,0:T(8,128)(2,1)S(1)}, bf16[1536,128]{1,0:T(8,128)(2,1)S(1)}, u32[]{:S(2)}, u32[]{:S(2)}) collective-permute-start(bf16[1536,128]{1,0:T(8,128)(2,1)S(1)} %get-tuple-element.146), channel_id=1, source_target_pairs={{0,1},{1,0},{2,3},{3,2},{4,5},{5,4},{6,7},{7,6},{8,9},{9,8},{10,11... | collective-permute-start | bytes 1179656 | tf_op jit(solution)/shard_map/ppermute | solution.py:614
  114.8 6.3 %collective-permute-start.17 = (bf16[1536,128]{1,0:T(8,128)(2,1)S(1)}, bf16[1536,128]{1,0:T(8,128)(2,1)S(1)}, u32[]{:S(2)}, u32[]{:S(2)}) collective-permute-start(bf16[1536,128]{1,0:T(8,128)(2,1)S(1)} %get-tuple-element.147), channel_id=1, source_target_pairs={{0,1},{1,0},{2,3},{3,2},{4,5},{5,4},{6,7},{7,6},{8,9},{9,8},{10,11... | collective-permute-start | bytes 1179656 | tf_op jit(solution)/shard_map/ppermute | solution.py:614
  119.3 1.9 collective-permute-start.18
  121.4 11.3 %collective-permute-start.24 = (bf16[1664,128]{1,0:T(8,128)(2,1)S(1)}, bf16[1664,128]{1,0:T(8,128)(2,1)S(1)}, u32[]{:S(2)}, u32[]{:S(2)}) collective-permute-start(bf16[1664,128]{1,0:T(8,128)(2,1)S(1)} %get-tuple-element.166), channel_id=1, source_target_pairs={{0,2},{1,3},{2,0},{3,1},{4,6},{5,7},{6,4},{7,5},{8,10},{9,11},{10,... | collective-permute-start | bytes 1277960 | tf_op jit(solution)/shard_map/ppermute | solution.py:614
  122.9 11.2 %collective-permute-start.22 = (bf16[2,208,512]{2,1,0:T(8,128)(2,1)S(1)}, bf16[2,208,512]{2,1,0:T(8,128)(2,1)S(1)}, u32[]{:S(2)}, u32[]{:S(2)}) collective-permute-start(bf16[2,208,512]{2,1,0:T(8,128)(2,1)S(1)} %get-tuple-element.163), channel_id=1, source_target_pairs={{0,8},{4,12},{8,0},{12,4},{16,24},{20,28},{24,16},{28,20},{1,9},{5... | collective-permute-start | bytes 1277960 | tf_op jit(solution)/shard_map/ppermute | solution.py:614
  124.5 10.9 %collective-permute-start.23 = (bf16[2,208,512]{2,1,0:T(8,128)(2,1)S(1)}, bf16[2,208,512]{2,1,0:T(8,128)(2,1)S(1)}, u32[]{:S(2)}, u32[]{:S(2)}) collective-permute-start(bf16[2,208,512]{2,1,0:T(8,128)(2,1)S(1)} %get-tuple-element.165), channel_id=1, source_target_pairs={{0,4},{4,0},{8,12},{12,8},{16,20},{20,16},{24,28},{28,24},{1,5},{5... | collective-permute-start | bytes 1277960 | tf_op jit(solution)/shard_map/ppermute | solution.py:614
  125.7 24.0 %collective-permute-start.21 = (bf16[1536,512]{1,0:T(8,128)(2,1)S(1)}, bf16[1536,512]{1,0:T(8,128)(2,1)S(1)}, u32[]{:S(2)}, u32[]{:S(2)}) collective-permute-start(bf16[1536,512]{1,0:T(8,128)(2,1)S(1)} %pair.2.refs_4_), channel_id=1, source_target_pairs={{0,1},{1,0},{2,3},{3,2},{4,5},{5,4},{6,7},{7,6},{8,9},{9,8},{10,11... | collective-permute-start | bytes 4718600 | tf_op jit(solution)/shard_map/ppermute | solution.py:614
  135.6 10.0 %collective-permute-start.25 = (bf16[416,512]{1,0:T(8,128)(2,1)S(1)}, bf16[416,512]{1,0:T(8,128)(2,1)S(1)}, u32[]{:S(2)}, u32[]{:S(2)}) collective-permute-start(bf16[416,512]{1,0:T(8,128)(2,1)S(1)} %get-tuple-element.169), channel_id=1, source_target_pairs={{0,2},{1,3},{2,0},{3,1},{4,6},{5,7},{6,4},{7,5},{8,10},{9,11},{10,... | collective-permute-start | bytes 1277960 | tf_op jit(solution)/shard_map/ppermute | solution.py:614
  136.2 5.8 %collective-permute-start.26 = (bf16[832,128]{1,0:T(8,128)(2,1)S(1)}, bf16[832,128]{1,0:T(8,128)(2,1)S(1)}, u32[]{:S(2)}, u32[]{:S(2)}) collective-permute-start(bf16[832,128]{1,0:T(8,128)(2,1)S(1)} %get-tuple-element.170), channel_id=1, source_target_pairs={{0,4},{4,0},{8,12},{12,8},{16,20},{20,16},{24,28},{28,24},{1,5},{5... | collective-permute-start | bytes 638984 | tf_op jit(solution)/shard_map/ppermute | solution.py:614
  145.7 19.5 %collective-permute-start.27 = (bf16[720,512]{1,0:T(8,128)(2,1)S(1)}, bf16[720,512]{1,0:T(8,128)(2,1)S(1)}, u32[]{:S(2)}, u32[]{:S(2)}) collective-permute-start(bf16[720,512]{1,0:T(8,128)(2,1)S(1)} %get-tuple-element.173.refs_2_), channel_id=1, source_target_pairs={{0,2},{1,3},{2,0},{3,1},{4,6},{5,7},{6,4},{7,5},{8,10},{9,11},{10,... | collective-permute-start | bytes 2211848 | tf_op jit(solution)/shard_map/ppermute | solution.py:614
  146.3 18.8 %collective-permute-start.28 = (bf16[416,512]{1,0:T(8,128)(2,1)S(1)}, bf16[416,512]{1,0:T(8,128)(2,1)S(1)}, u32[]{:S(2)}, u32[]{:S(2)}) collective-permute-start(bf16[416,512]{1,0:T(8,128)(2,1)S(1)} %sums.3.refs_6_.refs_2_), channel_id=1, source_target_pairs={{0,16},{4,20},{8,24},{12,28},{16,0},{20,4},{24,8},{28,12},{1,17},{... | collective-permute-start | bytes 1277960 | tf_op jit(solution)/shard_map/ppermute | solution.py:614
  148.9 8.6 %collective-permute-start.29 = (bf16[416,128]{1,0:T(8,128)(2,1)S(1)}, bf16[416,128]{1,0:T(8,128)(2,1)S(1)}, u32[]{:S(2)}, u32[]{:S(2)}) collective-permute-start(bf16[416,128]{1,0:T(8,128)(2,1)S(1)} %get-tuple-element.174), channel_id=1, source_target_pairs={{0,8},{4,12},{8,0},{12,4},{16,24},{20,28},{24,16},{28,20},{1,9},{5... | collective-permute-start | bytes 319496 | tf_op jit(solution)/shard_map/ppermute | solution.py:614
  165.3 15.3 %collective-permute-start.30 = (bf16[1440,512]{1,0:T(8,128)(2,1)S(1)}, bf16[1440,512]{1,0:T(8,128)(2,1)S(1)}, u32[]{:S(2)}, u32[]{:S(2)}) collective-permute-start(bf16[1440,512]{1,0:T(8,128)(2,1)S(1)} %pair.3.refs_4_), channel_id=1, source_target_pairs={{0,1},{1,0},{2,3},{3,2},{4,5},{5,4},{6,7},{7,6},{8,9},{9,8},{10,11... | collective-permute-start | bytes 4423688 | tf_op jit(solution)/shard_map/ppermute | solution.py:614
  165.4 11.6 %collective-permute-start.31 = (bf16[208,512]{1,0:T(8,128)(2,1)S(1)}, bf16[208,512]{1,0:T(8,128)(2,1)S(1)}, u32[]{:S(2)}, u32[]{:S(2)}) collective-permute-start(bf16[208,512]{1,0:T(8,128)(2,1)S(1)} %get-tuple-element.175.refs_4_.refs_2_), channel_id=1, source_target_pairs={{0,8},{4,12},{8,0},{12,4},{16,24},{20,28},{24,16},{28,20},{1,9},{5... | collective-permute-start | bytes 638984 | tf_op jit(solution)/shard_map/ppermute | solution.py:614
  165.8 11.2 %collective-permute-start.32 = (bf16[208,512]{1,0:T(8,128)(2,1)S(1)}, bf16[208,512]{1,0:T(8,128)(2,1)S(1)}, u32[]{:S(2)}, u32[]{:S(2)}) collective-permute-start(bf16[208,512]{1,0:T(8,128)(2,1)S(1)} %get-tuple-element.176.refs_4_), channel_id=1, source_target_pairs={{0,4},{4,0},{8,12},{12,8},{16,20},{20,16},{24,28},{28,24},{1,5},{5... | collective-permute-start | bytes 638984 | tf_op jit(solution)/shard_map/ppermute | solution.py:614
  168.2 8.7 %collective-permute-start.33 = (bf16[416,128]{1,0:T(8,128)(2,1)S(1)}, bf16[416,128]{1,0:T(8,128)(2,1)S(1)}, u32[]{:S(2)}, u32[]{:S(2)}) collective-permute-start(bf16[416,128]{1,0:T(8,128)(2,1)S(1)} %sums.4.refs_4_.refs_2_), channel_id=1, source_target_pairs={{0,16},{4,20},{8,24},{12,28},{16,0},{20,4},{24,8},{28,12},{1,17},{... | collective-permute-start | bytes 319496 | tf_op jit(solution)/shard_map/ppermute | solution.py:614
  177.8 17.0 %collective-permute-start.36 = (bf16[416,512]{1,0:T(8,128)(2,1)S(1)}, bf16[416,512]{1,0:T(8,128)(2,1)}, u32[]{:S(2)}, u32[]{:S(2)}) collective-permute-start(bf16[416,512]{1,0:T(8,128)(2,1)S(1)} %get-tuple-element.177.refs_6_.refs_2_), channel_id=1, source_target_pairs={{0,4},{4,0},{8,12},{12,8},{16,20},{20,16},{24,28},{28,24},{1,5},{5... | collective-permute-start | bytes 1277960 | tf_op jit(solution)/shard_map/ppermute | solution.py:614
  178.6 16.2 %collective-permute-start.37 = (bf16[416,512]{1,0:T(8,128)(2,1)}, bf16[416,512]{1,0:T(8,128)(2,1)}, u32[]{:S(2)}, u32[]{:S(2)}) collective-permute-start(bf16[416,512]{1,0:T(8,128)(2,1)} %get-tuple-element.178.refs_4_), channel_id=1, source_target_pairs={{0,8},{4,12},{8,0},{12,4},{16,24},{20,28},{24,16},{28,20},{1,9},{5... | collective-permute-start | bytes 1277960 | tf_op jit(solution)/shard_map/ppermute | solution.py:614
  180.6 12.0 %collective-permute-start.34 = (bf16[416,128]{1,0:T(8,128)(2,1)S(1)}, bf16[416,128]{1,0:T(8,128)(2,1)S(1)}, u32[]{:S(2)}, u32[]{:S(2)}) collective-permute-start(bf16[416,128]{1,0:T(8,128)(2,1)S(1)} %sums.5.refs_6_.refs_2_), channel_id=1, source_target_pairs={{0,8},{4,12},{8,0},{12,4},{16,24},{20,28},{24,16},{28,20},{1,9},{5... | collective-permute-start | bytes 319496 | tf_op jit(solution)/shard_map/ppermute | solution.py:614
  194.5 6.3 %collective-permute-start.35 = (bf16[832,128]{1,0:T(8,128)(2,1)S(1)}, bf16[832,128]{1,0:T(8,128)(2,1)S(1)}, u32[]{:S(2)}, u32[]{:S(2)}) collective-permute-start(bf16[832,128]{1,0:T(8,128)(2,1)S(1)} %joins.3.refs_6_.refs_2_), channel_id=1, source_target_pairs={{0,4},{4,0},{8,12},{12,8},{16,20},{20,16},{24,28},{28,24},{1,5},{5... | collective-permute-start | bytes 638984 | tf_op jit(solution)/shard_map/ppermute | solution.py:614
  (17 other events, 71.0 us)

commit v5 on v4

--- a/solution.py
+++ b/solution.py
@@ -14,8 +14,10 @@
 BF = jnp.bfloat16
 F32 = jnp.float32
 MIB = 1 << 20
-KNOBS = {'cost': 0, 'window': 'AM2', 'tail': 'OFpFOFOcFOgFOrF', 'out_tie': 'w', 'hs_tie': 's0', 'g_tie': 'O3', 'rb_need': 1}
+KNOBS = {'cost': 0, 'window': 'MA2', 'tail': 'OFpFOFOcFOgFrFO', 'out_tie': 'w', 'hs_tie': 'fq', 'rs_tie': '', 'g_tie': 'O3', 'vm': 18, 'vs': 16, 'vf': 60, 'vh': 16, 'vz': 24, 'ud_tie': 'a'}
 FB = 8
+GROUP = 16
+HEADS = 4
 RB = 16
 
 
@@ -66,8 +68,7 @@
     return z * cdf, cdf + z * (e * 0.3989422804014327)
 
 
-def feature_probabilities(q, k, feature_count):
-    scores = mm_nt(k, q) * SCALE
+def masked_softmax(scores, feature_count):
     key = lax.broadcasted_iota(jnp.int32, scores.shape, 0)
     return softmax_keys(jnp.where(key < feature_count, scores, NEGATIVE)).astype(BF)
 
@@ -117,7 +118,7 @@
     return jax.ShapeDtypeStruct(shape, dtype)
 
 
-def call(kernel, name, grid, t, ins, outs, scratch=(), vmem=32, us=1):
+def call(kernel, name, grid, t, ins, outs, scratch=(), vmem=KNOBS["vm"], us=1):
     t, after = t[:2], [a for a in t[2:]]
     count = 2 + len(ins)
 
@@ -188,10 +189,13 @@
     qkv = mm(low, three(w_ref))
     for c in range(3):
         qkv_scr[c, 0 : feature_count * rows, :] = qkv[:, c * HD : (c + 1) * HD]
-    for r in range(rows):
-        every = pl.ds(r, padded, stride=rows)
-        q, k, v = (qkv_scr[c, every, :].astype(BF) for c in range(3))
-        mix_scr[every, :] = mm_tn(feature_probabilities(q, k, feature_count), v)
+    for first in range(0, rows, GROUP):
+        places = [pl.ds(r, padded, stride=rows) for r in range(first, first + GROUP)]
+        parts = [[qkv_scr[c, every, :].astype(BF) for c in range(3)] for every in places]
+        scores = [mm_nt(k, q) * SCALE for q, k, _ in parts]
+        ps = [masked_softmax(x, feature_count) for x in scores]
+        for every, p, (_, _, v) in zip(places, ps, parts):
+            mix_scr[every, :] = mm_tn(p, v)
     count = o0.shape[1]
     for k, out in enumerate((o0, o1, o2, o3)):
         at = pl.multiple_of(lax.bitwise_xor(t_ref[0], k) * count, count)
@@ -208,7 +212,7 @@
         [(cells, pl.BlockSpec((feature_count, RB, width), lambda i, t, d: (0, i, 0)))]
         + [(a, full(a)) for a in (gains, shifts, weight, up, down)],
         [out] * 4 + [whole((up.shape[0] + down.shape[0], up.shape[1]))],
-        [pltpu.VMEM((3, padded * RB, HD), F32), pltpu.VMEM((padded * RB, HD), F32)], vmem=60, us=11
+        [pltpu.VMEM((3, padded * RB, HD), F32), pltpu.VMEM((padded * RB, HD), F32)], vmem=KNOBS["vf"], us=11
     )
 
 
@@ -245,15 +249,19 @@
     normed, _ = standardize(first)
     low = (normed * gains[1:2] + shifts[1:2]).astype(BF)
     n2_ref[...] = low
-    for h, w in enumerate((w0, w1, w2, w3)):
-        base = 3 * HD * h
-        qkv_ref[:, base : base + 3 * HD] = mm(low, stacked(w)).astype(BF)
-        for b in range(0, cells, side):
-            span = slice(b, b + side)
-            q, k, v = (qkv_ref[span, base + c * HD : base + (c + 1) * HD] for c in range(3))
-            p = softmax_keys(mm_nt(k, q) * SCALE + bias).astype(BF)
-            p_ref[h, b // side] = p
-            o2_ref[span, h * HD : (h + 1) * HD] = mm_tn(p, v).astype(BF)
+    spans = [slice(b, b + side) for b in range(0, cells, side)]
+    part = lambda h, span, c: qkv_ref[span, (3 * h + c) * HD : (3 * h + c + 1) * HD]
+    weights = (w0, w1, w2, w3)
+    for first_head in range(0, 4, HEADS):
+        heads = range(first_head, first_head + HEADS)
+        qkv_ref[:, 3 * HD * first_head : 3 * HD * (first_head + HEADS)] = mm(
+            low, jnp.concatenate([stacked(weights[h]) for h in heads], axis=-1)).astype(BF)
+        places = [(h, j, span) for h in heads for j, span in enumerate(spans)]
+        scores = [mm_nt(part(h, span, 1), part(h, span, 0)) * SCALE + bias for h, _, span in places]
+        ps = [softmax_keys(x).astype(BF) for x in scores]
+        for (h, j, span), p in zip(places, ps):
+            p_ref[h, j] = p
+            o2_ref[span, h * HD : (h + 1) * HD] = mm_tn(p, part(h, span, 2)).astype(BF)
     second = first + mm(o2_ref[...], wide((r0, r1, r2, r3))) + wr_bias[...].astype(F32)
     second_ref[...] = second
     normed, _ = standardize(second)
@@ -284,19 +292,36 @@
     g3 = live_columns(grad_ref[...], t_ref[0] * columns, feature_count).reshape(columns * rows, width)
     n3, gl = n3_ref[...], g3.astype(BF)
     n3_t, gl_t = n3.T, gl.T
+    hidden = ups[0].shape[1]
+    up = jnp.concatenate([u[...] for u in ups], axis=-1)
+    down = jnp.concatenate([d[...] for d in downs], axis=0)
+    bias = jnp.concatenate([p[...].astype(F32)[j : j + 1] for p in packs for j in range(4)], axis=-1)
     ms, dzs = [], []
-    for up, pack, down, grad_ref, bias_grad in zip(ups, packs, downs, grads, bias_grads):
-        bias = jnp.concatenate([pack[...].astype(F32)[j : j + 1] for j in range(4)], axis=-1)
-        act, slope = gelu_parts(mm(n3, up[...]) + bias)
+    step = 256
+    count = 2 * hidden // step
+    ahead = []
+
+    def begin(c):
+        span = slice(c * step, (c + 1) * step)
+        return mm(n3, up[:, span]) + bias[:, span], mm_nt(gl, down[span])
+
+    ahead = begin(0)
+    for c in range(count):
+        z, dm = ahead
+        if c + 1 < count:
+            ahead = begin(c + 1)
+        act, slope = gelu_parts(z)
         m = act.astype(BF)
-        dz = (mm_nt(gl, down[...]) * slope).astype(BF)
-        grad_ref[:width] = mm(n3_t, dz).astype(BF)
-        grad_ref[width:] = mm(gl_t, m).astype(BF)
-        bias_grad[...] = column_sum(dz.astype(F32))
+        dz = (dm * slope).astype(BF)
+        j, at = divmod(c * step, hidden)
+        span = slice(at, at + step)
+        grads[j][:width, span] = mm(n3_t, dz).astype(BF)
+        grads[j][width:, span] = mm(gl_t, m).astype(BF)
+        bias_grads[j][:, span] = column_sum(dz.astype(F32))
         ms.append(m)
         dzs.append(dz)
-    out = mm(jnp.concatenate(ms, axis=-1), jnp.concatenate([d[...] for d in downs], axis=0))
-    dn3 = mm_nt(jnp.concatenate(dzs, axis=-1), jnp.concatenate([u[...] for u in ups], axis=-1))
+    out = mm(jnp.concatenate(ms, axis=-1), down)
+    dn3 = mm_nt(jnp.concatenate(dzs, axis=-1), up)
     return g3, out, dn3
 
 
@@ -351,11 +376,14 @@
     return call(partial(kernel, feature_count=grads.shape[0]), name, (1,), t, ins, results, us=7)
 
 
-def attention_backward(q, k, v, p, do):
-    dp = mm_nt(v, do)
-    pf = p.astype(F32)
-    ds = (pf * (dp - jnp.sum(dp * pf, axis=0, keepdims=True))).astype(BF)
-    return mm_tn(ds, k) * SCALE, mm(ds, q) * SCALE, mm(p, do)
+def attentions_backward(blocks):
+    dps = [mm_nt(v, do) for _, _, v, _, do in blocks]
+    pfs = [b[3].astype(F32) for b in blocks]
+    dss = [(pf * (dp - jnp.sum(dp * pf, axis=0, keepdims=True))).astype(BF) for dp, pf in zip(dps, pfs)]
+    dvs = [mm(p, do) for _, _, _, p, do in blocks]
+    dks = [mm(ds, b[0]) * SCALE for ds, b in zip(dss, blocks)]
+    dqs = [mm_tn(ds, b[1]) * SCALE for ds, b in zip(dss, blocks)]
+    return list(zip(dqs, dks, dvs))
 
 
 def row_backward_kernel(
@@ -374,14 +402,16 @@
     side = p_ref.shape[2]
     gl2 = g2.astype(BF)
     do = mm_nt(gl2, wide((r0, r1, r2, r3))).astype(BF)
-    for h in range(4):
-        at = 3 * HD * h
-        for b in range(0, cells, side):
-            span = slice(b, b + side)
-            q, k, v = (qkv_ref[span, at + c * HD : at + (c + 1) * HD] for c in range(3))
-            parts = attention_backward(q, k, v, p_ref[h, b // side], do[span, HD * h : HD * (h + 1)])
+    spans = [slice(b, b + side) for b in range(0, cells, side)]
+    for first in range(0, 4, 2):
+        heads = range(first, first + 2)
+        blocks = [
+            [qkv_ref[span, (3 * h + c) * HD : (3 * h + c + 1) * HD] for c in range(3)]
+            + [p_ref[h, j], do[span, HD * h : HD * (h + 1)]] for h in heads for j, span in enumerate(spans)]
+        places = [(h, span) for h in heads for span in spans]
+        for (h, span), parts in zip(places, attentions_backward(blocks)):
             for c, part in enumerate(parts):
-                dqkv_ref[span, at + c * HD : at + (c + 1) * HD] = part.astype(BF)
+                dqkv_ref[span, (3 * h + c) * HD : (3 * h + c + 1) * HD] = part.astype(BF)
     dn2 = mm_nt(dqkv_ref[...], jnp.concatenate([stacked(w) for w in (w0, w1, w2, w3)], axis=-1))
     normed, inverse = standardize(first_ref[...])
     g1 = g2 + norm_backward(dn2, normed, inverse, gains_ref[...].astype(F32)[1:2])
@@ -461,15 +491,16 @@
     normed, _ = standardize(own_rows(t_ref, cells_ref, cell_scr, share))
     low = (normed * gains_ref[...].astype(F32)[0:1] + shifts_ref[...].astype(F32)[0:1]).astype(BF)
     n1_ref[...] = low
-    for h, w in enumerate((three(w0), unpacked(w1), three(w2), unpacked(w3))):
-        packed = mm(low, w)
-        for c in range(3):
-            qkv_scr[c] = packed[:, c * HD : (c + 1) * HD]
+    packed = mm(low, jnp.concatenate([three(w0), unpacked(w1), three(w2), unpacked(w3)], axis=-1))
+    for c in range(12):
+        qkv_scr[c] = packed[:, c * HD : (c + 1) * HD]
+    for h in range(4):
+        parts = [[qkv_scr[3 * h + c, pl.ds(r, padded, stride=share), :].astype(BF) for c in range(3)] for r in range(share)]
+        scores = [mm_nt(k, q) * SCALE for q, k, _ in parts]
         for r in range(share):
-            q, k, v = (qkv_scr[c, pl.ds(r, padded, stride=share), :].astype(BF) for c in range(3))
-            for c, part in enumerate((q, k, v)):
+            for c, part in enumerate(parts[r]):
                 qkv_ref[r, :, (3 * h + c) * HD : (3 * h + c + 1) * HD] = part
-            p_ref[r, h] = feature_probabilities(q, k, feature_count)
+            p_ref[r, h] = masked_softmax(scores[r], feature_count)
 
 
 def feature_again(t, cells, gains, shifts, fq, fq_far, near, columns, share):
@@ -479,7 +510,7 @@
         feature_again_kernel, "feature_again", (1,), t,
         [(cells, row_block(cells, share))] + [(a, full(a)) for a in (gains, shifts)] + four_weights(fq, fq_far, near),
         [whole((padded * share, width)), whole((share, padded, 12 * HD)), whole((share, 4, padded, padded))],
-        [pltpu.VMEM((padded, RB, width), F32), pltpu.VMEM((3, padded * share, HD), F32)], vmem=28, us=4
+        [pltpu.VMEM((padded, RB, width), F32), pltpu.VMEM((12, padded * share, HD), F32)], vmem=KNOBS["vs"], us=4
     )
 
 
@@ -499,12 +530,15 @@
         do_scr[h] = do[:, h * HD : (h + 1) * HD]
     n1_t = n1_ref[...].T
     for h in range(4):
-        for r in range(share):
-            every = pl.ds(r, padded, stride=share)
-            q, k, v = (qkv_ref[r, :, (3 * h + c) * HD : (3 * h + c + 1) * HD] for c in range(3))
-            parts = attention_backward(q, k, v, p_ref[r, h], do_scr[h, every, :].astype(BF))
+        rows = [pl.ds(r, padded, stride=share) for r in range(share)]
+        heads = range(h, h + HEADS) if h % HEADS == 0 else ()
+        blocks = [
+            [qkv_ref[r, :, (3 * g + c) * HD : (3 * g + c + 1) * HD] for c in range(3)]
+            + [p_ref[r, g], do_scr[g, every, :].astype(BF)] for g in heads for r, every in enumerate(rows)]
+        places = [(g, every) for g in heads for every in rows]
+        for (g, every), parts in zip(places, attentions_backward(blocks)):
             for c, part in enumerate(parts):
-                dqkv_scr[3 * h + c, every, :] = part
+                dqkv_scr[3 * g + c, every, :] = part
         out = ((keep0, keep1), (send0, send1))[h % 2]
         for c in range(3):
             dqkv_ref[:, (3 * h + c) * HD : (3 * h + c + 1) * HD] = dqkv_scr[3 * h + c].astype(BF)
@@ -554,7 +588,7 @@
     ins += four_weights(fq, fq_far, near) + [(a, full(a)) for a in sums]
     return call(
         feature_input_kernel, "feature_input", (1,), t, ins, [whole((kept, width)), whole((128, HD), F32)],
-        [pltpu.VMEM((count // share, RB, width), F32), pltpu.VMEM((32, width), F32)], vmem=28, us=2,
+        [pltpu.VMEM((count // share, RB, width), F32), pltpu.VMEM((32, width), F32)], vmem=KNOBS["vs"], us=2,
     )
 
 
@@ -582,7 +616,7 @@
     return call(
         columns_home_kernel, "columns_home", (4,), t,
         [(own, block(0)), (near, block(0)), (far, block(0)), (near, block(1))],
-        [(shaped((feature_count, rows, width)), pl.BlockSpec((columns, rows, width), lambda i, t, d: (i, 0, 0)))], vmem=16,
+        [(shaped((feature_count, rows, width)), pl.BlockSpec((columns, rows, width), lambda i, t, d: (i, 0, 0)))], vmem=KNOBS["vh"],
     )[0]
 
 
@@ -605,7 +639,7 @@
         rows_home_kernel, "rows_home", (steps,), t,
         [(own, block(0)), (near, block(0)), (far, block(0)), (near, block(steps))],
         [(shaped((feature_count, rows, width)), pl.BlockSpec((columns, rows, width), lambda i, t, d: (i, 0, 0)))],
-        [pltpu.VMEM((columns, rows, width), F32)], vmem=16,
+        [pltpu.VMEM((columns, rows, width), F32)], vmem=KNOBS["vh"],
     )[0]
 
 
@@ -783,7 +817,7 @@
     return call(
         partial(finish_kernel, masks=masks), "finish", (), t,
         [(x, VMEM) for x in (*a, *b)], [(o, VMEM) for o in outs],
-        [scr, scr, pltpu.VMEM((5 * width, HD), F32)], vmem=24)
+        [scr, scr, pltpu.VMEM((5 * width, HD), F32)], vmem=KNOBS["vz"])
 
 
 def finish_feature_kernel(t_ref, d_ref, own, other, qkv_ref, sums_ref, scr, *, mask):
@@ -831,7 +865,7 @@
     packs = own, core(own), own_far, core(own_far)
     mixed = [kept.value] + [swap(mixed[k], "tensor", k) for k in (1, 2, 3)]
     a2, a3 = Box(mixed[2]), Box(mixed[3])
-    both_far = swap(tied(both, a2, a3), "tensor", 2)
+    both_far = swap({"a": lambda: tied(both, a2, a3), "2": lambda: tied(both, a2), "": lambda: both}[KNOBS["ud_tie"]](), "tensor", 2)
     mixed[2:] = a2.value, a3.value
 
     first, n2, row_packed, row_p, o2, second, n3 = row_forward(
@@ -844,15 +878,21 @@
     out_f, g2, stats_a, hg2, hidden_send, bg2, bg3 = hidden_call(
         t, n3, grads, (both_far, core(both_far)), packs[2:], columns,
         [kept.value, dn3_a, second, dnb, norm_gains, hg1])
+    fq_box = Box(fq_far)
+    if KNOBS["hs_tie"] == "fq":
+        hidden_got = core(tied(hidden_send, fq_box))
+    fq_far = fq_box.value
     s0, near_send, s2, s3, stats_b, row_keep, row_send = row_backward(
         (*t, out_f), g2, first, row_packed, row_p, norm_gains, n2, o2, mixed, fq, fq_far, packs, row_count)
     pieces = [s0, core(near_send), swap(s2, "tensor", 2), swap(s3, "tensor", 3)]
     near_got = pieces[1]
     K = KNOBS
-    boxes = {"s0": Box(s0), "rs": Box(row_send)}
-    hidden_got = core(tied(hidden_send, boxes[K["hs_tie"]]) if K["hs_tie"] else hidden_send)
+    boxes = {"s0": Box(s0), "rs": Box(row_send), "near": Box(near_got)}
+    if K["hs_tie"] != "fq":
+        hidden_got = core(tied(hidden_send, boxes[K["hs_tie"]]) if K["hs_tie"] else hidden_send)
+    row_got = core(tied(row_send, boxes[K["rs_tie"]]) if K["rs_tie"] else boxes["rs"].value)
     pieces[0] = boxes["s0"].value
-    row_got = core(boxes["rs"].value)
+    pieces[1] = near_got = boxes["near"].value
 
     last = [s0]
     boxes.update(out=Box(out_f), w=Box(pieces[3]), w2=Box(pieces[2]))

time: 208 us -> 183 us (0.88)
  Pallas kernels: 87.3 us -> 60.4 us
  waiting for transfers between devices: 63.6 us -> 72.8 us
  local copies, waits for them, and re-layouts: 14.3 us -> 6.46 us
    pallas_call x27, Pallas kernels: 87.3 us -> 60.4 us  [call(): pl.pallas_call(body, grid_spec=spec, out_shape=[a for a, _ in outs], comp...]
    ppermute x38, waiting for transfers between devices: 63.6 us -> 72.8 us  [swap(): return lax.ppermute(values, axis, [(i, i ^ mask) for i in range(count)])]
    unnamed x54 -> x28, local copies, waits for them, and re-layouts: 13.7 us -> 5.85 us
  transfers between devices with their start and end apart: 38 -> 38, of which waited for: 17 -> 20; matrix products, arithmetic and copies ran while one was open for 0% -> 0% of each run, Pallas kernels for 35% -> 32%
where the time goes in v5:
time: 183 us; the launch traced here: 180 us
  waiting for transfers between devices  72.8 us (40%)
  Pallas kernels  60.4 us (33%)
  starting transfers between devices  37.7 us (21%)
  local copies, waits for them, and re-layouts  6.46 us (4%)
  between operations  1.84 us (1%)
    ppermute x38, waiting for transfers between devices, swap(): return lax.ppermute(values, axis, [(i, i ^ mask) for i in range(count)])  72.8 us
    pallas_call x27, Pallas kernels, call(): pl.pallas_call(body, grid_spec=spec, out_shape=[a for a, _ in outs], comp...  60.4 us
    ppermute x38, starting transfers between devices, swap(): return lax.ppermute(values, axis, [(i, i ^ mask) for i in range(count)])  37.7 us
    unnamed x28, local copies, waits for them, and re-layouts  5.85 us
  transfers between devices with their start and end apart: 38, of which 20 were waited for; matrix products, arithmetic and copies ran while one was open for 0% of the time, Pallas kernels for 32%

profile of v5, /device:TPU:0, one launch (start us, length us, event | category | flops | bytes accessed | tf_op | source)
XLA Modules:
  0.0 179.9 jit_solution(15071843833765002137)
XLA Ops:
  0.7 2.0 %pack.1.refs_8_.refs_12_.refs_16_.refs_6_.refs_15_.refs_19_ = bf16[2576,128]{1,0:T(8,128)(2,1)} custom-call(s32[1]{0:T(128)} %bitcast.refs_0_, s32[1]{0:T(128)} %bitcast.1.refs_1_, bf16[3,512,128]{2,1,0:T(8,128)(2,1)} %bitcast.39, bf16[128,512]{1,0:T(8,128)(2,1)} %refs_3_.3, bf16[128,512]{1,0:T(8,128)(2,1)} %refs_4_.3, bf16[512]{0:T(512)(128)(2,1)} %refs_5_.2), custom_call_target="tpu_custom_call" | custom-call | flops 1 | bytes 1 | tf_op jit(solution)/shard_map/pack/pallas_call | solution.py:135
  2.7 2.9 %collective-permute-start = (bf16[2576,128]{1,0:T(8,128)(2,1)}, bf16[2576,128]{1,0:T(8,128)(2,1)}, u32[]{:S(2)}, u32[]{:S(2)}) collective-permute-start(bf16[2576,128]{1,0:T(8,128)(2,1)} %pack.1.refs_8_.refs_12_.refs_16_.refs_6_.refs_15_.refs_19_), channel_id=1, source_target_pairs={{0,2},{1,3},{2,0},{3,1},{4,6},{5,7},{6,4},{7,5},{8,10},{9,11},{10,... | collective-permute-start | bytes 1978376 | tf_op jit(solution)/shard_map/ppermute | solution.py:648
  5.6 8.7 %feature_forward.1 = (bf16[2,384,128]{2,1,0:T(8,128)(2,1)}, bf16[2,384,128]{2,1,0:T(8,128)(2,1)}, bf16[2,384,128]{2,1,0:T(8,128)(2,1)}, bf16[2,384,128]{2,1,0:T(8,128)(2,1)}, bf16[1024,512]{1,0:T(8,128)(2,1)}) custom-call(s32[1]{0:T(128)} %bitcast.refs_0_, s32[1]{0:T(128)} %bitcast.1.refs_1_, bf16[89,32,512]{2,1,0:T(8,128)(2,1)} %bitcast.26, ...), custom_call_target="tpu_custom_call" | custom-call | flops 1 | bytes 1 | tf_op jit(solution)/shard_map/feature_forward/pallas_call | solution.py:135
  15.3 1.2 collective-permute-start.7
  16.5 9.2 %collective-permute-done.2.refs_5_.refs_11_ = bf16[2,384,128]{2,1,0:T(8,128)(2,1)S(1)} collective-permute-done((bf16[2,384,128]{2,1,0:T(8,128)(2,1)}, bf16[2,384,128]{2,1,0:T(8,128)(2,1)S(1)}, u32[]{:S(2)}, u32[]{:S(2)}) %collective-permute-start.2) | collective-permute-done | bytes 196640 | tf_op jit(solution)/shard_map/ppermute | solution.py:648
  25.7 2.8 %collective-permute-done.3.refs_6_.refs_12_ = bf16[2,384,128]{2,1,0:T(8,128)(2,1)S(1)} collective-permute-done((bf16[2,384,128]{2,1,0:T(8,128)(2,1)}, bf16[2,384,128]{2,1,0:T(8,128)(2,1)S(1)}, u32[]{:S(2)}, u32[]{:S(2)}) %collective-permute-start.3) | collective-permute-done | bytes 196640 | tf_op jit(solution)/shard_map/ppermute | solution.py:648
  28.4 1.2 collective-permute-start.6
  31.5 2.0 %collective-permute-done.1.refs_4_.refs_10_ = bf16[2,384,128]{2,1,0:T(8,128)(2,1)S(1)} collective-permute-done((bf16[2,384,128]{2,1,0:T(8,128)(2,1)}, bf16[2,384,128]{2,1,0:T(8,128)(2,1)S(1)}, u32[]{:S(2)}, u32[]{:S(2)}) %collective-permute-start.1) | collective-permute-done | bytes 196640 | tf_op jit(solution)/shard_map/ppermute | solution.py:648
  34.5 5.3 %row_forward.1 = (f32[768,512]{1,0:T(8,128)S(1)}, bf16[768,512]{1,0:T(8,128)(2,1)S(1)}, bf16[768,1536]{1,0:T(8,128)(2,1)S(1)}, bf16[4,6,128,128]{3,2,1,0:T(8,128...) custom-call(s32[1]{0:T(128)} %bitcast.refs_0_, s32[1]{0:T(128)} %bitcast.1.refs_1_, ...), custom_call_target="tpu_custom_call" | custom-call | flops 1 | bytes 1 | tf_op jit(solution)/shard_map/row_forward/pallas_call | solution.py:135
  39.8 6.5 %hidden_first.1 = (f32[768,512]{1,0:T(8,128)S(1)}, f32[768,512]{1,0:T(8,128)S(1)}, bf16[1024,512]{1,0:T(8,128)(2,1)S(1)}, bf16[1024,512]{1,0:T(8,128)(2,1)S(1)},...) custom-call(s32[1]{0:T(128)} %bitcast.refs_0_, s32[1]{0:T(128)} %bitcast.1.refs_1_, ...), custom_call_target="tpu_custom_call" | custom-call | flops 1 | bytes 1 | tf_op jit(solution)/shard_map/hidden_first/pallas_call | solution.py:135
  46.3 7.8 %collective-permute-done.6.refs_4_.refs_8_ = bf16[1024,512]{1,0:T(8,128)(2,1)S(1)} collective-permute-done((bf16[1024,512]{1,0:T(8,128)(2,1)}, bf16[1024,512]{1,0:T(8,128)(2,1)S(1)}, u32[]{:S(2)}, u32[]{:S(2)}) %collective-permute-start.6) | collective-permute-done | bytes 1048608 | tf_op jit(solution)/shard_map/ppermute | solution.py:648
  54.2 1.9 %collective-permute-start.9 = (bf16[3,512,128]{2,1,0:T(8,128)(2,1)S(1)}, bf16[3,512,128]{2,1,0:T(8,128)(2,1)S(1)}, u32[]{:S(2)}, u32[]{:S(2)}) collective-permute-start(bf16[3,512,128]{2,1,0:T(8,128)(2,1)S(1)} %bitcast.35), channel_id=1, source_target_pairs={{0,2},{1,3},{2,0},{3,1},{4,6},{5,7},{6,4},{7,5},{8,10},{9,11},{10,... | collective-permute-start | bytes 1179656 | tf_op jit(solution)/shard_map/ppermute | solution.py:648
  56.8 8.8 %hidden_second.1 = (bf16[768,512]{1,0:T(8,128)(2,1)S(1)}, f32[768,512]{1,0:T(8,128)S(1)}, f32[8,512]{1,0:T(8,128)S(1)}, bf16[1024,512]{1,0:T(8,128)(2,1)S(1)}, b...) custom-call(s32[1]{0:T(128)} %bitcast.refs_0_, s32[1]{0:T(128)} %bitcast.1.refs_1_, ...), custom_call_target="tpu_custom_call" | custom-call | flops 1 | bytes 1 | tf_op jit(solution)/shard_map/hidden_second/pallas_call | solution.py:135
  65.8 6.9 %row_backward.1 = (bf16[192,512]{1,0:T(8,128)(2,1)S(1)}, bf16[960,512]{1,0:T(8,128)(2,1)S(1)}, bf16[192,512]{1,0:T(8,128)(2,1)S(1)}, bf16[192,512]{1,0:T(8,128)(...) custom-call(s32[1]{0:T(128)} %bitcast.refs_0_, ...), custom_call_target="tpu_custom_call" | custom-call | flops 1 | bytes 1 | tf_op jit(solution)/shard_map/row_backward/pallas_call | solution.py:135
  73.3 1.7 collective-permute-start.10
  75.8 1.6 ab_first.1
  77.4 1.9 %collective-permute-start.19 = (bf16[2,416,512]{2,1,0:T(8,128)(2,1)S(1)}, bf16[2,416,512]{2,1,0:T(8,128)(2,1)S(1)}, u32[]{:S(2)}, u32[]{:S(2)}) collective-permute-start(bf16[2,416,512]{2,1,0:T(8,128)(2,1)S(1)} %get-tuple-element.157), channel_id=1, source_target_pairs={{0,4},{4,0},{8,12},{12,8},{16,20},{20,16},{24,28},{28,24},{1,5},{5... | collective-permute-start | bytes 2555912 | tf_op jit(solution)/shard_map/ppermute | solution.py:648
  79.3 1.6 collective-permute-start.20
  80.9 3.9 %collective-permute-done.11.refs_4_.refs_14_ = bf16[192,512]{1,0:T(8,128)(2,1)S(1)} collective-permute-done((bf16[192,512]{1,0:T(8,128)(2,1)S(1)}, bf16[192,512]{1,0:T(8,128)(2,1)S(1)}, u32[]{:S(2)}, u32[]{:S(2)}) %collective-permute-start.11) | collective-permute-done | bytes 196640 | tf_op jit(solution)/shard_map/ppermute | solution.py:648
  84.7 1.7 collective-permute-start.12
  86.5 3.2 %feature_again.1 = (bf16[768,512]{1,0:T(8,128)(2,1)S(1)}, bf16[8,96,1536]{2,1,0:T(8,128)(2,1)S(1)}, bf16[8,4,96,96]{3,2,1,0:T(8,128)(2,1)S(1)}) custom-call(s32[1]{0:T(128)} %bitcast.refs_0_, s32[1]{0:T(128)} %bitcast.1.refs_1_, bf16[89,32,512]{2,1,0:T(8,128)(2,1)S(1)} %bitcast.28, bf16[3,512]{1,0:T(4,128)(2,1)S(1)} %copy-done.9, ...), custom_call_target="tpu_custom_call" | custom-call | flops 1 | bytes 1 | tf_op jit(solution)/shard_map/feature_again/pallas_call | solution.py:135
  89.7 5.4 %feature_backward.1 = (f32[768,512]{1,0:T(8,128)S(1)}, bf16[768,1536]{1,0:T(8,128)(2,1)S(1)}, bf16[1536,128]{1,0:T(8,128)(2,1)S(1)}, bf16[1536,128]{1,0:T(8,128)...) custom-call(s32[1]{0:T(128)} %bitcast.refs_0_, s32[1]{0:T(128)} %bitcast.1.refs_1_, ...), custom_call_target="tpu_custom_call" | custom-call | flops 1 | bytes 1 | tf_op jit(solution)/shard_map/feature_backward/pallas_call | solution.py:135
  95.6 2.4 %feature_input.1 = (bf16[720,512]{1,0:T(8,128)(2,1)S(1)}, f32[128,128]{1,0:T(8,128)S(1)}) custom-call(s32[1]{0:T(128)} %bitcast.refs_0_, s32[1]{0:T(128)} %bitcast.1.refs_1_, bf16[89,32,512]{2,1,0:T(8,128)(2,1)S(1)} %bitcast.29, f32[768,512]{1,0:T(8,128)S(1)} %get-tuple-element.148.refs_3_, bf16[768,1536]{1,0:T(8,128)(2,1)S(1)} %get-tuple-element.149.refs_4_, ...), custom_call_target="tpu_custom_call" | custom-call | flops 1 | bytes 1 | tf_op jit(solution)/shard_map/feature_input/pallas_call | solution.py:135
  98.7 1.5 collective-permute-done.20.refs_5_
  100.8 1.5 collective-permute-start.24
  102.4 1.6 collective-permute-start.22
  103.9 1.1 collective-permute-start.23
  105.2 7.7 %collective-permute-done.24.refs_3_ = bf16[1664,128]{1,0:T(8,128)(2,1)S(1)} collective-permute-done((bf16[1664,128]{1,0:T(8,128)(2,1)S(1)}, bf16[1664,128]{1,0:T(8,128)(2,1)S(1)}, u32[]{:S(2)}, u32[]{:S(2)}) %collective-permute-start.24) | collective-permute-done | bytes 426016 | tf_op jit(solution)/shard_map/ppermute | solution.py:648
  113.6 1.3 collective-permute-done.23.refs_5_
  115.7 1.5 collective-permute-start.26
  117.2 4.3 %collective-permute-done.26.refs_3_ = bf16[832,128]{1,0:T(8,128)(2,1)S(1)} collective-permute-done((bf16[832,128]{1,0:T(8,128)(2,1)S(1)}, bf16[832,128]{1,0:T(8,128)(2,1)S(1)}, u32[]{:S(2)}, u32[]{:S(2)}) %collective-permute-start.26) | collective-permute-done | bytes 213024 | tf_op jit(solution)/shard_map/ppermute | solution.py:648
  121.6 3.5 %collective-permute-done.25.refs_3_ = bf16[416,512]{1,0:T(8,128)(2,1)S(1)} collective-permute-done((bf16[416,512]{1,0:T(8,128)(2,1)S(1)}, bf16[416,512]{1,0:T(8,128)(2,1)S(1)}, u32[]{:S(2)}, u32[]{:S(2)}) %collective-permute-start.25) | collective-permute-done | bytes 426016 | tf_op jit(solution)/shard_map/ppermute | solution.py:648
  126.3 2.6 %collective-permute-start.28 = (bf16[416,512]{1,0:T(8,128)(2,1)S(1)}, bf16[416,512]{1,0:T(8,128)(2,1)S(1)}, u32[]{:S(2)}, u32[]{:S(2)}) collective-permute-start(bf16[416,512]{1,0:T(8,128)(2,1)S(1)} %sums.3.refs_6_.refs_2_), channel_id=1, source_target_pairs={{0,16},{4,20},{8,24},{12,28},{16,0},{20,4},{24,8},{28,12},{1,17},{... | collective-permute-start | bytes 1277960 | tf_op jit(solution)/shard_map/ppermute | solution.py:648
  128.9 1.6 collective-permute-start.29
  130.5 2.1 %columns_home.1.refs_4_ = bf16[89,32,512]{2,1,0:T(8,128)(2,1)} custom-call(s32[1]{0:T(128)} %bitcast.refs_0_, s32[1]{0:T(128)} %bitcast.1.refs_1_, bf16[768,512]{1,0:T(8,128)(2,1)S(1)} %get-tuple-element.130.refs_23_.refs_2_, bf16[1536,512]{1,0:T(8,128)(2,1)S(1)} %collective-permute-done.21.refs_3_.refs_5_, ...), custom_call_target="tpu_custom_call" | custom-call | flops 1 | bytes 1 | tf_op jit(solution)/shard_map/columns_home/pallas_call | solution.py:135
  132.6 5.5 %collective-permute-done.29.refs_3_ = bf16[416,128]{1,0:T(8,128)(2,1)S(1)} collective-permute-done((bf16[416,128]{1,0:T(8,128)(2,1)S(1)}, bf16[416,128]{1,0:T(8,128)(2,1)S(1)}, u32[]{:S(2)}, u32[]{:S(2)}) %collective-permute-start.29) | collective-permute-done | bytes 106528 | tf_op jit(solution)/shard_map/ppermute | solution.py:648
  138.0 1.8 %copy-done.4 = bf16[89,32,512]{2,1,0:T(8,128)(2,1)S(1)} copy-done((bf16[89,32,512]{2,1,0:T(8,128)(2,1)S(1)}, bf16[89,32,512]{2,1,0:T(8,128)(2,1)}, u32[]{:S(2)}) %copy-start.4) | copy-done | bytes 2916376
  139.9 5.7 %collective-permute-done.28.refs_3_ = bf16[416,512]{1,0:T(8,128)(2,1)S(1)} collective-permute-done((bf16[416,512]{1,0:T(8,128)(2,1)S(1)}, bf16[416,512]{1,0:T(8,128)(2,1)S(1)}, u32[]{:S(2)}, u32[]{:S(2)}) %collective-permute-start.28) | collective-permute-done | bytes 426016 | tf_op jit(solution)/shard_map/ppermute | solution.py:648
  146.0 4.0 %collective-permute-start.34 = (bf16[208,512]{1,0:T(8,128)(2,1)S(1)}, bf16[208,512]{1,0:T(8,128)(2,1)S(1)}, u32[]{:S(2)}, u32[]{:S(2)}) collective-permute-start(bf16[208,512]{1,0:T(8,128)(2,1)S(1)} %get-tuple-element.175.refs_4_.refs_2_), channel_id=1, source_target_pairs={{0,8},{4,12},{8,0},{12,4},{16,24},{20,28},{24,16},{28,20},{1,9},{5... | collective-permute-start | bytes 638984 | tf_op jit(solution)/shard_map/ppermute | solution.py:648
  150.0 1.5 collective-permute-start.35
  151.5 3.0 %collective-permute-done.31.refs_3_ = bf16[416,128]{1,0:T(8,128)(2,1)S(1)} collective-permute-done((bf16[416,128]{1,0:T(8,128)(2,1)S(1)}, bf16[416,128]{1,0:T(8,128)(2,1)S(1)}, u32[]{:S(2)}, u32[]{:S(2)}) %collective-permute-start.31) | collective-permute-done | bytes 106528 | tf_op jit(solution)/shard_map/ppermute | solution.py:648
  154.7 2.9 %rows_home.1.refs_4_ = bf16[89,32,512]{2,1,0:T(8,128)(2,1)} custom-call(s32[1]{0:T(128)} %bitcast.refs_0_, s32[1]{0:T(128)} %bitcast.1.refs_1_, bf16[720,512]{1,0:T(8,128)(2,1)S(1)} %get-tuple-element.173.refs_2_, bf16[1440,512]{1,0:T(8,128)(2,1)S(1)} %collective-permute-done.30.refs_3_.refs_5_, ...), custom_call_target="tpu_custom_call" | custom-call | flops 1 | bytes 1 | tf_op jit(solution)/shard_map/rows_home/pallas_call | solution.py:135
  157.6 1.8 collective-permute-done.32.refs_3_
  159.4 1.8 %copy-done.2 = bf16[89,32,512]{2,1,0:T(8,128)(2,1)S(1)} copy-done((bf16[89,32,512]{2,1,0:T(8,128)(2,1)S(1)}, bf16[89,32,512]{2,1,0:T(8,128)(2,1)}, u32[]{:S(2)}) %copy-start.2) | copy-done | bytes 2916376
  161.3 1.6 collective-permute-start.36
  163.7 10.3 %collective-permute-done.36.refs_3_ = bf16[416,512]{1,0:T(8,128)(2,1)S(1)} collective-permute-done((bf16[416,512]{1,0:T(8,128)(2,1)S(1)}, bf16[416,512]{1,0:T(8,128)(2,1)S(1)}, u32[]{:S(2)}, u32[]{:S(2)}) %collective-permute-start.36) | collective-permute-done | bytes 426016 | tf_op jit(solution)/shard_map/ppermute | solution.py:648
  173.9 2.3 %finish.1 = (f32[512,512]{1,0:T(8,128)}, f32[512,512]{1,0:T(8,128)}, f32[1536,128]{1,0:T(8,128)}, f32[128,512]{1,0:T(8,128)}, f32[128,512]{1,0:T(8,128)}) custom-call(s32[1]{0:T(128)} %bitcast.refs_0_, s32[1]{0:T(128)} %bitcast.1.refs_1_, bf16[416,512]{1,0:T(8,128)(2,1)S(1)} %get-tuple-element.177.refs_2_.refs_6_, ...), custom_call_target="tpu_custom_call" | custom-call | flops 1 | bytes 1 | tf_op jit(solution)/shard_map/finish/pallas_call | solution.py:135
  176.2 1.2 copy-done.7
  (88 shorter events, 13.8 us)
Async XLA Ops:
  2.7 27.7 %collective-permute-start = (bf16[2576,128]{1,0:T(8,128)(2,1)}, bf16[2576,128]{1,0:T(8,128)(2,1)}, u32[]{:S(2)}, u32[]{:S(2)}) collective-permute-start(bf16[2576,128]{1,0:T(8,128)(2,1)} %pack.1.refs_8_.refs_12_.refs_16_.refs_6_.refs_15_.refs_19_), channel_id=1, source_target_pairs={{0,2},{1,3},{2,0},{3,1},{4,6},{5,7},{6,4},{7,5},{8,10},{9,11},{10,... | collective-permute-start | bytes 1978376 | tf_op jit(solution)/shard_map/ppermute | solution.py:648
  5.6 24.0 %copy-start.1 = (bf16[2576,128]{1,0:T(8,128)(2,1)S(1)}, bf16[2576,128]{1,0:T(8,128)(2,1)}, u32[]{:S(2)}) copy-start(bf16[2576,128]{1,0:T(8,128)(2,1)} %pack.1.refs_8_.refs_12_.refs_16_.refs_6_.refs_15_.refs_19_) | copy-start | bytes 1978372
  5.6 25.3 %copy-start.11 = (bf16[512]{0:T(512)(128)(2,1)S(1)}, bf16[512]{0:T(512)(128)(2,1)}, u32[]{:S(2)}) copy-start(bf16[512]{0:T(512)(128)(2,1)} %param.19) | copy-start | bytes 3076
  5.6 25.3 %copy-start.12 = (bf16[512]{0:T(512)(128)(2,1)S(1)}, bf16[512]{0:T(512)(128)(2,1)}, u32[]{:S(2)}) copy-start(bf16[512]{0:T(512)(128)(2,1)} %param.22) | copy-start | bytes 3076
  5.6 27.9 %copy-start = (bf16[1,32,89,512]{3,1,2,0:T(8,128)(2,1)S(1)}, bf16[1,32,89,512]{3,1,2,0:T(8,128)(2,1)}, u32[]{:S(2)}) copy-start(bf16[1,32,89,512]{3,1,2,0:T(8,128)(2,1)} %param.15) | copy-start | bytes 8749060
  5.6 27.9 %copy-start.9 = (bf16[3,512]{1,0:T(4,128)(2,1)S(1)}, bf16[3,512]{1,0:T(4,128)(2,1)}, u32[]{:S(2)}) copy-start(bf16[3,512]{1,0:T(4,128)(2,1)} %refs_5_.3) | copy-start | bytes 9220
  5.6 27.9 %copy-start.10 = (bf16[3,512]{1,0:T(4,128)(2,1)S(1)}, bf16[3,512]{1,0:T(4,128)(2,1)}, u32[]{:S(2)}) copy-start(bf16[3,512]{1,0:T(4,128)(2,1)} %refs_4_.5) | copy-start | bytes 9220
  14.3 11.4 %collective-permute-start.2 = (bf16[2,384,128]{2,1,0:T(8,128)(2,1)}, bf16[2,384,128]{2,1,0:T(8,128)(2,1)S(1)}, u32[]{:S(2)}, u32[]{:S(2)}) collective-permute-start(bf16[2,384,128]{2,1,0:T(8,128)(2,1)} %get-tuple-element.104), channel_id=1, source_target_pairs={{0,2},{1,3},{2,0},{3,1},{4,6},{5,7},{6,4},{7,5},{8,10},{9,11},{10,... | collective-permute-start | bytes 589832 | tf_op jit(solution)/shard_map/ppermute | solution.py:648
  14.4 14.0 %collective-permute-start.3 = (bf16[2,384,128]{2,1,0:T(8,128)(2,1)}, bf16[2,384,128]{2,1,0:T(8,128)(2,1)S(1)}, u32[]{:S(2)}, u32[]{:S(2)}) collective-permute-start(bf16[2,384,128]{2,1,0:T(8,128)(2,1)} %get-tuple-element.105), channel_id=1, source_target_pairs={{0,3},{1,2},{2,1},{3,0},{4,7},{5,6},{6,5},{7,4},{8,11},{9,10},{10,... | collective-permute-start | bytes 589832 | tf_op jit(solution)/shard_map/ppermute | solution.py:648
  15.3 24.5 %collective-permute-start.7 = (bf16[1024,512]{1,0:T(8,128)(2,1)}, bf16[1024,512]{1,0:T(8,128)(2,1)S(1)}, u32[]{:S(2)}, u32[]{:S(2)}) collective-permute-start(bf16[1024,512]{1,0:T(8,128)(2,1)} %get-tuple-element.110.refs_4_.refs_8_), channel_id=1, source_target_pairs={{0,1},{1,0},{2,3},{3,2},{4,5},{5,4},{6,7},{7,6},{8,9},{9,8},{10,11... | collective-permute-start | bytes 3145736 | tf_op jit(solution)/shard_map/ppermute | solution.py:648
  28.4 25.7 %collective-permute-start.6 = (bf16[1024,512]{1,0:T(8,128)(2,1)}, bf16[1024,512]{1,0:T(8,128)(2,1)S(1)}, u32[]{:S(2)}, u32[]{:S(2)}) collective-permute-start(bf16[1024,512]{1,0:T(8,128)(2,1)} %get-tuple-element.110.refs_4_.refs_8_), channel_id=1, source_target_pairs={{0,2},{1,3},{2,0},{3,1},{4,6},{5,7},{6,4},{7,5},{8,10},{9,11},{10,... | collective-permute-start | bytes 3145736 | tf_op jit(solution)/shard_map/ppermute | solution.py:648
  29.7 3.9 %collective-permute-start.4 = (bf16[2576,128]{1,0:T(8,128)(2,1)S(1)}, bf16[2576,128]{1,0:T(8,128)(2,1)S(1)}, u32[]{:S(2)}, u32[]{:S(2)}) collective-permute-start(bf16[2576,128]{1,0:T(8,128)(2,1)S(1)} %copy-done.1), channel_id=1, source_target_pairs={{0,1},{1,0},{2,3},{3,2},{4,5},{5,4},{6,7},{7,6},{8,9},{9,8},{10,11... | collective-permute-start | bytes 1978376 | tf_op jit(solution)/shard_map/ppermute | solution.py:648
  30.3 3.2 %collective-permute-start.5 = (bf16[2576,128]{1,0:T(8,128)(2,1)}, bf16[2576,128]{1,0:T(8,128)(2,1)S(1)}, u32[]{:S(2)}, u32[]{:S(2)}) collective-permute-start(bf16[2576,128]{1,0:T(8,128)(2,1)} %collective-permute-done.refs_10_.refs_14_.refs_18_.refs_6_.refs_17_.refs_21_.refs_8_), channel_id=1, source_target_pairs={{0,1},{1,0},{2,3},{3,2},{4,5},{5,4},{6,7},{7,6},{8,9},{9,8},{10,11... | collective-permute-start | bytes 1978376 | tf_op jit(solution)/shard_map/ppermute | solution.py:648
  30.4 3.1 %collective-permute-start.1 = (bf16[2,384,128]{2,1,0:T(8,128)(2,1)}, bf16[2,384,128]{2,1,0:T(8,128)(2,1)S(1)}, u32[]{:S(2)}, u32[]{:S(2)}) collective-permute-start(bf16[2,384,128]{2,1,0:T(8,128)(2,1)} %get-tuple-element.102), channel_id=1, source_target_pairs={{0,1},{1,0},{2,3},{3,2},{4,5},{5,4},{6,7},{7,6},{8,9},{9,8},{10,11... | collective-permute-start | bytes 589832 | tf_op jit(solution)/shard_map/ppermute | solution.py:648
  31.5 8.2 %copy-start.6 = (bf16[1024,512]{1,0:T(8,128)(2,1)S(1)}, bf16[1024,512]{1,0:T(8,128)(2,1)}, u32[]{:S(2)}) copy-start(bf16[1024,512]{1,0:T(8,128)(2,1)} %get-tuple-element.110.refs_4_.refs_8_) | copy-start | bytes 3145732
  34.5 5.3 %copy-start.3 = (bf16[1,32,89,512]{3,1,2,0:T(8,128)(2,1)S(1)}, bf16[1,32,89,512]{3,1,2,0:T(8,128)(2,1)}, u32[]{:S(2)}) copy-start(bf16[1,32,89,512]{3,1,2,0:T(8,128)(2,1)} %param.29) | copy-start | bytes 8749060
  39.8 14.4 %copy-start.5 = (bf16[512,3,128]{2,0,1:T(8,128)(2,1)S(1)}, bf16[512,3,128]{2,0,1:T(8,128)(2,1)}, u32[]{:S(2)}) copy-start(bf16[512,3,128]{2,0,1:T(8,128)(2,1)} %param.17) | copy-start | bytes 1179652
  39.8 16.3 %copy-start.13 = (bf16[512]{0:T(512)(128)(2,1)S(1)}, bf16[512]{0:T(512)(128)(2,1)}, u32[]{:S(2)}) copy-start(bf16[512]{0:T(512)(128)(2,1)} %param.26) | copy-start | bytes 3076
  54.2 2.7 %collective-permute-start.8 = (bf16[1024,512]{1,0:T(8,128)(2,1)S(1)}, bf16[1024,512]{1,0:T(8,128)(2,1)S(1)}, u32[]{:S(2)}, u32[]{:S(2)}) collective-permute-start(bf16[1024,512]{1,0:T(8,128)(2,1)S(1)} %collective-permute-done.6.refs_4_.refs_8_), channel_id=1, source_target_pairs={{0,1},{1,0},{2,3},{3,2},{4,5},{5,4},{6,7},{7,6},{8,9},{9,8},{10,11... | collective-permute-start | bytes 3145736 | tf_op jit(solution)/shard_map/ppermute | solution.py:648
  54.2 11.5 %collective-permute-start.9 = (bf16[3,512,128]{2,1,0:T(8,128)(2,1)S(1)}, bf16[3,512,128]{2,1,0:T(8,128)(2,1)S(1)}, u32[]{:S(2)}, u32[]{:S(2)}) collective-permute-start(bf16[3,512,128]{2,1,0:T(8,128)(2,1)S(1)} %bitcast.35), channel_id=1, source_target_pairs={{0,2},{1,3},{2,0},{3,1},{4,6},{5,7},{6,4},{7,5},{8,10},{9,11},{10,... | collective-permute-start | bytes 1179656 | tf_op jit(solution)/shard_map/ppermute | solution.py:648
  65.7 10.1 %collective-permute-start.14 = (bf16[2048,512]{1,0:T(8,128)(2,1)S(1)}, bf16[2048,512]{1,0:T(8,128)(2,1)S(1)}, u32[]{:S(2)}, u32[]{:S(2)}) collective-permute-start(bf16[2048,512]{1,0:T(8,128)(2,1)S(1)} %get-tuple-element.138), channel_id=1, source_target_pairs={{0,1},{1,0},{2,3},{3,2},{4,5},{5,4},{6,7},{7,6},{8,9},{9,8},{10,11... | collective-permute-start | bytes 6291464 | tf_op jit(solution)/shard_map/ppermute | solution.py:648
  72.7 3.1 %collective-permute-start.15 = (bf16[2,640,512]{2,1,0:T(8,128)(2,1)S(1)}, bf16[2,640,512]{2,1,0:T(8,128)(2,1)S(1)}, u32[]{:S(2)}, u32[]{:S(2)}) collective-permute-start(bf16[2,640,512]{2,1,0:T(8,128)(2,1)S(1)} %get-tuple-element.139), channel_id=1, source_target_pairs={{0,1},{1,0},{2,3},{3,2},{4,5},{5,4},{6,7},{7,6},{8,9},{9,8},{10,11... | collective-permute-start | bytes 3932168 | tf_op jit(solution)/shard_map/ppermute | solution.py:648
  73.2 13.3 %collective-permute-start.13 = (bf16[960,512]{1,0:T(8,128)(2,1)S(1)}, bf16[960,512]{1,0:T(8,128)(2,1)S(1)}, u32[]{:S(2)}, u32[]{:S(2)}) collective-permute-start(bf16[960,512]{1,0:T(8,128)(2,1)S(1)} %get-tuple-element.132), channel_id=1, source_target_pairs={{0,1},{1,0},{2,3},{3,2},{4,5},{5,4},{6,7},{7,6},{8,9},{9,8},{10,11... | collective-permute-start | bytes 2949128 | tf_op jit(solution)/shard_map/ppermute | solution.py:648
  73.3 7.6 %collective-permute-start.10 = (bf16[192,512]{1,0:T(8,128)(2,1)S(1)}, bf16[192,512]{1,0:T(8,128)(2,1)S(1)}, u32[]{:S(2)}, u32[]{:S(2)}) collective-permute-start(bf16[192,512]{1,0:T(8,128)(2,1)S(1)} %get-tuple-element.128), channel_id=1, source_target_pairs={{0,3},{1,2},{2,1},{3,0},{4,7},{5,6},{6,5},{7,4},{8,11},{9,10},{10,... | collective-permute-start | bytes 589832 | tf_op jit(solution)/shard_map/ppermute | solution.py:648
  75.0 9.7 %collective-permute-start.11 = (bf16[192,512]{1,0:T(8,128)(2,1)S(1)}, bf16[192,512]{1,0:T(8,128)(2,1)S(1)}, u32[]{:S(2)}, u32[]{:S(2)}) collective-permute-start(bf16[192,512]{1,0:T(8,128)(2,1)S(1)} %get-tuple-element.129), channel_id=1, source_target_pairs={{0,2},{1,3},{2,0},{3,1},{4,6},{5,7},{6,4},{7,5},{8,10},{9,11},{10,... | collective-permute-start | bytes 589832 | tf_op jit(solution)/shard_map/ppermute | solution.py:648
  77.4 21.3 %collective-permute-start.19 = (bf16[2,416,512]{2,1,0:T(8,128)(2,1)S(1)}, bf16[2,416,512]{2,1,0:T(8,128)(2,1)S(1)}, u32[]{:S(2)}, u32[]{:S(2)}) collective-permute-start(bf16[2,416,512]{2,1,0:T(8,128)(2,1)S(1)} %get-tuple-element.157), channel_id=1, source_target_pairs={{0,4},{4,0},{8,12},{12,8},{16,20},{20,16},{24,28},{28,24},{1,5},{5... | collective-permute-start | bytes 2555912 | tf_op jit(solution)/shard_map/ppermute | solution.py:648
  79.3 20.9 %collective-permute-start.20 = (bf16[2,416,512]{2,1,0:T(8,128)(2,1)S(1)}, bf16[2,416,512]{2,1,0:T(8,128)(2,1)S(1)}, u32[]{:S(2)}, u32[]{:S(2)}) collective-permute-start(bf16[2,416,512]{2,1,0:T(8,128)(2,1)S(1)} %get-tuple-element.159), channel_id=1, source_target_pairs={{0,8},{4,12},{8,0},{12,4},{16,24},{20,28},{24,16},{28,20},{1,9},{5... | collective-permute-start | bytes 2555912 | tf_op jit(solution)/shard_map/ppermute | solution.py:648
  84.7 20.3 %collective-permute-start.12 = (bf16[768,512]{1,0:T(8,128)(2,1)S(1)}, bf16[768,512]{1,0:T(8,128)(2,1)S(1)}, u32[]{:S(2)}, u32[]{:S(2)}) collective-permute-start(bf16[768,512]{1,0:T(8,128)(2,1)S(1)} %get-tuple-element.130.refs_23_.refs_2_), channel_id=1, source_target_pairs={{0,2},{1,3},{2,0},{3,1},{4,6},{5,7},{6,4},{7,5},{8,10},{9,11},{10,... | collective-permute-start | bytes 2359304 | tf_op jit(solution)/shard_map/ppermute | solution.py:648
  95.1 5.5 %collective-permute-start.16 = (bf16[1536,128]{1,0:T(8,128)(2,1)S(1)}, bf16[1536,128]{1,0:T(8,128)(2,1)S(1)}, u32[]{:S(2)}, u32[]{:S(2)}) collective-permute-start(bf16[1536,128]{1,0:T(8,128)(2,1)S(1)} %get-tuple-element.146), channel_id=1, source_target_pairs={{0,1},{1,0},{2,3},{3,2},{4,5},{5,4},{6,7},{7,6},{8,9},{9,8},{10,11... | collective-permute-start | bytes 1179656 | tf_op jit(solution)/shard_map/ppermute | solution.py:648
  95.2 5.5 %collective-permute-start.17 = (bf16[1536,128]{1,0:T(8,128)(2,1)S(1)}, bf16[1536,128]{1,0:T(8,128)(2,1)S(1)}, u32[]{:S(2)}, u32[]{:S(2)}) collective-permute-start(bf16[1536,128]{1,0:T(8,128)(2,1)S(1)} %get-tuple-element.147), channel_id=1, source_target_pairs={{0,1},{1,0},{2,3},{3,2},{4,5},{5,4},{6,7},{7,6},{8,9},{9,8},{10,11... | collective-permute-start | bytes 1179656 | tf_op jit(solution)/shard_map/ppermute | solution.py:648
  98.7 1.9 %collective-permute-start.18 = (f32[128,128]{1,0:T(8,128)S(1)}, f32[128,128]{1,0:T(8,128)S(1)}, u32[]{:S(2)}, u32[]{:S(2)}) collective-permute-start(f32[128,128]{1,0:T(8,128)S(1)} %get-tuple-element.156.refs_6_), channel_id=1, source_target_pairs={{0,1},{1,0},{2,3},{3,2},{4,5},{5,4},{6,7},{7,6},{8,9},{9,8},{10,11... | collective-permute-start | bytes 196616 | tf_op jit(solution)/shard_map/ppermute | solution.py:648
  100.8 12.1 %collective-permute-start.24 = (bf16[1664,128]{1,0:T(8,128)(2,1)S(1)}, bf16[1664,128]{1,0:T(8,128)(2,1)S(1)}, u32[]{:S(2)}, u32[]{:S(2)}) collective-permute-start(bf16[1664,128]{1,0:T(8,128)(2,1)S(1)} %get-tuple-element.166), channel_id=1, source_target_pairs={{0,2},{1,3},{2,0},{3,1},{4,6},{5,7},{6,4},{7,5},{8,10},{9,11},{10,... | collective-permute-start | bytes 1277960 | tf_op jit(solution)/shard_map/ppermute | solution.py:648
  102.4 11.2 %collective-permute-start.22 = (bf16[2,208,512]{2,1,0:T(8,128)(2,1)S(1)}, bf16[2,208,512]{2,1,0:T(8,128)(2,1)S(1)}, u32[]{:S(2)}, u32[]{:S(2)}) collective-permute-start(bf16[2,208,512]{2,1,0:T(8,128)(2,1)S(1)} %get-tuple-element.163), channel_id=1, source_target_pairs={{0,8},{4,12},{8,0},{12,4},{16,24},{20,28},{24,16},{28,20},{1,9},{5... | collective-permute-start | bytes 1277960 | tf_op jit(solution)/shard_map/ppermute | solution.py:648
  103.9 10.9 %collective-permute-start.23 = (bf16[2,208,512]{2,1,0:T(8,128)(2,1)S(1)}, bf16[2,208,512]{2,1,0:T(8,128)(2,1)S(1)}, u32[]{:S(2)}, u32[]{:S(2)}) collective-permute-start(bf16[2,208,512]{2,1,0:T(8,128)(2,1)S(1)} %get-tuple-element.165), channel_id=1, source_target_pairs={{0,4},{4,0},{8,12},{12,8},{16,20},{20,16},{24,28},{28,24},{1,5},{5... | collective-permute-start | bytes 1277960 | tf_op jit(solution)/shard_map/ppermute | solution.py:648
  105.2 25.3 %collective-permute-start.21 = (bf16[1536,512]{1,0:T(8,128)(2,1)S(1)}, bf16[1536,512]{1,0:T(8,128)(2,1)S(1)}, u32[]{:S(2)}, u32[]{:S(2)}) collective-permute-start(bf16[1536,512]{1,0:T(8,128)(2,1)S(1)} %pair.2.refs_4_), channel_id=1, source_target_pairs={{0,1},{1,0},{2,3},{3,2},{4,5},{5,4},{6,7},{7,6},{8,9},{9,8},{10,11... | collective-permute-start | bytes 4718600 | tf_op jit(solution)/shard_map/ppermute | solution.py:648
  115.1 10.1 %collective-permute-start.25 = (bf16[416,512]{1,0:T(8,128)(2,1)S(1)}, bf16[416,512]{1,0:T(8,128)(2,1)S(1)}, u32[]{:S(2)}, u32[]{:S(2)}) collective-permute-start(bf16[416,512]{1,0:T(8,128)(2,1)S(1)} %get-tuple-element.169), channel_id=1, source_target_pairs={{0,2},{1,3},{2,0},{3,1},{4,6},{5,7},{6,4},{7,5},{8,10},{9,11},{10,... | collective-permute-start | bytes 1277960 | tf_op jit(solution)/shard_map/ppermute | solution.py:648
  115.7 5.8 %collective-permute-start.26 = (bf16[832,128]{1,0:T(8,128)(2,1)S(1)}, bf16[832,128]{1,0:T(8,128)(2,1)S(1)}, u32[]{:S(2)}, u32[]{:S(2)}) collective-permute-start(bf16[832,128]{1,0:T(8,128)(2,1)S(1)} %get-tuple-element.170), channel_id=1, source_target_pairs={{0,4},{4,0},{8,12},{12,8},{16,20},{20,16},{24,28},{28,24},{1,5},{5... | collective-permute-start | bytes 638984 | tf_op jit(solution)/shard_map/ppermute | solution.py:648
  125.2 20.5 %collective-permute-start.27 = (bf16[720,512]{1,0:T(8,128)(2,1)S(1)}, bf16[720,512]{1,0:T(8,128)(2,1)S(1)}, u32[]{:S(2)}, u32[]{:S(2)}) collective-permute-start(bf16[720,512]{1,0:T(8,128)(2,1)S(1)} %get-tuple-element.173.refs_2_), channel_id=1, source_target_pairs={{0,2},{1,3},{2,0},{3,1},{4,6},{5,7},{6,4},{7,5},{8,10},{9,11},{10,... | collective-permute-start | bytes 2211848 | tf_op jit(solution)/shard_map/ppermute | solution.py:648
  126.3 19.3 %collective-permute-start.28 = (bf16[416,512]{1,0:T(8,128)(2,1)S(1)}, bf16[416,512]{1,0:T(8,128)(2,1)S(1)}, u32[]{:S(2)}, u32[]{:S(2)}) collective-permute-start(bf16[416,512]{1,0:T(8,128)(2,1)S(1)} %sums.3.refs_6_.refs_2_), channel_id=1, source_target_pairs={{0,16},{4,20},{8,24},{12,28},{16,0},{20,4},{24,8},{28,12},{1,17},{... | collective-permute-start | bytes 1277960 | tf_op jit(solution)/shard_map/ppermute | solution.py:648
  128.9 9.1 %collective-permute-start.29 = (bf16[416,128]{1,0:T(8,128)(2,1)S(1)}, bf16[416,128]{1,0:T(8,128)(2,1)S(1)}, u32[]{:S(2)}, u32[]{:S(2)}) collective-permute-start(bf16[416,128]{1,0:T(8,128)(2,1)S(1)} %get-tuple-element.174), channel_id=1, source_target_pairs={{0,8},{4,12},{8,0},{12,4},{16,24},{20,28},{24,16},{28,20},{1,9},{5... | collective-permute-start | bytes 319496 | tf_op jit(solution)/shard_map/ppermute | solution.py:648
  145.8 8.9 %collective-permute-start.30 = (bf16[1440,512]{1,0:T(8,128)(2,1)S(1)}, bf16[1440,512]{1,0:T(8,128)(2,1)S(1)}, u32[]{:S(2)}, u32[]{:S(2)}) collective-permute-start(bf16[1440,512]{1,0:T(8,128)(2,1)S(1)} %pair.3.refs_4_), channel_id=1, source_target_pairs={{0,1},{1,0},{2,3},{3,2},{4,5},{5,4},{6,7},{7,6},{8,9},{9,8},{10,11... | collective-permute-start | bytes 4423688 | tf_op jit(solution)/shard_map/ppermute | solution.py:648
  145.9 8.7 %collective-permute-start.31 = (bf16[416,128]{1,0:T(8,128)(2,1)S(1)}, bf16[416,128]{1,0:T(8,128)(2,1)S(1)}, u32[]{:S(2)}, u32[]{:S(2)}) collective-permute-start(bf16[416,128]{1,0:T(8,128)(2,1)S(1)} %sums.4.refs_4_.refs_2_), channel_id=1, source_target_pairs={{0,16},{4,20},{8,24},{12,28},{16,0},{20,4},{24,8},{28,12},{1,17},{... | collective-permute-start | bytes 319496 | tf_op jit(solution)/shard_map/ppermute | solution.py:648
  146.0 15.3 %collective-permute-start.34 = (bf16[208,512]{1,0:T(8,128)(2,1)S(1)}, bf16[208,512]{1,0:T(8,128)(2,1)S(1)}, u32[]{:S(2)}, u32[]{:S(2)}) collective-permute-start(bf16[208,512]{1,0:T(8,128)(2,1)S(1)} %get-tuple-element.175.refs_4_.refs_2_), channel_id=1, source_target_pairs={{0,8},{4,12},{8,0},{12,4},{16,24},{20,28},{24,16},{28,20},{1,9},{5... | collective-permute-start | bytes 638984 | tf_op jit(solution)/shard_map/ppermute | solution.py:648
  150.0 11.2 %collective-permute-start.35 = (bf16[208,512]{1,0:T(8,128)(2,1)S(1)}, bf16[208,512]{1,0:T(8,128)(2,1)S(1)}, u32[]{:S(2)}, u32[]{:S(2)}) collective-permute-start(bf16[208,512]{1,0:T(8,128)(2,1)S(1)} %get-tuple-element.176.refs_4_), channel_id=1, source_target_pairs={{0,4},{4,0},{8,12},{12,8},{16,20},{20,16},{24,28},{28,24},{1,5},{5... | collective-permute-start | bytes 638984 | tf_op jit(solution)/shard_map/ppermute | solution.py:648
  154.6 4.8 %collective-permute-start.32 = (bf16[416,128]{1,0:T(8,128)(2,1)S(1)}, bf16[416,128]{1,0:T(8,128)(2,1)S(1)}, u32[]{:S(2)}, u32[]{:S(2)}) collective-permute-start(bf16[416,128]{1,0:T(8,128)(2,1)S(1)} %sums.5.refs_6_.refs_2_), channel_id=1, source_target_pairs={{0,8},{4,12},{8,0},{12,4},{16,24},{20,28},{24,16},{28,20},{1,9},{5... | collective-permute-start | bytes 319496 | tf_op jit(solution)/shard_map/ppermute | solution.py:648
  161.3 12.6 %collective-permute-start.36 = (bf16[416,512]{1,0:T(8,128)(2,1)S(1)}, bf16[416,512]{1,0:T(8,128)(2,1)S(1)}, u32[]{:S(2)}, u32[]{:S(2)}) collective-permute-start(bf16[416,512]{1,0:T(8,128)(2,1)S(1)} %get-tuple-element.177.refs_2_.refs_6_), channel_id=1, source_target_pairs={{0,4},{4,0},{8,12},{12,8},{16,20},{20,16},{24,28},{28,24},{1,5},{5... | collective-permute-start | bytes 1277960 | tf_op jit(solution)/shard_map/ppermute | solution.py:648
  162.9 11.0 %collective-permute-start.37 = (bf16[416,512]{1,0:T(8,128)(2,1)S(1)}, bf16[416,512]{1,0:T(8,128)(2,1)S(1)}, u32[]{:S(2)}, u32[]{:S(2)}) collective-permute-start(bf16[416,512]{1,0:T(8,128)(2,1)S(1)} %get-tuple-element.178.refs_4_), channel_id=1, source_target_pairs={{0,8},{4,12},{8,0},{12,4},{16,24},{20,28},{24,16},{28,20},{1,9},{5... | collective-permute-start | bytes 1277960 | tf_op jit(solution)/shard_map/ppermute | solution.py:648
  163.2 13.1 %collective-permute-start.33 = (bf16[832,128]{1,0:T(8,128)(2,1)S(1)}, bf16[832,128]{1,0:T(8,128)(2,1)S(1)}, u32[]{:S(2)}, u32[]{:S(2)}) collective-permute-start(bf16[832,128]{1,0:T(8,128)(2,1)S(1)} %joins.2.refs_6_.refs_2_), channel_id=1, source_target_pairs={{0,4},{4,0},{8,12},{12,8},{16,20},{20,16},{24,28},{28,24},{1,5},{5... | collective-permute-start | bytes 638984 | tf_op jit(solution)/shard_map/ppermute | solution.py:648
  (4 other events, 5.8 us)

commit v6 on v5

--- a/solution.py
+++ b/solution.py
@@ -14,7 +14,7 @@
 BF = jnp.bfloat16
 F32 = jnp.float32
 MIB = 1 << 20
-KNOBS = {'cost': 0, 'window': 'MA2', 'tail': 'OFpFOFOcFOgFrFO', 'out_tie': 'w', 'hs_tie': 'fq', 'rs_tie': '', 'g_tie': 'O3', 'vm': 18, 'vs': 16, 'vf': 60, 'vh': 16, 'vz': 24, 'ud_tie': 'a'}
+KNOBS = {'cost': 0, 'window': 'MA2', 'tail': 'OFpFOFOcFOgFrFO', 'out_tie': 'Aw', 'hs_tie': 'fq', 'rs_tie': '', 'g_tie': 'O3', 'vm': 18, 'vs': 16, 'vf': 60, 'vh': 16, 'vz': 16, 'ud_tie': 'a'}
 FB = 8
 GROUP = 16
 HEADS = 4
@@ -820,21 +820,30 @@
         [scr, scr, pltpu.VMEM((5 * width, HD), F32)], vmem=KNOBS["vz"])
 
 
-def finish_feature_kernel(t_ref, d_ref, own, other, qkv_ref, sums_ref, scr, *, mask):
+def finish_feature_kernel(
+    t_ref, d_ref, own, other, qkv_ref, feat_bias, row_bias, up_bias, down_bias, gains, shifts, scr, sums, *, mask
+):
     joined(d_ref, own, other, mask, scr)
     rows = qkv_ref.shape[0]
     qkv_ref[...] = scr[0:rows]
-    tall = sums_ref.shape[0]
+    tall = sums.shape[0]
     for j in range(4):
-        sums_ref[:, j * HD : (j + 1) * HD] = scr[rows + j * tall : rows + (j + 1) * tall]
+        sums[:, j * HD : (j + 1) * HD] = scr[rows + j * tall : rows + (j + 1) * tall]
+    down_bias[...] = sums[0:1]
+    row_bias[...] = sums[1:2]
+    feat_bias[...] = sums[8:9]
+    up_bias[...] = sums[pl.ds(16 + t_ref[0], 1), :]
+    for out, places in ((gains, (4, 9, 2)), (shifts, (5, 10, 3))):
+        for i, place in enumerate(places):
+            out[i : i + 1] = sums[place : place + 1]
 
 
 def finish_feature(t, own, other, mask, width, small):
     rows, w = own.shape
     return call(
         partial(finish_feature_kernel, mask=mask), "finish_feature", (), t, [(own, VMEM), (other, VMEM)],
-        [(shaped((3 * width, w), F32), VMEM), (shaped((small, 4 * HD), F32), VMEM)],
-        [pltpu.VMEM((2 * rows, w), F32)], vmem=16)
+        [(shaped((3 * width, w), F32), VMEM)] + [(shaped((n, width), F32), VMEM) for n in (1, 1, 1, 1, 3, 3)],
+        [pltpu.VMEM((2 * rows, w), F32), pltpu.VMEM((small, width), F32)], vmem=16)
 
 
 def shards(
@@ -864,9 +873,9 @@
     own_far = tied(own_far, kept)
     packs = own, core(own), own_far, core(own_far)
     mixed = [kept.value] + [swap(mixed[k], "tensor", k) for k in (1, 2, 3)]
-    a2, a3 = Box(mixed[2]), Box(mixed[3])
-    both_far = swap({"a": lambda: tied(both, a2, a3), "2": lambda: tied(both, a2), "": lambda: both}[KNOBS["ud_tie"]](), "tensor", 2)
-    mixed[2:] = a2.value, a3.value
+    a1, a2, a3 = Box(mixed[1]), Box(mixed[2]), Box(mixed[3])
+    both_far = swap({"c": lambda: tied(both, a1, a2, a3), "a": lambda: tied(both, a2, a3), "2": lambda: tied(both, a2), "": lambda: both}[KNOBS["ud_tie"]](), "tensor", 2)
+    mixed[1:] = a1.value, a2.value, a3.value
 
     first, n2, row_packed, row_p, o2, second, n3 = row_forward(
         t, splits, mixed, cells, packs, fob, rob, norm_gains, norm_biases, columns)
@@ -913,8 +922,12 @@
             ar, br = over(a_sent, near[0]), over(b_sent, near[1])
         else:
             last = [*last, pieces[2], pieces[3]]
-    if K["out_tie"] == "w":
-        out_far = swap(tied(out_f, boxes["w"], boxes["w2"]), "tensor", 2)
+    if K["out_tie"] in ("w", "Aw"):
+        after = [Box(feat_p)] if K["out_tie"] == "Aw" else []
+        out_far = swap(tied(out_f, boxes["w"], boxes["w2"], *after), "tensor", 2)
+        if after:
+            feat_p = after[0].value
+            last = [feat_p]
         pieces[2:] = boxes["w2"].value, boxes["w"].value
 
     g1, dqkv_f, f0, f2, f1, f3 = feature_backward((*t, *last), pieces, packs, feat_packed, feat_p, n1)
@@ -971,7 +984,7 @@
             fk, = out = joins(tt, ((fk, fr),), (near[1],))
             fr = over(fk, near[0])
         else:
-            feat_grad, small_sums = out = finish_feature(tt, fk, fr, near[0], width, small.shape[0] // 4)
+            feat_grad, *small_sums = out = finish_feature(tt, fk, fr, near[0], width, small.shape[0] // 4)
         state["F"] += 1
         return out[:1]
 
@@ -1002,7 +1015,7 @@
             box = Box(last[0])
             g0_far = swap(tied(g0, box), "tensor", 2)
             last = [box.value]
-    small = small_sums
+    feat_bias, row_bias, up_bias_grad, down_bias_grad, gain_grad, shift_grad = small_sums
 
     def qkv_shape(grad):
         return jnp.transpose(grad.reshape(3, width, HD), (1, 0, 2))
@@ -1013,16 +1026,16 @@
         home(input_grad),
         qkv_shape(feat_grad),
         grads_other[4],
-        small[8],
+        feat_bias.reshape(width),
         qkv_shape(grads_other[2]),
         grads_other[3],
-        small[1],
+        row_bias.reshape(width),
         grads_other[0],
-        lax.dynamic_index_in_dim(small, 16 + t[0][0], 0, keepdims=False),
+        up_bias_grad.reshape(up_bias.shape),
         grads_other[1],
-        small[0],
-        jnp.stack([small[4], small[9], small[2]]),
-        jnp.stack([small[5], small[10], small[3]]),
+        down_bias_grad.reshape(width),
+        gain_grad,
+        shift_grad,
     )
 
 

time: 183 us -> 182 us (level)
  no operation moved by 1% of the time
where the time goes in v6:
time: 182 us; the launch traced here: 179 us
  waiting for transfers between devices  72.9 us (40%)
  Pallas kernels  60.4 us (33%)
  starting transfers between devices  37.7 us (21%)
  local copies, waits for them, and re-layouts  5.86 us (3%)
  between operations  1.85 us (1%)
    ppermute x38, waiting for transfers between devices, swap(): return lax.ppermute(values, axis, [(i, i ^ mask) for i in range(count)])  72.9 us
    pallas_call x27, Pallas kernels, call(): pl.pallas_call(body, grid_spec=spec, out_shape=[a for a, _ in outs], comp...  60.4 us
    ppermute x38, starting transfers between devices, swap(): return lax.ppermute(values, axis, [(i, i ^ mask) for i in range(count)])  37.7 us
    unnamed x28, local copies, waits for them, and re-layouts  5.85 us
  transfers between devices with their start and end apart: 38, of which 20 were waited for; matrix products, arithmetic and copies ran while one was open for 0% of the time, Pallas kernels for 32%

profile of v6, /device:TPU:0, one launch (start us, length us, event | category | flops | bytes accessed | tf_op | source)
XLA Modules:
  0.0 178.7 jit_solution(13097600054285978674)
XLA Ops:
  0.7 2.0 %pack.1.refs_8_.refs_12_.refs_16_.refs_6_.refs_15_.refs_19_ = bf16[2576,128]{1,0:T(8,128)(2,1)} custom-call(s32[1]{0:T(128)} %bitcast.refs_0_, s32[1]{0:T(128)} %bitcast.1.refs_1_, bf16[3,512,128]{2,1,0:T(8,128)(2,1)} %bitcast.39, bf16[128,512]{1,0:T(8,128)(2,1)} %refs_3_.3, bf16[128,512]{1,0:T(8,128)(2,1)} %refs_4_.3, bf16[512]{0:T(512)(128)(2,1)} %refs_5_.2), custom_call_target="tpu_custom_call" | custom-call | flops 1 | bytes 1 | tf_op jit(solution)/shard_map/pack/pallas_call | solution.py:135
  2.7 2.9 %collective-permute-start = (bf16[2576,128]{1,0:T(8,128)(2,1)}, bf16[2576,128]{1,0:T(8,128)(2,1)}, u32[]{:S(2)}, u32[]{:S(2)}) collective-permute-start(bf16[2576,128]{1,0:T(8,128)(2,1)} %pack.1.refs_8_.refs_12_.refs_16_.refs_6_.refs_15_.refs_19_), channel_id=1, source_target_pairs={{0,2},{1,3},{2,0},{3,1},{4,6},{5,7},{6,4},{7,5},{8,10},{9,11},{10,... | collective-permute-start | bytes 1978376 | tf_op jit(solution)/shard_map/ppermute | solution.py:648
  5.6 8.7 %feature_forward.1 = (bf16[2,384,128]{2,1,0:T(8,128)(2,1)}, bf16[2,384,128]{2,1,0:T(8,128)(2,1)}, bf16[2,384,128]{2,1,0:T(8,128)(2,1)}, bf16[2,384,128]{2,1,0:T(8,128)(2,1)}, bf16[1024,512]{1,0:T(8,128)(2,1)}) custom-call(s32[1]{0:T(128)} %bitcast.refs_0_, s32[1]{0:T(128)} %bitcast.1.refs_1_, bf16[89,32,512]{2,1,0:T(8,128)(2,1)} %bitcast.26, ...), custom_call_target="tpu_custom_call" | custom-call | flops 1 | bytes 1 | tf_op jit(solution)/shard_map/feature_forward/pallas_call | solution.py:135
  15.3 1.2 collective-permute-start.7
  16.5 9.2 %collective-permute-done.2.refs_5_.refs_11_ = bf16[2,384,128]{2,1,0:T(8,128)(2,1)S(1)} collective-permute-done((bf16[2,384,128]{2,1,0:T(8,128)(2,1)}, bf16[2,384,128]{2,1,0:T(8,128)(2,1)S(1)}, u32[]{:S(2)}, u32[]{:S(2)}) %collective-permute-start.2) | collective-permute-done | bytes 196640 | tf_op jit(solution)/shard_map/ppermute | solution.py:648
  25.7 2.8 %collective-permute-done.3.refs_6_.refs_12_ = bf16[2,384,128]{2,1,0:T(8,128)(2,1)S(1)} collective-permute-done((bf16[2,384,128]{2,1,0:T(8,128)(2,1)}, bf16[2,384,128]{2,1,0:T(8,128)(2,1)S(1)}, u32[]{:S(2)}, u32[]{:S(2)}) %collective-permute-start.3) | collective-permute-done | bytes 196640 | tf_op jit(solution)/shard_map/ppermute | solution.py:648
  28.4 1.2 collective-permute-start.6
  31.5 2.0 %collective-permute-done.1.refs_4_.refs_10_ = bf16[2,384,128]{2,1,0:T(8,128)(2,1)S(1)} collective-permute-done((bf16[2,384,128]{2,1,0:T(8,128)(2,1)}, bf16[2,384,128]{2,1,0:T(8,128)(2,1)S(1)}, u32[]{:S(2)}, u32[]{:S(2)}) %collective-permute-start.1) | collective-permute-done | bytes 196640 | tf_op jit(solution)/shard_map/ppermute | solution.py:648
  34.5 5.3 %row_forward.1 = (f32[768,512]{1,0:T(8,128)S(1)}, bf16[768,512]{1,0:T(8,128)(2,1)S(1)}, bf16[768,1536]{1,0:T(8,128)(2,1)S(1)}, bf16[4,6,128,128]{3,2,1,0:T(8,128...) custom-call(s32[1]{0:T(128)} %bitcast.refs_0_, s32[1]{0:T(128)} %bitcast.1.refs_1_, ...), custom_call_target="tpu_custom_call" | custom-call | flops 1 | bytes 1 | tf_op jit(solution)/shard_map/row_forward/pallas_call | solution.py:135
  39.8 6.5 %hidden_first.1 = (f32[768,512]{1,0:T(8,128)S(1)}, f32[768,512]{1,0:T(8,128)S(1)}, bf16[1024,512]{1,0:T(8,128)(2,1)S(1)}, bf16[1024,512]{1,0:T(8,128)(2,1)S(1)},...) custom-call(s32[1]{0:T(128)} %bitcast.refs_0_, s32[1]{0:T(128)} %bitcast.1.refs_1_, ...), custom_call_target="tpu_custom_call" | custom-call | flops 1 | bytes 1 | tf_op jit(solution)/shard_map/hidden_first/pallas_call | solution.py:135
  46.3 7.8 %collective-permute-done.6.refs_4_.refs_8_ = bf16[1024,512]{1,0:T(8,128)(2,1)S(1)} collective-permute-done((bf16[1024,512]{1,0:T(8,128)(2,1)}, bf16[1024,512]{1,0:T(8,128)(2,1)S(1)}, u32[]{:S(2)}, u32[]{:S(2)}) %collective-permute-start.6) | collective-permute-done | bytes 1048608 | tf_op jit(solution)/shard_map/ppermute | solution.py:648
  54.2 1.9 %collective-permute-start.9 = (bf16[3,512,128]{2,1,0:T(8,128)(2,1)S(1)}, bf16[3,512,128]{2,1,0:T(8,128)(2,1)S(1)}, u32[]{:S(2)}, u32[]{:S(2)}) collective-permute-start(bf16[3,512,128]{2,1,0:T(8,128)(2,1)S(1)} %bitcast.35), channel_id=1, source_target_pairs={{0,2},{1,3},{2,0},{3,1},{4,6},{5,7},{6,4},{7,5},{8,10},{9,11},{10,... | collective-permute-start | bytes 1179656 | tf_op jit(solution)/shard_map/ppermute | solution.py:648
  56.8 8.8 %hidden_second.1 = (bf16[768,512]{1,0:T(8,128)(2,1)S(1)}, f32[768,512]{1,0:T(8,128)S(1)}, f32[8,512]{1,0:T(8,128)S(1)}, bf16[1024,512]{1,0:T(8,128)(2,1)S(1)}, b...) custom-call(s32[1]{0:T(128)} %bitcast.refs_0_, s32[1]{0:T(128)} %bitcast.1.refs_1_, ...), custom_call_target="tpu_custom_call" | custom-call | flops 1 | bytes 1 | tf_op jit(solution)/shard_map/hidden_second/pallas_call | solution.py:135
  65.8 6.9 %row_backward.1 = (bf16[192,512]{1,0:T(8,128)(2,1)S(1)}, bf16[960,512]{1,0:T(8,128)(2,1)S(1)}, bf16[192,512]{1,0:T(8,128)(2,1)S(1)}, bf16[192,512]{1,0:T(8,128)(...) custom-call(s32[1]{0:T(128)} %bitcast.refs_0_, ...), custom_call_target="tpu_custom_call" | custom-call | flops 1 | bytes 1 | tf_op jit(solution)/shard_map/row_backward/pallas_call | solution.py:135
  73.3 1.7 collective-permute-start.10
  75.8 1.6 ab_first.1
  77.4 1.9 %collective-permute-start.19 = (bf16[2,416,512]{2,1,0:T(8,128)(2,1)S(1)}, bf16[2,416,512]{2,1,0:T(8,128)(2,1)S(1)}, u32[]{:S(2)}, u32[]{:S(2)}) collective-permute-start(bf16[2,416,512]{2,1,0:T(8,128)(2,1)S(1)} %get-tuple-element.164), channel_id=1, source_target_pairs={{0,4},{4,0},{8,12},{12,8},{16,20},{20,16},{24,28},{28,24},{1,5},{5... | collective-permute-start | bytes 2555912 | tf_op jit(solution)/shard_map/ppermute | solution.py:648
  79.3 1.6 collective-permute-start.20
  80.9 3.2 %feature_again.1 = (bf16[768,512]{1,0:T(8,128)(2,1)S(1)}, bf16[8,96,1536]{2,1,0:T(8,128)(2,1)S(1)}, bf16[8,4,96,96]{3,2,1,0:T(8,128)(2,1)S(1)}) custom-call(s32[1]{0:T(128)} %bitcast.refs_0_, s32[1]{0:T(128)} %bitcast.1.refs_1_, bf16[89,32,512]{2,1,0:T(8,128)(2,1)S(1)} %bitcast.28, bf16[3,512]{1,0:T(4,128)(2,1)S(1)} %copy-done.9, ...), custom_call_target="tpu_custom_call" | custom-call | flops 1 | bytes 1 | tf_op jit(solution)/shard_map/feature_again/pallas_call | solution.py:135
  84.7 1.7 collective-permute-start.15
  86.5 5.4 %feature_backward.1 = (f32[768,512]{1,0:T(8,128)S(1)}, bf16[768,1536]{1,0:T(8,128)(2,1)S(1)}, bf16[1536,128]{1,0:T(8,128)(2,1)S(1)}, bf16[1536,128]{1,0:T(8,128)...) custom-call(s32[1]{0:T(128)} %bitcast.refs_0_, s32[1]{0:T(128)} %bitcast.1.refs_1_, ...), custom_call_target="tpu_custom_call" | custom-call | flops 1 | bytes 1 | tf_op jit(solution)/shard_map/feature_backward/pallas_call | solution.py:135
  92.4 2.4 %feature_input.1 = (bf16[720,512]{1,0:T(8,128)(2,1)S(1)}, f32[128,128]{1,0:T(8,128)S(1)}) custom-call(s32[1]{0:T(128)} %bitcast.refs_0_, s32[1]{0:T(128)} %bitcast.1.refs_1_, bf16[89,32,512]{2,1,0:T(8,128)(2,1)S(1)} %bitcast.29, f32[768,512]{1,0:T(8,128)S(1)} %get-tuple-element.155.refs_3_, bf16[768,1536]{1,0:T(8,128)(2,1)S(1)} %get-tuple-element.156.refs_4_, ...), custom_call_target="tpu_custom_call" | custom-call | flops 1 | bytes 1 | tf_op jit(solution)/shard_map/feature_input/pallas_call | solution.py:135
  94.8 3.9 %collective-permute-done.19.refs_3_ = bf16[2,416,512]{2,1,0:T(8,128)(2,1)S(1)} collective-permute-done((bf16[2,416,512]{2,1,0:T(8,128)(2,1)S(1)}, bf16[2,416,512]{2,1,0:T(8,128)(2,1)S(1)}, u32[]{:S(2)}, u32[]{:S(2)}) %collective-permute-start.19) | collective-permute-done | bytes 852000 | tf_op jit(solution)/shard_map/ppermute | solution.py:648
  98.7 1.5 collective-permute-done.20.refs_5_
  100.8 1.5 collective-permute-start.24
  102.4 1.6 collective-permute-start.22
  104.0 1.1 collective-permute-start.23
  105.3 7.7 %collective-permute-done.24.refs_3_ = bf16[1664,128]{1,0:T(8,128)(2,1)S(1)} collective-permute-done((bf16[1664,128]{1,0:T(8,128)(2,1)S(1)}, bf16[1664,128]{1,0:T(8,128)(2,1)S(1)}, u32[]{:S(2)}, u32[]{:S(2)}) %collective-permute-start.24) | collective-permute-done | bytes 426016 | tf_op jit(solution)/shard_map/ppermute | solution.py:648
  113.6 1.3 collective-permute-done.23.refs_5_
  115.7 1.5 collective-permute-start.26
  117.2 4.3 %collective-permute-done.26.refs_3_ = bf16[832,128]{1,0:T(8,128)(2,1)S(1)} collective-permute-done((bf16[832,128]{1,0:T(8,128)(2,1)S(1)}, bf16[832,128]{1,0:T(8,128)(2,1)S(1)}, u32[]{:S(2)}, u32[]{:S(2)}) %collective-permute-start.26) | collective-permute-done | bytes 213024 | tf_op jit(solution)/shard_map/ppermute | solution.py:648
  121.6 3.5 %collective-permute-done.25.refs_3_ = bf16[416,512]{1,0:T(8,128)(2,1)S(1)} collective-permute-done((bf16[416,512]{1,0:T(8,128)(2,1)S(1)}, bf16[416,512]{1,0:T(8,128)(2,1)S(1)}, u32[]{:S(2)}, u32[]{:S(2)}) %collective-permute-start.25) | collective-permute-done | bytes 426016 | tf_op jit(solution)/shard_map/ppermute | solution.py:648
  126.3 2.6 %collective-permute-start.28 = (bf16[416,512]{1,0:T(8,128)(2,1)S(1)}, bf16[416,512]{1,0:T(8,128)(2,1)S(1)}, u32[]{:S(2)}, u32[]{:S(2)}) collective-permute-start(bf16[416,512]{1,0:T(8,128)(2,1)S(1)} %sums.3.refs_6_.refs_2_), channel_id=1, source_target_pairs={{0,16},{4,20},{8,24},{12,28},{16,0},{20,4},{24,8},{28,12},{1,17},{... | collective-permute-start | bytes 1277960 | tf_op jit(solution)/shard_map/ppermute | solution.py:648
  128.9 1.6 collective-permute-start.29
  130.5 2.1 %columns_home.1.refs_4_ = bf16[89,32,512]{2,1,0:T(8,128)(2,1)} custom-call(s32[1]{0:T(128)} %bitcast.refs_0_, s32[1]{0:T(128)} %bitcast.1.refs_1_, bf16[768,512]{1,0:T(8,128)(2,1)S(1)} %get-tuple-element.145.refs_23_.refs_2_, bf16[1536,512]{1,0:T(8,128)(2,1)S(1)} %collective-permute-done.21.refs_3_.refs_5_, ...), custom_call_target="tpu_custom_call" | custom-call | flops 1 | bytes 1 | tf_op jit(solution)/shard_map/columns_home/pallas_call | solution.py:135
  132.6 5.4 %collective-permute-done.29.refs_3_ = bf16[416,128]{1,0:T(8,128)(2,1)S(1)} collective-permute-done((bf16[416,128]{1,0:T(8,128)(2,1)S(1)}, bf16[416,128]{1,0:T(8,128)(2,1)S(1)}, u32[]{:S(2)}, u32[]{:S(2)}) %collective-permute-start.29) | collective-permute-done | bytes 106528 | tf_op jit(solution)/shard_map/ppermute | solution.py:648
  138.0 1.8 %copy-done.4 = bf16[89,32,512]{2,1,0:T(8,128)(2,1)S(1)} copy-done((bf16[89,32,512]{2,1,0:T(8,128)(2,1)S(1)}, bf16[89,32,512]{2,1,0:T(8,128)(2,1)}, u32[]{:S(2)}) %copy-start.4) | copy-done | bytes 2916376
  139.9 5.8 %collective-permute-done.28.refs_3_ = bf16[416,512]{1,0:T(8,128)(2,1)S(1)} collective-permute-done((bf16[416,512]{1,0:T(8,128)(2,1)S(1)}, bf16[416,512]{1,0:T(8,128)(2,1)S(1)}, u32[]{:S(2)}, u32[]{:S(2)}) %collective-permute-start.28) | collective-permute-done | bytes 426016 | tf_op jit(solution)/shard_map/ppermute | solution.py:648
  146.0 4.0 %collective-permute-start.34 = (bf16[208,512]{1,0:T(8,128)(2,1)S(1)}, bf16[208,512]{1,0:T(8,128)(2,1)S(1)}, u32[]{:S(2)}, u32[]{:S(2)}) collective-permute-start(bf16[208,512]{1,0:T(8,128)(2,1)S(1)} %get-tuple-element.182.refs_4_.refs_2_), channel_id=1, source_target_pairs={{0,8},{4,12},{8,0},{12,4},{16,24},{20,28},{24,16},{28,20},{1,9},{5... | collective-permute-start | bytes 638984 | tf_op jit(solution)/shard_map/ppermute | solution.py:648
  150.0 1.5 collective-permute-start.35
  151.5 3.1 %collective-permute-done.31.refs_3_ = bf16[416,128]{1,0:T(8,128)(2,1)S(1)} collective-permute-done((bf16[416,128]{1,0:T(8,128)(2,1)S(1)}, bf16[416,128]{1,0:T(8,128)(2,1)S(1)}, u32[]{:S(2)}, u32[]{:S(2)}) %collective-permute-start.31) | collective-permute-done | bytes 106528 | tf_op jit(solution)/shard_map/ppermute | solution.py:648
  154.7 2.9 %rows_home.1.refs_4_ = bf16[89,32,512]{2,1,0:T(8,128)(2,1)} custom-call(s32[1]{0:T(128)} %bitcast.refs_0_, s32[1]{0:T(128)} %bitcast.1.refs_1_, bf16[720,512]{1,0:T(8,128)(2,1)S(1)} %get-tuple-element.180.refs_2_, bf16[1440,512]{1,0:T(8,128)(2,1)S(1)} %collective-permute-done.30.refs_3_.refs_5_, ...), custom_call_target="tpu_custom_call" | custom-call | flops 1 | bytes 1 | tf_op jit(solution)/shard_map/rows_home/pallas_call | solution.py:135
  157.6 1.8 %collective-permute-done.32.refs_3_ = bf16[416,128]{1,0:T(8,128)(2,1)S(1)} collective-permute-done((bf16[416,128]{1,0:T(8,128)(2,1)S(1)}, bf16[416,128]{1,0:T(8,128)(2,1)S(1)}, u32[]{:S(2)}, u32[]{:S(2)}) %collective-permute-start.32) | collective-permute-done | bytes 106528 | tf_op jit(solution)/shard_map/ppermute | solution.py:648
  159.4 1.8 %copy-done.2 = bf16[89,32,512]{2,1,0:T(8,128)(2,1)S(1)} copy-done((bf16[89,32,512]{2,1,0:T(8,128)(2,1)S(1)}, bf16[89,32,512]{2,1,0:T(8,128)(2,1)}, u32[]{:S(2)}) %copy-start.2) | copy-done | bytes 2916376
  161.4 1.6 collective-permute-start.36
  163.7 10.3 %collective-permute-done.36.refs_3_ = bf16[416,512]{1,0:T(8,128)(2,1)S(1)} collective-permute-done((bf16[416,512]{1,0:T(8,128)(2,1)S(1)}, bf16[416,512]{1,0:T(8,128)(2,1)S(1)}, u32[]{:S(2)}, u32[]{:S(2)}) %collective-permute-start.36) | collective-permute-done | bytes 426016 | tf_op jit(solution)/shard_map/ppermute | solution.py:648
  174.0 2.3 %finish.1 = (f32[512,512]{1,0:T(8,128)}, f32[512,512]{1,0:T(8,128)}, f32[1536,128]{1,0:T(8,128)}, f32[128,512]{1,0:T(8,128)}, f32[128,512]{1,0:T(8,128)}) custom-call(s32[1]{0:T(128)} %bitcast.refs_0_, s32[1]{0:T(128)} %bitcast.1.refs_1_, bf16[416,512]{1,0:T(8,128)(2,1)S(1)} %get-tuple-element.184.refs_2_.refs_6_, ...), custom_call_target="tpu_custom_call" | custom-call | flops 1 | bytes 1 | tf_op jit(solution)/shard_map/finish/pallas_call | solution.py:135
  176.3 1.2 copy-done.7
  (86 shorter events, 12.6 us)
Async XLA Ops:
  2.7 27.7 %collective-permute-start = (bf16[2576,128]{1,0:T(8,128)(2,1)}, bf16[2576,128]{1,0:T(8,128)(2,1)}, u32[]{:S(2)}, u32[]{:S(2)}) collective-permute-start(bf16[2576,128]{1,0:T(8,128)(2,1)} %pack.1.refs_8_.refs_12_.refs_16_.refs_6_.refs_15_.refs_19_), channel_id=1, source_target_pairs={{0,2},{1,3},{2,0},{3,1},{4,6},{5,7},{6,4},{7,5},{8,10},{9,11},{10,... | collective-permute-start | bytes 1978376 | tf_op jit(solution)/shard_map/ppermute | solution.py:648
  5.6 24.0 %copy-start.1 = (bf16[2576,128]{1,0:T(8,128)(2,1)S(1)}, bf16[2576,128]{1,0:T(8,128)(2,1)}, u32[]{:S(2)}) copy-start(bf16[2576,128]{1,0:T(8,128)(2,1)} %pack.1.refs_8_.refs_12_.refs_16_.refs_6_.refs_15_.refs_19_) | copy-start | bytes 1978372
  5.6 25.3 %copy-start.11 = (bf16[512]{0:T(512)(128)(2,1)S(1)}, bf16[512]{0:T(512)(128)(2,1)}, u32[]{:S(2)}) copy-start(bf16[512]{0:T(512)(128)(2,1)} %param.19) | copy-start | bytes 3076
  5.6 25.3 %copy-start.12 = (bf16[512]{0:T(512)(128)(2,1)S(1)}, bf16[512]{0:T(512)(128)(2,1)}, u32[]{:S(2)}) copy-start(bf16[512]{0:T(512)(128)(2,1)} %param.22) | copy-start | bytes 3076
  5.6 27.9 %copy-start = (bf16[1,32,89,512]{3,1,2,0:T(8,128)(2,1)S(1)}, bf16[1,32,89,512]{3,1,2,0:T(8,128)(2,1)}, u32[]{:S(2)}) copy-start(bf16[1,32,89,512]{3,1,2,0:T(8,128)(2,1)} %param.15) | copy-start | bytes 8749060
  5.6 27.9 %copy-start.9 = (bf16[3,512]{1,0:T(4,128)(2,1)S(1)}, bf16[3,512]{1,0:T(4,128)(2,1)}, u32[]{:S(2)}) copy-start(bf16[3,512]{1,0:T(4,128)(2,1)} %refs_5_.3) | copy-start | bytes 9220
  5.6 27.9 %copy-start.10 = (bf16[3,512]{1,0:T(4,128)(2,1)S(1)}, bf16[3,512]{1,0:T(4,128)(2,1)}, u32[]{:S(2)}) copy-start(bf16[3,512]{1,0:T(4,128)(2,1)} %refs_4_.5) | copy-start | bytes 9220
  14.3 11.4 %collective-permute-start.2 = (bf16[2,384,128]{2,1,0:T(8,128)(2,1)}, bf16[2,384,128]{2,1,0:T(8,128)(2,1)S(1)}, u32[]{:S(2)}, u32[]{:S(2)}) collective-permute-start(bf16[2,384,128]{2,1,0:T(8,128)(2,1)} %get-tuple-element.110), channel_id=1, source_target_pairs={{0,2},{1,3},{2,0},{3,1},{4,6},{5,7},{6,4},{7,5},{8,10},{9,11},{10,... | collective-permute-start | bytes 589832 | tf_op jit(solution)/shard_map/ppermute | solution.py:648
  14.4 14.0 %collective-permute-start.3 = (bf16[2,384,128]{2,1,0:T(8,128)(2,1)}, bf16[2,384,128]{2,1,0:T(8,128)(2,1)S(1)}, u32[]{:S(2)}, u32[]{:S(2)}) collective-permute-start(bf16[2,384,128]{2,1,0:T(8,128)(2,1)} %get-tuple-element.111), channel_id=1, source_target_pairs={{0,3},{1,2},{2,1},{3,0},{4,7},{5,6},{6,5},{7,4},{8,11},{9,10},{10,... | collective-permute-start | bytes 589832 | tf_op jit(solution)/shard_map/ppermute | solution.py:648
  15.3 24.5 %collective-permute-start.7 = (bf16[1024,512]{1,0:T(8,128)(2,1)}, bf16[1024,512]{1,0:T(8,128)(2,1)S(1)}, u32[]{:S(2)}, u32[]{:S(2)}) collective-permute-start(bf16[1024,512]{1,0:T(8,128)(2,1)} %get-tuple-element.116.refs_4_.refs_8_), channel_id=1, source_target_pairs={{0,1},{1,0},{2,3},{3,2},{4,5},{5,4},{6,7},{7,6},{8,9},{9,8},{10,11... | collective-permute-start | bytes 3145736 | tf_op jit(solution)/shard_map/ppermute | solution.py:648
  28.4 25.7 %collective-permute-start.6 = (bf16[1024,512]{1,0:T(8,128)(2,1)}, bf16[1024,512]{1,0:T(8,128)(2,1)S(1)}, u32[]{:S(2)}, u32[]{:S(2)}) collective-permute-start(bf16[1024,512]{1,0:T(8,128)(2,1)} %get-tuple-element.116.refs_4_.refs_8_), channel_id=1, source_target_pairs={{0,2},{1,3},{2,0},{3,1},{4,6},{5,7},{6,4},{7,5},{8,10},{9,11},{10,... | collective-permute-start | bytes 3145736 | tf_op jit(solution)/shard_map/ppermute | solution.py:648
  29.7 3.9 %collective-permute-start.4 = (bf16[2576,128]{1,0:T(8,128)(2,1)S(1)}, bf16[2576,128]{1,0:T(8,128)(2,1)S(1)}, u32[]{:S(2)}, u32[]{:S(2)}) collective-permute-start(bf16[2576,128]{1,0:T(8,128)(2,1)S(1)} %copy-done.1), channel_id=1, source_target_pairs={{0,1},{1,0},{2,3},{3,2},{4,5},{5,4},{6,7},{7,6},{8,9},{9,8},{10,11... | collective-permute-start | bytes 1978376 | tf_op jit(solution)/shard_map/ppermute | solution.py:648
  30.3 3.2 %collective-permute-start.5 = (bf16[2576,128]{1,0:T(8,128)(2,1)}, bf16[2576,128]{1,0:T(8,128)(2,1)S(1)}, u32[]{:S(2)}, u32[]{:S(2)}) collective-permute-start(bf16[2576,128]{1,0:T(8,128)(2,1)} %collective-permute-done.refs_10_.refs_14_.refs_18_.refs_6_.refs_17_.refs_21_.refs_8_), channel_id=1, source_target_pairs={{0,1},{1,0},{2,3},{3,2},{4,5},{5,4},{6,7},{7,6},{8,9},{9,8},{10,11... | collective-permute-start | bytes 1978376 | tf_op jit(solution)/shard_map/ppermute | solution.py:648
  30.4 3.1 %collective-permute-start.1 = (bf16[2,384,128]{2,1,0:T(8,128)(2,1)}, bf16[2,384,128]{2,1,0:T(8,128)(2,1)S(1)}, u32[]{:S(2)}, u32[]{:S(2)}) collective-permute-start(bf16[2,384,128]{2,1,0:T(8,128)(2,1)} %get-tuple-element.108), channel_id=1, source_target_pairs={{0,1},{1,0},{2,3},{3,2},{4,5},{5,4},{6,7},{7,6},{8,9},{9,8},{10,11... | collective-permute-start | bytes 589832 | tf_op jit(solution)/shard_map/ppermute | solution.py:648
  31.5 8.2 %copy-start.6 = (bf16[1024,512]{1,0:T(8,128)(2,1)S(1)}, bf16[1024,512]{1,0:T(8,128)(2,1)}, u32[]{:S(2)}) copy-start(bf16[1024,512]{1,0:T(8,128)(2,1)} %get-tuple-element.116.refs_4_.refs_8_) | copy-start | bytes 3145732
  34.5 5.3 %copy-start.3 = (bf16[1,32,89,512]{3,1,2,0:T(8,128)(2,1)S(1)}, bf16[1,32,89,512]{3,1,2,0:T(8,128)(2,1)}, u32[]{:S(2)}) copy-start(bf16[1,32,89,512]{3,1,2,0:T(8,128)(2,1)} %param.29) | copy-start | bytes 8749060
  39.8 14.4 %copy-start.5 = (bf16[512,3,128]{2,0,1:T(8,128)(2,1)S(1)}, bf16[512,3,128]{2,0,1:T(8,128)(2,1)}, u32[]{:S(2)}) copy-start(bf16[512,3,128]{2,0,1:T(8,128)(2,1)} %param.17) | copy-start | bytes 1179652
  39.8 16.3 %copy-start.13 = (bf16[512]{0:T(512)(128)(2,1)S(1)}, bf16[512]{0:T(512)(128)(2,1)}, u32[]{:S(2)}) copy-start(bf16[512]{0:T(512)(128)(2,1)} %param.26) | copy-start | bytes 3076
  54.2 2.7 %collective-permute-start.8 = (bf16[1024,512]{1,0:T(8,128)(2,1)S(1)}, bf16[1024,512]{1,0:T(8,128)(2,1)S(1)}, u32[]{:S(2)}, u32[]{:S(2)}) collective-permute-start(bf16[1024,512]{1,0:T(8,128)(2,1)S(1)} %collective-permute-done.6.refs_4_.refs_8_), channel_id=1, source_target_pairs={{0,1},{1,0},{2,3},{3,2},{4,5},{5,4},{6,7},{7,6},{8,9},{9,8},{10,11... | collective-permute-start | bytes 3145736 | tf_op jit(solution)/shard_map/ppermute | solution.py:648
  54.2 11.5 %collective-permute-start.9 = (bf16[3,512,128]{2,1,0:T(8,128)(2,1)S(1)}, bf16[3,512,128]{2,1,0:T(8,128)(2,1)S(1)}, u32[]{:S(2)}, u32[]{:S(2)}) collective-permute-start(bf16[3,512,128]{2,1,0:T(8,128)(2,1)S(1)} %bitcast.35), channel_id=1, source_target_pairs={{0,2},{1,3},{2,0},{3,1},{4,6},{5,7},{6,4},{7,5},{8,10},{9,11},{10,... | collective-permute-start | bytes 1179656 | tf_op jit(solution)/shard_map/ppermute | solution.py:648
  65.7 10.1 %collective-permute-start.13 = (bf16[2048,512]{1,0:T(8,128)(2,1)S(1)}, bf16[2048,512]{1,0:T(8,128)(2,1)S(1)}, u32[]{:S(2)}, u32[]{:S(2)}) collective-permute-start(bf16[2048,512]{1,0:T(8,128)(2,1)S(1)} %get-tuple-element.140), channel_id=1, source_target_pairs={{0,1},{1,0},{2,3},{3,2},{4,5},{5,4},{6,7},{7,6},{8,9},{9,8},{10,11... | collective-permute-start | bytes 6291464 | tf_op jit(solution)/shard_map/ppermute | solution.py:648
  72.7 3.1 %collective-permute-start.14 = (bf16[2,640,512]{2,1,0:T(8,128)(2,1)S(1)}, bf16[2,640,512]{2,1,0:T(8,128)(2,1)S(1)}, u32[]{:S(2)}, u32[]{:S(2)}) collective-permute-start(bf16[2,640,512]{2,1,0:T(8,128)(2,1)S(1)} %get-tuple-element.141), channel_id=1, source_target_pairs={{0,1},{1,0},{2,3},{3,2},{4,5},{5,4},{6,7},{7,6},{8,9},{9,8},{10,11... | collective-permute-start | bytes 3932168 | tf_op jit(solution)/shard_map/ppermute | solution.py:648
  73.2 7.7 %collective-permute-start.12 = (bf16[960,512]{1,0:T(8,128)(2,1)S(1)}, bf16[960,512]{1,0:T(8,128)(2,1)S(1)}, u32[]{:S(2)}, u32[]{:S(2)}) collective-permute-start(bf16[960,512]{1,0:T(8,128)(2,1)S(1)} %get-tuple-element.136), channel_id=1, source_target_pairs={{0,1},{1,0},{2,3},{3,2},{4,5},{5,4},{6,7},{7,6},{8,9},{9,8},{10,11... | collective-permute-start | bytes 2949128 | tf_op jit(solution)/shard_map/ppermute | solution.py:648
  73.3 10.8 %collective-permute-start.10 = (bf16[192,512]{1,0:T(8,128)(2,1)S(1)}, bf16[192,512]{1,0:T(8,128)(2,1)S(1)}, u32[]{:S(2)}, u32[]{:S(2)}) collective-permute-start(bf16[192,512]{1,0:T(8,128)(2,1)S(1)} %get-tuple-element.134), channel_id=1, source_target_pairs={{0,3},{1,2},{2,1},{3,0},{4,7},{5,6},{6,5},{7,4},{8,11},{9,10},{10,... | collective-permute-start | bytes 589832 | tf_op jit(solution)/shard_map/ppermute | solution.py:648
  75.0 9.7 %collective-permute-start.11 = (bf16[192,512]{1,0:T(8,128)(2,1)S(1)}, bf16[192,512]{1,0:T(8,128)(2,1)S(1)}, u32[]{:S(2)}, u32[]{:S(2)}) collective-permute-start(bf16[192,512]{1,0:T(8,128)(2,1)S(1)} %get-tuple-element.135), channel_id=1, source_target_pairs={{0,2},{1,3},{2,0},{3,1},{4,6},{5,7},{6,4},{7,5},{8,10},{9,11},{10,... | collective-permute-start | bytes 589832 | tf_op jit(solution)/shard_map/ppermute | solution.py:648
  77.4 21.3 %collective-permute-start.19 = (bf16[2,416,512]{2,1,0:T(8,128)(2,1)S(1)}, bf16[2,416,512]{2,1,0:T(8,128)(2,1)S(1)}, u32[]{:S(2)}, u32[]{:S(2)}) collective-permute-start(bf16[2,416,512]{2,1,0:T(8,128)(2,1)S(1)} %get-tuple-element.164), channel_id=1, source_target_pairs={{0,4},{4,0},{8,12},{12,8},{16,20},{20,16},{24,28},{28,24},{1,5},{5... | collective-permute-start | bytes 2555912 | tf_op jit(solution)/shard_map/ppermute | solution.py:648
  79.3 20.9 %collective-permute-start.20 = (bf16[2,416,512]{2,1,0:T(8,128)(2,1)S(1)}, bf16[2,416,512]{2,1,0:T(8,128)(2,1)S(1)}, u32[]{:S(2)}, u32[]{:S(2)}) collective-permute-start(bf16[2,416,512]{2,1,0:T(8,128)(2,1)S(1)} %get-tuple-element.166), channel_id=1, source_target_pairs={{0,8},{4,12},{8,0},{12,4},{16,24},{20,28},{24,16},{28,20},{1,9},{5... | collective-permute-start | bytes 2555912 | tf_op jit(solution)/shard_map/ppermute | solution.py:648
  84.7 20.4 %collective-permute-start.15 = (bf16[768,512]{1,0:T(8,128)(2,1)S(1)}, bf16[768,512]{1,0:T(8,128)(2,1)S(1)}, u32[]{:S(2)}, u32[]{:S(2)}) collective-permute-start(bf16[768,512]{1,0:T(8,128)(2,1)S(1)} %get-tuple-element.145.refs_23_.refs_2_), channel_id=1, source_target_pairs={{0,2},{1,3},{2,0},{3,1},{4,6},{5,7},{6,4},{7,5},{8,10},{9,11},{10,... | collective-permute-start | bytes 2359304 | tf_op jit(solution)/shard_map/ppermute | solution.py:648
  91.9 8.8 %collective-permute-start.16 = (bf16[1536,128]{1,0:T(8,128)(2,1)S(1)}, bf16[1536,128]{1,0:T(8,128)(2,1)S(1)}, u32[]{:S(2)}, u32[]{:S(2)}) collective-permute-start(bf16[1536,128]{1,0:T(8,128)(2,1)S(1)} %get-tuple-element.153), channel_id=1, source_target_pairs={{0,1},{1,0},{2,3},{3,2},{4,5},{5,4},{6,7},{7,6},{8,9},{9,8},{10,11... | collective-permute-start | bytes 1179656 | tf_op jit(solution)/shard_map/ppermute | solution.py:648
  91.9 8.7 %collective-permute-start.17 = (bf16[1536,128]{1,0:T(8,128)(2,1)S(1)}, bf16[1536,128]{1,0:T(8,128)(2,1)S(1)}, u32[]{:S(2)}, u32[]{:S(2)}) collective-permute-start(bf16[1536,128]{1,0:T(8,128)(2,1)S(1)} %get-tuple-element.154), channel_id=1, source_target_pairs={{0,1},{1,0},{2,3},{3,2},{4,5},{5,4},{6,7},{7,6},{8,9},{9,8},{10,11... | collective-permute-start | bytes 1179656 | tf_op jit(solution)/shard_map/ppermute | solution.py:648
  98.7 1.9 %collective-permute-start.18 = (f32[128,128]{1,0:T(8,128)S(1)}, f32[128,128]{1,0:T(8,128)S(1)}, u32[]{:S(2)}, u32[]{:S(2)}) collective-permute-start(f32[128,128]{1,0:T(8,128)S(1)} %get-tuple-element.163.refs_6_), channel_id=1, source_target_pairs={{0,1},{1,0},{2,3},{3,2},{4,5},{5,4},{6,7},{7,6},{8,9},{9,8},{10,11... | collective-permute-start | bytes 196616 | tf_op jit(solution)/shard_map/ppermute | solution.py:648
  100.8 12.1 %collective-permute-start.24 = (bf16[1664,128]{1,0:T(8,128)(2,1)S(1)}, bf16[1664,128]{1,0:T(8,128)(2,1)S(1)}, u32[]{:S(2)}, u32[]{:S(2)}) collective-permute-start(bf16[1664,128]{1,0:T(8,128)(2,1)S(1)} %get-tuple-element.173), channel_id=1, source_target_pairs={{0,2},{1,3},{2,0},{3,1},{4,6},{5,7},{6,4},{7,5},{8,10},{9,11},{10,... | collective-permute-start | bytes 1277960 | tf_op jit(solution)/shard_map/ppermute | solution.py:648
  102.4 11.2 %collective-permute-start.22 = (bf16[2,208,512]{2,1,0:T(8,128)(2,1)S(1)}, bf16[2,208,512]{2,1,0:T(8,128)(2,1)S(1)}, u32[]{:S(2)}, u32[]{:S(2)}) collective-permute-start(bf16[2,208,512]{2,1,0:T(8,128)(2,1)S(1)} %get-tuple-element.170), channel_id=1, source_target_pairs={{0,8},{4,12},{8,0},{12,4},{16,24},{20,28},{24,16},{28,20},{1,9},{5... | collective-permute-start | bytes 1277960 | tf_op jit(solution)/shard_map/ppermute | solution.py:648
  104.0 10.9 %collective-permute-start.23 = (bf16[2,208,512]{2,1,0:T(8,128)(2,1)S(1)}, bf16[2,208,512]{2,1,0:T(8,128)(2,1)S(1)}, u32[]{:S(2)}, u32[]{:S(2)}) collective-permute-start(bf16[2,208,512]{2,1,0:T(8,128)(2,1)S(1)} %get-tuple-element.172), channel_id=1, source_target_pairs={{0,4},{4,0},{8,12},{12,8},{16,20},{20,16},{24,28},{28,24},{1,5},{5... | collective-permute-start | bytes 1277960 | tf_op jit(solution)/shard_map/ppermute | solution.py:648
  105.2 25.3 %collective-permute-start.21 = (bf16[1536,512]{1,0:T(8,128)(2,1)S(1)}, bf16[1536,512]{1,0:T(8,128)(2,1)S(1)}, u32[]{:S(2)}, u32[]{:S(2)}) collective-permute-start(bf16[1536,512]{1,0:T(8,128)(2,1)S(1)} %pair.2.refs_4_), channel_id=1, source_target_pairs={{0,1},{1,0},{2,3},{3,2},{4,5},{5,4},{6,7},{7,6},{8,9},{9,8},{10,11... | collective-permute-start | bytes 4718600 | tf_op jit(solution)/shard_map/ppermute | solution.py:648
  115.1 10.1 %collective-permute-start.25 = (bf16[416,512]{1,0:T(8,128)(2,1)S(1)}, bf16[416,512]{1,0:T(8,128)(2,1)S(1)}, u32[]{:S(2)}, u32[]{:S(2)}) collective-permute-start(bf16[416,512]{1,0:T(8,128)(2,1)S(1)} %get-tuple-element.176), channel_id=1, source_target_pairs={{0,2},{1,3},{2,0},{3,1},{4,6},{5,7},{6,4},{7,5},{8,10},{9,11},{10,... | collective-permute-start | bytes 1277960 | tf_op jit(solution)/shard_map/ppermute | solution.py:648
  115.7 5.8 %collective-permute-start.26 = (bf16[832,128]{1,0:T(8,128)(2,1)S(1)}, bf16[832,128]{1,0:T(8,128)(2,1)S(1)}, u32[]{:S(2)}, u32[]{:S(2)}) collective-permute-start(bf16[832,128]{1,0:T(8,128)(2,1)S(1)} %get-tuple-element.177), channel_id=1, source_target_pairs={{0,4},{4,0},{8,12},{12,8},{16,20},{20,16},{24,28},{28,24},{1,5},{5... | collective-permute-start | bytes 638984 | tf_op jit(solution)/shard_map/ppermute | solution.py:648
  125.2 20.5 %collective-permute-start.27 = (bf16[720,512]{1,0:T(8,128)(2,1)S(1)}, bf16[720,512]{1,0:T(8,128)(2,1)S(1)}, u32[]{:S(2)}, u32[]{:S(2)}) collective-permute-start(bf16[720,512]{1,0:T(8,128)(2,1)S(1)} %get-tuple-element.180.refs_2_), channel_id=1, source_target_pairs={{0,2},{1,3},{2,0},{3,1},{4,6},{5,7},{6,4},{7,5},{8,10},{9,11},{10,... | collective-permute-start | bytes 2211848 | tf_op jit(solution)/shard_map/ppermute | solution.py:648
  126.3 19.3 %collective-permute-start.28 = (bf16[416,512]{1,0:T(8,128)(2,1)S(1)}, bf16[416,512]{1,0:T(8,128)(2,1)S(1)}, u32[]{:S(2)}, u32[]{:S(2)}) collective-permute-start(bf16[416,512]{1,0:T(8,128)(2,1)S(1)} %sums.3.refs_6_.refs_2_), channel_id=1, source_target_pairs={{0,16},{4,20},{8,24},{12,28},{16,0},{20,4},{24,8},{28,12},{1,17},{... | collective-permute-start | bytes 1277960 | tf_op jit(solution)/shard_map/ppermute | solution.py:648
  128.9 9.1 %collective-permute-start.29 = (bf16[416,128]{1,0:T(8,128)(2,1)S(1)}, bf16[416,128]{1,0:T(8,128)(2,1)S(1)}, u32[]{:S(2)}, u32[]{:S(2)}) collective-permute-start(bf16[416,128]{1,0:T(8,128)(2,1)S(1)} %get-tuple-element.181), channel_id=1, source_target_pairs={{0,8},{4,12},{8,0},{12,4},{16,24},{20,28},{24,16},{28,20},{1,9},{5... | collective-permute-start | bytes 319496 | tf_op jit(solution)/shard_map/ppermute | solution.py:648
  145.8 8.9 %collective-permute-start.30 = (bf16[1440,512]{1,0:T(8,128)(2,1)S(1)}, bf16[1440,512]{1,0:T(8,128)(2,1)S(1)}, u32[]{:S(2)}, u32[]{:S(2)}) collective-permute-start(bf16[1440,512]{1,0:T(8,128)(2,1)S(1)} %pair.3.refs_4_), channel_id=1, source_target_pairs={{0,1},{1,0},{2,3},{3,2},{4,5},{5,4},{6,7},{7,6},{8,9},{9,8},{10,11... | collective-permute-start | bytes 4423688 | tf_op jit(solution)/shard_map/ppermute | solution.py:648
  145.9 8.7 %collective-permute-start.31 = (bf16[416,128]{1,0:T(8,128)(2,1)S(1)}, bf16[416,128]{1,0:T(8,128)(2,1)S(1)}, u32[]{:S(2)}, u32[]{:S(2)}) collective-permute-start(bf16[416,128]{1,0:T(8,128)(2,1)S(1)} %sums.4.refs_4_.refs_2_), channel_id=1, source_target_pairs={{0,16},{4,20},{8,24},{12,28},{16,0},{20,4},{24,8},{28,12},{1,17},{... | collective-permute-start | bytes 319496 | tf_op jit(solution)/shard_map/ppermute | solution.py:648
  146.0 15.3 %collective-permute-start.34 = (bf16[208,512]{1,0:T(8,128)(2,1)S(1)}, bf16[208,512]{1,0:T(8,128)(2,1)S(1)}, u32[]{:S(2)}, u32[]{:S(2)}) collective-permute-start(bf16[208,512]{1,0:T(8,128)(2,1)S(1)} %get-tuple-element.182.refs_4_.refs_2_), channel_id=1, source_target_pairs={{0,8},{4,12},{8,0},{12,4},{16,24},{20,28},{24,16},{28,20},{1,9},{5... | collective-permute-start | bytes 638984 | tf_op jit(solution)/shard_map/ppermute | solution.py:648
  150.0 11.3 %collective-permute-start.35 = (bf16[208,512]{1,0:T(8,128)(2,1)S(1)}, bf16[208,512]{1,0:T(8,128)(2,1)S(1)}, u32[]{:S(2)}, u32[]{:S(2)}) collective-permute-start(bf16[208,512]{1,0:T(8,128)(2,1)S(1)} %get-tuple-element.183.refs_4_), channel_id=1, source_target_pairs={{0,4},{4,0},{8,12},{12,8},{16,20},{20,16},{24,28},{28,24},{1,5},{5... | collective-permute-start | bytes 638984 | tf_op jit(solution)/shard_map/ppermute | solution.py:648
  154.6 4.8 %collective-permute-start.32 = (bf16[416,128]{1,0:T(8,128)(2,1)S(1)}, bf16[416,128]{1,0:T(8,128)(2,1)S(1)}, u32[]{:S(2)}, u32[]{:S(2)}) collective-permute-start(bf16[416,128]{1,0:T(8,128)(2,1)S(1)} %sums.5.refs_6_.refs_2_), channel_id=1, source_target_pairs={{0,8},{4,12},{8,0},{12,4},{16,24},{20,28},{24,16},{28,20},{1,9},{5... | collective-permute-start | bytes 319496 | tf_op jit(solution)/shard_map/ppermute | solution.py:648
  161.4 12.6 %collective-permute-start.36 = (bf16[416,512]{1,0:T(8,128)(2,1)S(1)}, bf16[416,512]{1,0:T(8,128)(2,1)S(1)}, u32[]{:S(2)}, u32[]{:S(2)}) collective-permute-start(bf16[416,512]{1,0:T(8,128)(2,1)S(1)} %get-tuple-element.184.refs_2_.refs_6_), channel_id=1, source_target_pairs={{0,4},{4,0},{8,12},{12,8},{16,20},{20,16},{24,28},{28,24},{1,5},{5... | collective-permute-start | bytes 1277960 | tf_op jit(solution)/shard_map/ppermute | solution.py:648
  162.9 11.0 %collective-permute-start.37 = (bf16[416,512]{1,0:T(8,128)(2,1)S(1)}, bf16[416,512]{1,0:T(8,128)(2,1)S(1)}, u32[]{:S(2)}, u32[]{:S(2)}) collective-permute-start(bf16[416,512]{1,0:T(8,128)(2,1)S(1)} %get-tuple-element.185.refs_4_), channel_id=1, source_target_pairs={{0,8},{4,12},{8,0},{12,4},{16,24},{20,28},{24,16},{28,20},{1,9},{5... | collective-permute-start | bytes 1277960 | tf_op jit(solution)/shard_map/ppermute | solution.py:648
  163.2 13.1 %collective-permute-start.33 = (bf16[832,128]{1,0:T(8,128)(2,1)S(1)}, bf16[832,128]{1,0:T(8,128)(2,1)S(1)}, u32[]{:S(2)}, u32[]{:S(2)}) collective-permute-start(bf16[832,128]{1,0:T(8,128)(2,1)S(1)} %joins.2.refs_6_.refs_2_), channel_id=1, source_target_pairs={{0,4},{4,0},{8,12},{12,8},{16,20},{20,16},{24,28},{28,24},{1,5},{5... | collective-permute-start | bytes 638984 | tf_op jit(solution)/shard_map/ppermute | solution.py:648
  (4 other events, 5.8 us)

commit v7 on v6

--- a/solution.py
+++ b/solution.py
@@ -693,32 +693,32 @@
 
 
 def first_halves(t, hg0, hg2, row_keep, got, row_got, masks):
-    hidden = hg0.shape[0] // 2
-    half = row_keep.shape[1] // 2
-    rows, width = hidden + half, hg0.shape[1]
-
-    def kernel(t_ref, d_ref, g0, g2, keep, r, row_r, ak, as_, bk, bs, scr):
-        for group, mine in enumerate((g0, g2)):
-            for which, (kept, sent, mask) in enumerate(((ak, as_, masks[0]), (bk, bs, masks[1]))):
-                at = which * hidden
-                scr[:hidden] = added(mine[at : at + hidden], r[2 * hidden * group + at : 2 * hidden * group + at + hidden])
-                at = which * half
-                scr[hidden:] = added(keep[group, at : at + half], row_r[group, at : at + half])
-                for out, first in zip((kept, sent), halves(d_ref, mask, rows // 2)):
-                    out[group] = scr[pl.ds(first, rows // 2), :].astype(BF)
-
-    return merge("ab_first", kernel, t, (hg0, hg2, row_keep, got, row_got), [(2, rows // 2, width)] * 4,
-                 [pltpu.VMEM((rows, width), F32)], vmem=20)
-
-
-def second_halves(t, a, ar, b, br, masks):
+    hidden, width = hg0.shape[0] // 2, hg0.shape[1]
+    tall, low = hidden // 2, row_keep.shape[1] // 4
+
+    def kernel(t_ref, d_ref, g0, g2, keep, r, row_r, ak, as_, bk, bs):
+        for which, (kept, sent, mask) in enumerate(((ak, as_, masks[0]), (bk, bs, masks[1]))):
+            for out, first in zip((kept, sent), halves(d_ref, mask, tall)):
+                for group, mine in enumerate((g0, g2)):
+                    here = pl.multiple_of(which * hidden + first, tall)
+                    there = pl.multiple_of((2 * group + which) * hidden + first, tall)
+                    out[group, :tall] = added(mine[pl.ds(here, tall), :], r[pl.ds(there, tall), :]).astype(BF)
+            for out, first in zip((kept, sent), halves(d_ref, mask, low)):
+                span = (slice(None), pl.ds(pl.multiple_of(2 * which * low + first, low), low), slice(None))
+                out[:, tall:] = added(keep[span], row_r[span]).astype(BF)
+
+    return merge("ab_first", kernel, t, (hg0, hg2, row_keep, got, row_got), [(2, tall + low, width)] * 4, vmem=20)
+
+
+def second_halves(t, a, ar, b, br, masks, tall):
     _, rows, width = a.shape
 
     def kernel(t_ref, d_ref, a, ar, b, br, ak, as_, bk, bs):
         for x, y, kept, sent, mask in ((a, ar, ak, as_, masks[1]), (b, br, bk, bs, masks[0])):
-            for out, first in zip((kept, sent), halves(d_ref, mask, rows // 2)):
-                span = (slice(None), pl.ds(first, rows // 2), slice(None))
-                out[...] = added(x[span], y[span]).astype(BF)
+            for base, half in ((0, tall // 2), (tall, (rows - tall) // 2)):
+                for out, first in zip((kept, sent), halves(d_ref, mask, half)):
+                    span = (slice(None), pl.ds(pl.multiple_of(base + first, 16), half), slice(None))
+                    out[:, base // 2 : base // 2 + half] = added(x[span], y[span]).astype(BF)
 
     return merge("ab_second", kernel, t, (a, ar, b, br), [(2, rows // 2, width)] * 4)
 
@@ -751,12 +751,14 @@
     return merge("ab_apart", kernel, t, (k, r), [(rows, width)] * 2)
 
 
-def joins(t, pairs, masks):
+def joins(t, pairs, masks, first_part=None):
     def kernel(t_ref, d_ref, *refs):
         for j, mask in enumerate(masks):
             own, other, out = refs[2 * j], refs[2 * j + 1], refs[2 * len(masks) + j]
-            for source, first in zip((own, other), halves(d_ref, mask, own.shape[0])):
-                out[pl.ds(first, own.shape[0]), :] = source[...]
+            rows = own.shape[0]
+            for base, count in [(0, rows)] if first_part is None else [(0, first_part), (first_part, rows - first_part)]:
+                for source, first in zip((own, other), halves(d_ref, mask, count)):
+                    out[pl.ds(pl.multiple_of(2 * base + first, 16), count), :] = source[base : base + count]
 
     return merge("joins", kernel, t, [a for p in pairs for a in p], [(2 * p[0].shape[0], p[0].shape[1]) for p in pairs])
 
@@ -793,9 +795,11 @@
 
 
 def finish_kernel(t_ref, d_ref, a0, a1, b0, b1, up_ref, down_ref, qkv_ref, row_out_ref, feat_out_ref, scr_a, scr_b, tall, *, masks):
-    joined(d_ref, a0, a1, masks[0], scr_a)
-    joined(d_ref, b0, b1, masks[1], scr_b)
     width = up_ref.shape[0]
+    for own, other, mask, scr in ((a0, a1, masks[0], scr_a), (b0, b1, masks[1], scr_b)):
+        for base, count in ((0, width // 2), (width // 2, own.shape[0] - width // 2)):
+            for source, first in zip((own, other), halves(d_ref, mask, count)):
+                scr[pl.ds(pl.multiple_of(2 * base + first, 16), count), :] = source[base : base + count].astype(F32)
     half = scr_a.shape[0] - width
     up_ref[...] = scr_a[0:width]
     down_ref[...] = scr_b[0:width].T
@@ -945,7 +949,7 @@
         here = state["O"]
         tt = (*t, *last)
         if here == 0:
-            ak, a_sent, bk, b_sent = out = second_halves(tt, ak, ar, bk, br, near)
+            ak, a_sent, bk, b_sent = out = second_halves(tt, ak, ar, bk, br, near, width // 2)
             ar, br = over(a_sent, near[1]), over(b_sent, near[0])
         elif here == 1:
             ab, sent = out = groups_apart(tt, ak, ar, bk, br)
@@ -957,7 +961,7 @@
             ak, bk = out = sums_apart(tt, ab, abr)
             ar, br = over(ak, near[1]), over(bk, near[0])
         elif here == 3 + len(far):
-            ak, bk = out = joins(tt, ((ak, ar), (bk, br)), (near[1], near[0]))
+            ak, bk = out = joins(tt, ((ak, ar), (bk, br)), (near[1], near[0]), width // 4)
             ar, br = over(ak, near[0]), over(bk, near[1])
         else:
             grads_other = out = finish(tt, (ak, ar), (bk, br), near, width)

time: 182 us -> 181 us (level)
  no operation moved by 1% of the time
where the time goes in v7:
time: 181 us; the launch traced here: 178 us
  waiting for transfers between devices  72.5 us (40%)
  Pallas kernels  59.9 us (33%)
  starting transfers between devices  38.1 us (21%)
  local copies, waits for them, and re-layouts  5.86 us (3%)
  between operations  1.85 us (1%)
    ppermute x38, waiting for transfers between devices, swap(): return lax.ppermute(values, axis, [(i, i ^ mask) for i in range(count)])  72.5 us
    pallas_call x27, Pallas kernels, call(): pl.pallas_call(body, grid_spec=spec, out_shape=[a for a, _ in outs], comp...  59.9 us
    ppermute x38, starting transfers between devices, swap(): return lax.ppermute(values, axis, [(i, i ^ mask) for i in range(count)])  38.1 us
    unnamed x28, local copies, waits for them, and re-layouts  5.85 us
  transfers between devices with their start and end apart: 38, of which 20 were waited for; matrix products, arithmetic and copies ran while one was open for 0% of the time, Pallas kernels for 32%

profile of v7, /device:TPU:0, one launch (start us, length us, event | category | flops | bytes accessed | tf_op | source)
XLA Modules:
  0.0 178.2 jit_solution(1745405550973842079)
XLA Ops:
  0.7 2.0 %pack.1.refs_8_.refs_12_.refs_16_.refs_6_.refs_15_.refs_19_ = bf16[2576,128]{1,0:T(8,128)(2,1)} custom-call(s32[1]{0:T(128)} %bitcast.refs_0_, s32[1]{0:T(128)} %bitcast.1.refs_1_, bf16[3,512,128]{2,1,0:T(8,128)(2,1)} %bitcast.39, bf16[128,512]{1,0:T(8,128)(2,1)} %refs_3_.3, bf16[128,512]{1,0:T(8,128)(2,1)} %refs_4_.3, bf16[512]{0:T(512)(128)(2,1)} %refs_5_.2), custom_call_target="tpu_custom_call" | custom-call | flops 1 | bytes 1 | tf_op jit(solution)/shard_map/pack/pallas_call | solution.py:135
  2.7 2.9 %collective-permute-start = (bf16[2576,128]{1,0:T(8,128)(2,1)}, bf16[2576,128]{1,0:T(8,128)(2,1)}, u32[]{:S(2)}, u32[]{:S(2)}) collective-permute-start(bf16[2576,128]{1,0:T(8,128)(2,1)} %pack.1.refs_8_.refs_12_.refs_16_.refs_6_.refs_15_.refs_19_), channel_id=1, source_target_pairs={{0,2},{1,3},{2,0},{3,1},{4,6},{5,7},{6,4},{7,5},{8,10},{9,11},{10,... | collective-permute-start | bytes 1978376 | tf_op jit(solution)/shard_map/ppermute | solution.py:648
  5.6 8.7 %feature_forward.1 = (bf16[2,384,128]{2,1,0:T(8,128)(2,1)}, bf16[2,384,128]{2,1,0:T(8,128)(2,1)}, bf16[2,384,128]{2,1,0:T(8,128)(2,1)}, bf16[2,384,128]{2,1,0:T(8,128)(2,1)}, bf16[1024,512]{1,0:T(8,128)(2,1)}) custom-call(s32[1]{0:T(128)} %bitcast.refs_0_, s32[1]{0:T(128)} %bitcast.1.refs_1_, bf16[89,32,512]{2,1,0:T(8,128)(2,1)} %bitcast.26, ...), custom_call_target="tpu_custom_call" | custom-call | flops 1 | bytes 1 | tf_op jit(solution)/shard_map/feature_forward/pallas_call | solution.py:135
  15.3 1.2 collective-permute-start.7
  16.5 9.2 %collective-permute-done.2.refs_5_.refs_11_ = bf16[2,384,128]{2,1,0:T(8,128)(2,1)S(1)} collective-permute-done((bf16[2,384,128]{2,1,0:T(8,128)(2,1)}, bf16[2,384,128]{2,1,0:T(8,128)(2,1)S(1)}, u32[]{:S(2)}, u32[]{:S(2)}) %collective-permute-start.2) | collective-permute-done | bytes 196640 | tf_op jit(solution)/shard_map/ppermute | solution.py:648
  25.7 2.8 %collective-permute-done.3.refs_6_.refs_12_ = bf16[2,384,128]{2,1,0:T(8,128)(2,1)S(1)} collective-permute-done((bf16[2,384,128]{2,1,0:T(8,128)(2,1)}, bf16[2,384,128]{2,1,0:T(8,128)(2,1)S(1)}, u32[]{:S(2)}, u32[]{:S(2)}) %collective-permute-start.3) | collective-permute-done | bytes 196640 | tf_op jit(solution)/shard_map/ppermute | solution.py:648
  28.4 1.2 collective-permute-start.6
  31.5 2.0 %collective-permute-done.1.refs_4_.refs_10_ = bf16[2,384,128]{2,1,0:T(8,128)(2,1)S(1)} collective-permute-done((bf16[2,384,128]{2,1,0:T(8,128)(2,1)}, bf16[2,384,128]{2,1,0:T(8,128)(2,1)S(1)}, u32[]{:S(2)}, u32[]{:S(2)}) %collective-permute-start.1) | collective-permute-done | bytes 196640 | tf_op jit(solution)/shard_map/ppermute | solution.py:648
  34.5 5.3 %row_forward.1 = (f32[768,512]{1,0:T(8,128)S(1)}, bf16[768,512]{1,0:T(8,128)(2,1)S(1)}, bf16[768,1536]{1,0:T(8,128)(2,1)S(1)}, bf16[4,6,128,128]{3,2,1,0:T(8,128...) custom-call(s32[1]{0:T(128)} %bitcast.refs_0_, s32[1]{0:T(128)} %bitcast.1.refs_1_, ...), custom_call_target="tpu_custom_call" | custom-call | flops 1 | bytes 1 | tf_op jit(solution)/shard_map/row_forward/pallas_call | solution.py:135
  39.8 6.5 %hidden_first.1 = (f32[768,512]{1,0:T(8,128)S(1)}, f32[768,512]{1,0:T(8,128)S(1)}, bf16[1024,512]{1,0:T(8,128)(2,1)S(1)}, bf16[1024,512]{1,0:T(8,128)(2,1)S(1)},...) custom-call(s32[1]{0:T(128)} %bitcast.refs_0_, s32[1]{0:T(128)} %bitcast.1.refs_1_, ...), custom_call_target="tpu_custom_call" | custom-call | flops 1 | bytes 1 | tf_op jit(solution)/shard_map/hidden_first/pallas_call | solution.py:135
  46.3 7.8 %collective-permute-done.6.refs_4_.refs_8_ = bf16[1024,512]{1,0:T(8,128)(2,1)S(1)} collective-permute-done((bf16[1024,512]{1,0:T(8,128)(2,1)}, bf16[1024,512]{1,0:T(8,128)(2,1)S(1)}, u32[]{:S(2)}, u32[]{:S(2)}) %collective-permute-start.6) | collective-permute-done | bytes 1048608 | tf_op jit(solution)/shard_map/ppermute | solution.py:648
  54.2 1.9 %collective-permute-start.9 = (bf16[3,512,128]{2,1,0:T(8,128)(2,1)S(1)}, bf16[3,512,128]{2,1,0:T(8,128)(2,1)S(1)}, u32[]{:S(2)}, u32[]{:S(2)}) collective-permute-start(bf16[3,512,128]{2,1,0:T(8,128)(2,1)S(1)} %bitcast.35), channel_id=1, source_target_pairs={{0,2},{1,3},{2,0},{3,1},{4,6},{5,7},{6,4},{7,5},{8,10},{9,11},{10,... | collective-permute-start | bytes 1179656 | tf_op jit(solution)/shard_map/ppermute | solution.py:648
  56.8 8.8 %hidden_second.1 = (bf16[768,512]{1,0:T(8,128)(2,1)S(1)}, f32[768,512]{1,0:T(8,128)S(1)}, f32[8,512]{1,0:T(8,128)S(1)}, bf16[1024,512]{1,0:T(8,128)(2,1)S(1)}, b...) custom-call(s32[1]{0:T(128)} %bitcast.refs_0_, s32[1]{0:T(128)} %bitcast.1.refs_1_, ...), custom_call_target="tpu_custom_call" | custom-call | flops 1 | bytes 1 | tf_op jit(solution)/shard_map/hidden_second/pallas_call | solution.py:135
  65.8 6.9 %row_backward.1 = (bf16[192,512]{1,0:T(8,128)(2,1)S(1)}, bf16[960,512]{1,0:T(8,128)(2,1)S(1)}, bf16[192,512]{1,0:T(8,128)(2,1)S(1)}, bf16[192,512]{1,0:T(8,128)(...) custom-call(s32[1]{0:T(128)} %bitcast.refs_0_, ...), custom_call_target="tpu_custom_call" | custom-call | flops 1 | bytes 1 | tf_op jit(solution)/shard_map/row_backward/pallas_call | solution.py:135
  73.3 1.7 collective-permute-start.10
  76.6 1.9 %collective-permute-start.19 = (bf16[2,416,512]{2,1,0:T(8,128)(2,1)S(1)}, bf16[2,416,512]{2,1,0:T(8,128)(2,1)S(1)}, u32[]{:S(2)}, u32[]{:S(2)}) collective-permute-start(bf16[2,416,512]{2,1,0:T(8,128)(2,1)S(1)} %get-tuple-element.164), channel_id=1, source_target_pairs={{0,4},{4,0},{8,12},{12,8},{16,20},{20,16},{24,28},{28,24},{1,5},{5... | collective-permute-start | bytes 2555912 | tf_op jit(solution)/shard_map/ppermute | solution.py:648
  78.4 1.6 collective-permute-start.20
  80.0 3.4 %feature_again.1 = (bf16[768,512]{1,0:T(8,128)(2,1)S(1)}, bf16[8,96,1536]{2,1,0:T(8,128)(2,1)S(1)}, bf16[8,4,96,96]{3,2,1,0:T(8,128)(2,1)S(1)}) custom-call(s32[1]{0:T(128)} %bitcast.refs_0_, s32[1]{0:T(128)} %bitcast.1.refs_1_, bf16[89,32,512]{2,1,0:T(8,128)(2,1)S(1)} %bitcast.28, bf16[3,512]{1,0:T(4,128)(2,1)S(1)} %copy-done.9, ...), custom_call_target="tpu_custom_call" | custom-call | flops 1 | bytes 1 | tf_op jit(solution)/shard_map/feature_again/pallas_call | solution.py:135
  83.4 1.3 collective-permute-done.11.refs_4_
  84.7 1.7 collective-permute-start.15
  86.5 5.4 %feature_backward.1 = (f32[768,512]{1,0:T(8,128)S(1)}, bf16[768,1536]{1,0:T(8,128)(2,1)S(1)}, bf16[1536,128]{1,0:T(8,128)(2,1)S(1)}, bf16[1536,128]{1,0:T(8,128)...) custom-call(s32[1]{0:T(128)} %bitcast.refs_0_, s32[1]{0:T(128)} %bitcast.1.refs_1_, ...), custom_call_target="tpu_custom_call" | custom-call | flops 1 | bytes 1 | tf_op jit(solution)/shard_map/feature_backward/pallas_call | solution.py:135
  92.4 2.4 %feature_input.1 = (bf16[720,512]{1,0:T(8,128)(2,1)S(1)}, f32[128,128]{1,0:T(8,128)S(1)}) custom-call(s32[1]{0:T(128)} %bitcast.refs_0_, s32[1]{0:T(128)} %bitcast.1.refs_1_, bf16[89,32,512]{2,1,0:T(8,128)(2,1)S(1)} %bitcast.29, f32[768,512]{1,0:T(8,128)S(1)} %get-tuple-element.155.refs_3_, bf16[768,1536]{1,0:T(8,128)(2,1)S(1)} %get-tuple-element.156.refs_4_, ...), custom_call_target="tpu_custom_call" | custom-call | flops 1 | bytes 1 | tf_op jit(solution)/shard_map/feature_input/pallas_call | solution.py:135
  94.8 3.1 %collective-permute-done.19.refs_3_ = bf16[2,416,512]{2,1,0:T(8,128)(2,1)S(1)} collective-permute-done((bf16[2,416,512]{2,1,0:T(8,128)(2,1)S(1)}, bf16[2,416,512]{2,1,0:T(8,128)(2,1)S(1)}, u32[]{:S(2)}, u32[]{:S(2)}) %collective-permute-start.19) | collective-permute-done | bytes 852000 | tf_op jit(solution)/shard_map/ppermute | solution.py:648
  97.9 1.5 collective-permute-done.20.refs_5_
  100.0 1.5 collective-permute-start.24
  101.6 1.6 collective-permute-start.22
  103.1 1.1 collective-permute-start.23
  105.4 7.6 %collective-permute-done.24.refs_3_ = bf16[1664,128]{1,0:T(8,128)(2,1)S(1)} collective-permute-done((bf16[1664,128]{1,0:T(8,128)(2,1)S(1)}, bf16[1664,128]{1,0:T(8,128)(2,1)S(1)}, u32[]{:S(2)}, u32[]{:S(2)}) %collective-permute-start.24) | collective-permute-done | bytes 426016 | tf_op jit(solution)/shard_map/ppermute | solution.py:648
  115.1 1.5 collective-permute-start.26
  116.6 4.3 %collective-permute-done.26.refs_3_ = bf16[832,128]{1,0:T(8,128)(2,1)S(1)} collective-permute-done((bf16[832,128]{1,0:T(8,128)(2,1)S(1)}, bf16[832,128]{1,0:T(8,128)(2,1)S(1)}, u32[]{:S(2)}, u32[]{:S(2)}) %collective-permute-start.26) | collective-permute-done | bytes 213024 | tf_op jit(solution)/shard_map/ppermute | solution.py:648
  121.0 3.3 %collective-permute-done.25.refs_3_ = bf16[416,512]{1,0:T(8,128)(2,1)S(1)} collective-permute-done((bf16[416,512]{1,0:T(8,128)(2,1)S(1)}, bf16[416,512]{1,0:T(8,128)(2,1)S(1)}, u32[]{:S(2)}, u32[]{:S(2)}) %collective-permute-start.25) | collective-permute-done | bytes 426016 | tf_op jit(solution)/shard_map/ppermute | solution.py:648
  124.4 1.3 collective-permute-start.27
  125.7 2.6 %collective-permute-start.28 = (bf16[416,512]{1,0:T(8,128)(2,1)S(1)}, bf16[416,512]{1,0:T(8,128)(2,1)S(1)}, u32[]{:S(2)}, u32[]{:S(2)}) collective-permute-start(bf16[416,512]{1,0:T(8,128)(2,1)S(1)} %sums.3.refs_6_.refs_2_), channel_id=1, source_target_pairs={{0,16},{4,20},{8,24},{12,28},{16,0},{20,4},{24,8},{28,12},{1,17},{... | collective-permute-start | bytes 1277960 | tf_op jit(solution)/shard_map/ppermute | solution.py:648
  128.3 1.6 collective-permute-start.29
  129.9 2.1 %columns_home.1.refs_4_ = bf16[89,32,512]{2,1,0:T(8,128)(2,1)} custom-call(s32[1]{0:T(128)} %bitcast.refs_0_, s32[1]{0:T(128)} %bitcast.1.refs_1_, bf16[768,512]{1,0:T(8,128)(2,1)S(1)} %get-tuple-element.145.refs_23_.refs_2_, bf16[1536,512]{1,0:T(8,128)(2,1)S(1)} %collective-permute-done.21.refs_3_.refs_5_, ...), custom_call_target="tpu_custom_call" | custom-call | flops 1 | bytes 1 | tf_op jit(solution)/shard_map/columns_home/pallas_call | solution.py:135
  131.9 5.4 %collective-permute-done.29.refs_3_ = bf16[416,128]{1,0:T(8,128)(2,1)S(1)} collective-permute-done((bf16[416,128]{1,0:T(8,128)(2,1)S(1)}, bf16[416,128]{1,0:T(8,128)(2,1)S(1)}, u32[]{:S(2)}, u32[]{:S(2)}) %collective-permute-start.29) | collective-permute-done | bytes 106528 | tf_op jit(solution)/shard_map/ppermute | solution.py:648
  137.4 1.8 %copy-done.4 = bf16[89,32,512]{2,1,0:T(8,128)(2,1)S(1)} copy-done((bf16[89,32,512]{2,1,0:T(8,128)(2,1)S(1)}, bf16[89,32,512]{2,1,0:T(8,128)(2,1)}, u32[]{:S(2)}) %copy-start.4) | copy-done | bytes 2916376
  139.2 5.7 %collective-permute-done.28.refs_3_ = bf16[416,512]{1,0:T(8,128)(2,1)S(1)} collective-permute-done((bf16[416,512]{1,0:T(8,128)(2,1)S(1)}, bf16[416,512]{1,0:T(8,128)(2,1)S(1)}, u32[]{:S(2)}, u32[]{:S(2)}) %collective-permute-start.28) | collective-permute-done | bytes 426016 | tf_op jit(solution)/shard_map/ppermute | solution.py:648
  145.4 4.0 %collective-permute-start.34 = (bf16[208,512]{1,0:T(8,128)(2,1)S(1)}, bf16[208,512]{1,0:T(8,128)(2,1)S(1)}, u32[]{:S(2)}, u32[]{:S(2)}) collective-permute-start(bf16[208,512]{1,0:T(8,128)(2,1)S(1)} %get-tuple-element.182.refs_4_.refs_2_), channel_id=1, source_target_pairs={{0,8},{4,12},{8,0},{12,4},{16,24},{20,28},{24,16},{28,20},{1,9},{5... | collective-permute-start | bytes 638984 | tf_op jit(solution)/shard_map/ppermute | solution.py:648
  149.4 1.5 collective-permute-start.35
  150.9 3.0 %collective-permute-done.31.refs_3_ = bf16[416,128]{1,0:T(8,128)(2,1)S(1)} collective-permute-done((bf16[416,128]{1,0:T(8,128)(2,1)S(1)}, bf16[416,128]{1,0:T(8,128)(2,1)S(1)}, u32[]{:S(2)}, u32[]{:S(2)}) %collective-permute-start.31) | collective-permute-done | bytes 106528 | tf_op jit(solution)/shard_map/ppermute | solution.py:648
  154.1 2.9 %rows_home.1.refs_4_ = bf16[89,32,512]{2,1,0:T(8,128)(2,1)} custom-call(s32[1]{0:T(128)} %bitcast.refs_0_, s32[1]{0:T(128)} %bitcast.1.refs_1_, bf16[720,512]{1,0:T(8,128)(2,1)S(1)} %get-tuple-element.180.refs_2_, bf16[1440,512]{1,0:T(8,128)(2,1)S(1)} %collective-permute-done.30.refs_3_.refs_5_, ...), custom_call_target="tpu_custom_call" | custom-call | flops 1 | bytes 1 | tf_op jit(solution)/shard_map/rows_home/pallas_call | solution.py:135
  157.0 1.8 %collective-permute-done.32.refs_3_ = bf16[416,128]{1,0:T(8,128)(2,1)S(1)} collective-permute-done((bf16[416,128]{1,0:T(8,128)(2,1)S(1)}, bf16[416,128]{1,0:T(8,128)(2,1)S(1)}, u32[]{:S(2)}, u32[]{:S(2)}) %collective-permute-start.32) | collective-permute-done | bytes 106528 | tf_op jit(solution)/shard_map/ppermute | solution.py:648
  158.8 1.8 %copy-done.2 = bf16[89,32,512]{2,1,0:T(8,128)(2,1)S(1)} copy-done((bf16[89,32,512]{2,1,0:T(8,128)(2,1)S(1)}, bf16[89,32,512]{2,1,0:T(8,128)(2,1)}, u32[]{:S(2)}) %copy-start.2) | copy-done | bytes 2916376
  160.7 1.6 collective-permute-start.36
  163.0 10.3 %collective-permute-done.36.refs_3_ = bf16[416,512]{1,0:T(8,128)(2,1)S(1)} collective-permute-done((bf16[416,512]{1,0:T(8,128)(2,1)S(1)}, bf16[416,512]{1,0:T(8,128)(2,1)S(1)}, u32[]{:S(2)}, u32[]{:S(2)}) %collective-permute-start.36) | collective-permute-done | bytes 426016 | tf_op jit(solution)/shard_map/ppermute | solution.py:648
  173.3 2.4 %finish.1 = (f32[512,512]{1,0:T(8,128)}, f32[512,512]{1,0:T(8,128)}, f32[1536,128]{1,0:T(8,128)}, f32[128,512]{1,0:T(8,128)}, f32[128,512]{1,0:T(8,128)}) custom-call(s32[1]{0:T(128)} %bitcast.refs_0_, s32[1]{0:T(128)} %bitcast.1.refs_1_, bf16[416,512]{1,0:T(8,128)(2,1)S(1)} %get-tuple-element.184.refs_2_.refs_6_, ...), custom_call_target="tpu_custom_call" | custom-call | flops 1 | bytes 1 | tf_op jit(solution)/shard_map/finish/pallas_call | solution.py:135
  175.7 1.2 copy-done.7
  (86 shorter events, 13.2 us)
Async XLA Ops:
  2.7 27.7 %collective-permute-start = (bf16[2576,128]{1,0:T(8,128)(2,1)}, bf16[2576,128]{1,0:T(8,128)(2,1)}, u32[]{:S(2)}, u32[]{:S(2)}) collective-permute-start(bf16[2576,128]{1,0:T(8,128)(2,1)} %pack.1.refs_8_.refs_12_.refs_16_.refs_6_.refs_15_.refs_19_), channel_id=1, source_target_pairs={{0,2},{1,3},{2,0},{3,1},{4,6},{5,7},{6,4},{7,5},{8,10},{9,11},{10,... | collective-permute-start | bytes 1978376 | tf_op jit(solution)/shard_map/ppermute | solution.py:648
  5.6 24.0 %copy-start.1 = (bf16[2576,128]{1,0:T(8,128)(2,1)S(1)}, bf16[2576,128]{1,0:T(8,128)(2,1)}, u32[]{:S(2)}) copy-start(bf16[2576,128]{1,0:T(8,128)(2,1)} %pack.1.refs_8_.refs_12_.refs_16_.refs_6_.refs_15_.refs_19_) | copy-start | bytes 1978372
  5.6 25.3 %copy-start.11 = (bf16[512]{0:T(512)(128)(2,1)S(1)}, bf16[512]{0:T(512)(128)(2,1)}, u32[]{:S(2)}) copy-start(bf16[512]{0:T(512)(128)(2,1)} %param.19) | copy-start | bytes 3076
  5.6 25.3 %copy-start.12 = (bf16[512]{0:T(512)(128)(2,1)S(1)}, bf16[512]{0:T(512)(128)(2,1)}, u32[]{:S(2)}) copy-start(bf16[512]{0:T(512)(128)(2,1)} %param.22) | copy-start | bytes 3076
  5.6 27.9 %copy-start = (bf16[1,32,89,512]{3,1,2,0:T(8,128)(2,1)S(1)}, bf16[1,32,89,512]{3,1,2,0:T(8,128)(2,1)}, u32[]{:S(2)}) copy-start(bf16[1,32,89,512]{3,1,2,0:T(8,128)(2,1)} %param.15) | copy-start | bytes 8749060
  5.6 27.9 %copy-start.9 = (bf16[3,512]{1,0:T(4,128)(2,1)S(1)}, bf16[3,512]{1,0:T(4,128)(2,1)}, u32[]{:S(2)}) copy-start(bf16[3,512]{1,0:T(4,128)(2,1)} %refs_5_.3) | copy-start | bytes 9220
  5.6 27.9 %copy-start.10 = (bf16[3,512]{1,0:T(4,128)(2,1)S(1)}, bf16[3,512]{1,0:T(4,128)(2,1)}, u32[]{:S(2)}) copy-start(bf16[3,512]{1,0:T(4,128)(2,1)} %refs_4_.5) | copy-start | bytes 9220
  14.3 11.4 %collective-permute-start.2 = (bf16[2,384,128]{2,1,0:T(8,128)(2,1)}, bf16[2,384,128]{2,1,0:T(8,128)(2,1)S(1)}, u32[]{:S(2)}, u32[]{:S(2)}) collective-permute-start(bf16[2,384,128]{2,1,0:T(8,128)(2,1)} %get-tuple-element.110), channel_id=1, source_target_pairs={{0,2},{1,3},{2,0},{3,1},{4,6},{5,7},{6,4},{7,5},{8,10},{9,11},{10,... | collective-permute-start | bytes 589832 | tf_op jit(solution)/shard_map/ppermute | solution.py:648
  14.4 14.0 %collective-permute-start.3 = (bf16[2,384,128]{2,1,0:T(8,128)(2,1)}, bf16[2,384,128]{2,1,0:T(8,128)(2,1)S(1)}, u32[]{:S(2)}, u32[]{:S(2)}) collective-permute-start(bf16[2,384,128]{2,1,0:T(8,128)(2,1)} %get-tuple-element.111), channel_id=1, source_target_pairs={{0,3},{1,2},{2,1},{3,0},{4,7},{5,6},{6,5},{7,4},{8,11},{9,10},{10,... | collective-permute-start | bytes 589832 | tf_op jit(solution)/shard_map/ppermute | solution.py:648
  15.3 24.5 %collective-permute-start.7 = (bf16[1024,512]{1,0:T(8,128)(2,1)}, bf16[1024,512]{1,0:T(8,128)(2,1)S(1)}, u32[]{:S(2)}, u32[]{:S(2)}) collective-permute-start(bf16[1024,512]{1,0:T(8,128)(2,1)} %get-tuple-element.116.refs_4_.refs_8_), channel_id=1, source_target_pairs={{0,1},{1,0},{2,3},{3,2},{4,5},{5,4},{6,7},{7,6},{8,9},{9,8},{10,11... | collective-permute-start | bytes 3145736 | tf_op jit(solution)/shard_map/ppermute | solution.py:648
  28.4 25.7 %collective-permute-start.6 = (bf16[1024,512]{1,0:T(8,128)(2,1)}, bf16[1024,512]{1,0:T(8,128)(2,1)S(1)}, u32[]{:S(2)}, u32[]{:S(2)}) collective-permute-start(bf16[1024,512]{1,0:T(8,128)(2,1)} %get-tuple-element.116.refs_4_.refs_8_), channel_id=1, source_target_pairs={{0,2},{1,3},{2,0},{3,1},{4,6},{5,7},{6,4},{7,5},{8,10},{9,11},{10,... | collective-permute-start | bytes 3145736 | tf_op jit(solution)/shard_map/ppermute | solution.py:648
  29.7 3.9 %collective-permute-start.4 = (bf16[2576,128]{1,0:T(8,128)(2,1)S(1)}, bf16[2576,128]{1,0:T(8,128)(2,1)S(1)}, u32[]{:S(2)}, u32[]{:S(2)}) collective-permute-start(bf16[2576,128]{1,0:T(8,128)(2,1)S(1)} %copy-done.1), channel_id=1, source_target_pairs={{0,1},{1,0},{2,3},{3,2},{4,5},{5,4},{6,7},{7,6},{8,9},{9,8},{10,11... | collective-permute-start | bytes 1978376 | tf_op jit(solution)/shard_map/ppermute | solution.py:648
  30.3 3.2 %collective-permute-start.5 = (bf16[2576,128]{1,0:T(8,128)(2,1)}, bf16[2576,128]{1,0:T(8,128)(2,1)S(1)}, u32[]{:S(2)}, u32[]{:S(2)}) collective-permute-start(bf16[2576,128]{1,0:T(8,128)(2,1)} %collective-permute-done.refs_10_.refs_14_.refs_18_.refs_6_.refs_17_.refs_21_.refs_8_), channel_id=1, source_target_pairs={{0,1},{1,0},{2,3},{3,2},{4,5},{5,4},{6,7},{7,6},{8,9},{9,8},{10,11... | collective-permute-start | bytes 1978376 | tf_op jit(solution)/shard_map/ppermute | solution.py:648
  30.4 3.1 %collective-permute-start.1 = (bf16[2,384,128]{2,1,0:T(8,128)(2,1)}, bf16[2,384,128]{2,1,0:T(8,128)(2,1)S(1)}, u32[]{:S(2)}, u32[]{:S(2)}) collective-permute-start(bf16[2,384,128]{2,1,0:T(8,128)(2,1)} %get-tuple-element.108), channel_id=1, source_target_pairs={{0,1},{1,0},{2,3},{3,2},{4,5},{5,4},{6,7},{7,6},{8,9},{9,8},{10,11... | collective-permute-start | bytes 589832 | tf_op jit(solution)/shard_map/ppermute | solution.py:648
  31.5 8.2 %copy-start.6 = (bf16[1024,512]{1,0:T(8,128)(2,1)S(1)}, bf16[1024,512]{1,0:T(8,128)(2,1)}, u32[]{:S(2)}) copy-start(bf16[1024,512]{1,0:T(8,128)(2,1)} %get-tuple-element.116.refs_4_.refs_8_) | copy-start | bytes 3145732
  34.5 5.3 %copy-start.3 = (bf16[1,32,89,512]{3,1,2,0:T(8,128)(2,1)S(1)}, bf16[1,32,89,512]{3,1,2,0:T(8,128)(2,1)}, u32[]{:S(2)}) copy-start(bf16[1,32,89,512]{3,1,2,0:T(8,128)(2,1)} %param.29) | copy-start | bytes 8749060
  39.8 14.4 %copy-start.5 = (bf16[512,3,128]{2,0,1:T(8,128)(2,1)S(1)}, bf16[512,3,128]{2,0,1:T(8,128)(2,1)}, u32[]{:S(2)}) copy-start(bf16[512,3,128]{2,0,1:T(8,128)(2,1)} %param.17) | copy-start | bytes 1179652
  39.8 16.3 %copy-start.13 = (bf16[512]{0:T(512)(128)(2,1)S(1)}, bf16[512]{0:T(512)(128)(2,1)}, u32[]{:S(2)}) copy-start(bf16[512]{0:T(512)(128)(2,1)} %param.26) | copy-start | bytes 3076
  54.2 2.7 %collective-permute-start.8 = (bf16[1024,512]{1,0:T(8,128)(2,1)S(1)}, bf16[1024,512]{1,0:T(8,128)(2,1)S(1)}, u32[]{:S(2)}, u32[]{:S(2)}) collective-permute-start(bf16[1024,512]{1,0:T(8,128)(2,1)S(1)} %collective-permute-done.6.refs_4_.refs_8_), channel_id=1, source_target_pairs={{0,1},{1,0},{2,3},{3,2},{4,5},{5,4},{6,7},{7,6},{8,9},{9,8},{10,11... | collective-permute-start | bytes 3145736 | tf_op jit(solution)/shard_map/ppermute | solution.py:648
  54.2 11.5 %collective-permute-start.9 = (bf16[3,512,128]{2,1,0:T(8,128)(2,1)S(1)}, bf16[3,512,128]{2,1,0:T(8,128)(2,1)S(1)}, u32[]{:S(2)}, u32[]{:S(2)}) collective-permute-start(bf16[3,512,128]{2,1,0:T(8,128)(2,1)S(1)} %bitcast.35), channel_id=1, source_target_pairs={{0,2},{1,3},{2,0},{3,1},{4,6},{5,7},{6,4},{7,5},{8,10},{9,11},{10,... | collective-permute-start | bytes 1179656 | tf_op jit(solution)/shard_map/ppermute | solution.py:648
  65.7 10.1 %collective-permute-start.13 = (bf16[2048,512]{1,0:T(8,128)(2,1)S(1)}, bf16[2048,512]{1,0:T(8,128)(2,1)S(1)}, u32[]{:S(2)}, u32[]{:S(2)}) collective-permute-start(bf16[2048,512]{1,0:T(8,128)(2,1)S(1)} %get-tuple-element.140), channel_id=1, source_target_pairs={{0,1},{1,0},{2,3},{3,2},{4,5},{5,4},{6,7},{7,6},{8,9},{9,8},{10,11... | collective-permute-start | bytes 6291464 | tf_op jit(solution)/shard_map/ppermute | solution.py:648
  72.7 3.1 %collective-permute-start.14 = (bf16[2,640,512]{2,1,0:T(8,128)(2,1)S(1)}, bf16[2,640,512]{2,1,0:T(8,128)(2,1)S(1)}, u32[]{:S(2)}, u32[]{:S(2)}) collective-permute-start(bf16[2,640,512]{2,1,0:T(8,128)(2,1)S(1)} %get-tuple-element.141), channel_id=1, source_target_pairs={{0,1},{1,0},{2,3},{3,2},{4,5},{5,4},{6,7},{7,6},{8,9},{9,8},{10,11... | collective-permute-start | bytes 3932168 | tf_op jit(solution)/shard_map/ppermute | solution.py:648
  73.2 6.9 %collective-permute-start.12 = (bf16[960,512]{1,0:T(8,128)(2,1)S(1)}, bf16[960,512]{1,0:T(8,128)(2,1)S(1)}, u32[]{:S(2)}, u32[]{:S(2)}) collective-permute-start(bf16[960,512]{1,0:T(8,128)(2,1)S(1)} %get-tuple-element.136), channel_id=1, source_target_pairs={{0,1},{1,0},{2,3},{3,2},{4,5},{5,4},{6,7},{7,6},{8,9},{9,8},{10,11... | collective-permute-start | bytes 2949128 | tf_op jit(solution)/shard_map/ppermute | solution.py:648
  73.3 10.1 %collective-permute-start.10 = (bf16[192,512]{1,0:T(8,128)(2,1)S(1)}, bf16[192,512]{1,0:T(8,128)(2,1)S(1)}, u32[]{:S(2)}, u32[]{:S(2)}) collective-permute-start(bf16[192,512]{1,0:T(8,128)(2,1)S(1)} %get-tuple-element.134), channel_id=1, source_target_pairs={{0,3},{1,2},{2,1},{3,0},{4,7},{5,6},{6,5},{7,4},{8,11},{9,10},{10,... | collective-permute-start | bytes 589832 | tf_op jit(solution)/shard_map/ppermute | solution.py:648
  75.0 9.7 %collective-permute-start.11 = (bf16[192,512]{1,0:T(8,128)(2,1)S(1)}, bf16[192,512]{1,0:T(8,128)(2,1)S(1)}, u32[]{:S(2)}, u32[]{:S(2)}) collective-permute-start(bf16[192,512]{1,0:T(8,128)(2,1)S(1)} %get-tuple-element.135), channel_id=1, source_target_pairs={{0,2},{1,3},{2,0},{3,1},{4,6},{5,7},{6,4},{7,5},{8,10},{9,11},{10,... | collective-permute-start | bytes 589832 | tf_op jit(solution)/shard_map/ppermute | solution.py:648
  76.6 21.3 %collective-permute-start.19 = (bf16[2,416,512]{2,1,0:T(8,128)(2,1)S(1)}, bf16[2,416,512]{2,1,0:T(8,128)(2,1)S(1)}, u32[]{:S(2)}, u32[]{:S(2)}) collective-permute-start(bf16[2,416,512]{2,1,0:T(8,128)(2,1)S(1)} %get-tuple-element.164), channel_id=1, source_target_pairs={{0,4},{4,0},{8,12},{12,8},{16,20},{20,16},{24,28},{28,24},{1,5},{5... | collective-permute-start | bytes 2555912 | tf_op jit(solution)/shard_map/ppermute | solution.py:648
  78.4 20.9 %collective-permute-start.20 = (bf16[2,416,512]{2,1,0:T(8,128)(2,1)S(1)}, bf16[2,416,512]{2,1,0:T(8,128)(2,1)S(1)}, u32[]{:S(2)}, u32[]{:S(2)}) collective-permute-start(bf16[2,416,512]{2,1,0:T(8,128)(2,1)S(1)} %get-tuple-element.166), channel_id=1, source_target_pairs={{0,8},{4,12},{8,0},{12,4},{16,24},{20,28},{24,16},{28,20},{1,9},{5... | collective-permute-start | bytes 2555912 | tf_op jit(solution)/shard_map/ppermute | solution.py:648
  84.7 20.5 %collective-permute-start.15 = (bf16[768,512]{1,0:T(8,128)(2,1)S(1)}, bf16[768,512]{1,0:T(8,128)(2,1)S(1)}, u32[]{:S(2)}, u32[]{:S(2)}) collective-permute-start(bf16[768,512]{1,0:T(8,128)(2,1)S(1)} %get-tuple-element.145.refs_23_.refs_2_), channel_id=1, source_target_pairs={{0,2},{1,3},{2,0},{3,1},{4,6},{5,7},{6,4},{7,5},{8,10},{9,11},{10,... | collective-permute-start | bytes 2359304 | tf_op jit(solution)/shard_map/ppermute | solution.py:648
  91.9 7.9 %collective-permute-start.16 = (bf16[1536,128]{1,0:T(8,128)(2,1)S(1)}, bf16[1536,128]{1,0:T(8,128)(2,1)S(1)}, u32[]{:S(2)}, u32[]{:S(2)}) collective-permute-start(bf16[1536,128]{1,0:T(8,128)(2,1)S(1)} %get-tuple-element.153), channel_id=1, source_target_pairs={{0,1},{1,0},{2,3},{3,2},{4,5},{5,4},{6,7},{7,6},{8,9},{9,8},{10,11... | collective-permute-start | bytes 1179656 | tf_op jit(solution)/shard_map/ppermute | solution.py:648
  91.9 7.9 %collective-permute-start.17 = (bf16[1536,128]{1,0:T(8,128)(2,1)S(1)}, bf16[1536,128]{1,0:T(8,128)(2,1)S(1)}, u32[]{:S(2)}, u32[]{:S(2)}) collective-permute-start(bf16[1536,128]{1,0:T(8,128)(2,1)S(1)} %get-tuple-element.154), channel_id=1, source_target_pairs={{0,1},{1,0},{2,3},{3,2},{4,5},{5,4},{6,7},{7,6},{8,9},{9,8},{10,11... | collective-permute-start | bytes 1179656 | tf_op jit(solution)/shard_map/ppermute | solution.py:648
  97.9 1.9 %collective-permute-start.18 = (f32[128,128]{1,0:T(8,128)S(1)}, f32[128,128]{1,0:T(8,128)S(1)}, u32[]{:S(2)}, u32[]{:S(2)}) collective-permute-start(f32[128,128]{1,0:T(8,128)S(1)} %get-tuple-element.163.refs_6_), channel_id=1, source_target_pairs={{0,1},{1,0},{2,3},{3,2},{4,5},{5,4},{6,7},{7,6},{8,9},{9,8},{10,11... | collective-permute-start | bytes 196616 | tf_op jit(solution)/shard_map/ppermute | solution.py:648
  100.0 12.9 %collective-permute-start.24 = (bf16[1664,128]{1,0:T(8,128)(2,1)S(1)}, bf16[1664,128]{1,0:T(8,128)(2,1)S(1)}, u32[]{:S(2)}, u32[]{:S(2)}) collective-permute-start(bf16[1664,128]{1,0:T(8,128)(2,1)S(1)} %get-tuple-element.173), channel_id=1, source_target_pairs={{0,2},{1,3},{2,0},{3,1},{4,6},{5,7},{6,4},{7,5},{8,10},{9,11},{10,... | collective-permute-start | bytes 1277960 | tf_op jit(solution)/shard_map/ppermute | solution.py:648
  101.6 11.5 %collective-permute-start.22 = (bf16[2,208,512]{2,1,0:T(8,128)(2,1)S(1)}, bf16[2,208,512]{2,1,0:T(8,128)(2,1)S(1)}, u32[]{:S(2)}, u32[]{:S(2)}) collective-permute-start(bf16[2,208,512]{2,1,0:T(8,128)(2,1)S(1)} %get-tuple-element.170), channel_id=1, source_target_pairs={{0,8},{4,12},{8,0},{12,4},{16,24},{20,28},{24,16},{28,20},{1,9},{5... | collective-permute-start | bytes 1277960 | tf_op jit(solution)/shard_map/ppermute | solution.py:648
  103.1 10.9 %collective-permute-start.23 = (bf16[2,208,512]{2,1,0:T(8,128)(2,1)S(1)}, bf16[2,208,512]{2,1,0:T(8,128)(2,1)S(1)}, u32[]{:S(2)}, u32[]{:S(2)}) collective-permute-start(bf16[2,208,512]{2,1,0:T(8,128)(2,1)S(1)} %get-tuple-element.172), channel_id=1, source_target_pairs={{0,4},{4,0},{8,12},{12,8},{16,20},{20,16},{24,28},{28,24},{1,5},{5... | collective-permute-start | bytes 1277960 | tf_op jit(solution)/shard_map/ppermute | solution.py:648
  105.3 24.6 %collective-permute-start.21 = (bf16[1536,512]{1,0:T(8,128)(2,1)S(1)}, bf16[1536,512]{1,0:T(8,128)(2,1)S(1)}, u32[]{:S(2)}, u32[]{:S(2)}) collective-permute-start(bf16[1536,512]{1,0:T(8,128)(2,1)S(1)} %pair.2.refs_4_), channel_id=1, source_target_pairs={{0,1},{1,0},{2,3},{3,2},{4,5},{5,4},{6,7},{7,6},{8,9},{9,8},{10,11... | collective-permute-start | bytes 4718600 | tf_op jit(solution)/shard_map/ppermute | solution.py:648
  114.3 10.1 %collective-permute-start.25 = (bf16[416,512]{1,0:T(8,128)(2,1)S(1)}, bf16[416,512]{1,0:T(8,128)(2,1)S(1)}, u32[]{:S(2)}, u32[]{:S(2)}) collective-permute-start(bf16[416,512]{1,0:T(8,128)(2,1)S(1)} %get-tuple-element.176), channel_id=1, source_target_pairs={{0,2},{1,3},{2,0},{3,1},{4,6},{5,7},{6,4},{7,5},{8,10},{9,11},{10,... | collective-permute-start | bytes 1277960 | tf_op jit(solution)/shard_map/ppermute | solution.py:648
  115.1 5.8 %collective-permute-start.26 = (bf16[832,128]{1,0:T(8,128)(2,1)S(1)}, bf16[832,128]{1,0:T(8,128)(2,1)S(1)}, u32[]{:S(2)}, u32[]{:S(2)}) collective-permute-start(bf16[832,128]{1,0:T(8,128)(2,1)S(1)} %get-tuple-element.177), channel_id=1, source_target_pairs={{0,4},{4,0},{8,12},{12,8},{16,20},{20,16},{24,28},{28,24},{1,5},{5... | collective-permute-start | bytes 638984 | tf_op jit(solution)/shard_map/ppermute | solution.py:648
  124.4 20.7 %collective-permute-start.27 = (bf16[720,512]{1,0:T(8,128)(2,1)S(1)}, bf16[720,512]{1,0:T(8,128)(2,1)S(1)}, u32[]{:S(2)}, u32[]{:S(2)}) collective-permute-start(bf16[720,512]{1,0:T(8,128)(2,1)S(1)} %get-tuple-element.180.refs_2_), channel_id=1, source_target_pairs={{0,2},{1,3},{2,0},{3,1},{4,6},{5,7},{6,4},{7,5},{8,10},{9,11},{10,... | collective-permute-start | bytes 2211848 | tf_op jit(solution)/shard_map/ppermute | solution.py:648
  125.7 19.3 %collective-permute-start.28 = (bf16[416,512]{1,0:T(8,128)(2,1)S(1)}, bf16[416,512]{1,0:T(8,128)(2,1)S(1)}, u32[]{:S(2)}, u32[]{:S(2)}) collective-permute-start(bf16[416,512]{1,0:T(8,128)(2,1)S(1)} %sums.3.refs_6_.refs_2_), channel_id=1, source_target_pairs={{0,16},{4,20},{8,24},{12,28},{16,0},{20,4},{24,8},{28,12},{1,17},{... | collective-permute-start | bytes 1277960 | tf_op jit(solution)/shard_map/ppermute | solution.py:648
  128.3 9.1 %collective-permute-start.29 = (bf16[416,128]{1,0:T(8,128)(2,1)S(1)}, bf16[416,128]{1,0:T(8,128)(2,1)S(1)}, u32[]{:S(2)}, u32[]{:S(2)}) collective-permute-start(bf16[416,128]{1,0:T(8,128)(2,1)S(1)} %get-tuple-element.181), channel_id=1, source_target_pairs={{0,8},{4,12},{8,0},{12,4},{16,24},{20,28},{24,16},{28,20},{1,9},{5... | collective-permute-start | bytes 319496 | tf_op jit(solution)/shard_map/ppermute | solution.py:648
  145.2 8.9 %collective-permute-start.30 = (bf16[1440,512]{1,0:T(8,128)(2,1)S(1)}, bf16[1440,512]{1,0:T(8,128)(2,1)S(1)}, u32[]{:S(2)}, u32[]{:S(2)}) collective-permute-start(bf16[1440,512]{1,0:T(8,128)(2,1)S(1)} %pair.3.refs_4_), channel_id=1, source_target_pairs={{0,1},{1,0},{2,3},{3,2},{4,5},{5,4},{6,7},{7,6},{8,9},{9,8},{10,11... | collective-permute-start | bytes 4423688 | tf_op jit(solution)/shard_map/ppermute | solution.py:648
  145.3 8.7 %collective-permute-start.31 = (bf16[416,128]{1,0:T(8,128)(2,1)S(1)}, bf16[416,128]{1,0:T(8,128)(2,1)S(1)}, u32[]{:S(2)}, u32[]{:S(2)}) collective-permute-start(bf16[416,128]{1,0:T(8,128)(2,1)S(1)} %sums.4.refs_4_.refs_2_), channel_id=1, source_target_pairs={{0,16},{4,20},{8,24},{12,28},{16,0},{20,4},{24,8},{28,12},{1,17},{... | collective-permute-start | bytes 319496 | tf_op jit(solution)/shard_map/ppermute | solution.py:648
  145.4 15.3 %collective-permute-start.34 = (bf16[208,512]{1,0:T(8,128)(2,1)S(1)}, bf16[208,512]{1,0:T(8,128)(2,1)S(1)}, u32[]{:S(2)}, u32[]{:S(2)}) collective-permute-start(bf16[208,512]{1,0:T(8,128)(2,1)S(1)} %get-tuple-element.182.refs_4_.refs_2_), channel_id=1, source_target_pairs={{0,8},{4,12},{8,0},{12,4},{16,24},{20,28},{24,16},{28,20},{1,9},{5... | collective-permute-start | bytes 638984 | tf_op jit(solution)/shard_map/ppermute | solution.py:648
  149.4 11.2 %collective-permute-start.35 = (bf16[208,512]{1,0:T(8,128)(2,1)S(1)}, bf16[208,512]{1,0:T(8,128)(2,1)S(1)}, u32[]{:S(2)}, u32[]{:S(2)}) collective-permute-start(bf16[208,512]{1,0:T(8,128)(2,1)S(1)} %get-tuple-element.183.refs_4_), channel_id=1, source_target_pairs={{0,4},{4,0},{8,12},{12,8},{16,20},{20,16},{24,28},{28,24},{1,5},{5... | collective-permute-start | bytes 638984 | tf_op jit(solution)/shard_map/ppermute | solution.py:648
  154.0 4.8 %collective-permute-start.32 = (bf16[416,128]{1,0:T(8,128)(2,1)S(1)}, bf16[416,128]{1,0:T(8,128)(2,1)S(1)}, u32[]{:S(2)}, u32[]{:S(2)}) collective-permute-start(bf16[416,128]{1,0:T(8,128)(2,1)S(1)} %sums.5.refs_6_.refs_2_), channel_id=1, source_target_pairs={{0,8},{4,12},{8,0},{12,4},{16,24},{20,28},{24,16},{28,20},{1,9},{5... | collective-permute-start | bytes 319496 | tf_op jit(solution)/shard_map/ppermute | solution.py:648
  160.7 12.6 %collective-permute-start.36 = (bf16[416,512]{1,0:T(8,128)(2,1)S(1)}, bf16[416,512]{1,0:T(8,128)(2,1)S(1)}, u32[]{:S(2)}, u32[]{:S(2)}) collective-permute-start(bf16[416,512]{1,0:T(8,128)(2,1)S(1)} %get-tuple-element.184.refs_2_.refs_6_), channel_id=1, source_target_pairs={{0,4},{4,0},{8,12},{12,8},{16,20},{20,16},{24,28},{28,24},{1,5},{5... | collective-permute-start | bytes 1277960 | tf_op jit(solution)/shard_map/ppermute | solution.py:648
  162.3 11.0 %collective-permute-start.37 = (bf16[416,512]{1,0:T(8,128)(2,1)S(1)}, bf16[416,512]{1,0:T(8,128)(2,1)S(1)}, u32[]{:S(2)}, u32[]{:S(2)}) collective-permute-start(bf16[416,512]{1,0:T(8,128)(2,1)S(1)} %get-tuple-element.185.refs_4_), channel_id=1, source_target_pairs={{0,8},{4,12},{8,0},{12,4},{16,24},{20,28},{24,16},{28,20},{1,9},{5... | collective-permute-start | bytes 1277960 | tf_op jit(solution)/shard_map/ppermute | solution.py:648
  162.5 13.2 %collective-permute-start.33 = (bf16[832,128]{1,0:T(8,128)(2,1)S(1)}, bf16[832,128]{1,0:T(8,128)(2,1)S(1)}, u32[]{:S(2)}, u32[]{:S(2)}) collective-permute-start(bf16[832,128]{1,0:T(8,128)(2,1)S(1)} %joins.2.refs_6_.refs_2_), channel_id=1, source_target_pairs={{0,4},{4,0},{8,12},{12,8},{16,20},{20,16},{24,28},{28,24},{1,5},{5... | collective-permute-start | bytes 638984 | tf_op jit(solution)/shard_map/ppermute | solution.py:648
  (4 other events, 5.8 us)
